TPU v7x, 128 devices: a whole 4x4x4 slice. The times are simulated.
128 devices in a mesh: blk: 4 (over x_lo, core), tensor: 32 (over y, z, x_hi).
Axes of the slice: x: 4 (x_hi: 2, x_lo: 2; x = x_hi * 2 + x_lo), y: 4, z: 4, core: 2. Of those that a mesh axis runs over, the one named last changes fastest.
Arguments:
- tokens: bfloat16 [4096, 8192], P('tensor', 'blk'), may hold values from -6 to 6
- norm_gain: float32 [8192], P('blk'), may hold values from 0.1 to 1.9
- segment_ids: int32 [4096], replicated, may hold values from 0 to 15, never falling along the last dimension, each value on 1 to 2049 neighbouring positions
- w_query: bfloat16 [8192, 8192], P('blk', 'tensor'), may hold values from -0.0625 to 0.0625
- key_weight: bfloat16 [8192, 1024], P('blk'), may hold values from -0.0625 to 0.0625
- value_weight: bfloat16 [8192, 1024], P('blk'), may hold values from -0.0625 to 0.0625
- w_output: bfloat16 [8192, 8192], P('tensor', 'blk'), may hold values from -0.25 to 0.25
Outputs:
- block_out: bfloat16 [4096, 8192], P('tensor', 'blk')
Inputs may be any that keep to these rules, and one draw needn't show every extreme that they name: `segment_ids`: segment ids never fall along the tokens; each rollout holds 1 to 2049 consecutive tokens and one holds exactly 2049.
All inputs are finite; a program needn't handle non-finite values.
Results may differ from a plain program's by a relative error of at most 0.04.
Values may be sent and summed in bfloat16 or wider, within the bound.
No kernel may reach another device: no remote copies, remote signals or barrier semaphores. Data moves between devices by JAX's collectives and lax.ppermute only.
A program may use at most 128 MiB of HBM per device.

v0:
```python
import math

import jax
import jax.numpy as jnp
from jax import lax
from jax.sharding import PartitionSpec as P

MODEL_WIDTH = 8192
QUERY_HEADS = 64
KEY_VALUE_HEADS = 8
HEAD_SIZE = 128


norm_eps = 1e-05
rope_base = 500000.0


def positions_of(segment_ids):
    length = segment_ids.shape[0]
    indices = jnp.arange(length, dtype=jnp.int32)
    changed = jnp.concatenate([jnp.ones((1,), jnp.bool_), segment_ids[1:] != segment_ids[:-1]])
    starts = lax.cummax(jnp.where(changed, indices, jnp.int32(0)), axis=0)
    return (indices - starts).astype(jnp.float32)


def rotate(values, places):
    half_dim = values.shape[-1] // 2
    freqs = jnp.exp(
        jnp.arange(half_dim, dtype=jnp.float32)
        * jnp.float32(-2.0 * math.log(rope_base) / values.shape[-1])
    )
    angles = places[:, None] * freqs[None, :]
    cosine = jnp.cos(angles)[:, None, :]
    sine = jnp.sin(angles)[:, None, :]
    first = values[..., :half_dim]
    second = values[..., half_dim:]
    return jnp.concatenate(
        [first * cosine - second * sine, second * cosine + first * sine], axis=-1
    )


def shards(tokens, norm_gain, segment_ids, w_query, key_weight, value_weight, w_output):
    shard_index = lax.axis_index("tensor")
    block_index = lax.axis_index("blk")
    block_count = lax.axis_size("blk")
    floats = tokens.astype(jnp.float32)
    squares = lax.psum(jnp.sum(floats * floats, axis=-1), "blk")
    scale_rows = lax.rsqrt(squares / MODEL_WIDTH + norm_eps)[:, None]
    normalized_input = (floats * scale_rows * norm_gain[None, :]).astype(jnp.bfloat16)
    group_rows = lax.all_gather(normalized_input, "tensor", axis=0, tiled=True)
    heads_per_device = w_query.shape[1] // HEAD_SIZE
    shared_head = shard_index * heads_per_device // (QUERY_HEADS // KEY_VALUE_HEADS)
    key_cols = lax.dynamic_slice_in_dim(key_weight, shared_head * HEAD_SIZE, HEAD_SIZE, 1)
    value_cols = lax.dynamic_slice_in_dim(value_weight, shared_head * HEAD_SIZE, HEAD_SIZE, 1)
    joined = jnp.concatenate([w_query, key_cols, value_cols], axis=1)
    row_total = group_rows.shape[0]
    query_rows = row_total // block_count
    projected = lax.psum_scatter(
        jnp.dot(group_rows, joined, preferred_element_type=jnp.float32).astype(jnp.bfloat16),
        "blk",
        scatter_dimension=0,
        tiled=True,
    ).astype(jnp.float32)
    places_all = positions_of(segment_ids)
    first_row = block_index * query_rows
    places = lax.dynamic_slice_in_dim(places_all, first_row, query_rows, 0)
    query_part = projected[:, : heads_per_device * HEAD_SIZE].reshape(
        query_rows, heads_per_device, HEAD_SIZE
    )
    queries = rotate(query_part, places).astype(jnp.bfloat16)
    key_part = projected[
        :, heads_per_device * HEAD_SIZE : (heads_per_device + 1) * HEAD_SIZE
    ].reshape(query_rows, 1, HEAD_SIZE)
    own_keys = rotate(key_part, places).reshape(query_rows, HEAD_SIZE).astype(jnp.bfloat16)
    own_values = projected[:, (heads_per_device + 1) * HEAD_SIZE :].astype(jnp.bfloat16)
    all_keys, all_values = (
        lax.all_gather(own_keys, "blk", axis=0, tiled=True),
        lax.all_gather(own_values, "blk", axis=0, tiled=True),
    )
    query_index = first_row + jnp.arange(query_rows, dtype=jnp.int32)
    key_index = jnp.arange(row_total, dtype=jnp.int32)
    query_segs = lax.dynamic_slice_in_dim(segment_ids, first_row, query_rows, 0)
    allowed = (query_segs[:, None] == segment_ids[None, :]) & (
        key_index[None, :] <= query_index[:, None]
    )
    score_scale = float(HEAD_SIZE) ** (-0.5)
    scores = (
        jnp.einsum("qhd,kd->hqk", queries, all_keys, preferred_element_type=jnp.float32)
        * score_scale
    )
    masked = jnp.where(allowed[None], scores, -jnp.inf)
    highest = jnp.max(masked, axis=-1, keepdims=True)
    probs = jnp.where(allowed[None], jnp.exp(masked - highest), jnp.float32(0.0))
    totals = jnp.sum(probs, axis=-1, keepdims=True)
    mixed = jnp.einsum(
        "hqk,kd->qhd", probs.astype(jnp.bfloat16), all_values, preferred_element_type=jnp.float32
    )
    mixed = mixed / jnp.transpose(totals, (1, 0, 2))
    attended = mixed.reshape(query_rows, heads_per_device * HEAD_SIZE).astype(jnp.bfloat16)
    partial_out = jnp.dot(
        lax.all_gather(attended, "blk", axis=0, tiled=True),
        w_output,
        preferred_element_type=jnp.float32,
    )
    summed = lax.psum_scatter(
        partial_out.astype(jnp.bfloat16), "tensor", scatter_dimension=0, tiled=True
    )
    return summed


def solution(mesh):
    placed = (
        P("tensor", "blk"),
        P("blk"),
        P(),
        P("blk", "tensor"),
        P("blk", None),
        P("blk", None),
        P("tensor", "blk"),
    )
    return jax.shard_map(
        shards, mesh=mesh, in_specs=placed, out_specs=P("tensor", "blk"), check_vma=False
    )
```

profile of v0, /device:TPU:96, one launch (start us, length us, event | category | flops | bytes accessed | tf_op | source)
XLA Modules:
  0.0 699.5 jit_solution(16983838502382211761)
XLA Ops:
  6.5 0.0 copy-start
  6.5 0.0 all-gather.6.cloned.1.call-start
  6.5 1.3 fusion.24
  7.9 6.9 psum.7
  14.8 2.0 fusion.26
  16.8 0.0 all-gather.6.cloned.1.call-update
  16.8 0.0 reduce-scatter.3.cloned.1.call-start
  16.9 1.3 constant_dynamic-slice_fusion
  18.2 156.6 %all-gather.6.cloned.1.call-done = bf16[4096,2048]{1,0:T(8,128)(2,1)} async-done(((bf16[128,2048]{1,0:T(8,128)(2,1)}), bf16[4096,2048]{1,0:T(8,128)(2,1)}) %all-gather.6.cloned.1.call-update) | async-done | bytes 16777232 | tf_op jit(solution)/shard_map/all_gather | solution.py:50
  174.8 0.0 copy-start.2
  174.8 14.2 %convolution_convert_fusion.1 = bf16[4096,512]{0,1:T(8,128)(2,1)} fusion(bf16[4096,2048]{1,0:T(8,128)(2,1)} %all-gather.6.cloned.1.call-done, bf16[2048,128]{1,0:T(8,128)(2,1)S(1)} %get-tuple-element.15, bf16[2048,128]{1,0:T(8,128)(2,1)S(1)} %get-tuple-element.16, bf16[2048,256]{1,0:T(8,128)(2,1)} %param.10), kind=kOutput, calls=%fused_computation.12 | convolution fusion | flops 8598323200 | bytes 23068672 | tf_op jit(solution)/shard_map/dot_general | solution.py:59
  189.0 0.0 reduce-scatter.3.cloned.1.call-update
  189.0 0.0 all-gather.12.cloned.1.call-start
  189.0 0.0 copy-done.2
  189.1 0.1 slice_compare_fusion
  189.1 0.1 add_select_fusion
  189.2 0.3 reduce-window.9
  189.5 0.1 slice.49
  189.6 0.1 reduce-window.12
  189.7 0.1 slice_reduce_fusion
  189.8 0.1 maximum_bitcast_fusion
  189.9 42.6 %reduce-scatter.3.cloned.1.call-done = bf16[1024,512]{0,1:T(8,128)(2,1)} async-done(((bf16[4096,512]{0,1:T(8,128)(2,1)}), bf16[1024,512]{0,1:T(8,128)(2,1)}) %reduce-scatter.3.cloned.1.call-update) | async-done | bytes 1048592 | tf_op jit(solution)/shard_map/reduce_scatter | solution.py:58
  232.4 0.0 copy-start.1
  232.4 1.5 convert_element_type.36
  234.0 1.2 fusion.40
  235.2 0.7 pad_maximum_fusion.1
  235.9 0.0 all-gather.12.cloned.1.call-update
  236.0 0.0 all-gather.8.cloned.1.call-start
  236.0 3.1 multiply_cosine_fusion
  239.1 4.6 fusion.6
  243.7 0.0 copy-done.1
  243.7 0.1 slice.52
  243.8 1.1 fusion.51
  244.9 1.4 copy.26
  246.3 2.4 copy.25
  248.7 0.7 slice.46
  249.4 0.0 all-gather.8.cloned.1.call-update
  249.4 0.2 all-gather.10.cloned.1.call-start
  249.7 1.8 subtract_convert_fusion
  251.5 6.2 all-gather.12.cloned.1.call-done
  257.7 22.0 %fusion.52 = (f32[2,1024]{1,0:T(2,128)S(1)}, bf16[2,1024,4096]{1,2,0:T(8,128)(2,1)}) fusion(pred[1024,4096]{0,1:T(8,128)(4,1)} %fusion.6, bf16[4096,1,128]{0,2,1:T(8,128)(2,1)} %all-gather.12.cloned.1.call-done, bf16[1024,2,64]{2,0,1:T(8,128)(2,1)S(1)} %get-tuple-element.6, bf16[1024,2,64]{2,0,1:T(8,128)(2,1)S(1)} %get-tuple-element.5), kind=kOutput, calls=%fused_computation.66 | convolution fusion | flops 2198867968 | bytes 22552576 | tf_op jit(solution)/shard_map/sub | solution.py:93
  279.8 1.3 all-gather.8.cloned.1.call-done
  281.0 9.2 %fusion.21 = bf16[1024,2,128]{0,2,1:T(8,128)(2,1)} fusion(bf16[2,1024,4096]{1,2,0:T(8,128)(2,1)} %get-tuple-element.14, bf16[4096,128]{0,1:T(8,128)(2,1)} %all-gather.8.cloned.1.call-done, f32[1024,2]{0,1:T(2,128)S(1)} %bitcast.56), kind=kOutput, calls=%fused_computation.23 | convolution fusion | flops 2148007936 | bytes 18358272 | tf_op jit(solution)/shard_map/hqk,kd->qhd/dot_general | solution.py:95
  290.3 0.0 all-gather.10.cloned.1.call-update
  290.3 0.0 reduce-scatter.5.cloned.1.call-start
  290.4 30.0 %all-gather.10.cloned.1.call-done = bf16[4096,256]{0,1:T(8,128)(2,1)} async-done(((bf16[1024,256]{0,1:T(8,128)(2,1)}), bf16[4096,256]{0,1:T(8,128)(2,1)}) %all-gather.10.cloned.1.call-update) | async-done | bytes 2097168 | tf_op jit(solution)/shard_map/all_gather | solution.py:101
  320.3 0.0 copy-done
  320.3 9.7 %convolution_convert_fusion = bf16[4096,2048]{1,0:T(8,128)(2,1)} fusion(bf16[4096,256]{0,1:T(8,128)(2,1)} %all-gather.10.cloned.1.call-done, bf16[256,2048]{1,0:T(8,128)(2,1)S(1)} %copy-done), kind=kOutput, calls=%fused_computation.11 | convolution fusion | flops 4303355904 | bytes 19922944 | tf_op jit(solution)/shard_map/dot_general | solution.py:100
  330.1 0.0 reduce-scatter.5.cloned.1.call-update
  330.1 362.6 %reduce-scatter.5.cloned.1.call-done = bf16[128,2048]{1,0:T(8,128)(2,1)} async-done(((bf16[4096,2048]{1,0:T(8,128)(2,1)}), bf16[128,2048]{1,0:T(8,128)(2,1)}) %reduce-scatter.5.cloned.1.call-update) | async-done | bytes 524304 | tf_op jit(solution)/shard_map/reduce_scatter | solution.py:105
  (6 shorter events, 0.1 us)
Async XLA Ops:
  6.5 313.8 %copy-start = (bf16[256,2048]{1,0:T(8,128)(2,1)S(1)}, bf16[256,2048]{1,0:T(8,128)(2,1)}, u32[]{:S(2)}) copy-start(bf16[256,2048]{1,0:T(8,128)(2,1)} %param.13) | copy-start | bytes 3145732
  6.5 168.2 %all-gather.6.cloned.1.call-start = ((), (), s32[]{:S(2)}) async-start(), calls=%async_computation.2 | async-start | bytes 17301504 | tf_op jit(solution)/shard_map/all_gather | solution.py:50
  16.8 215.6 %reduce-scatter.3.cloned.1.call-start = ((), (), s32[]{:S(2)}) async-start(), calls=%async_computation.3 | async-start | bytes 5242880 | tf_op jit(solution)/shard_map/reduce_scatter | solution.py:58
  174.8 14.3 %copy-start.2 = (s32[4096]{0:T(1024)S(1)}, s32[4096]{0:T(1024)}, u32[]{:S(2)}) copy-start(s32[4096]{0:T(1024)} %param.9) | copy-start | bytes 49156
  189.0 68.8 %all-gather.12.cloned.1.call-start = ((), (), s32[]{:S(2)}) async-start(), calls=%async_computation.7 | async-start | bytes 1310720 | tf_op jit(solution)/shard_map/all_gather | solution.py:77
  232.4 11.3 %copy-start.1 = (bf16[1024,512]{0,1:T(8,128)(2,1)S(1)}, bf16[1024,512]{0,1:T(8,128)(2,1)}, u32[]{:S(2)}) copy-start(bf16[1024,512]{0,1:T(8,128)(2,1)} %reduce-scatter.3.cloned.1.call-done) | copy-start | bytes 3145732
  236.0 45.1 %all-gather.8.cloned.1.call-start = ((), (), s32[]{:S(2)}) async-start(), calls=%async_computation.4 | async-start | bytes 1310720 | tf_op jit(solution)/shard_map/all_gather | solution.py:78
  249.4 70.9 %all-gather.10.cloned.1.call-start = ((), (), s32[]{:S(2)}) async-start(), calls=%async_computation.5 | async-start | bytes 2621440 | tf_op jit(solution)/shard_map/all_gather | solution.py:101
  290.3 402.4 %reduce-scatter.5.cloned.1.call-start = ((), (), s32[]{:S(2)}) async-start(), calls=%async_computation.6 | async-start | bytes 17301504 | tf_op jit(solution)/shard_map/reduce_scatter | solution.py:105
Sparse Core Ops, SparseCore 0:
  16.9 157.7 all-gather.5
  189.1 43.2 reduce-scatter.2
  236.1 21.6 all-gather.11
  259.4 21.6 all-gather.7
  290.4 29.8 all-gather.9
  330.2 362.4 reduce-scatter.4
where the time goes:
time: 705 us; the launch traced here: 700 us
  waiting for transfers between devices  599 us (85%)
  matrix products  55.2 us (8%)
  other arithmetic  16.9 us (2%)
  between operations  13.6 us (2%)
  local copies, waits for them, and re-layouts  7.23 us (1%)
    reduce_scatter x1, waiting for transfers between devices, shards(): lax.psum_scatter(partial_out.astype(jnp.bfloat16), 'tensor', scatter_dime...  363 us
    all_gather x1, waiting for transfers between devices, shards(): group_rows = lax.all_gather(normalized_input, 'tensor', axis=0, tiled=True)  157 us
    reduce_scatter x1, waiting for transfers between devices, shards(): lax.psum_scatter(jnp.dot(group_rows, joined, preferred_element_type=jnp.f...  42.6 us
    all_gather x1, waiting for transfers between devices, shards(): lax.all_gather(attended, 'blk', axis=0, tiled=True)  30 us
    sub x1, matrix products, shards(): masked - highest  22 us
    dot_general x1, matrix products, shards(): jnp.dot(group_rows, joined, preferred_element_type=jnp.float32)  14.2 us
  transfers between devices with their start and end apart: 6, of which 6 were waited for; matrix products, arithmetic and copies ran while one was open for 6% of the time, Pallas kernels for 0%

commit v1 on v0

v1 whole, which is shorter than its diff:
```python
import functools
import math

import jax
import jax.numpy as jnp
from jax import lax
from jax.experimental import pallas as pl
from jax.experimental.pallas import tpu as pltpu
from jax.sharding import Mesh, PartitionSpec as P

MODEL_WIDTH = 8192
QUERY_HEADS = 64
KEY_VALUE_HEADS = 8
HEAD_SIZE = 128
TOKENS = 4096
SEGMENTS = 16
GROUP_ROWS = 1024
TILE = 256

norm_eps = 1e-05
rope_base = 500000.0
MASKED = -1e30

f32 = jnp.float32
bf16 = jnp.bfloat16


def receive(value, axis, step):
    n = lax.axis_size(axis)
    return lax.ppermute(value, axis, [((i + step) % n, i) for i in range(n)])


def attention_kernel(scalars, q_ref, index_ref, start_ref, k0, k1, k2, v0, v1, v2, out_ref):
    dz = pl.program_id(0)
    y, z, xh = scalars[4], scalars[5], scalars[6]
    tile_low = scalars[dz]
    tile_high = y * 4 + lax.rem(z + dz, 4)
    q = jnp.concatenate([q_ref[:, :HEAD_SIZE], q_ref[:, HEAD_SIZE:]], axis=0)
    q_index = jnp.concatenate([index_ref[...], index_ref[...]], axis=0)
    q_start = jnp.concatenate([start_ref[...], start_ref[...]], axis=0)
    lane = lax.broadcasted_iota(jnp.int32, (1, TILE), 1) ^ (xh * 128)

    def step(k_ref, v_ref, tile, carry):
        top, total, acc = carry
        slot = lax.rem(lax.rem(tile, 4) - z + 4, 4) * TILE
        slot = pl.multiple_of(slot, TILE)
        k = k_ref[pl.ds(slot, TILE), :]
        v = v_ref[pl.ds(slot, TILE), :]
        s = lax.dot_general(q, k, (((1,), (1,)), ((), ())), preferred_element_type=f32)
        k_index = lane + tile * TILE
        allowed = (k_index <= q_index) & (k_index >= q_start)
        s = jnp.where(allowed, s, MASKED)
        new_top = jnp.maximum(top, jnp.max(s, axis=1, keepdims=True))
        p = jnp.exp2(s - new_top)
        decay = jnp.exp2(top - new_top)
        total = total * decay + jnp.sum(p, axis=1, keepdims=True)
        acc = acc * decay + jnp.dot(p.astype(bf16), v, preferred_element_type=f32)
        return new_top, total, acc

    carry = (
        jnp.full((2 * TILE, 1), MASKED, f32),
        jnp.zeros((2 * TILE, 1), f32),
        jnp.zeros((2 * TILE, HEAD_SIZE), f32),
    )
    for back, k_ref, v_ref in ((2, k2, v2), (1, k1, v1), (0, k0, v0)):
        first = (y - back) * 4
        low = jnp.maximum(tile_low, first)
        high = jnp.minimum(tile_high, first + 3)
        carry = lax.fori_loop(
            low, high + 1, functools.partial(step, k_ref, v_ref), carry
        )
    top, total, acc = carry
    result = (acc / total).astype(bf16)
    out_ref[:, :HEAD_SIZE] = result[:TILE]
    out_ref[:, HEAD_SIZE:] = result[TILE:]


def attention(scalars, q, index, start, keys, values):
    whole = pl.BlockSpec((GROUP_ROWS, HEAD_SIZE), lambda i: (0, 0))
    column = pl.BlockSpec((TILE, 1), lambda i: (i, 0))
    rows = pl.BlockSpec((TILE, 2 * HEAD_SIZE), lambda i: (i, 0))
    return pl.pallas_call(
        attention_kernel,
        grid=(4,),
        out_shape=jax.ShapeDtypeStruct((GROUP_ROWS, 2 * HEAD_SIZE), bf16),
        in_specs=[pl.BlockSpec(memory_space=pltpu.SMEM), rows, column, column] + [whole] * 6,
        out_specs=rows,
        compiler_params=pltpu.CompilerParams(vmem_limit_bytes=32 * 2**20),
        cost_estimate=pl.CostEstimate(flops=3 * 10**9, bytes_accessed=4 * 2**20, transcendentals=4 * 10**6),
    )(scalars, q, index, start, *keys, *values)


def rotate(values, cosine, sine):
    half = HEAD_SIZE // 2
    first, second = values[..., :half], values[..., half:]
    return jnp.concatenate([first * cosine - second * sine, second * cosine + first * sine], axis=-1)


def shards(tokens, norm_gain, segment_ids, w_query, key_weight, value_weight, w_output):
    xl, c, y, z, xh = (lax.axis_index(a) for a in ("xl", "c", "y", "z", "xh"))

    floats = tokens.astype(f32)
    scaled = (floats * norm_gain[None, :]).astype(bf16)
    x = {(0, 0): scaled}
    x[1, 0] = receive(scaled, "z", 1)
    x[3, 0] = receive(scaled, "z", -1)
    x[0, 1] = receive(scaled, "xh", 1)
    wq = {0: w_query}
    wq[1] = receive(w_query, "y", 1)
    wq[3] = receive(w_query, "y", -1)
    x[1, 1] = receive(x[0, 1], "z", 1)
    x[3, 1] = receive(x[0, 1], "z", -1)
    for dx in (0, 1):
        x[2, dx] = jnp.concatenate(
            [receive(x[1, dx][:64], "z", 1), receive(x[3, dx][64:], "z", -1)], axis=0
        )
    half = MODEL_WIDTH // 8
    wq[2] = jnp.concatenate([receive(wq[1][:half], "y", 1), receive(wq[3][half:], "y", -1)], axis=0)
    gathered = jnp.concatenate([x[dz, dx] for dz in range(4) for dx in range(2)], axis=0)

    squares = lax.psum(jnp.sum(floats * floats, axis=-1), ("xl", "c"))
    own_scale = lax.rsqrt(squares / MODEL_WIDTH + norm_eps)
    scale = lax.all_gather(own_scale, ("z", "xh"), axis=0, tiled=True).reshape(4, 2, 128)

    def relative(by_place):
        turned = lax.dynamic_slice_in_dim(jnp.concatenate([by_place, by_place], axis=0), z, 4, 0)
        return jnp.where(xh == 0, turned, turned[:, ::-1]).reshape(GROUP_ROWS)

    scale = relative(scale)[:, None]
    own_rows = lax.dynamic_slice_in_dim(segment_ids, y * GROUP_ROWS, GROUP_ROWS, 0)
    segments = relative(own_rows.reshape(4, 2, 128))
    index = relative((y * GROUP_ROWS + jnp.arange(GROUP_ROWS, dtype=jnp.int32)).reshape(4, 2, 128))
    ids = jnp.arange(SEGMENTS, dtype=jnp.int32)
    before = jnp.sum((segment_ids[None, :] < ids[:, None]).astype(jnp.int32), axis=1)
    start = jnp.sum(jnp.where(segments[:, None] == ids[None, :], before[None, :], 0), axis=1)
    places = (index - start).astype(f32)
    freqs = jnp.exp(jnp.arange(64, dtype=f32) * f32(-2.0 * math.log(rope_base) / HEAD_SIZE))
    angles = places[:, None] * freqs[None, :]
    cosine, sine = jnp.cos(angles) * scale, jnp.sin(angles) * scale

    def kv_weight(core):
        parts = []
        for other in (0, 1):
            which = (xl ^ other) * 4 + core * 2 + z // 2
            parts.append(lax.dynamic_slice_in_dim(key_weight, which * 128, 128, 1))
            parts.append(lax.dynamic_slice_in_dim(value_weight, which * 128, 128, 1))
        return jnp.concatenate(parts, axis=1)

    def summed_over_blk(weight_of, width):
        away = jnp.dot(gathered, weight_of(1 - c), preferred_element_type=f32).astype(bf16)
        got = receive(away, "c", 1)
        home = jnp.dot(gathered, weight_of(c), preferred_element_type=f32)
        both = home + got.astype(f32)
        far = receive(both[:, width:].astype(bf16), "xl", 1)
        return both[:, :width] + far.astype(f32)

    kv = summed_over_blk(kv_weight, 256)
    k_own = rotate(kv[:, :128], cosine, sine).astype(bf16)
    v_own = (kv[:, 128:] * scale).astype(bf16)
    k_1 = receive(k_own, "y", -1)
    v_1 = receive(v_own, "y", -1)
    v_up = receive(v_own, "y", 1)
    k_2 = receive(k_1, "y", -1)
    v_2 = receive(v_up, "y", 1)

    wq_all = jnp.stack([wq[i] for i in range(4)], axis=0)

    def query_weight(core):
        parts = []
        for other in (0, 1):
            which = lax.rem((xl ^ other) * 2 + core - y + 4, 4)
            parts.append(lax.dynamic_index_in_dim(wq_all, which, 0, keepdims=False))
        return jnp.concatenate(parts, axis=1)

    q = summed_over_blk(query_weight, 256)
    unit = f32(HEAD_SIZE ** (-0.5) * math.log2(math.e))
    q = rotate(
        q.reshape(GROUP_ROWS, 2, HEAD_SIZE), (cosine * unit)[:, None, :], (sine * unit)[:, None, :]
    ).reshape(GROUP_ROWS, 2 * HEAD_SIZE).astype(bf16)

    lows = jnp.min(start.reshape(4, TILE), axis=1) // TILE
    scalars = jnp.concatenate([lows, jnp.stack([y, z, xh, jnp.int32(0)])]).astype(jnp.int32)
    mixed = attention(
        scalars, q, index[:, None], start[:, None], (k_own, k_1, k_2), (v_own, v_1, v_2)
    )

    across = receive(mixed, "xl", 1)
    low, high = jnp.where(xl == 0, mixed, across), jnp.where(xl == 0, across, mixed)
    pair = jnp.concatenate([low, high], axis=1)
    other = receive(pair, "c", 1)
    even, odd = jnp.where(c == 0, pair, other), jnp.where(c == 0, other, pair)
    heads = jnp.concatenate([even[:, :256], odd[:, :256], even[:, 256:], odd[:, 256:]], axis=1)

    w_out_own, _ = lax.optimization_barrier((w_output, wq[2][:8, :128]))
    w_out = lax.all_gather(w_out_own, "y", axis=0, tiled=True)
    columns = w_out.shape[1] // 2

    def part(dz, side):
        return jnp.dot(
            heads[dz * TILE : (dz + 1) * TILE],
            w_out[:, side * columns : (side + 1) * columns],
            preferred_element_type=f32,
        )

    up = receive(part(2, 0).astype(bf16), "z", -1)
    down = receive(part(2, 1).astype(bf16), "z", 1)
    up_right = receive(part(1, 1).astype(bf16), "z", -1)
    down_left = receive(part(3, 0).astype(bf16), "z", 1)
    up_left = receive((part(1, 0) + up.astype(f32)).astype(bf16), "z", -1)
    down_right = receive((part(3, 1) + down.astype(f32)).astype(bf16), "z", 1)
    left = part(0, 0) + down_left.astype(f32) + up_left.astype(f32)
    right = part(0, 1) + up_right.astype(f32) + down_right.astype(f32)
    rows = jnp.concatenate([left, right], axis=1)
    last = receive(rows[128:].astype(bf16), "xh", 1)
    return (rows[:128] + last.astype(f32)).astype(bf16)


def solution(mesh):
    fine = Mesh(mesh.devices.reshape(2, 2, 4, 4, 2), ("xl", "c", "y", "z", "xh"))
    blk, tensor = ("xl", "c"), ("y", "z", "xh")
    placed = (
        P(tensor, blk),
        P(blk),
        P(),
        P(blk, tensor),
        P(blk, None),
        P(blk, None),
        P(tensor, blk),
    )
    return jax.shard_map(
        shards, mesh=fine, in_specs=placed, out_specs=P(tensor, blk), check_vma=False
    )
```

time: 705 us -> 238 us (0.34)
  the two profiles are of different devices: /device:TPU:96 before, /device:TPU:16 now
where the time goes in v1:
time: 238 us; the launch traced here: 237 us
  waiting for transfers between devices  82.8 us (35%)
  starting transfers between devices  33.3 us (14%)
  blocking collectives  28.9 us (12%)
  local copies, waits for them, and re-layouts  23.9 us (10%)
  matrix products  19.4 us (8%)
  Pallas kernels  18.7 us (8%)
  other arithmetic  15.4 us (6%)
  between operations  14.1 us (6%)
    ppermute x31, waiting for transfers between devices, receive(): return lax.ppermute(value, axis, [((i + step) % n, i) for i in range(n)])  82.8 us
    ppermute x31, starting transfers between devices, receive(): return lax.ppermute(value, axis, [((i + step) % n, i) for i in range(n)])  33.3 us
    all_gather x1, blocking collectives, shards(): lax.all_gather(own_scale, ('z', 'xh'), axis=0, tiled=True)  22 us
    pallas_call x1, Pallas kernels, attention(): pl.pallas_call(attention_kernel, grid=(4,), out_shape=jax.ShapeDtypeStruc...  18.7 us
    unnamed x37, local copies, waits for them, and re-layouts  13.9 us
    dot_general x8, matrix products, part(): jnp.dot(heads[dz * TILE:(dz + 1) * TILE], w_out[:, side * columns:(side +...  7.6 us
    dot_general x2, matrix products, summed_over_blk(): jnp.dot(gathered, weight_of(1 - c), preferred_element_type=f32).astype(bf16)  7.04 us
    psum x1, blocking collectives, shards(): squares = lax.psum(jnp.sum(floats * floats, axis=-1), ('xl', 'c'))  6.87 us
  transfers between devices with their start and end apart: 32, of which 13 were waited for; matrix products, arithmetic and copies ran while one was open for 21% of the time, Pallas kernels for 8%

profile of v1, /device:TPU:16, one launch (start us, length us, event | category | flops | bytes accessed | tf_op | source)
XLA Modules:
  0.0 236.5 jit_solution(2148089325726914978)
XLA Ops:
  6.5 2.2 constant_dynamic-update-slice_fusion.9
  8.7 3.0 %collective-permute-start = (bf16[128,2048]{1,0:T(8,128)(2,1)}, bf16[128,2048]{1,0:T(8,128)(2,1)}, u32[]{:S(2)}, u32[]{:S(2)}) collective-permute-start(bf16[128,2048]{1,0:T(8,128)(2,1)} %get-tuple-element.6), channel_id=1, source_target_pairs={{1,0},{0,1},{3,2},{2,3},{5,4},{4,5},{7,6},{6,7},{9,8},{8,9},{11,10... | collective-permute-start | bytes 1572872 | tf_op jit(solution)/shard_map/ppermute | solution.py:30
  11.7 4.0 %collective-permute-start.1 = (bf16[128,2048]{1,0:T(8,128)(2,1)}, bf16[128,2048]{1,0:T(8,128)(2,1)S(1)}, u32[]{:S(2)}, u32[]{:S(2)}) collective-permute-start(bf16[128,2048]{1,0:T(8,128)(2,1)} %get-tuple-element.6), channel_id=1, source_target_pairs={{2,0},{4,2},{6,4},{0,6},{3,1},{5,3},{7,5},{1,7},{10,8},{12,10},{14... | collective-permute-start | bytes 1572872 | tf_op jit(solution)/shard_map/ppermute | solution.py:30
  16.2 1.6 collective-permute-start.11
  17.9 1.2 fusion.87
  19.9 6.9 %psum.7 = f32[128]{0:T(128)S(1)} all-reduce(f32[128]{0:T(128)S(1)} %fusion.87), channel_id=1, replica_groups=mesh['xl'=2,'c'=2,'y'=4,'z'=4,'xh'=2] {'xl','c'}, use_global_device_ids=true, to_apply=%region_4.5 | all-reduce | flops 128 | bytes 1024 | tf_op jit(solution)/shard_map/psum | solution.py:121
  26.8 22.0 %all-gather = f32[8,1,128]{2,1,0:T(1,128)S(1)} all-gather(f32[1,1,128]{2,1,0:T(1,128)S(1)} %rsqrt_bitcast_fusion), channel_id=1, replica_groups=mesh['xl'=2,'c'=2,'y'=4,'z'=4,'xh'=2] {'z','xh'}, dimensions={0}, use_global_device_ids=true | all-gather | bytes 4608 | tf_op jit(solution)/shard_map/all_gather | solution.py:123
  48.9 4.4 %constant_dynamic-slice_fusion.6 = (bf16[2048,128]{1,0:T(8,128)(2,1)}, bf16[2048,128]{1,0:T(8,128)(2,1)}, bf16[2048,128]{1,0:T(8,128)(2,1)}, bf16[2048,128]{1,0:...) fusion(bf16[2048,1024]{1,0:T(8,128)(2,1)} %param.12, ...), kind=kLoop, calls=%fused_computation.138 | loop fusion | bytes 8388624 | tf_op jit(solution)/shard_map/dynamic_slice | solution.py:146
  53.6 2.0 collective-permute-start.7
  55.6 2.0 constant_dynamic-update-slice_fusion.8
  57.6 1.4 collective-permute-start.3
  59.0 0.8 constant_dynamic-update-slice_fusion.7
  59.8 8.6 %collective-permute-done.2 = bf16[128,2048]{1,0:T(8,128)(2,1)} collective-permute-done((bf16[128,2048]{1,0:T(8,128)(2,1)}, bf16[128,2048]{1,0:T(8,128)(2,1)}, u32[]{:S(2)}, u32[]{:S(2)}) %collective-permute-start.2) | collective-permute-done | bytes 524320 | tf_op jit(solution)/shard_map/ppermute | solution.py:30
  68.5 1.9 constant_dynamic-update-slice_fusion.6
  70.4 1.0 slice.127
  71.3 3.3 %collective-permute-start.6 = (bf16[64,2048]{1,0:T(8,128)(2,1)S(1)}, bf16[64,2048]{1,0:T(8,128)(2,1)S(1)}, u32[]{:S(2)}, u32[]{:S(2)}) collective-permute-start(bf16[64,2048]{1,0:T(8,128)(2,1)S(1)} %slice.127), channel_id=1, source_target_pairs={{2,0},{4,2},{6,4},{0,6},{3,1},{5,3},{7,5},{1,7},{10,8},{12,10},{14... | collective-permute-start | bytes 786440 | tf_op jit(solution)/shard_map/ppermute | solution.py:30
  75.4 1.7 collective-permute-start.12
  77.8 0.7 constant_dynamic-update-slice_fusion.4
  79.2 3.1 %collective-permute-done.8 = bf16[64,2048]{1,0:T(8,128)(2,1)S(1)} collective-permute-done((bf16[64,2048]{1,0:T(8,128)(2,1)S(1)}, bf16[64,2048]{1,0:T(8,128)(2,1)S(1)}, u32[]{:S(2)}, u32[]{:S(2)}) %collective-permute-start.8) | collective-permute-done | bytes 262176 | tf_op jit(solution)/shard_map/ppermute | solution.py:30
  83.1 0.9 constant_dynamic-update-slice_fusion.1
  83.9 0.9 constant_dynamic-update-slice_fusion
  84.8 4.6 %fusion.28 = bf16[1024,512]{1,0:T(8,128)(2,1)S(1)} fusion(bf16[1024,2048]{1,0:T(8,128)(2,1)} %constant_dynamic-update-slice_fusion, bf16[2048,128]{1,0:T(8,128)(2,1)S(1)} %copy-done.6, bf16[2048,128]{1,0:T(8,128)(2,1)S(1)} %copy-done.9, bf16[2048,128]{1,0:T(8,128)(2,1)S(1)} %copy-done.7, bf16[2048,128]{1,0:T(8,128)(2,1)S(1)} %copy-done.8), kind=kOutput, calls=%fused_computation.30 | convolution fusion | flops 2156396544 | bytes 7340032 | tf_op jit(solution)/shard_map/dot_general | solution.py:150
  90.5 1.9 copy-done.10
  92.4 2.4 %fusion.31 = bf16[1024,512]{0,1:T(8,128)(2,1)S(1)} fusion(bf16[1024,2048]{1,0:T(8,128)(2,1)S(1)} %copy-done.10, bf16[2048,256]{1,0:T(8,128)(2,1)S(1)} %get-tuple-element.16, bf16[2048,256]{1,0:T(8,128)(2,1)S(1)} %get-tuple-element.17), kind=kOutput, calls=%fused_computation.31 | convolution fusion | flops 2152202240 | bytes 7340032 | tf_op jit(solution)/shard_map/dot_general | solution.py:150
  94.9 0.7 collective-permute-start.13
  95.7 2.3 convert_add_fusion
  98.4 2.4 %convert_add_fusion.1 = f32[1024,512]{0,1:T(8,128)S(1)} fusion(bf16[1024,512]{0,1:T(8,128)(2,1)S(1)} %collective-permute-done.13, bf16[1024,2048]{1,0:T(8,128)(2,1)S(1)} %copy-done.10, bf16[2048,256]{1,0:T(8,128)(2,1)S(1)} %get-tuple-element.18, bf16[2048,256]{1,0:T(8,128)(2,1)S(1)} %get-tuple-element.15), kind=kOutput, calls=%fused_computation.29 | convolution fusion | flops 2152726528 | bytes 9437184 | tf_op jit(solution)/shard_map/dot_general | solution.py:152
  100.9 1.0 slice.230
  101.9 1.8 collective-permute-start.14
  103.7 9.3 %collective-permute-done.16 = bf16[1024,256]{1,0:T(8,128)(2,1)S(1)} collective-permute-done((bf16[1024,256]{1,0:T(8,128)(2,1)S(1)}, bf16[1024,256]{1,0:T(8,128)(2,1)S(1)}, u32[]{:S(2)}, u32[]{:S(2)}) %collective-permute-start.16) | collective-permute-done | bytes 524320 | tf_op jit(solution)/shard_map/ppermute | solution.py:30
  113.2 3.3 %fusion.97 = (bf16[1024,64]{1,0:T(8,128)(2,1)S(1)}, bf16[1024,64]{1,0:T(8,128)(2,1)S(1)}, f32[1024,64]{1,0:T(8,128)}, f32[1024,64]{1,0:T(8,128)}) fusion(f32[1024,256]{1,0:T(8,128)S(1)} %slice_add_fusion, f32[1024]{0:T(1024)S(1)} %bitcast.47, f32[64]{0:T(128)S(1)} %multiply_exponential_fusion, f32[1024]{0:T(1024)S(1)} %subtract_convert_fusion.1), kind=kLoop, calls=%fused_computation.90 | loop fusion | flops 851968 | bytes 1319168 | tf_op jit(solution)/shard_map/convert.1
  116.6 1.3 collective-permute-start.17
  118.1 0.9 collective-permute-start.20
  119.7 1.2 collective-permute-start.19
  120.9 5.0 %collective-permute-done.17.k1 = bf16[1024,128]{1,0:T(8,128)(2,1)S(1)} collective-permute-done((bf16[1024,128]{1,0:T(8,128)(2,1)S(1)}, bf16[1024,128]{1,0:T(8,128)(2,1)S(1)}, u32[]{:S(2)}, u32[]{:S(2)}) %collective-permute-start.17) | collective-permute-done | bytes 262176 | tf_op jit(solution)/shard_map/ppermute | solution.py:30
  126.0 1.2 collective-permute-start.18
  127.2 0.8 collective-permute-start.21
  128.0 1.4 slice_add_fusion.1
  129.3 0.9 fusion.123
  130.2 2.2 copy.32
  132.4 1.3 copy.33
  133.7 2.5 %subtract_convert_fusion = (bf16[1024,2,64]{2,1,0:T(2,128)(2,1)S(1)}, bf16[1024,2,64]{2,1,0:T(2,128)(2,1)S(1)}) fusion(f32[1024,2,64]{2,1,0:T(2,128)} %copy.33, f32[1024,2,64]{2,1,0:T(2,128)} %copy.32, f32[1024,64]{1,0:T(8,128)} %get-tuple-element.33, f32[1024,64]{1,0:T(8,128)} %get-tuple-element.34), kind=kLoop, calls=%fused_computation.76 | loop fusion | flops 1048576 | bytes 2097152 | tf_op jit(solution)/shard_map/convert.4
  136.2 1.4 pad_maximum_fusion.4
  137.8 18.7 %shard_map.73 = bf16[1024,256]{1,0:T(8,128)(2,1)S(1)} custom-call(s32[8]{0:T(128)S(1)} %concatenate.48.scalars, bf16[1024,256]{1,0:T(8,128)(2,1)S(1)} %bitcast.40, s32[1024,1]{1,0:T(8,128)S(1)} %copy.28.index_ref, s32[1024,1]{1,0:T(8,128)S(1)} %copy.29.start_ref, bf16[1024,128]{1,0:T(8,128)(2,1)S(1)} %pad_maximum_fusion.5.k0, ...), custom_call_target="tpu_custom_call" | custom-call | flops 3000000000 | bytes 4194304 | tf_op jit(solution)/shard_map/pallas_call | solution.py:82
  157.1 8.7 %collective-permute-done.22 = bf16[1024,256]{1,0:T(8,128)(2,1)S(1)} collective-permute-done((bf16[1024,256]{1,0:T(8,128)(2,1)S(1)}, bf16[1024,256]{1,0:T(8,128)(2,1)S(1)}, u32[]{:S(2)}, u32[]{:S(2)}) %collective-permute-start.22) | collective-permute-done | bytes 524320 | tf_op jit(solution)/shard_map/ppermute | solution.py:30
  166.0 2.6 %collective-permute-done.23 = bf16[1024,512]{1,0:T(8,128)(2,1)S(1)} collective-permute-done((bf16[1024,512]{1,0:T(8,128)(2,1)S(1)}, bf16[1024,512]{1,0:T(8,128)(2,1)S(1)}, u32[]{:S(2)}, u32[]{:S(2)}) %collective-permute-start.23) | collective-permute-done | bytes 1048608 | tf_op jit(solution)/shard_map/ppermute | solution.py:30
  169.5 2.4 %fusion.77 = bf16[256,1024]{1,0:T(8,128)(2,1)S(1)} fusion(bf16[1024,2048]{1,0:T(8,128)(2,1)} %all-gather.3.cloned.1.call-done, bf16[1024,1024]{1,0:T(8,128)(2,1)S(1)} %pad_maximum_fusion.1), kind=kOutput, calls=%fused_computation.59 | convolution fusion | flops 537133056 | bytes 3145728 | tf_op jit(solution)/shard_map/dot_general | solution.py:199
  172.7 0.7 fusion.74
  173.4 1.5 collective-permute-start.27
  174.9 0.7 fusion.71
  175.7 10.3 %collective-permute-done.28 = bf16[256,1024]{1,0:T(8,128)(2,1)S(1)} collective-permute-done((bf16[256,1024]{1,0:T(8,128)(2,1)S(1)}, bf16[256,1024]{1,0:T(8,128)(2,1)S(1)}, u32[]{:S(2)}, u32[]{:S(2)}) %collective-permute-start.28) | collective-permute-done | bytes 524320 | tf_op jit(solution)/shard_map/ppermute | solution.py:30
  186.0 0.7 fusion.83
  186.8 1.9 collective-permute-start.29
  188.6 0.7 fusion.68
  189.5 10.1 %collective-permute-done.25 = bf16[256,1024]{1,0:T(8,128)(2,1)S(1)} collective-permute-done((bf16[256,1024]{1,0:T(8,128)(2,1)S(1)}, bf16[256,1024]{1,0:T(8,128)(2,1)S(1)}, u32[]{:S(2)}, u32[]{:S(2)}) %collective-permute-start.25) | collective-permute-done | bytes 524320 | tf_op jit(solution)/shard_map/ppermute | solution.py:30
  199.6 0.7 fusion.80
  200.6 1.1 collective-permute-done.29
  201.7 0.8 fusion.45
  202.5 8.7 %collective-permute-done.24 = bf16[256,1024]{1,0:T(8,128)(2,1)S(1)} collective-permute-done((bf16[256,1024]{1,0:T(8,128)(2,1)S(1)}, bf16[256,1024]{1,0:T(8,128)(2,1)S(1)}, u32[]{:S(2)}, u32[]{:S(2)}) %collective-permute-start.24) | collective-permute-done | bytes 524320 | tf_op jit(solution)/shard_map/ppermute | solution.py:30
  211.2 3.2 %collective-permute-done.26 = bf16[256,1024]{1,0:T(8,128)(2,1)S(1)} collective-permute-done((bf16[256,1024]{1,0:T(8,128)(2,1)S(1)}, bf16[256,1024]{1,0:T(8,128)(2,1)S(1)}, u32[]{:S(2)}, u32[]{:S(2)}) %collective-permute-start.26) | collective-permute-done | bytes 524320 | tf_op jit(solution)/shard_map/ppermute | solution.py:30
  214.4 0.8 fusion.62
  215.3 1.7 collective-permute-start.30
  216.9 11.8 %collective-permute-done.30 = bf16[128,2048]{1,0:T(8,128)(2,1)S(1)} collective-permute-done((bf16[128,2048]{1,0:T(8,128)(2,1)S(1)}, bf16[128,2048]{1,0:T(8,128)(2,1)S(1)}, u32[]{:S(2)}, u32[]{:S(2)}) %collective-permute-start.30) | collective-permute-done | bytes 524320 | tf_op jit(solution)/shard_map/ppermute | solution.py:30
  228.8 0.9 fusion.90
  (105 shorter events, 10.1 us)
Async XLA Ops:
  6.5 163.0 %all-gather.3.cloned.1.call-start = ((), (), s32[]{:S(2)}) async-start(), calls=%async_computation | async-start | bytes 5242880 | tf_op jit(solution)/shard_map/all_gather | solution.py:195
  8.7 44.7 %collective-permute-start = (bf16[128,2048]{1,0:T(8,128)(2,1)}, bf16[128,2048]{1,0:T(8,128)(2,1)}, u32[]{:S(2)}, u32[]{:S(2)}) collective-permute-start(bf16[128,2048]{1,0:T(8,128)(2,1)} %get-tuple-element.6), channel_id=1, source_target_pairs={{1,0},{0,1},{3,2},{2,3},{5,4},{4,5},{7,6},{6,7},{9,8},{8,9},{11,10... | collective-permute-start | bytes 1572872 | tf_op jit(solution)/shard_map/ppermute | solution.py:30
  11.7 41.9 %collective-permute-start.1 = (bf16[128,2048]{1,0:T(8,128)(2,1)}, bf16[128,2048]{1,0:T(8,128)(2,1)S(1)}, u32[]{:S(2)}, u32[]{:S(2)}) collective-permute-start(bf16[128,2048]{1,0:T(8,128)(2,1)} %get-tuple-element.6), channel_id=1, source_target_pairs={{2,0},{4,2},{6,4},{0,6},{3,1},{5,3},{7,5},{1,7},{10,8},{12,10},{14... | collective-permute-start | bytes 1572872 | tf_op jit(solution)/shard_map/ppermute | solution.py:30
  15.8 41.8 %collective-permute-start.4 = (bf16[128,2048]{1,0:T(8,128)(2,1)}, bf16[128,2048]{1,0:T(8,128)(2,1)S(1)}, u32[]{:S(2)}, u32[]{:S(2)}) collective-permute-start(bf16[128,2048]{1,0:T(8,128)(2,1)} %get-tuple-element.6), channel_id=1, source_target_pairs={{6,0},{0,2},{2,4},{4,6},{7,1},{1,3},{3,5},{5,7},{14,8},{8,10},{10,... | collective-permute-start | bytes 1572872 | tf_op jit(solution)/shard_map/ppermute | solution.py:30
  15.8 58.9 %collective-permute-start.9 = (bf16[2048,256]{1,0:T(8,128)(2,1)}, bf16[2048,256]{1,0:T(8,128)(2,1)S(1)}, u32[]{:S(2)}, u32[]{:S(2)}) collective-permute-start(bf16[2048,256]{1,0:T(8,128)(2,1)} %param.10), channel_id=1, source_target_pairs={{8,0},{16,8},{24,16},{0,24},{9,1},{17,9},{25,17},{1,25},{10,2},{18... | collective-permute-start | bytes 3145736 | tf_op jit(solution)/shard_map/ppermute | solution.py:30
  16.2 58.6 %collective-permute-start.11 = (bf16[2048,256]{1,0:T(8,128)(2,1)}, bf16[2048,256]{1,0:T(8,128)(2,1)S(1)}, u32[]{:S(2)}, u32[]{:S(2)}) collective-permute-start(bf16[2048,256]{1,0:T(8,128)(2,1)} %param.10), channel_id=1, source_target_pairs={{24,0},{0,8},{8,16},{16,24},{25,1},{1,9},{9,17},{17,25},{26,2},{2,... | collective-permute-start | bytes 3145736 | tf_op jit(solution)/shard_map/ppermute | solution.py:30
  48.9 4.4 %copy-start.11 = (s32[4096]{0:T(1024)S(1)}, s32[4096]{0:T(1024)}, u32[]{:S(2)}) copy-start(s32[4096]{0:T(1024)} %param.9) | copy-start | bytes 49156
  53.4 15.0 %collective-permute-start.2 = (bf16[128,2048]{1,0:T(8,128)(2,1)}, bf16[128,2048]{1,0:T(8,128)(2,1)}, u32[]{:S(2)}, u32[]{:S(2)}) collective-permute-start(bf16[128,2048]{1,0:T(8,128)(2,1)} %collective-permute-done), channel_id=1, source_target_pairs={{2,0},{4,2},{6,4},{0,6},{3,1},{5,3},{7,5},{1,7},{10,8},{12,10},{14... | collective-permute-start | bytes 1572872 | tf_op jit(solution)/shard_map/ppermute | solution.py:30
  53.6 17.7 %collective-permute-start.7 = (bf16[128,2048]{1,0:T(8,128)(2,1)}, bf16[128,2048]{1,0:T(8,128)(2,1)S(1)}, u32[]{:S(2)}, u32[]{:S(2)}) collective-permute-start(bf16[128,2048]{1,0:T(8,128)(2,1)} %collective-permute-done), channel_id=1, source_target_pairs={{6,0},{0,2},{2,4},{4,6},{7,1},{1,3},{3,5},{5,7},{14,8},{8,10},{10,... | collective-permute-start | bytes 1572872 | tf_op jit(solution)/shard_map/ppermute | solution.py:30
  57.6 17.8 %collective-permute-start.3 = (bf16[64,2048]{1,0:T(8,128)(2,1)S(1)}, bf16[64,2048]{1,0:T(8,128)(2,1)S(1)}, u32[]{:S(2)}, u32[]{:S(2)}) collective-permute-start(bf16[64,2048]{1,0:T(8,128)(2,1)S(1)} %slice.125), channel_id=1, source_target_pairs={{2,0},{4,2},{6,4},{0,6},{3,1},{5,3},{7,5},{1,7},{10,8},{12,10},{14... | collective-permute-start | bytes 786440 | tf_op jit(solution)/shard_map/ppermute | solution.py:30
  59.8 25.0 %copy-start.6 = (bf16[2048,128]{1,0:T(8,128)(2,1)S(1)}, bf16[2048,128]{1,0:T(8,128)(2,1)}, u32[]{:S(2)}) copy-start(bf16[2048,128]{1,0:T(8,128)(2,1)} %get-tuple-element.13) | copy-start | bytes 1572868
  59.8 25.0 %copy-start.7 = (bf16[2048,128]{1,0:T(8,128)(2,1)S(1)}, bf16[2048,128]{1,0:T(8,128)(2,1)}, u32[]{:S(2)}) copy-start(bf16[2048,128]{1,0:T(8,128)(2,1)} %get-tuple-element.14) | copy-start | bytes 1572868
  59.8 25.0 %copy-start.8 = (bf16[2048,128]{1,0:T(8,128)(2,1)S(1)}, bf16[2048,128]{1,0:T(8,128)(2,1)}, u32[]{:S(2)}) copy-start(bf16[2048,128]{1,0:T(8,128)(2,1)} %get-tuple-element.37) | copy-start | bytes 1572868
  59.8 25.0 %copy-start.9 = (bf16[2048,128]{1,0:T(8,128)(2,1)S(1)}, bf16[2048,128]{1,0:T(8,128)(2,1)}, u32[]{:S(2)}) copy-start(bf16[2048,128]{1,0:T(8,128)(2,1)} %get-tuple-element.38) | copy-start | bytes 1572868
  68.5 9.3 %collective-permute-start.5 = (bf16[64,2048]{1,0:T(8,128)(2,1)S(1)}, bf16[64,2048]{1,0:T(8,128)(2,1)S(1)}, u32[]{:S(2)}, u32[]{:S(2)}) collective-permute-start(bf16[64,2048]{1,0:T(8,128)(2,1)S(1)} %slice.126), channel_id=1, source_target_pairs={{6,0},{0,2},{2,4},{4,6},{7,1},{1,3},{3,5},{5,7},{14,8},{8,10},{10,... | collective-permute-start | bytes 786440 | tf_op jit(solution)/shard_map/ppermute | solution.py:30
  71.3 7.2 %collective-permute-start.6 = (bf16[64,2048]{1,0:T(8,128)(2,1)S(1)}, bf16[64,2048]{1,0:T(8,128)(2,1)S(1)}, u32[]{:S(2)}, u32[]{:S(2)}) collective-permute-start(bf16[64,2048]{1,0:T(8,128)(2,1)S(1)} %slice.127), channel_id=1, source_target_pairs={{2,0},{4,2},{6,4},{0,6},{3,1},{5,3},{7,5},{1,7},{10,8},{12,10},{14... | collective-permute-start | bytes 786440 | tf_op jit(solution)/shard_map/ppermute | solution.py:30
  74.7 7.7 %collective-permute-start.8 = (bf16[64,2048]{1,0:T(8,128)(2,1)S(1)}, bf16[64,2048]{1,0:T(8,128)(2,1)S(1)}, u32[]{:S(2)}, u32[]{:S(2)}) collective-permute-start(bf16[64,2048]{1,0:T(8,128)(2,1)S(1)} %slice.128), channel_id=1, source_target_pairs={{6,0},{0,2},{2,4},{4,6},{7,1},{1,3},{3,5},{5,7},{14,8},{8,10},{10,... | collective-permute-start | bytes 786440 | tf_op jit(solution)/shard_map/ppermute | solution.py:30
  74.8 14.7 %collective-permute-start.10 = (bf16[1024,256]{1,0:T(8,128)(2,1)S(1)}, bf16[1024,256]{1,0:T(8,128)(2,1)S(1)}, u32[]{:S(2)}, u32[]{:S(2)}) collective-permute-start(bf16[1024,256]{1,0:T(8,128)(2,1)S(1)} %slice.129), channel_id=1, source_target_pairs={{8,0},{16,8},{24,16},{0,24},{9,1},{17,9},{25,17},{1,25},{10,2},{18... | collective-permute-start | bytes 1572872 | tf_op jit(solution)/shard_map/ppermute | solution.py:30
  75.4 14.2 %collective-permute-start.12 = (bf16[1024,256]{1,0:T(8,128)(2,1)S(1)}, bf16[1024,256]{1,0:T(8,128)(2,1)S(1)}, u32[]{:S(2)}, u32[]{:S(2)}) collective-permute-start(bf16[1024,256]{1,0:T(8,128)(2,1)S(1)} %slice.130), channel_id=1, source_target_pairs={{24,0},{0,8},{8,16},{16,24},{25,1},{1,9},{9,17},{17,25},{26,2},{2,... | collective-permute-start | bytes 1572872 | tf_op jit(solution)/shard_map/ppermute | solution.py:30
  84.8 4.8 %copy-start.1 = (bf16[2048,256]{1,0:T(8,128)(2,1)S(1)}, bf16[2048,256]{1,0:T(8,128)(2,1)}, u32[]{:S(2)}) copy-start(bf16[2048,256]{1,0:T(8,128)(2,1)} %param.10) | copy-start | bytes 3145732
  89.4 6.3 %collective-permute-start.15 = (bf16[1024,512]{1,0:T(8,128)(2,1)S(1)}, bf16[1024,512]{1,0:T(8,128)(2,1)S(1)}, u32[]{:S(2)}, u32[]{:S(2)}) collective-permute-start(bf16[1024,512]{1,0:T(8,128)(2,1)S(1)} %fusion.28), channel_id=1, source_target_pairs={{32,0},{0,32},{33,1},{1,33},{34,2},{2,34},{35,3},{3,35},{36,4},{4,... | collective-permute-start | bytes 3145736 | tf_op jit(solution)/shard_map/ppermute | solution.py:30
  90.2 2.2 copy-start.10
  92.4 3.3 %copy-start.2 = (bf16[2048,128]{1,0:T(8,128)(2,1)S(1)}, bf16[2048,128]{1,0:T(8,128)(2,1)}, u32[]{:S(2)}) copy-start(bf16[2048,128]{1,0:T(8,128)(2,1)} %get-tuple-element.11) | copy-start | bytes 1572868
  92.4 3.3 %copy-start.3 = (bf16[2048,128]{1,0:T(8,128)(2,1)S(1)}, bf16[2048,128]{1,0:T(8,128)(2,1)}, u32[]{:S(2)}) copy-start(bf16[2048,128]{1,0:T(8,128)(2,1)} %get-tuple-element.12) | copy-start | bytes 1572868
  92.4 3.3 %copy-start.4 = (bf16[2048,128]{1,0:T(8,128)(2,1)S(1)}, bf16[2048,128]{1,0:T(8,128)(2,1)}, u32[]{:S(2)}) copy-start(bf16[2048,128]{1,0:T(8,128)(2,1)} %get-tuple-element.39) | copy-start | bytes 1572868
  92.4 3.3 %copy-start.5 = (bf16[2048,128]{1,0:T(8,128)(2,1)S(1)}, bf16[2048,128]{1,0:T(8,128)(2,1)}, u32[]{:S(2)}) copy-start(bf16[2048,128]{1,0:T(8,128)(2,1)} %get-tuple-element.40) | copy-start | bytes 1572868
  94.9 3.6 %collective-permute-start.13 = (bf16[1024,512]{0,1:T(8,128)(2,1)S(1)}, bf16[1024,512]{0,1:T(8,128)(2,1)S(1)}, u32[]{:S(2)}, u32[]{:S(2)}) collective-permute-start(bf16[1024,512]{0,1:T(8,128)(2,1)S(1)} %fusion.31), channel_id=1, source_target_pairs={{32,0},{0,32},{33,1},{1,33},{34,2},{2,34},{35,3},{3,35},{36,4},{4,... | collective-permute-start | bytes 3145736 | tf_op jit(solution)/shard_map/ppermute | solution.py:30
  98.2 14.9 %collective-permute-start.16 = (bf16[1024,256]{1,0:T(8,128)(2,1)S(1)}, bf16[1024,256]{1,0:T(8,128)(2,1)S(1)}, u32[]{:S(2)}, u32[]{:S(2)}) collective-permute-start(bf16[1024,256]{1,0:T(8,128)(2,1)S(1)} %slice.229), channel_id=1, source_target_pairs={{64,0},{0,64},{65,1},{1,65},{66,2},{2,66},{67,3},{3,67},{68,4},{4,... | collective-permute-start | bytes 1572872 | tf_op jit(solution)/shard_map/ppermute | solution.py:30
  100.9 2.8 %copy-start = (f32[1024,512]{0,1:T(8,128)}, f32[1024,512]{0,1:T(8,128)S(1)}, u32[]{:S(2)}) copy-start(f32[1024,512]{0,1:T(8,128)S(1)} %convert_add_fusion.1) | copy-start | bytes 6291460
  101.9 26.1 %collective-permute-start.14 = (bf16[1024,256]{0,1:T(8,128)(2,1)}, bf16[1024,256]{0,1:T(8,128)(2,1)S(1)}, u32[]{:S(2)}, u32[]{:S(2)}) collective-permute-start(bf16[1024,256]{0,1:T(8,128)(2,1)} %slice.230), channel_id=1, source_target_pairs={{64,0},{0,64},{65,1},{1,65},{66,2},{2,66},{67,3},{3,67},{68,4},{4,... | collective-permute-start | bytes 1572872 | tf_op jit(solution)/shard_map/ppermute | solution.py:30
  116.6 9.3 %collective-permute-start.17 = (bf16[1024,128]{1,0:T(8,128)(2,1)S(1)}, bf16[1024,128]{1,0:T(8,128)(2,1)S(1)}, u32[]{:S(2)}, u32[]{:S(2)}) collective-permute-start(bf16[1024,128]{1,0:T(8,128)(2,1)S(1)} %pad_maximum_fusion.5.k0), channel_id=1, source_target_pairs={{24,0},{0,8},{8,16},{16,24},{25,1},{1,9},{9,17},{17,25},{26,2},{2,... | collective-permute-start | bytes 786440 | tf_op jit(solution)/shard_map/ppermute | solution.py:30
  118.1 9.0 %collective-permute-start.20 = (bf16[1024,128]{1,0:T(8,128)(2,1)S(1)}, bf16[1024,128]{1,0:T(8,128)(2,1)}, u32[]{:S(2)}, u32[]{:S(2)}) collective-permute-start(bf16[1024,128]{1,0:T(8,128)(2,1)S(1)} %fusion.104.v0), channel_id=1, source_target_pairs={{8,0},{16,8},{24,16},{0,24},{9,1},{17,9},{25,17},{1,25},{10,2},{18... | collective-permute-start | bytes 786440 | tf_op jit(solution)/shard_map/ppermute | solution.py:30
  119.7 18.0 %collective-permute-start.19 = (bf16[1024,128]{1,0:T(8,128)(2,1)S(1)}, bf16[1024,128]{1,0:T(8,128)(2,1)S(1)}, u32[]{:S(2)}, u32[]{:S(2)}) collective-permute-start(bf16[1024,128]{1,0:T(8,128)(2,1)S(1)} %fusion.104.v0), channel_id=1, source_target_pairs={{24,0},{0,8},{8,16},{16,24},{25,1},{1,9},{9,17},{17,25},{26,2},{2,... | collective-permute-start | bytes 786440 | tf_op jit(solution)/shard_map/ppermute | solution.py:30
  126.0 11.8 %collective-permute-start.18 = (bf16[1024,128]{1,0:T(8,128)(2,1)S(1)}, bf16[1024,128]{1,0:T(8,128)(2,1)S(1)}, u32[]{:S(2)}, u32[]{:S(2)}) collective-permute-start(bf16[1024,128]{1,0:T(8,128)(2,1)S(1)} %collective-permute-done.17.k1), channel_id=1, source_target_pairs={{24,0},{0,8},{8,16},{16,24},{25,1},{1,9},{9,17},{17,25},{26,2},{2,... | collective-permute-start | bytes 786440 | tf_op jit(solution)/shard_map/ppermute | solution.py:30
  127.2 10.6 %collective-permute-start.21 = (bf16[1024,128]{1,0:T(8,128)(2,1)}, bf16[1024,128]{1,0:T(8,128)(2,1)S(1)}, u32[]{:S(2)}, u32[]{:S(2)}) collective-permute-start(bf16[1024,128]{1,0:T(8,128)(2,1)} %collective-permute-done.20), channel_id=1, source_target_pairs={{8,0},{16,8},{24,16},{0,24},{9,1},{17,9},{25,17},{1,25},{10,2},{18... | collective-permute-start | bytes 786440 | tf_op jit(solution)/shard_map/ppermute | solution.py:30
  156.5 9.3 %collective-permute-start.22 = (bf16[1024,256]{1,0:T(8,128)(2,1)S(1)}, bf16[1024,256]{1,0:T(8,128)(2,1)S(1)}, u32[]{:S(2)}, u32[]{:S(2)}) collective-permute-start(bf16[1024,256]{1,0:T(8,128)(2,1)S(1)} %shard_map.73), channel_id=1, source_target_pairs={{64,0},{0,64},{65,1},{1,65},{66,2},{2,66},{67,3},{3,67},{68,4},{4,... | collective-permute-start | bytes 1572872 | tf_op jit(solution)/shard_map/ppermute | solution.py:30
  165.9 2.7 %collective-permute-start.23 = (bf16[1024,512]{1,0:T(8,128)(2,1)S(1)}, bf16[1024,512]{1,0:T(8,128)(2,1)S(1)}, u32[]{:S(2)}, u32[]{:S(2)}) collective-permute-start(bf16[1024,512]{1,0:T(8,128)(2,1)S(1)} %pad_maximum_fusion.3), channel_id=1, source_target_pairs={{32,0},{0,32},{33,1},{1,33},{34,2},{2,34},{35,3},{3,35},{36,4},{4,... | collective-permute-start | bytes 3145736 | tf_op jit(solution)/shard_map/ppermute | solution.py:30
  169.5 3.1 %copy-start.12 = (bf16[1024,2048]{1,0:T(8,128)(2,1)S(1)}, bf16[1024,2048]{1,0:T(8,128)(2,1)}, u32[]{:S(2)}) copy-start(bf16[1024,2048]{1,0:T(8,128)(2,1)} %all-gather.3.cloned.1.call-done) | copy-start | bytes 12582916
  172.0 14.0 %collective-permute-start.28 = (bf16[256,1024]{1,0:T(8,128)(2,1)S(1)}, bf16[256,1024]{1,0:T(8,128)(2,1)S(1)}, u32[]{:S(2)}, u32[]{:S(2)}) collective-permute-start(bf16[256,1024]{1,0:T(8,128)(2,1)S(1)} %fusion.77), channel_id=1, source_target_pairs={{2,0},{4,2},{6,4},{0,6},{3,1},{5,3},{7,5},{1,7},{10,8},{12,10},{14... | collective-permute-start | bytes 1572872 | tf_op jit(solution)/shard_map/ppermute | solution.py:30
  173.4 27.2 %collective-permute-start.27 = (bf16[256,1024]{1,0:T(8,128)(2,1)S(1)}, bf16[256,1024]{1,0:T(8,128)(2,1)S(1)}, u32[]{:S(2)}, u32[]{:S(2)}) collective-permute-start(bf16[256,1024]{1,0:T(8,128)(2,1)S(1)} %fusion.74), channel_id=1, source_target_pairs={{6,0},{0,2},{2,4},{4,6},{7,1},{1,3},{3,5},{5,7},{14,8},{8,10},{10,... | collective-permute-start | bytes 1572872 | tf_op jit(solution)/shard_map/ppermute | solution.py:30
  175.6 24.0 %collective-permute-start.25 = (bf16[256,1024]{1,0:T(8,128)(2,1)S(1)}, bf16[256,1024]{1,0:T(8,128)(2,1)S(1)}, u32[]{:S(2)}, u32[]{:S(2)}) collective-permute-start(bf16[256,1024]{1,0:T(8,128)(2,1)S(1)} %fusion.71), channel_id=1, source_target_pairs={{6,0},{0,2},{2,4},{4,6},{7,1},{1,3},{3,5},{5,7},{14,8},{8,10},{10,... | collective-permute-start | bytes 1572872 | tf_op jit(solution)/shard_map/ppermute | solution.py:30
  186.8 14.9 %collective-permute-start.29 = (bf16[256,1024]{1,0:T(8,128)(2,1)S(1)}, bf16[256,1024]{1,0:T(8,128)(2,1)S(1)}, u32[]{:S(2)}, u32[]{:S(2)}) collective-permute-start(bf16[256,1024]{1,0:T(8,128)(2,1)S(1)} %fusion.83), channel_id=1, source_target_pairs={{2,0},{4,2},{6,4},{0,6},{3,1},{5,3},{7,5},{1,7},{10,8},{12,10},{14... | collective-permute-start | bytes 1572872 | tf_op jit(solution)/shard_map/ppermute | solution.py:30
  189.4 21.8 %collective-permute-start.24 = (bf16[256,1024]{1,0:T(8,128)(2,1)S(1)}, bf16[256,1024]{1,0:T(8,128)(2,1)S(1)}, u32[]{:S(2)}, u32[]{:S(2)}) collective-permute-start(bf16[256,1024]{1,0:T(8,128)(2,1)S(1)} %fusion.68), channel_id=1, source_target_pairs={{2,0},{4,2},{6,4},{0,6},{3,1},{5,3},{7,5},{1,7},{10,8},{12,10},{14... | collective-permute-start | bytes 1572872 | tf_op jit(solution)/shard_map/ppermute | solution.py:30
  200.3 14.1 %collective-permute-start.26 = (bf16[256,1024]{1,0:T(8,128)(2,1)S(1)}, bf16[256,1024]{1,0:T(8,128)(2,1)S(1)}, u32[]{:S(2)}, u32[]{:S(2)}) collective-permute-start(bf16[256,1024]{1,0:T(8,128)(2,1)S(1)} %fusion.80), channel_id=1, source_target_pairs={{6,0},{0,2},{2,4},{4,6},{7,1},{1,3},{3,5},{5,7},{14,8},{8,10},{10,... | collective-permute-start | bytes 1572872 | tf_op jit(solution)/shard_map/ppermute | solution.py:30
  215.3 13.5 %collective-permute-start.30 = (bf16[128,2048]{1,0:T(8,128)(2,1)S(1)}, bf16[128,2048]{1,0:T(8,128)(2,1)S(1)}, u32[]{:S(2)}, u32[]{:S(2)}) collective-permute-start(bf16[128,2048]{1,0:T(8,128)(2,1)S(1)} %fusion.91), channel_id=1, source_target_pairs={{1,0},{0,1},{3,2},{2,3},{5,4},{4,5},{7,6},{6,7},{9,8},{8,9},{11,10... | collective-permute-start | bytes 1572872 | tf_op jit(solution)/shard_map/ppermute | solution.py:30
Sparse Core Ops, SparseCore 0:
  17.9 59.8 all-gather.2

commit v2 on v1

v2 whole, which is shorter than its diff:
```python
import functools
import math

import jax
import jax.numpy as jnp
from jax import lax
from jax.experimental import pallas as pl
from jax.experimental.pallas import tpu as pltpu
from jax.sharding import Mesh, PartitionSpec as P

MODEL_WIDTH = 8192
QUERY_HEADS = 64
KEY_VALUE_HEADS = 8
HEAD_SIZE = 128
TOKENS = 4096
SEGMENTS = 16
GROUP_ROWS = 1024
TILE = 256
PART = 512

norm_eps = 1e-05
rope_base = 500000.0
MASKED = -1e30

f32 = jnp.float32
bf16 = jnp.bfloat16


def receive(value, axis, step):
    n = lax.axis_size(axis)
    return lax.ppermute(value, axis, [((i + step) % n, i) for i in range(n)])


def scale_rows(x_refs, gain_ref, scaled, squares=None):
    for i, ref in enumerate(x_refs):
        rows = pl.ds(i * 128, 128)
        floats = ref[...].astype(f32)
        scaled[rows, :] = (floats * gain_ref[...]).astype(bf16)
        if squares is not None:
            squares[:, rows] = lax.dot_general(
                jnp.ones((8, floats.shape[1]), bf16),
                (floats * floats).astype(bf16),
                (((1,), (1,)), ((), ())),
                preferred_element_type=f32,
            )


def kv_kernel(which, x0, x1, x2, x3, gain, key, value, out, squares, scaled):
    @pl.when(pl.program_id(0) == 0)
    def _():
        scale_rows((x0, x1, x2, x3), gain, scaled, squares)

    weight = jnp.concatenate([key[...], value[...]], axis=1)
    out[0] = jnp.dot(scaled[...], weight, preferred_element_type=f32).astype(bf16)


def project_kv(which, pieces, gain, key_weight, value_weight):
    depth = key_weight.shape[0]
    whole = pl.BlockSpec((128, depth), lambda j, w: (0, 0))
    column = pl.BlockSpec((depth, HEAD_SIZE), lambda j, w: (0, w[j]))
    return pl.pallas_call(
        kv_kernel,
        grid_spec=pltpu.PrefetchScalarGridSpec(
            num_scalar_prefetch=1,
            grid=(4,),
            in_specs=[whole] * 4 + [pl.BlockSpec((1, depth), lambda j, w: (0, 0)), column, column],
            out_specs=[
                pl.BlockSpec((1, PART, 2 * HEAD_SIZE), lambda j, w: (j, 0, 0)),
                pl.BlockSpec((8, PART), lambda j, w: (0, 0)),
            ],
            scratch_shapes=[pltpu.VMEM((PART, depth), bf16)],
        ),
        out_shape=[
            jax.ShapeDtypeStruct((4, PART, 2 * HEAD_SIZE), bf16),
            jax.ShapeDtypeStruct((8, PART), f32),
        ],
        compiler_params=pltpu.CompilerParams(vmem_limit_bytes=32 * 2**20),
        cost_estimate=pl.CostEstimate(flops=2 * PART * 2048 * 1024, bytes_accessed=8 * 2**20, transcendentals=0),
    )(which, *pieces, gain, key_weight, value_weight)


def query_kernel(place, x0, x1, x2, x3, x4, x5, x6, x7, gain, w0, w1, w2a, w2b, w3, out, scaled):
    step = pl.program_id(0)

    @pl.when(step == 0)
    def _():
        scale_rows((x0, x1, x2, x3, x4, x5, x6, x7), gain, scaled)

    for i, ref in ((0, w0), (1, w1), (3, w3)):

        @pl.when(step == i)
        def _():
            out[0] = jnp.dot(scaled[...], ref[...], preferred_element_type=f32).astype(bf16)

    @pl.when(step == 2)
    def _():
        half = w2a.shape[0]
        total = jnp.dot(scaled[:, :half], w2a[...], preferred_element_type=f32)
        total += jnp.dot(scaled[:, half:], w2b[...], preferred_element_type=f32)
        out[0] = total.astype(bf16)


def project_queries(place, pieces, gain, weights):
    depth, width = weights[0].shape
    return pl.pallas_call(
        query_kernel,
        grid_spec=pltpu.PrefetchScalarGridSpec(
            num_scalar_prefetch=1,
            grid=(4,),
            in_specs=[pl.BlockSpec(a.shape, lambda j, w: (0, 0)) for a in (*pieces, gain, *weights)],
            out_specs=pl.BlockSpec((1, GROUP_ROWS, width), lambda j, w: (w[j], 0, 0)),
            scratch_shapes=[pltpu.VMEM((GROUP_ROWS, depth), bf16)],
        ),
        out_shape=jax.ShapeDtypeStruct((4, GROUP_ROWS, width), bf16),
        compiler_params=pltpu.CompilerParams(vmem_limit_bytes=40 * 2**20),
        cost_estimate=pl.CostEstimate(
            flops=2 * GROUP_ROWS * 2048 * 1024, bytes_accessed=10 * 2**20, transcendentals=0
        ),
    )(place, *pieces, gain, *weights)


def turn(u, cosine, sine):
    return u * cosine + pltpu.roll(u, HEAD_SIZE // 2, 1) * sine


def finish_kernel(home, got, far, cosine, sine, columns, out):
    total = home[0].astype(f32) + got[0].astype(f32) + far[...].astype(f32)
    total = total * columns[:, 0:1]
    out[0] = turn(total[:, :HEAD_SIZE], cosine[...], sine[...]).astype(bf16)
    out[1] = total[:, HEAD_SIZE:].astype(bf16)


def finish_kv(out, got, far, cosine, sine, columns):
    wide = 2 * HEAD_SIZE
    rows = pl.BlockSpec((PART, HEAD_SIZE), lambda i: (0, 0))
    return pl.pallas_call(
        finish_kernel,
        grid=(1,),
        in_specs=[
            pl.BlockSpec((1, PART, wide), lambda i: (2, 0, 0)),
            pl.BlockSpec((1, PART, wide), lambda i: (0, 0, 0)),
            pl.BlockSpec((PART, wide), lambda i: (0, 0)),
            rows,
            rows,
            pl.BlockSpec((PART, 4), lambda i: (0, 0)),
        ],
        out_specs=pl.BlockSpec((2, PART, HEAD_SIZE), lambda i: (0, 0, 0)),
        out_shape=jax.ShapeDtypeStruct((2, PART, HEAD_SIZE), bf16),
        compiler_params=pltpu.CompilerParams(vmem_limit_bytes=16 * 2**20),
        cost_estimate=pl.CostEstimate(flops=PART * 2048, bytes_accessed=2 * 2**20, transcendentals=0),
    )(out, got, far, cosine, sine, columns)


def attention_kernel(
    scalars, home, got, far, cosine, sine, columns,
    own0, own1, up0, up1, k20, k21, v20, v21, out_ref, keys, values,
):
    dz = pl.program_id(0)
    y, z, xh = scalars[8], scalars[9], scalars[10]

    @pl.when(dz == 0)
    def _():
        for back, k_refs, v_refs in (
            (0, (own0.at[0], own1.at[0]), (own0.at[1], own1.at[1])),
            (1, (up0.at[0], up1.at[0]), (up0.at[1], up1.at[1])),
            (2, (k20, k21), (v20, v21)),
        ):
            for i in range(4):
                for dx in (0, 1):
                    at = ((2 - back) * 4 + lax.rem(z + i, 4)) * TILE + (xh ^ dx) * 128
                    at = pl.ds(pl.multiple_of(at, 128), 128)
                    keys[at, :] = k_refs[dx][i * 128 : (i + 1) * 128, :]
                    values[at, :] = v_refs[dx][i * 128 : (i + 1) * 128, :]

    def both(ref):
        return jnp.concatenate([ref[0], ref[1]], axis=0)

    cos, sin, cols = both(cosine), both(sine), both(columns)
    unit = f32(HEAD_SIZE ** (-0.5) * math.log2(math.e))
    raw = both(home[0]).astype(f32) + both(got[0]).astype(f32) + both(far).astype(f32)
    raw = raw * (cols[:, 0:1] * unit)
    q = jnp.concatenate(
        [turn(raw[:, :HEAD_SIZE], cos, sin), turn(raw[:, HEAD_SIZE:], cos, sin)], axis=0
    ).astype(bf16)
    shift = (y - 2) * GROUP_ROWS
    q_index = cols[:, 1:2].astype(jnp.int32) - shift
    q_start = cols[:, 2:3].astype(jnp.int32) - shift
    q_index = jnp.concatenate([q_index, q_index], axis=0)
    q_start = jnp.concatenate([q_start, q_start], axis=0)
    lane = lax.broadcasted_iota(jnp.int32, (1, TILE), 1)

    def step(masked, tile, carry):
        top, total, acc = carry
        at = pl.ds(pl.multiple_of(tile * TILE, TILE), TILE)
        s = lax.dot_general(q, keys[at, :], (((1,), (1,)), ((), ())), preferred_element_type=f32)
        if masked:
            k_index = lane + tile * TILE
            s = jnp.where((k_index <= q_index) & (k_index >= q_start), s, MASKED)
        new_top = jnp.maximum(top, jnp.max(s, axis=1, keepdims=True))
        p = jnp.exp2(s - new_top)
        decay = jnp.exp2(top - new_top)
        total = total * decay + jnp.sum(p, axis=1, keepdims=True)
        acc = acc * decay + jnp.dot(p.astype(bf16), values[at, :], preferred_element_type=f32)
        return new_top, total, acc

    carry = (
        jnp.full((2 * TILE, 1), MASKED, f32),
        jnp.zeros((2 * TILE, 1), f32),
        jnp.zeros((2 * TILE, HEAD_SIZE), f32),
    )
    last = 8 + lax.rem(z + dz, 4)
    first = jnp.maximum(scalars[dz] - shift // TILE, 0)
    clear = jnp.minimum(scalars[4 + dz] - shift // TILE, last)
    carry = lax.fori_loop(first, clear, functools.partial(step, True), carry)
    carry = lax.fori_loop(clear, last, functools.partial(step, False), carry)
    top, total, acc = step(True, last, carry)
    result = (acc / total).astype(bf16)
    for head in (0, 1):
        for dx in (0, 1):
            at = head * TILE + dx * 128
            out_ref[0, dx, :, head * HEAD_SIZE : (head + 1) * HEAD_SIZE] = result[at : at + 128]


def attention(scalars, out, got, far, cosine, sine, columns, own, up, k2, v2):
    wide = 2 * HEAD_SIZE
    out = out.reshape(4, 2, PART, wide)
    got = got.reshape(2, 2, PART, wide)
    far = far.reshape(2, PART, wide)
    two = pl.BlockSpec((2, PART, HEAD_SIZE), lambda i: (0, 0, 0))
    one = pl.BlockSpec((PART, HEAD_SIZE), lambda i: (0, 0))
    rows = pl.BlockSpec((2, 128, HEAD_SIZE), lambda i: (0, i, 0))
    return pl.pallas_call(
        attention_kernel,
        grid=(4,),
        in_specs=[
            pl.BlockSpec(memory_space=pltpu.SMEM),
            pl.BlockSpec((1, 2, 128, wide), lambda i: (2, 0, i, 0)),
            pl.BlockSpec((1, 2, 128, wide), lambda i: (0, 0, i, 0)),
            pl.BlockSpec((2, 128, wide), lambda i: (0, i, 0)),
            rows,
            rows,
            pl.BlockSpec((2, 128, 4), lambda i: (0, i, 0)),
        ]
        + [two] * 4
        + [one] * 4,
        out_specs=pl.BlockSpec((1, 2, 128, wide), lambda i: (i, 0, 0, 0)),
        out_shape=jax.ShapeDtypeStruct((4, 2, 128, wide), bf16),
        scratch_shapes=[pltpu.VMEM((3 * GROUP_ROWS, HEAD_SIZE), bf16)] * 2,
        compiler_params=pltpu.CompilerParams(vmem_limit_bytes=32 * 2**20),
        cost_estimate=pl.CostEstimate(flops=3 * 10**9, bytes_accessed=4 * 2**20, transcendentals=4 * 10**6),
    )(scalars, out, got, far, cosine, sine, columns, *own, *up, *k2, *v2)


def shards(tokens, norm_gain, segment_ids, w_query, key_weight, value_weight, w_output):
    xl, c, y, z, xh = (lax.axis_index(a) for a in ("xl", "c", "y", "z", "xh"))

    x = {(0, 0): tokens}
    x[1, 0] = receive(tokens, "z", 1)
    x[3, 0] = receive(tokens, "z", -1)
    x[0, 1] = receive(tokens, "xh", 1)
    w1 = receive(w_query, "y", 1)
    w3 = receive(w_query, "y", -1)
    x[2, 0] = jnp.concatenate(
        [receive(x[1, 0][:64], "z", 1), receive(x[3, 0][64:], "z", -1)], axis=0
    )
    near, x[2, 0] = lax.optimization_barrier((x[0, 1], x[2, 0]))
    x[1, 1] = receive(near, "z", 1)
    x[3, 1] = receive(near, "z", -1)
    x[2, 1] = receive(x[2, 0], "xh", 1)
    half = w_query.shape[0] // 2
    w2a = receive(w1[:half], "y", 1)
    w2b = receive(w3[half:], "y", -1)
    w_out_own, w2a, w2b = lax.optimization_barrier((w_output, w2a, w2b))
    w_out = lax.all_gather(w_out_own, "y", axis=0, tiled=True)

    def relative(by_place):
        turned = lax.dynamic_slice_in_dim(jnp.concatenate([by_place, by_place], axis=0), z, 4, 0)
        swapped = jnp.where(xh == 0, turned, turned[:, ::-1])
        return jnp.transpose(swapped, (1, 0, 2)).reshape(2, PART)

    own_rows = lax.dynamic_slice_in_dim(segment_ids, y * GROUP_ROWS, GROUP_ROWS, 0)
    segments = relative(own_rows.reshape(4, 2, 128))
    index = relative((y * GROUP_ROWS + jnp.arange(GROUP_ROWS, dtype=jnp.int32)).reshape(4, 2, 128))
    ids = jnp.arange(SEGMENTS, dtype=jnp.int32)
    before = jnp.sum((segment_ids[None, :] < ids[:, None]).astype(jnp.int32), axis=1)
    start = jnp.sum(jnp.where(segments[None] == ids[:, None, None], before[:, None, None], 0), axis=0)
    places = (index - start).astype(f32)
    freqs = jnp.exp(jnp.arange(64, dtype=f32) * f32(-2.0 * math.log(rope_base) / HEAD_SIZE))
    angles = places[:, :, None] * freqs
    cosine, sine = jnp.cos(angles), jnp.sin(angles)
    cosine = jnp.concatenate([cosine, cosine], axis=2)
    sine = jnp.concatenate([-sine, sine], axis=2)
    by_tile = start.reshape(2, 4, 128)
    lows = jnp.min(by_tile, axis=(0, 2)) // TILE
    clears = (jnp.max(by_tile, axis=(0, 2)) + TILE - 1) // TILE
    zero = jnp.int32(0)
    scalars = jnp.concatenate([lows, clears, jnp.stack([y, z, xh, zero])]).astype(jnp.int32)

    def gather_blk_sum(out):
        got = receive(out[:2], "c", 1)
        far = receive((out[3].astype(f32) + got[1].astype(f32)).astype(bf16), "xl", 1)
        return got, far

    gain = norm_gain[None, :]
    targets = [(xl * 2 + (1 - c)), ((1 - xl) * 2 + (1 - c)), (xl * 2 + c), ((1 - xl) * 2 + c)]
    which = jnp.stack([b * 2 + z // 2 for b in targets]).astype(jnp.int32)
    own, up, k2, v2, columns = [], [], [], [], []
    for dx in (0, 1):
        out, squares = project_kv(which, [x[dz, dx] for dz in range(4)], gain, key_weight, value_weight)
        got, far = gather_blk_sum(out)
        squares = squares + receive(squares, "c", 1)
        squares = squares + receive(squares, "xl", 1)
        scale = lax.rsqrt(squares[0] / MODEL_WIDTH + norm_eps)
        columns.append(
            jnp.stack([scale, index[dx].astype(f32), start[dx].astype(f32), jnp.zeros_like(scale)], axis=1)
        )
        kv = finish_kv(out, got, far, cosine[dx], sine[dx], columns[dx])
        one_up = receive(kv, "y", -1)
        v_down = receive(kv[1], "y", 1)
        own.append(kv)
        up.append(one_up)
        k2.append(receive(one_up[0], "y", -1))
        v2.append(receive(v_down, "y", 1))

    place = []
    for i in range(4):
        b = lax.rem(y + i, 4)
        place.append(jnp.where(b % 2 == c, 2, 0) + jnp.where(b // 2 == xl, 0, 1))
    place = jnp.stack(place).astype(jnp.int32)
    out = project_queries(
        place, [x[dz, dx] for dx in (0, 1) for dz in range(4)], gain, (w_query, w1, w2a, w2b, w3)
    )
    got, far = gather_blk_sum(out)
    mixed = attention(
        scalars, out, got, far, cosine, sine, jnp.stack(columns), own, up, k2, v2
    ).reshape(GROUP_ROWS, 2 * HEAD_SIZE)

    across = receive(mixed, "xl", 1)
    low, high = jnp.where(xl == 0, mixed, across), jnp.where(xl == 0, across, mixed)
    pair = jnp.concatenate([low, high], axis=1)
    other = receive(pair, "c", 1)
    even, odd = jnp.where(c == 0, pair, other), jnp.where(c == 0, other, pair)
    heads = jnp.concatenate([even[:, :256], odd[:, :256], even[:, 256:], odd[:, 256:]], axis=1)

    columns = w_out.shape[1] // 2

    def part(dz, side):
        return jnp.dot(
            heads[dz * TILE : (dz + 1) * TILE],
            w_out[:, side * columns : (side + 1) * columns],
            preferred_element_type=f32,
        )

    up = receive(part(2, 0).astype(bf16), "z", -1)
    down = receive(part(2, 1).astype(bf16), "z", 1)
    up_right = receive(part(1, 1).astype(bf16), "z", -1)
    down_left = receive(part(3, 0).astype(bf16), "z", 1)
    up_left = receive((part(1, 0) + up.astype(f32)).astype(bf16), "z", -1)
    down_right = receive((part(3, 1) + down.astype(f32)).astype(bf16), "z", 1)
    left = part(0, 0) + down_left.astype(f32) + up_left.astype(f32)
    right = part(0, 1) + up_right.astype(f32) + down_right.astype(f32)
    rows = jnp.concatenate([left, right], axis=1)
    last = receive(rows[128:].astype(bf16), "xh", 1)
    return (rows[:128] + last.astype(f32)).astype(bf16)


def solution(mesh):
    fine = Mesh(mesh.devices.reshape(2, 2, 4, 4, 2), ("xl", "c", "y", "z", "xh"))
    blk, tensor = ("xl", "c"), ("y", "z", "xh")
    placed = (
        P(tensor, blk),
        P(blk),
        P(),
        P(blk, tensor),
        P(blk, None),
        P(blk, None),
        P(tensor, blk),
    )
    return jax.shard_map(
        shards, mesh=fine, in_specs=placed, out_specs=P(tensor, blk), check_vma=False
    )
```

time: 238 us -> 247 us (1.038)
  the two profiles are of different devices: /device:TPU:16 before, /device:TPU:12 now
where the time goes in v2:
time: 247 us; the launch traced here: 245 us
  waiting for transfers between devices  87 us (35%)
  starting transfers between devices  41.3 us (17%)
  local copies, waits for them, and re-layouts  39.9 us (16%)
  Pallas kernels  39.7 us (16%)
  other arithmetic  15.8 us (6%)
  between operations  14.1 us (6%)
  matrix products  7.63 us (3%)
    ppermute x39, waiting for transfers between devices, receive(): return lax.ppermute(value, axis, [((i + step) % n, i) for i in range(n)])  87 us
    ppermute x39, starting transfers between devices, receive(): return lax.ppermute(value, axis, [((i + step) % n, i) for i in range(n)])  41.3 us
    unnamed x86, local copies, waits for them, and re-layouts  29.7 us
    pallas_call x1, Pallas kernels, attention(): pl.pallas_call(attention_kernel, grid=(4,), in_specs=[pl.BlockSpec(memory...  16.9 us
    pallas_call x2, Pallas kernels, project_kv(): pl.pallas_call(kv_kernel, grid_spec=pltpu.PrefetchScalarGridSpec(num_scal...  11.8 us
    pallas_call x1, Pallas kernels, project_queries(): pl.pallas_call(query_kernel, grid_spec=pltpu.PrefetchScalarGridSpec(num_s...  8.33 us
    dot_general x8, matrix products, part(): jnp.dot(heads[dz * TILE:(dz + 1) * TILE], w_out[:, side * columns:(side +...  7.63 us
    convert_element_type x3, other arithmetic, gather_blk_sum(): (out[3].astype(f32) + got[1].astype(f32)).astype(bf16)  5.02 us
  transfers between devices with their start and end apart: 40, of which 15 were waited for; matrix products, arithmetic and copies ran while one was open for 12% of the time, Pallas kernels for 16%

profile of v2, /device:TPU:12, one launch (start us, length us, event | category | flops | bytes accessed | tf_op | source)
XLA Modules:
  0.0 245.4 jit_solution(3819226000033792636)
XLA Ops:
  6.5 4.0 %collective-permute-start = (bf16[128,2048]{1,0:T(8,128)(2,1)}, bf16[128,2048]{1,0:T(8,128)(2,1)S(1)}, u32[]{:S(2)}, u32[]{:S(2)}) collective-permute-start(bf16[128,2048]{1,0:T(8,128)(2,1)} %x0.3), channel_id=1, source_target_pairs={{2,0},{4,2},{6,4},{0,6},{3,1},{5,3},{7,5},{1,7},{10,8},{12,10},{14... | collective-permute-start | bytes 1572872 | tf_op jit(solution)/shard_map/ppermute | solution.py:31
  11.1 1.6 collective-permute-start.10
  15.0 1.9 fusion.75
  16.9 5.1 %collective-permute-done.x1 = bf16[128,2048]{1,0:T(8,128)(2,1)S(1)} collective-permute-done((bf16[128,2048]{1,0:T(8,128)(2,1)}, bf16[128,2048]{1,0:T(8,128)(2,1)S(1)}, u32[]{:S(2)}, u32[]{:S(2)}) %collective-permute-start) | collective-permute-done | bytes 524320 | tf_op jit(solution)/shard_map/ppermute | solution.py:31
  22.1 3.7 %collective-permute-start.2 = (bf16[64,2048]{1,0:T(8,128)(2,1)S(1)}, bf16[64,2048]{1,0:T(8,128)(2,1)S(1)}, u32[]{:S(2)}, u32[]{:S(2)}) collective-permute-start(bf16[64,2048]{1,0:T(8,128)(2,1)S(1)} %slice.169), channel_id=1, source_target_pairs={{2,0},{4,2},{6,4},{0,6},{3,1},{5,3},{7,5},{1,7},{10,8},{12,10},{14... | collective-permute-start | bytes 786440 | tf_op jit(solution)/shard_map/ppermute | solution.py:31
  25.9 1.2 fusion.68
  27.1 3.3 %collective-permute-done.2 = bf16[64,2048]{1,0:T(8,128)(2,1)S(1)} collective-permute-done((bf16[64,2048]{1,0:T(8,128)(2,1)S(1)}, bf16[64,2048]{1,0:T(8,128)(2,1)S(1)}, u32[]{:S(2)}, u32[]{:S(2)}) %collective-permute-start.2) | collective-permute-done | bytes 262176 | tf_op jit(solution)/shard_map/ppermute | solution.py:31
  30.5 3.5 %collective-permute-done.4 = bf16[64,2048]{1,0:T(8,128)(2,1)S(1)} collective-permute-done((bf16[64,2048]{1,0:T(8,128)(2,1)S(1)}, bf16[64,2048]{1,0:T(8,128)(2,1)S(1)}, u32[]{:S(2)}, u32[]{:S(2)}) %collective-permute-start.4) | collective-permute-done | bytes 262176 | tf_op jit(solution)/shard_map/ppermute | solution.py:31
  35.1 1.8 collective-permute-start.7
  37.0 2.2 copy-done
  39.2 2.2 copy-done.2
  41.4 5.3 %shard_map.74 = (bf16[4,512,256]{2,1,0:T(8,128)(2,1)S(1)}, f32[8,512]{1,0:T(8,128)S(1)}) custom-call(s32[4]{0:T(128)S(1)} %pad_add_fusion.1.which, bf16[128,2048]{1,0:T(8,128)(2,1)S(1)} %copy-done.16, bf16[128,2048]{1,0:T(8,128)(2,1)S(1)} %collective-permute-done.x1, bf16[128,2048]{1,0:T(8,128)(2,1)S(1)} %pad_maximum_fusion.3.x2, ...), custom_call_target="tpu_custom_call" | custom-call | flops 2147483648 | bytes 8388608 | tf_op jit(solution)/shard_map/pallas_call | solution.py:61
  48.0 1.1 slice.172
  49.7 1.1 slice.171
  50.8 1.6 collective-permute-start.11
  53.0 2.1 collective-permute-start.15
  55.0 2.2 copy-done.1
  57.2 2.2 copy-done.3
  59.4 6.6 %shard_map.75 = (bf16[4,512,256]{2,1,0:T(8,128)(2,1)S(1)}, f32[8,512]{1,0:T(8,128)S(1)}) custom-call(s32[4]{0:T(128)S(1)} %pad_add_fusion.1.which, bf16[128,2048]{1,0:T(8,128)(2,1)} %collective-permute-done.1.x4.x0, bf16[128,2048]{1,0:T(8,128)(2,1)} %collective-permute-done.5.x5.x1, bf16[128,2048]{1,0:T(8,128)(2,1)} %collective-permute-done.6.x6.x2, ...), custom_call_target="tpu_custom_call" | custom-call | flops 2147483648 | bytes 8388608 | tf_op jit(solution)/shard_map/pallas_call | solution.py:61
  69.2 1.8 fusion.73
  70.9 2.0 collective-permute-start.19
  73.0 1.0 copy-done.5
  74.0 1.0 copy-done.17
  75.0 1.2 copy-done.24
  76.3 1.0 copy-done.26
  77.3 1.1 copy-done.28
  78.4 8.3 %shard_map.73 = bf16[4,1024,256]{2,1,0:T(8,128)(2,1)S(1)} custom-call(s32[4]{0:T(128)S(1)} %pad_add_fusion.place, bf16[128,2048]{1,0:T(8,128)(2,1)S(1)} %copy-done.17, bf16[128,2048]{1,0:T(8,128)(2,1)S(1)} %collective-permute-done.x1, bf16[128,2048]{1,0:T(8,128)(2,1)S(1)} %pad_maximum_fusion.3.x2, bf16[128,2048]{1,0:T(8,128)(2,1)S(1)} %copy-done.5, ...), custom_call_target="tpu_custom_call" | custom-call | flops 4294967296 | bytes 10485760 | tf_op jit(solution)/shard_map/pallas_call | solution.py:105
  86.7 1.4 copy-done.6
  88.1 1.1 slice.173
  90.2 1.0 copy-done.9
  91.1 0.9 copy-done.11
  92.1 1.3 shard_map.76.own0
  93.4 1.1 fusion.74
  94.7 1.8 collective-permute-start.26
  97.5 6.3 %collective-permute-done.26 = bf16[512,128]{1,0:T(8,128)(2,1)} collective-permute-done((bf16[512,128]{1,0:T(8,128)(2,1)S(1)}, bf16[512,128]{1,0:T(8,128)(2,1)}, u32[]{:S(2)}, u32[]{:S(2)}) %collective-permute-start.26) | collective-permute-done | bytes 131104 | tf_op jit(solution)/shard_map/ppermute | solution.py:31
  103.8 1.8 collective-permute-start.27
  105.6 0.9 copy-done.8
  106.6 1.3 shard_map.77.own1
  108.2 2.8 %collective-permute-start.28 = (bf16[512,128]{1,0:T(8,128)(2,1)S(1)}, bf16[512,128]{1,0:T(8,128)(2,1)}, u32[]{:S(2)}, u32[]{:S(2)}) collective-permute-start(bf16[512,128]{1,0:T(8,128)(2,1)S(1)} %slice_bitcast_fusion), channel_id=1, source_target_pairs={{8,0},{16,8},{24,16},{0,24},{9,1},{17,9},{25,17},{1,25},{10,2},{18... | collective-permute-start | bytes 393224 | tf_op jit(solution)/shard_map/ppermute | solution.py:31
  111.0 2.1 fusion.56
  113.2 1.8 collective-permute-start.13
  115.1 3.3 %collective-permute-done.28 = bf16[512,128]{1,0:T(8,128)(2,1)} collective-permute-done((bf16[512,128]{1,0:T(8,128)(2,1)S(1)}, bf16[512,128]{1,0:T(8,128)(2,1)}, u32[]{:S(2)}, u32[]{:S(2)}) %collective-permute-start.28) | collective-permute-done | bytes 131104 | tf_op jit(solution)/shard_map/ppermute | solution.py:31
  118.4 2.2 collective-permute-start.29
  120.6 3.0 %collective-permute-done.23.up1 = bf16[2,512,128]{2,1,0:T(8,128)(2,1)S(1)} collective-permute-done((bf16[2,512,128]{2,1,0:T(8,128)(2,1)S(1)}, bf16[2,512,128]{2,1,0:T(8,128)(2,1)S(1)}, u32[]{:S(2)}, u32[]{:S(2)}) %collective-permute-start.23) | collective-permute-done | bytes 262176 | tf_op jit(solution)/shard_map/ppermute | solution.py:31
  124.4 1.3 pad_maximum_fusion.4
  126.4 1.3 pad_maximum_fusion.6
  127.7 1.8 copy.19.columns
  130.8 1.2 collective-permute-done.25.k21
  133.6 1.0 copy-done.18
  134.7 1.0 copy-done.19
  135.7 1.0 copy-done.20
  140.4 16.9 %shard_map.78 = bf16[4,2,128,256]{3,2,1,0:T(8,128)(2,1)} custom-call(s32[12]{0:T(128)S(1)} %concatenate.28.scalars, bf16[4,2,512,256]{3,2,1,0:T(8,128)(2,1)S(1)} %bitcast.71, bf16[2,2,512,256]{3,2,1,0:T(8,128)(2,1)} %bitcast.14.got, bf16[2,512,256]{2,1,0:T(8,128)(2,1)} %bitcast.16.far, f32[2,512,128]{2,1,0:T(8,128)S(1)} %copy-done.18, ...), custom_call_target="tpu_custom_call" | custom-call | flops 3000000000 | bytes 4194304 | tf_op jit(solution)/shard_map/pallas_call | solution.py:232
  157.4 1.2 collective-permute-start.30
  158.5 12.7 %collective-permute-done.30 = bf16[1024,256]{1,0:T(8,128)(2,1)S(1)} collective-permute-done((bf16[1024,256]{1,0:T(8,128)(2,1)}, bf16[1024,256]{1,0:T(8,128)(2,1)S(1)}, u32[]{:S(2)}, u32[]{:S(2)}) %collective-permute-start.30) | collective-permute-done | bytes 524320 | tf_op jit(solution)/shard_map/ppermute | solution.py:31
  171.2 1.1 broadcast_select_fusion.3
  172.5 2.6 %collective-permute-done.31 = bf16[1024,512]{1,0:T(8,128)(2,1)S(1)} collective-permute-done((bf16[1024,512]{1,0:T(8,128)(2,1)S(1)}, bf16[1024,512]{1,0:T(8,128)(2,1)S(1)}, u32[]{:S(2)}, u32[]{:S(2)}) %collective-permute-start.31) | collective-permute-done | bytes 1048608 | tf_op jit(solution)/shard_map/ppermute | solution.py:31
  176.0 2.5 %fusion.43 = bf16[256,1024]{1,0:T(8,128)(2,1)S(1)} fusion(bf16[1024,2048]{1,0:T(8,128)(2,1)} %all-gather.2.cloned.1.call-done, bf16[1024,1024]{1,0:T(8,128)(2,1)S(1)} %pad_maximum_fusion), kind=kOutput, calls=%fused_computation.28 | convolution fusion | flops 537133056 | bytes 3145728 | tf_op jit(solution)/shard_map/dot_general | solution.py:348
  178.5 3.0 %collective-permute-start.36 = (bf16[256,1024]{1,0:T(8,128)(2,1)S(1)}, bf16[256,1024]{1,0:T(8,128)(2,1)S(1)}, u32[]{:S(2)}, u32[]{:S(2)}) collective-permute-start(bf16[256,1024]{1,0:T(8,128)(2,1)S(1)} %fusion.43), channel_id=1, source_target_pairs={{2,0},{4,2},{6,4},{0,6},{3,1},{5,3},{7,5},{1,7},{10,8},{12,10},{14... | collective-permute-start | bytes 1572872 | tf_op jit(solution)/shard_map/ppermute | solution.py:31
  183.8 9.2 %collective-permute-done.36 = bf16[256,1024]{1,0:T(8,128)(2,1)S(1)} collective-permute-done((bf16[256,1024]{1,0:T(8,128)(2,1)S(1)}, bf16[256,1024]{1,0:T(8,128)(2,1)S(1)}, u32[]{:S(2)}, u32[]{:S(2)}) %collective-permute-start.36) | collective-permute-done | bytes 524320 | tf_op jit(solution)/shard_map/ppermute | solution.py:31
  193.8 3.8 %collective-permute-start.37 = (bf16[256,1024]{1,0:T(8,128)(2,1)S(1)}, bf16[256,1024]{1,0:T(8,128)(2,1)S(1)}, u32[]{:S(2)}, u32[]{:S(2)}) collective-permute-start(bf16[256,1024]{1,0:T(8,128)(2,1)S(1)} %fusion.49), channel_id=1, source_target_pairs={{2,0},{4,2},{6,4},{0,6},{3,1},{5,3},{7,5},{1,7},{10,8},{12,10},{14... | collective-permute-start | bytes 1572872 | tf_op jit(solution)/shard_map/ppermute | solution.py:31
  198.4 10.1 %collective-permute-done.33 = bf16[256,1024]{1,0:T(8,128)(2,1)S(1)} collective-permute-done((bf16[256,1024]{1,0:T(8,128)(2,1)S(1)}, bf16[256,1024]{1,0:T(8,128)(2,1)S(1)}, u32[]{:S(2)}, u32[]{:S(2)}) %collective-permute-start.33) | collective-permute-done | bytes 524320 | tf_op jit(solution)/shard_map/ppermute | solution.py:31
  210.7 8.7 %collective-permute-done.32 = bf16[256,1024]{1,0:T(8,128)(2,1)S(1)} collective-permute-done((bf16[256,1024]{1,0:T(8,128)(2,1)S(1)}, bf16[256,1024]{1,0:T(8,128)(2,1)S(1)}, u32[]{:S(2)}, u32[]{:S(2)}) %collective-permute-start.32) | collective-permute-done | bytes 524320 | tf_op jit(solution)/shard_map/ppermute | solution.py:31
  219.4 3.9 %collective-permute-done.34 = bf16[256,1024]{1,0:T(8,128)(2,1)S(1)} collective-permute-done((bf16[256,1024]{1,0:T(8,128)(2,1)S(1)}, bf16[256,1024]{1,0:T(8,128)(2,1)S(1)}, u32[]{:S(2)}, u32[]{:S(2)}) %collective-permute-start.34) | collective-permute-done | bytes 524320 | tf_op jit(solution)/shard_map/ppermute | solution.py:31
  224.4 13.2 %collective-permute-done.38 = bf16[128,2048]{1,0:T(8,128)(2,1)S(1)} collective-permute-done((bf16[128,2048]{1,0:T(8,128)(2,1)S(1)}, bf16[128,2048]{1,0:T(8,128)(2,1)S(1)}, u32[]{:S(2)}, u32[]{:S(2)}) %collective-permute-start.38) | collective-permute-done | bytes 524320 | tf_op jit(solution)/shard_map/ppermute | solution.py:31
  (173 shorter events, 29.2 us)
Async XLA Ops:
  6.5 169.5 %all-gather.2.cloned.1.call-start = ((), (), s32[]{:S(2)}) async-start(), calls=%async_computation | async-start | bytes 5242880 | tf_op jit(solution)/shard_map/all_gather | solution.py:274
  6.5 15.5 %collective-permute-start = (bf16[128,2048]{1,0:T(8,128)(2,1)}, bf16[128,2048]{1,0:T(8,128)(2,1)S(1)}, u32[]{:S(2)}, u32[]{:S(2)}) collective-permute-start(bf16[128,2048]{1,0:T(8,128)(2,1)} %x0.3), channel_id=1, source_target_pairs={{2,0},{4,2},{6,4},{0,6},{3,1},{5,3},{7,5},{1,7},{10,8},{12,10},{14... | collective-permute-start | bytes 1572872 | tf_op jit(solution)/shard_map/ppermute | solution.py:31
  10.6 15.2 %collective-permute-start.3 = (bf16[128,2048]{1,0:T(8,128)(2,1)}, bf16[128,2048]{1,0:T(8,128)(2,1)S(1)}, u32[]{:S(2)}, u32[]{:S(2)}) collective-permute-start(bf16[128,2048]{1,0:T(8,128)(2,1)} %x0.3), channel_id=1, source_target_pairs={{6,0},{0,2},{2,4},{4,6},{7,1},{1,3},{3,5},{5,7},{14,8},{8,10},{10,... | collective-permute-start | bytes 1572872 | tf_op jit(solution)/shard_map/ppermute | solution.py:31
  10.6 23.4 %collective-permute-start.1 = (bf16[128,2048]{1,0:T(8,128)(2,1)}, bf16[128,2048]{1,0:T(8,128)(2,1)}, u32[]{:S(2)}, u32[]{:S(2)}) collective-permute-start(bf16[128,2048]{1,0:T(8,128)(2,1)} %x0.3), channel_id=1, source_target_pairs={{1,0},{0,1},{3,2},{2,3},{5,4},{4,5},{7,6},{6,7},{9,8},{8,9},{11,10... | collective-permute-start | bytes 1572872 | tf_op jit(solution)/shard_map/ppermute | solution.py:31
  11.1 35.6 %collective-permute-start.10 = (bf16[2048,256]{1,0:T(8,128)(2,1)}, bf16[2048,256]{1,0:T(8,128)(2,1)}, u32[]{:S(2)}, u32[]{:S(2)}) collective-permute-start(bf16[2048,256]{1,0:T(8,128)(2,1)} %w0.1), channel_id=1, source_target_pairs={{24,0},{0,8},{8,16},{16,24},{25,1},{1,9},{9,17},{17,25},{26,2},{2,... | collective-permute-start | bytes 3145736 | tf_op jit(solution)/shard_map/ppermute | solution.py:31
  12.7 36.4 %collective-permute-start.8 = (bf16[2048,256]{1,0:T(8,128)(2,1)}, bf16[2048,256]{1,0:T(8,128)(2,1)}, u32[]{:S(2)}, u32[]{:S(2)}) collective-permute-start(bf16[2048,256]{1,0:T(8,128)(2,1)} %w0.1), channel_id=1, source_target_pairs={{8,0},{16,8},{24,16},{0,24},{9,1},{17,9},{25,17},{1,25},{10,2},{18... | collective-permute-start | bytes 3145736 | tf_op jit(solution)/shard_map/ppermute | solution.py:31
  16.9 9.0 %copy-start.35 = (f32[2,512,64]{2,1,0:T(8,128)}, f32[2,512,64]{2,1,0:T(8,128)S(1)}, u32[]{:S(2)}) copy-start(f32[2,512,64]{2,1,0:T(8,128)S(1)} %get-tuple-element.37) | copy-start | bytes 786436
  16.9 9.0 %copy-start.37 = (f32[2,512,64]{2,1,0:T(8,128)}, f32[2,512,64]{2,1,0:T(8,128)S(1)}, u32[]{:S(2)}) copy-start(f32[2,512,64]{2,1,0:T(8,128)S(1)} %get-tuple-element.38) | copy-start | bytes 786436
  16.9 9.0 %copy-start.39 = (f32[2,512,64]{2,1,0:T(8,128)}, f32[2,512,64]{2,1,0:T(8,128)S(1)}, u32[]{:S(2)}) copy-start(f32[2,512,64]{2,1,0:T(8,128)S(1)} %get-tuple-element.39) | copy-start | bytes 786436
  22.1 14.9 %copy-start.16 = (bf16[128,2048]{1,0:T(8,128)(2,1)S(1)}, bf16[128,2048]{1,0:T(8,128)(2,1)}, u32[]{:S(2)}) copy-start(bf16[128,2048]{1,0:T(8,128)(2,1)} %x0.3) | copy-start | bytes 1572868
  22.1 14.9 %copy-start.23 = (f32[2048]{0:T(1024)S(1)}, f32[2048]{0:T(1024)}, u32[]{:S(2)}) copy-start(f32[2048]{0:T(1024)} %param.8) | copy-start | bytes 24580
  22.1 8.3 %collective-permute-start.2 = (bf16[64,2048]{1,0:T(8,128)(2,1)S(1)}, bf16[64,2048]{1,0:T(8,128)(2,1)S(1)}, u32[]{:S(2)}, u32[]{:S(2)}) collective-permute-start(bf16[64,2048]{1,0:T(8,128)(2,1)S(1)} %slice.169), channel_id=1, source_target_pairs={{2,0},{4,2},{6,4},{0,6},{3,1},{5,3},{7,5},{1,7},{10,8},{12,10},{14... | collective-permute-start | bytes 786440 | tf_op jit(solution)/shard_map/ppermute | solution.py:31
  25.8 11.2 %copy-start.4 = (bf16[128,2048]{1,0:T(8,128)(2,1)}, bf16[128,2048]{1,0:T(8,128)(2,1)S(1)}, u32[]{:S(2)}) copy-start(bf16[128,2048]{1,0:T(8,128)(2,1)S(1)} %collective-permute-done.3.x3) | copy-start | bytes 1572868
  25.8 8.2 %collective-permute-start.4 = (bf16[64,2048]{1,0:T(8,128)(2,1)S(1)}, bf16[64,2048]{1,0:T(8,128)(2,1)S(1)}, u32[]{:S(2)}, u32[]{:S(2)}) collective-permute-start(bf16[64,2048]{1,0:T(8,128)(2,1)S(1)} %slice.170), channel_id=1, source_target_pairs={{6,0},{0,2},{2,4},{4,6},{7,1},{1,3},{3,5},{5,7},{14,8},{8,10},{10,... | collective-permute-start | bytes 786440 | tf_op jit(solution)/shard_map/ppermute | solution.py:31
  34.0 18.4 %collective-permute-start.6 = (bf16[128,2048]{1,0:T(8,128)(2,1)S(1)}, bf16[128,2048]{1,0:T(8,128)(2,1)}, u32[]{:S(2)}, u32[]{:S(2)}) collective-permute-start(bf16[128,2048]{1,0:T(8,128)(2,1)S(1)} %pad_maximum_fusion.3.x2), channel_id=1, source_target_pairs={{1,0},{0,1},{3,2},{2,3},{5,4},{4,5},{7,6},{6,7},{9,8},{8,9},{11,10... | collective-permute-start | bytes 1572872 | tf_op jit(solution)/shard_map/ppermute | solution.py:31
  34.8 18.1 %collective-permute-start.5 = (bf16[128,2048]{1,0:T(8,128)(2,1)}, bf16[128,2048]{1,0:T(8,128)(2,1)}, u32[]{:S(2)}, u32[]{:S(2)}) collective-permute-start(bf16[128,2048]{1,0:T(8,128)(2,1)} %collective-permute-done.1.x4.x0), channel_id=1, source_target_pairs={{2,0},{4,2},{6,4},{0,6},{3,1},{5,3},{7,5},{1,7},{10,8},{12,10},{14... | collective-permute-start | bytes 1572872 | tf_op jit(solution)/shard_map/ppermute | solution.py:31
  35.1 19.9 %collective-permute-start.7 = (bf16[128,2048]{1,0:T(8,128)(2,1)}, bf16[128,2048]{1,0:T(8,128)(2,1)}, u32[]{:S(2)}, u32[]{:S(2)}) collective-permute-start(bf16[128,2048]{1,0:T(8,128)(2,1)} %collective-permute-done.1.x4.x0), channel_id=1, source_target_pairs={{6,0},{0,2},{2,4},{4,6},{7,1},{1,3},{3,5},{5,7},{14,8},{8,10},{10,... | collective-permute-start | bytes 1572872 | tf_op jit(solution)/shard_map/ppermute | solution.py:31
  37.0 2.2 copy-start
  39.2 2.2 copy-start.2
  46.7 4.1 %collective-permute-start.14 = (f32[8,512]{1,0:T(8,128)S(1)}, f32[8,512]{1,0:T(8,128)S(1)}, u32[]{:S(2)}, u32[]{:S(2)}) collective-permute-start(f32[8,512]{1,0:T(8,128)S(1)} %get-tuple-element.18), channel_id=1, source_target_pairs={{32,0},{0,32},{33,1},{1,33},{34,2},{2,34},{35,3},{3,35},{36,4},{4,... | collective-permute-start | bytes 49160 | tf_op jit(solution)/shard_map/ppermute | solution.py:31
  49.1 20.1 %collective-permute-start.18 = (bf16[2,512,256]{2,1,0:T(8,128)(2,1)}, bf16[2,512,256]{2,1,0:T(8,128)(2,1)}, u32[]{:S(2)}, u32[]{:S(2)}) collective-permute-start(bf16[2,512,256]{2,1,0:T(8,128)(2,1)} %slice.143), channel_id=1, source_target_pairs={{32,0},{0,32},{33,1},{1,33},{34,2},{2,34},{35,3},{3,35},{36,4},{4,... | collective-permute-start | bytes 1572872 | tf_op jit(solution)/shard_map/ppermute | solution.py:31
  50.8 16.8 %collective-permute-start.11 = (bf16[1024,256]{1,0:T(8,128)(2,1)S(1)}, bf16[1024,256]{1,0:T(8,128)(2,1)S(1)}, u32[]{:S(2)}, u32[]{:S(2)}) collective-permute-start(bf16[1024,256]{1,0:T(8,128)(2,1)S(1)} %slice.172), channel_id=1, source_target_pairs={{24,0},{0,8},{8,16},{16,24},{25,1},{1,9},{9,17},{17,25},{26,2},{2,... | collective-permute-start | bytes 1572872 | tf_op jit(solution)/shard_map/ppermute | solution.py:31
  52.4 15.9 %collective-permute-start.9 = (bf16[1024,256]{1,0:T(8,128)(2,1)S(1)}, bf16[1024,256]{1,0:T(8,128)(2,1)S(1)}, u32[]{:S(2)}, u32[]{:S(2)}) collective-permute-start(bf16[1024,256]{1,0:T(8,128)(2,1)S(1)} %slice.171), channel_id=1, source_target_pairs={{8,0},{16,8},{24,16},{0,24},{9,1},{17,9},{25,17},{1,25},{10,2},{18... | collective-permute-start | bytes 1572872 | tf_op jit(solution)/shard_map/ppermute | solution.py:31
  53.0 13.1 %collective-permute-start.15 = (f32[8,512]{1,0:T(8,128)S(1)}, f32[8,512]{1,0:T(8,128)S(1)}, u32[]{:S(2)}, u32[]{:S(2)}) collective-permute-start(f32[8,512]{1,0:T(8,128)S(1)} %add.176), channel_id=1, source_target_pairs={{64,0},{0,64},{65,1},{1,65},{66,2},{2,66},{67,3},{3,67},{68,4},{4,... | collective-permute-start | bytes 49160 | tf_op jit(solution)/shard_map/ppermute | solution.py:31
  55.0 2.2 copy-start.1
  57.2 2.2 copy-start.3
  66.0 1.4 collective-permute-start.16
  66.9 26.4 %collective-permute-start.20 = (bf16[2,512,256]{2,1,0:T(8,128)(2,1)}, bf16[2,512,256]{2,1,0:T(8,128)(2,1)}, u32[]{:S(2)}, u32[]{:S(2)}) collective-permute-start(bf16[2,512,256]{2,1,0:T(8,128)(2,1)} %slice.148), channel_id=1, source_target_pairs={{32,0},{0,32},{33,1},{1,33},{34,2},{2,34},{35,3},{3,35},{36,4},{4,... | collective-permute-start | bytes 1572872 | tf_op jit(solution)/shard_map/ppermute | solution.py:31
  67.4 5.5 %collective-permute-start.17 = (f32[8,512]{1,0:T(8,128)S(1)}, f32[8,512]{1,0:T(8,128)S(1)}, u32[]{:S(2)}, u32[]{:S(2)}) collective-permute-start(f32[8,512]{1,0:T(8,128)S(1)} %add.179), channel_id=1, source_target_pairs={{64,0},{0,64},{65,1},{1,65},{66,2},{2,66},{67,3},{3,67},{68,4},{4,... | collective-permute-start | bytes 49160 | tf_op jit(solution)/shard_map/ppermute | solution.py:31
  70.9 19.2 %collective-permute-start.19 = (bf16[512,256]{1,0:T(8,128)(2,1)}, bf16[512,256]{1,0:T(8,128)(2,1)}, u32[]{:S(2)}, u32[]{:S(2)}) collective-permute-start(bf16[512,256]{1,0:T(8,128)(2,1)} %fusion.73), channel_id=1, source_target_pairs={{64,0},{0,64},{65,1},{1,65},{66,2},{2,66},{67,3},{3,67},{68,4},{4,... | collective-permute-start | bytes 786440 | tf_op jit(solution)/shard_map/ppermute | solution.py:31
  75.0 1.2 copy-start.24
  77.3 1.1 copy-start.28
  86.7 1.4 copy-start.6
  88.1 2.1 copy-start.10
  89.2 21.8 %collective-permute-start.12 = (bf16[2,1024,256]{2,1,0:T(8,128)(2,1)}, bf16[2,1024,256]{2,1,0:T(8,128)(2,1)}, u32[]{:S(2)}, u32[]{:S(2)}) collective-permute-start(bf16[2,1024,256]{2,1,0:T(8,128)(2,1)} %slice.173), channel_id=1, source_target_pairs={{32,0},{0,32},{33,1},{1,33},{34,2},{2,34},{35,3},{3,35},{36,4},{4,... | collective-permute-start | bytes 3145736 | tf_op jit(solution)/shard_map/ppermute | solution.py:31
  89.3 7.7 %copy-start.41 = (f32[512,4]{0,1:T(4,128)}, f32[512,4]{0,1:T(4,128)S(1)}, u32[]{:S(2)}) copy-start(f32[512,4]{0,1:T(4,128)S(1)} %get-tuple-element.46) | copy-start | bytes 24580
  93.3 3.7 %copy-start.12 = (bf16[2,512,128]{2,1,0:T(8,128)(2,1)}, bf16[2,512,128]{2,1,0:T(8,128)(2,1)S(1)}, u32[]{:S(2)}) copy-start(bf16[2,512,128]{2,1,0:T(8,128)(2,1)S(1)} %shard_map.76.own0) | copy-start | bytes 786436
  94.5 11.1 %collective-permute-start.21 = (bf16[512,256]{1,0:T(8,128)(2,1)S(1)}, bf16[512,256]{1,0:T(8,128)(2,1)S(1)}, u32[]{:S(2)}, u32[]{:S(2)}) collective-permute-start(bf16[512,256]{1,0:T(8,128)(2,1)S(1)} %fusion.74), channel_id=1, source_target_pairs={{64,0},{0,64},{65,1},{1,65},{66,2},{2,66},{67,3},{3,67},{68,4},{4,... | collective-permute-start | bytes 786440 | tf_op jit(solution)/shard_map/ppermute | solution.py:31
  94.7 9.1 %collective-permute-start.26 = (bf16[512,128]{1,0:T(8,128)(2,1)S(1)}, bf16[512,128]{1,0:T(8,128)(2,1)}, u32[]{:S(2)}, u32[]{:S(2)}) collective-permute-start(bf16[512,128]{1,0:T(8,128)(2,1)S(1)} %slice_bitcast_fusion.1), channel_id=1, source_target_pairs={{8,0},{16,8},{24,16},{0,24},{9,1},{17,9},{25,17},{1,25},{10,2},{18... | collective-permute-start | bytes 393224 | tf_op jit(solution)/shard_map/ppermute | solution.py:31
  97.2 17.8 %collective-permute-start.22 = (bf16[2,512,128]{2,1,0:T(8,128)(2,1)}, bf16[2,512,128]{2,1,0:T(8,128)(2,1)S(1)}, u32[]{:S(2)}, u32[]{:S(2)}) collective-permute-start(bf16[2,512,128]{2,1,0:T(8,128)(2,1)} %copy-done.12), channel_id=1, source_target_pairs={{24,0},{0,8},{8,16},{16,24},{25,1},{1,9},{9,17},{17,25},{26,2},{2,... | collective-permute-start | bytes 786440 | tf_op jit(solution)/shard_map/ppermute | solution.py:31
  103.8 25.7 %collective-permute-start.27 = (bf16[512,128]{1,0:T(8,128)(2,1)}, bf16[512,128]{1,0:T(8,128)(2,1)S(1)}, u32[]{:S(2)}, u32[]{:S(2)}) collective-permute-start(bf16[512,128]{1,0:T(8,128)(2,1)} %collective-permute-done.26), channel_id=1, source_target_pairs={{8,0},{16,8},{24,16},{0,24},{9,1},{17,9},{25,17},{1,25},{10,2},{18... | collective-permute-start | bytes 393224 | tf_op jit(solution)/shard_map/ppermute | solution.py:31
  106.6 17.9 %copy-start.36 = (f32[2,512,64]{2,1,0:T(8,128)S(1)}, f32[2,512,64]{2,1,0:T(8,128)}, u32[]{:S(2)}) copy-start(f32[2,512,64]{2,1,0:T(8,128)} %copy-done.35) | copy-start | bytes 786436
  106.6 17.9 %copy-start.38 = (f32[2,512,64]{2,1,0:T(8,128)S(1)}, f32[2,512,64]{2,1,0:T(8,128)}, u32[]{:S(2)}) copy-start(f32[2,512,64]{2,1,0:T(8,128)} %copy-done.37) | copy-start | bytes 786436
  106.6 17.9 %copy-start.40 = (f32[2,512,64]{2,1,0:T(8,128)S(1)}, f32[2,512,64]{2,1,0:T(8,128)}, u32[]{:S(2)}) copy-start(f32[2,512,64]{2,1,0:T(8,128)} %copy-done.39) | copy-start | bytes 786436
  107.9 17.9 %copy-start.14 = (bf16[2,512,128]{2,1,0:T(8,128)(2,1)}, bf16[2,512,128]{2,1,0:T(8,128)(2,1)S(1)}, u32[]{:S(2)}) copy-start(bf16[2,512,128]{2,1,0:T(8,128)(2,1)S(1)} %shard_map.77.own1) | copy-start | bytes 786436
  107.9 15.8 %collective-permute-start.23 = (bf16[2,512,128]{2,1,0:T(8,128)(2,1)S(1)}, bf16[2,512,128]{2,1,0:T(8,128)(2,1)S(1)}, u32[]{:S(2)}, u32[]{:S(2)}) collective-permute-start(bf16[2,512,128]{2,1,0:T(8,128)(2,1)S(1)} %shard_map.77.own1), channel_id=1, source_target_pairs={{24,0},{0,8},{8,16},{16,24},{25,1},{1,9},{9,17},{17,25},{26,2},{2,... | collective-permute-start | bytes 786440 | tf_op jit(solution)/shard_map/ppermute | solution.py:31
  108.2 10.2 %collective-permute-start.28 = (bf16[512,128]{1,0:T(8,128)(2,1)S(1)}, bf16[512,128]{1,0:T(8,128)(2,1)}, u32[]{:S(2)}, u32[]{:S(2)}) collective-permute-start(bf16[512,128]{1,0:T(8,128)(2,1)S(1)} %slice_bitcast_fusion), channel_id=1, source_target_pairs={{8,0},{16,8},{24,16},{0,24},{9,1},{17,9},{25,17},{1,25},{10,2},{18... | collective-permute-start | bytes 393224 | tf_op jit(solution)/shard_map/ppermute | solution.py:31
  113.2 19.5 %copy-start.7 = (bf16[4,1024,256]{2,1,0:T(8,128)(2,1)S(1)}, bf16[4,1024,256]{2,1,0:T(8,128)(2,1)}, u32[]{:S(2)}) copy-start(bf16[4,1024,256]{2,1,0:T(8,128)(2,1)} %copy-done.6) | copy-start | bytes 6291460
  113.2 19.5 %copy-start.13 = (bf16[2,512,128]{2,1,0:T(8,128)(2,1)S(1)}, bf16[2,512,128]{2,1,0:T(8,128)(2,1)}, u32[]{:S(2)}) copy-start(bf16[2,512,128]{2,1,0:T(8,128)(2,1)} %copy-done.12) | copy-start | bytes 786436
  113.2 19.5 %collective-permute-start.13 = (bf16[1024,256]{1,0:T(8,128)(2,1)}, bf16[1024,256]{1,0:T(8,128)(2,1)}, u32[]{:S(2)}, u32[]{:S(2)}) collective-permute-start(bf16[1024,256]{1,0:T(8,128)(2,1)} %fusion.56), channel_id=1, source_target_pairs={{64,0},{0,64},{65,1},{1,65},{66,2},{2,66},{67,3},{3,67},{68,4},{4,... | collective-permute-start | bytes 1572872 | tf_op jit(solution)/shard_map/ppermute | solution.py:31
  115.0 17.6 %copy-start.21 = (bf16[2,512,128]{2,1,0:T(8,128)(2,1)}, bf16[2,512,128]{2,1,0:T(8,128)(2,1)S(1)}, u32[]{:S(2)}) copy-start(bf16[2,512,128]{2,1,0:T(8,128)(2,1)S(1)} %collective-permute-done.22.up0) | copy-start | bytes 786436
  115.0 14.5 %collective-permute-start.24 = (bf16[512,128]{1,0:T(8,128)(2,1)S(1)}, bf16[512,128]{1,0:T(8,128)(2,1)S(1)}, u32[]{:S(2)}, u32[]{:S(2)}) collective-permute-start(bf16[512,128]{1,0:T(8,128)(2,1)S(1)} %slice_bitcast_fusion.3), channel_id=1, source_target_pairs={{24,0},{0,8},{8,16},{16,24},{25,1},{1,9},{9,17},{17,25},{26,2},{2,... | collective-permute-start | bytes 393224 | tf_op jit(solution)/shard_map/ppermute | solution.py:31
  118.4 11.7 %collective-permute-start.29 = (bf16[512,128]{1,0:T(8,128)(2,1)}, bf16[512,128]{1,0:T(8,128)(2,1)S(1)}, u32[]{:S(2)}, u32[]{:S(2)}) collective-permute-start(bf16[512,128]{1,0:T(8,128)(2,1)} %collective-permute-done.28), channel_id=1, source_target_pairs={{8,0},{16,8},{24,16},{0,24},{9,1},{17,9},{25,17},{1,25},{10,2},{18... | collective-permute-start | bytes 393224 | tf_op jit(solution)/shard_map/ppermute | solution.py:31
  124.3 7.7 %collective-permute-start.25 = (bf16[512,128]{1,0:T(8,128)(2,1)}, bf16[512,128]{1,0:T(8,128)(2,1)S(1)}, u32[]{:S(2)}, u32[]{:S(2)}) collective-permute-start(bf16[512,128]{1,0:T(8,128)(2,1)} %slice_bitcast_fusion.2), channel_id=1, source_target_pairs={{24,0},{0,8},{8,16},{16,24},{25,1},{1,9},{9,17},{17,25},{26,2},{2,... | collective-permute-start | bytes 393224 | tf_op jit(solution)/shard_map/ppermute | solution.py:31
  157.4 13.8 %collective-permute-start.30 = (bf16[1024,256]{1,0:T(8,128)(2,1)}, bf16[1024,256]{1,0:T(8,128)(2,1)S(1)}, u32[]{:S(2)}, u32[]{:S(2)}) collective-permute-start(bf16[1024,256]{1,0:T(8,128)(2,1)} %bitcast.41), channel_id=1, source_target_pairs={{64,0},{0,64},{65,1},{1,65},{66,2},{2,66},{67,3},{3,67},{68,4},{4,... | collective-permute-start | bytes 1572872 | tf_op jit(solution)/shard_map/ppermute | solution.py:31
  172.4 2.7 %collective-permute-start.31 = (bf16[1024,512]{1,0:T(8,128)(2,1)S(1)}, bf16[1024,512]{1,0:T(8,128)(2,1)S(1)}, u32[]{:S(2)}, u32[]{:S(2)}) collective-permute-start(bf16[1024,512]{1,0:T(8,128)(2,1)S(1)} %pad_maximum_fusion.2), channel_id=1, source_target_pairs={{32,0},{0,32},{33,1},{1,33},{34,2},{2,34},{35,3},{3,35},{36,4},{4,... | collective-permute-start | bytes 3145736 | tf_op jit(solution)/shard_map/ppermute | solution.py:31
  176.0 5.5 %copy-start.42 = (bf16[1024,2048]{1,0:T(8,128)(2,1)S(1)}, bf16[1024,2048]{1,0:T(8,128)(2,1)}, u32[]{:S(2)}) copy-start(bf16[1024,2048]{1,0:T(8,128)(2,1)} %all-gather.2.cloned.1.call-done) | copy-start | bytes 12582916
  178.5 14.5 %collective-permute-start.36 = (bf16[256,1024]{1,0:T(8,128)(2,1)S(1)}, bf16[256,1024]{1,0:T(8,128)(2,1)S(1)}, u32[]{:S(2)}, u32[]{:S(2)}) collective-permute-start(bf16[256,1024]{1,0:T(8,128)(2,1)S(1)} %fusion.43), channel_id=1, source_target_pairs={{2,0},{4,2},{6,4},{0,6},{3,1},{5,3},{7,5},{1,7},{10,8},{12,10},{14... | collective-permute-start | bytes 1572872 | tf_op jit(solution)/shard_map/ppermute | solution.py:31
  182.3 27.0 %collective-permute-start.35 = (bf16[256,1024]{1,0:T(8,128)(2,1)S(1)}, bf16[256,1024]{1,0:T(8,128)(2,1)S(1)}, u32[]{:S(2)}, u32[]{:S(2)}) collective-permute-start(bf16[256,1024]{1,0:T(8,128)(2,1)S(1)} %fusion.40), channel_id=1, source_target_pairs={{6,0},{0,2},{2,4},{4,6},{7,1},{1,3},{3,5},{5,7},{14,8},{8,10},{10,... | collective-permute-start | bytes 1572872 | tf_op jit(solution)/shard_map/ppermute | solution.py:31
  183.1 25.4 %collective-permute-start.33 = (bf16[256,1024]{1,0:T(8,128)(2,1)S(1)}, bf16[256,1024]{1,0:T(8,128)(2,1)S(1)}, u32[]{:S(2)}, u32[]{:S(2)}) collective-permute-start(bf16[256,1024]{1,0:T(8,128)(2,1)S(1)} %fusion.37), channel_id=1, source_target_pairs={{6,0},{0,2},{2,4},{4,6},{7,1},{1,3},{3,5},{5,7},{14,8},{8,10},{10,... | collective-permute-start | bytes 1572872 | tf_op jit(solution)/shard_map/ppermute | solution.py:31
  193.8 16.1 %collective-permute-start.37 = (bf16[256,1024]{1,0:T(8,128)(2,1)S(1)}, bf16[256,1024]{1,0:T(8,128)(2,1)S(1)}, u32[]{:S(2)}, u32[]{:S(2)}) collective-permute-start(bf16[256,1024]{1,0:T(8,128)(2,1)S(1)} %fusion.49), channel_id=1, source_target_pairs={{2,0},{4,2},{6,4},{0,6},{3,1},{5,3},{7,5},{1,7},{10,8},{12,10},{14... | collective-permute-start | bytes 1572872 | tf_op jit(solution)/shard_map/ppermute | solution.py:31
  198.3 21.1 %collective-permute-start.32 = (bf16[256,1024]{1,0:T(8,128)(2,1)S(1)}, bf16[256,1024]{1,0:T(8,128)(2,1)S(1)}, u32[]{:S(2)}, u32[]{:S(2)}) collective-permute-start(bf16[256,1024]{1,0:T(8,128)(2,1)S(1)} %fusion.34), channel_id=1, source_target_pairs={{2,0},{4,2},{6,4},{0,6},{3,1},{5,3},{7,5},{1,7},{10,8},{12,10},{14... | collective-permute-start | bytes 1572872 | tf_op jit(solution)/shard_map/ppermute | solution.py:31
  209.2 14.1 %collective-permute-start.34 = (bf16[256,1024]{1,0:T(8,128)(2,1)S(1)}, bf16[256,1024]{1,0:T(8,128)(2,1)S(1)}, u32[]{:S(2)}, u32[]{:S(2)}) collective-permute-start(bf16[256,1024]{1,0:T(8,128)(2,1)S(1)} %fusion.46), channel_id=1, source_target_pairs={{6,0},{0,2},{2,4},{4,6},{7,1},{1,3},{3,5},{5,7},{14,8},{8,10},{10,... | collective-permute-start | bytes 1572872 | tf_op jit(solution)/shard_map/ppermute | solution.py:31
  224.2 13.5 %collective-permute-start.38 = (bf16[128,2048]{1,0:T(8,128)(2,1)S(1)}, bf16[128,2048]{1,0:T(8,128)(2,1)S(1)}, u32[]{:S(2)}, u32[]{:S(2)}) collective-permute-start(bf16[128,2048]{1,0:T(8,128)(2,1)S(1)} %fusion.55), channel_id=1, source_target_pairs={{1,0},{0,1},{3,2},{2,3},{5,4},{4,5},{7,6},{6,7},{9,8},{8,9},{11,10... | collective-permute-start | bytes 1572872 | tf_op jit(solution)/shard_map/ppermute | solution.py:31
  (19 other events, 17.3 us)
Sparse Core Ops, SparseCore 0:
  69.3 60.9 all-gather.1

commit v3 on v0

v3 whole, which is shorter than its diff:
```python
import functools
import math

import jax
import jax.numpy as jnp
from jax import lax
from jax.experimental import pallas as pl
from jax.experimental.pallas import tpu as pltpu
from jax.sharding import Mesh, PartitionSpec as P

MODEL_WIDTH = 8192
QUERY_HEADS = 64
KEY_VALUE_HEADS = 8
HEAD_SIZE = 128
TOKENS = 4096
SEGMENTS = 16
GROUP_ROWS = 1024
TILE = 256
PART = 512
WIDE = 2 * HEAD_SIZE

norm_eps = 1e-05
rope_base = 500000.0
MASKED = -1e30
VMEM = 60 * 2**20

f32 = jnp.float32
bf16 = jnp.bfloat16


def receive(value, axis, step):
    n = lax.axis_size(axis)
    return lax.ppermute(value, axis, [((i + step) % n, i) for i in range(n)])


def turn(u, cosine, sine):
    return u * cosine + pltpu.roll(u, HEAD_SIZE // 2, 1) * sine


def finish_kernel(core, home, far, cosine, sine, scale, out):
    total = (home[...].astype(f32) + far[...].astype(f32)) * scale[...]
    out[0] = turn(total[:, :HEAD_SIZE], cosine[0], sine[0]).astype(bf16)
    out[1] = total[:, HEAD_SIZE:].astype(bf16)


def finish_kv(core, home, far, cosine, sine, scale):
    rows = pl.BlockSpec((PART, WIDE), lambda i, core: (0, 0))
    angle = pl.BlockSpec((1, PART, HEAD_SIZE), lambda i, core: (core[0], 0, 0))
    return pl.pallas_call(
        finish_kernel,
        grid_spec=pltpu.PrefetchScalarGridSpec(
            num_scalar_prefetch=1,
            grid=(1,),
            in_specs=[rows, rows, angle, angle, pl.BlockSpec((PART, 1), lambda i, core: (core[0], 0))],
            out_specs=pl.BlockSpec((2, PART, HEAD_SIZE), lambda i, core: (0, 0, 0)),
        ),
        out_shape=jax.ShapeDtypeStruct((2, PART, HEAD_SIZE), bf16),
        compiler_params=pltpu.CompilerParams(vmem_limit_bytes=VMEM),
        cost_estimate=pl.CostEstimate(flops=PART * 2048, bytes_accessed=2 * 2**20, transcendentals=0),
    )(core, home, far, cosine, sine, scale)


def attention_kernel(
    tiles, scalars, home0, home1, far0, far1, cosine, sine, scale0, scale1, bounds,
    m0, m1, m2, m3, t0, t1, t2, t3, out_ref, keys, values,
):
    place = pl.program_id(0)
    dy = jnp.where(place == 0, tiles[0], tiles[1])
    y, z, xh, c = scalars[8], scalars[9], scalars[10], scalars[11]

    @pl.when(place == 0)
    def _():
        for halves, dx in (((m0, m1, m2, m3), c), ((t0, t1, t2, t3), 1 - c)):
            for dz, ref in enumerate(halves):
                for i in range(4):
                    at = (lax.rem(y + i, 4) * 4 + lax.rem(z + dz, 4)) * TILE + (xh ^ dx) * 128
                    at = pl.ds(pl.multiple_of(at, 128), 128)
                    keys[at, :] = ref[0, i * 128 : (i + 1) * 128, :]
                    values[at, :] = ref[1, i * 128 : (i + 1) * 128, :]

    unit = f32(HEAD_SIZE ** (-0.5) * math.log2(math.e))
    turned = []
    for dx, (home, far, scale) in enumerate(((home0, far0, scale0), (home1, far1, scale1))):
        raw = (home[...].astype(f32) + far[...].astype(f32)) * (scale[...] * unit)
        for head in (0, 1):
            u = raw[:, head * HEAD_SIZE : (head + 1) * HEAD_SIZE]
            turned.append(turn(u, cosine[dx], sine[dx]).astype(bf16))
    q = jnp.concatenate([turned[0], turned[2], turned[1], turned[3]], axis=0)
    q_index = bounds[0, 0:1, :]
    q_start = bounds[0, 1:2, :]

    def step(masked, width, tile, carry):
        top, total, acc = carry
        first_key = tile * width
        at = pl.ds(pl.multiple_of(first_key, TILE), width)
        s = lax.dot_general(keys[at, :], q, (((1,), (1,)), ((), ())), preferred_element_type=f32)
        if masked:
            k_index = lax.broadcasted_iota(jnp.int32, (width, 1), 0) + first_key
            s = jnp.where((k_index <= q_index) & (k_index >= q_start), s, MASKED)
        new_top = jnp.maximum(top, jnp.max(s, axis=0, keepdims=True))
        p = jnp.exp2(s - new_top)
        decay = jnp.exp2(top - new_top)
        total = total * decay + jnp.sum(p, axis=0, keepdims=True)
        added = lax.dot_general(
            values[at, :], p.astype(bf16), (((0,), (0,)), ((), ())), preferred_element_type=f32
        )
        return new_top, total, acc * decay + added

    carry = (
        jnp.full((1, 2 * TILE), MASKED, f32),
        jnp.zeros((1, 2 * TILE), f32),
        jnp.zeros((HEAD_SIZE, 2 * TILE), f32),
    )
    last = lax.rem(y + dy, 4) * 4 + z
    first = scalars[dy]
    clear = jnp.minimum(scalars[4 + dy], last)
    big = 4
    big_first = (clear + big - 1) // big
    big_last = jnp.maximum(last // big, big_first)
    middle = jnp.minimum(big_first * big, last)
    one = functools.partial(step, False, TILE)
    carry = lax.fori_loop(first, clear, functools.partial(step, True, TILE), carry)
    carry = lax.fori_loop(clear, middle, one, carry)
    carry = lax.fori_loop(big_first, big_last, functools.partial(step, False, big * TILE), carry)
    carry = lax.fori_loop(jnp.maximum(big_last * big, middle), last, one, carry)
    top, total, acc = step(True, TILE, last, carry)
    result = (acc / total).T.astype(bf16)
    for head in (0, 1):
        for dx in (0, 1):
            at = head * TILE + dx * 128
            out_ref[0, dx, :, head * HEAD_SIZE : (head + 1) * HEAD_SIZE] = result[at : at + 128]


def attention(tiles, scalars, home, far, cosine, sine, scale, bounds, mine, theirs):
    def tile(i):
        return jnp.where(i == 0, tiles[0], tiles[1])

    half = pl.BlockSpec((2, PART, HEAD_SIZE), lambda i: (0, 0, 0))
    rows = [pl.BlockSpec((128, WIDE), lambda i, dx=dx: (4 * dx + tile(i), 0)) for dx in (0, 1)]
    angle = pl.BlockSpec((2, 128, HEAD_SIZE), lambda i: (0, tile(i), 0))
    column = [pl.BlockSpec((128, 1), lambda i, dx=dx: (4 * dx + tile(i), 0)) for dx in (0, 1)]
    return pl.pallas_call(
        functools.partial(attention_kernel, tiles),
        grid=(2,),
        in_specs=[pl.BlockSpec(memory_space=pltpu.SMEM)]
        + rows * 2
        + [angle] * 2
        + column
        + [pl.BlockSpec((1, 2, 2 * TILE), lambda i: (tile(i), 0, 0))]
        + [half] * 8,
        out_specs=pl.BlockSpec((1, 2, 128, WIDE), lambda i: (i, 0, 0, 0)),
        out_shape=jax.ShapeDtypeStruct((2, 2, 128, WIDE), bf16),
        scratch_shapes=[pltpu.VMEM((TOKENS, HEAD_SIZE), bf16)] * 2,
        compiler_params=pltpu.CompilerParams(vmem_limit_bytes=VMEM),
        cost_estimate=pl.CostEstimate(
            flops=3 * 10**9, bytes_accessed=4 * 2**20, transcendentals=4 * 10**6
        ),
    )(scalars, home, home, far, far, cosine, sine, scale, scale, bounds, *mine, *theirs)


def shards(tokens, norm_gain, segment_ids, w_query, key_weight, value_weight, w_output):
    xl, c, y, z, xh = (lax.axis_index(a) for a in ("xl", "c", "y", "z", "xh"))
    barrier = lax.optimization_barrier

    x = {(0, 0): tokens}
    x[1, 0] = receive(tokens, "y", 1)
    x[3, 0] = receive(tokens, "y", -1)
    x[0, 1] = receive(tokens, "xh", 1)
    x[2, 0] = receive(tokens, "y", 2)
    key_weight, value_weight, segment_ids, x[0, 1] = barrier(
        (key_weight, value_weight, segment_ids, x[0, 1])
    )
    x[1, 1] = receive(x[0, 1], "y", 1)
    x[3, 1] = receive(x[0, 1], "y", -1)
    x[2, 1] = receive(x[2, 0], "xh", 1)

    weights = lax.all_gather(w_query, "z", axis=0, tiled=True)
    w_output, weights = barrier((w_output, weights))
    weights = weights.reshape(4, w_query.shape[0], w_query.shape[1])
    w_out = lax.all_gather(w_output, "z", axis=0, tiled=True)

    def relative(by_place):
        turned = lax.dynamic_slice_in_dim(jnp.concatenate([by_place, by_place], axis=0), y, 4, 0)
        swapped = jnp.where(xh == 0, turned, turned[:, ::-1])
        return jnp.transpose(swapped, (1, 0, 2)).reshape(2, PART)

    def own_rows(values):
        return relative(lax.dynamic_index_in_dim(values.reshape(4, 4, 2, 128), z, 1, keepdims=False))

    segments = own_rows(segment_ids)
    index = own_rows(jnp.arange(TOKENS, dtype=jnp.int32))
    ids = jnp.arange(SEGMENTS, dtype=jnp.int32)
    before = jnp.sum((segment_ids[None, :] < ids[:, None]).astype(jnp.int32), axis=1)
    start = jnp.sum(jnp.where(segments[None] == ids[:, None, None], before[:, None, None], 0), axis=0)
    places = (index - start).astype(f32)
    freqs = jnp.exp(jnp.arange(64, dtype=f32) * f32(-2.0 * math.log(rope_base) / HEAD_SIZE))
    angles = places[:, :, None] * freqs
    cosine, sine = jnp.cos(angles), jnp.sin(angles)
    cosine = jnp.concatenate([cosine, cosine], axis=2)
    sine = jnp.concatenate([-sine, sine], axis=2)
    by_tile = start.reshape(2, 4, 128)
    lows = jnp.min(by_tile, axis=(0, 2)) // TILE
    clears = (jnp.max(by_tile, axis=(0, 2)) + TILE - 1) // TILE
    scalars = jnp.concatenate([lows, clears, jnp.stack([y, z, xh, c])]).astype(jnp.int32)

    def per_tile(values):
        rows = jnp.transpose(values.reshape(2, 4, 128), (1, 0, 2)).reshape(4, TILE)
        return jnp.concatenate([rows, rows], axis=1)

    bounds = jnp.stack([per_tile(index), per_tile(start)], axis=1)

    def kv_weight(across):
        which = y * 2 + (xl ^ across)
        parts = [lax.dynamic_slice_in_dim(w, which * 128, 128, 1) for w in (key_weight, value_weight)]
        return jnp.concatenate(parts, axis=1)

    kv_weights = barrier([kv_weight(0), kv_weight(1)])
    gain = norm_gain[None, :]
    pieces = [x[dy, dx].astype(f32) for dx in (0, 1) for dy in range(4)]
    rows = jnp.concatenate([(piece * gain).astype(bf16) for piece in pieces], axis=0)
    squares = jnp.stack([jnp.sum(piece * piece, axis=1) for piece in pieces])

    def half(rows, core):
        return lax.dynamic_slice_in_dim(rows, core * PART, PART, 0)

    def product(rows, weight):
        return jnp.dot(rows, weight, preferred_element_type=f32)

    away = half(rows, 1 - c)
    got_across = receive(product(away, kv_weights[1]).astype(bf16), "c", 1)
    got = receive(product(away, kv_weights[0]).astype(bf16), "c", 1)
    across = (product(half(rows, c), kv_weights[1]) + got_across.astype(f32)).astype(bf16)
    rows, across, squares = barrier((rows, across, squares))
    kv_far = receive(across, "xl", 1)
    kv_home = (product(half(rows, c), kv_weights[0]) + got.astype(f32)).astype(bf16)
    squares = squares + receive(squares, "c", 1)
    squares = squares + receive(squares, "xl", 1)
    scale = lax.rsqrt(squares.reshape(GROUP_ROWS, 1) / MODEL_WIDTH + norm_eps)
    kv = finish_kv(c.astype(jnp.int32)[None], kv_home, kv_far, cosine, sine, scale)
    mine = [kv] + [receive(kv, "z", step) for step in (1, 2, 3)]
    theirs = [receive(part, "c", 1) for part in mine]

    rows, kv_home = barrier((rows, kv_home))

    def query_weight(core, across):
        return lax.dynamic_index_in_dim(weights, (xl ^ across) * 2 + core, 0, keepdims=False)

    got_across = receive(product(rows, query_weight(1 - c, 1)).astype(bf16), "c", 1)
    got = receive(product(rows, query_weight(1 - c, 0)).astype(bf16), "c", 1)
    across = (product(rows, query_weight(c, 1)) + got_across.astype(f32)).astype(bf16)
    rows, across = barrier((rows, across))
    q_far = receive(across, "xl", 1)
    q_home = (product(rows, query_weight(c, 0)) + got.astype(f32)).astype(bf16)

    def all_heads(mixed, before):
        across = receive(mixed, "xl", 1)
        if before:
            across, *before = barrier((across, *before))
        low, high = jnp.where(xl == 0, mixed, across), jnp.where(xl == 0, across, mixed)
        pair = jnp.concatenate([low, high], axis=1)
        other = receive(pair, "c", 1)
        even, odd = jnp.where(c == 0, pair, other), jnp.where(c == 0, other, pair)
        heads = jnp.concatenate([even[:, :WIDE], odd[:, :WIDE], even[:, WIDE:], odd[:, WIDE:]], axis=1)
        return heads, before

    columns = w_out.shape[1] // 2
    y_first, xh_first = {}, {}
    mixed = [
        attention(tiles, scalars, q_home, q_far, cosine, sine, scale, bounds, mine, theirs)
        for tiles in ((2, 3), (1, 0))
    ]
    sent, seconds = [mixed[1]], []
    for step, tiles in enumerate(((2, 3), (1, 0))):
        heads, sent = all_heads(mixed[step].reshape(PART, WIDE), sent)
        if step == 0:
            mixed[1] = sent[0]
        else:
            y_first[2], y_first[3], seconds[0] = sent
        for i, dy in enumerate(tiles):
            y_first[dy] = jnp.dot(
                heads[i * TILE : (i + 1) * TILE], w_out[:, :columns], preferred_element_type=f32
            ).astype(bf16)
        seconds.append(jnp.dot(heads, w_out[:, columns:], preferred_element_type=f32).astype(bf16))
        sent = [y_first[tiles[0]], y_first[tiles[1]], seconds[-1]]
    for step, tiles in enumerate(((2, 3), (1, 0))):
        second = seconds[step].reshape(2, 2, 128, columns)
        got = receive(second[:, 1], "xh", 1)
        if step == 1:
            got, xh_first[2], xh_first[3] = barrier((got, xh_first[2], xh_first[3]))
        for i, dy in enumerate(tiles):
            xh_first[dy] = (second[i, 0].astype(f32) + got[i].astype(f32)).astype(bf16)

    def sum_over_y(parts):
        total = parts[0].astype(f32)
        for dy in (2, 3, 1):
            total = total + receive(parts[dy], "y", -dy).astype(f32)
        return total

    first = sum_over_y(y_first)
    second = sum_over_y(xh_first)
    first = first[:128] + receive(first[128:].astype(bf16), "xh", 1).astype(f32)
    return jnp.concatenate([first, second], axis=1).astype(bf16)


def solution(mesh):
    fine = Mesh(mesh.devices.reshape(2, 2, 4, 4, 2), ("xl", "c", "y", "z", "xh"))
    blk, tensor = ("xl", "c"), ("y", "z", "xh")
    placed = (
        P(tensor, blk),
        P(blk),
        P(),
        P(blk, tensor),
        P(blk, None),
        P(blk, None),
        P(tensor, blk),
    )
    return jax.shard_map(
        shards, mesh=fine, in_specs=placed, out_specs=P(tensor, blk), check_vma=False
    )
```

time: 705 us -> 201 us (0.29)
  waiting for transfers between devices: 599 us -> 65.3 us
  starting transfers between devices: 0.39 us -> 43.8 us
  matrix products: 55.2 us -> 28 us
  Pallas kernels: 0 us -> 17.5 us
    reduce_scatter x2 -> x0, waiting for transfers between devices: 405 us -> none  [the longest x1 363 us: shards(): lax.psum_scatter(partial_out.astype(jnp.bfloat16), 'tensor', scatter_dime...]
    all_gather x4 -> x2, waiting for transfers between devices: 194 us -> 9.31 us  [the longest x1 9.29 us: shards(): weights = lax.all_gather(w_query, 'z', axis=0, tiled=True)]
    ppermute x0 -> x35, waiting for transfers between devices: none -> 55.9 us  [receive(): return lax.ppermute(value, axis, [((i + step) % n, i) for i in range(n)])]
    ppermute x0 -> x35, starting transfers between devices: none -> 43.7 us  [receive(): return lax.ppermute(value, axis, [((i + step) % n, i) for i in range(n)])]
    sub x1 -> x0, matrix products: 22 us -> none  [shards(): masked - highest]
    pallas_call x0 -> x3, Pallas kernels: none -> 17.5 us  [the longest x2 15.3 us: attention(): pl.pallas_call(functools.partial(attention_kernel, tiles), grid=(2,), in_...]
    unnamed x0 -> x8, other arithmetic: none -> 8.59 us
    dot_general x3 -> x14, matrix products: 33.2 us -> 28 us  [the longest x8 20.9 us: product(): return jnp.dot(rows, weight, preferred_element_type=f32)]
  transfers between devices with their start and end apart: 6 -> 37, of which waited for: 6 -> 16; matrix products, arithmetic and copies ran while one was open for 6% -> 27% of each run, Pallas kernels for 0% -> 9%
where the time goes in v3:
time: 201 us; the launch traced here: 199 us
  waiting for transfers between devices  65.3 us (32%)
  starting transfers between devices  43.8 us (22%)
  matrix products  28 us (14%)
  other arithmetic  23 us (11%)
  Pallas kernels  17.5 us (9%)
  between operations  14 us (7%)
  local copies, waits for them, and re-layouts  7 us (3%)
    ppermute x35, waiting for transfers between devices, receive(): return lax.ppermute(value, axis, [((i + step) % n, i) for i in range(n)])  55.9 us
    ppermute x35, starting transfers between devices, receive(): return lax.ppermute(value, axis, [((i + step) % n, i) for i in range(n)])  43.7 us
    dot_general x8, matrix products, product(): return jnp.dot(rows, weight, preferred_element_type=f32)  20.9 us
    pallas_call x2, Pallas kernels, attention(): pl.pallas_call(functools.partial(attention_kernel, tiles), grid=(2,), in_...  15.3 us
    all_gather x1, waiting for transfers between devices, shards(): weights = lax.all_gather(w_query, 'z', axis=0, tiled=True)  9.29 us
    unnamed x8, other arithmetic  8.59 us
    dot_general x2, matrix products, shards(): jnp.dot(heads, w_out[:, columns:], preferred_element_type=f32).astype(bf16)  4.24 us
  transfers between devices with their start and end apart: 37, of which 16 were waited for; matrix products, arithmetic and copies ran while one was open for 27% of the time, Pallas kernels for 9%

profile of v3, /device:TPU:96, one launch (start us, length us, event | category | flops | bytes accessed | tf_op | source)
XLA Modules:
  0.0 198.6 jit_solution(10722399039947532060)
XLA Ops:
  6.5 3.0 %collective-permute-start = (bf16[128,2048]{1,0:T(8,128)(2,1)}, bf16[128,2048]{1,0:T(8,128)(2,1)S(1)}, u32[]{:S(2)}, u32[]{:S(2)}) collective-permute-start(bf16[128,2048]{1,0:T(8,128)(2,1)} %param.7), channel_id=1, source_target_pairs={{1,0},{0,1},{3,2},{2,3},{5,4},{4,5},{7,6},{6,7},{9,8},{8,9},{11,10... | collective-permute-start | bytes 1572872 | tf_op jit(solution)/shard_map/ppermute | solution.py:33
  9.6 3.2 %collective-permute-start.2 = (bf16[128,2048]{1,0:T(8,128)(2,1)}, bf16[128,2048]{1,0:T(8,128)(2,1)S(1)}, u32[]{:S(2)}, u32[]{:S(2)}) collective-permute-start(bf16[128,2048]{1,0:T(8,128)(2,1)} %param.7), channel_id=1, source_target_pairs={{16,0},{24,8},{0,16},{8,24},{17,1},{25,9},{1,17},{9,25},{18,2},{26... | collective-permute-start | bytes 1572872 | tf_op jit(solution)/shard_map/ppermute | solution.py:33
  12.8 1.1 collective-permute-start.1
  13.8 1.0 collective-permute-start.3
  15.0 2.0 %fusion.90 = bf16[1024,2048]{1,0:T(8,128)(2,1)} fusion(bf16[128,2048]{1,0:T(8,128)(2,1)} %param.7, f32[2048]{0:T(1024)} %param.8), kind=kLoop, calls=%fused_computation.91 | loop fusion | flops 786431 | bytes 1056768
  17.1 1.2 fusion.54
  18.3 3.6 %collective-permute-done = bf16[128,2048]{1,0:T(8,128)(2,1)S(1)} collective-permute-done((bf16[128,2048]{1,0:T(8,128)(2,1)}, bf16[128,2048]{1,0:T(8,128)(2,1)S(1)}, u32[]{:S(2)}, u32[]{:S(2)}) %collective-permute-start) | collective-permute-done | bytes 524320 | tf_op jit(solution)/shard_map/ppermute | solution.py:33
  21.9 3.0 %collective-permute-start.4 = (bf16[128,2048]{1,0:T(8,128)(2,1)S(1)}, bf16[128,2048]{1,0:T(8,128)(2,1)S(1)}, u32[]{:S(2)}, u32[]{:S(2)}) collective-permute-start(bf16[128,2048]{1,0:T(8,128)(2,1)S(1)} %collective-permute-done), channel_id=1, source_target_pairs={{8,0},{16,8},{24,16},{0,24},{9,1},{17,9},{25,17},{1,25},{10,2},{18... | collective-permute-start | bytes 1572872 | tf_op jit(solution)/shard_map/ppermute | solution.py:33
  25.7 0.9 convert_reduce_fusion
  26.7 1.9 fusion.100
  28.6 1.4 pad_maximum_fusion.4
  30.0 3.0 %collective-permute-start.5 = (bf16[128,2048]{1,0:T(8,128)(2,1)S(1)}, bf16[128,2048]{1,0:T(8,128)(2,1)}, u32[]{:S(2)}, u32[]{:S(2)}) collective-permute-start(bf16[128,2048]{1,0:T(8,128)(2,1)S(1)} %collective-permute-done.2), channel_id=1, source_target_pairs={{1,0},{0,1},{3,2},{2,3},{5,4},{4,5},{7,6},{6,7},{9,8},{8,9},{11,10... | collective-permute-start | bytes 1572872 | tf_op jit(solution)/shard_map/ppermute | solution.py:33
  33.6 4.1 %collective-permute-done.1 = bf16[128,2048]{1,0:T(8,128)(2,1)S(1)} collective-permute-done((bf16[128,2048]{1,0:T(8,128)(2,1)}, bf16[128,2048]{1,0:T(8,128)(2,1)S(1)}, u32[]{:S(2)}, u32[]{:S(2)}) %collective-permute-start.1) | collective-permute-done | bytes 524320 | tf_op jit(solution)/shard_map/ppermute | solution.py:33
  38.2 1.8 constant_dynamic-slice_fusion
  39.9 1.1 pad_maximum_fusion
  41.0 1.1 pad_maximum_fusion.1
  42.1 0.9 fusion.89
  43.0 0.9 fusion.88
  43.9 0.9 fusion.87
  44.8 0.9 fusion.86
  46.4 1.1 collective-permute-done.4
  47.5 0.9 fusion.85
  48.4 2.0 %fusion.84 = bf16[1024,2048]{1,0:T(8,128)(2,1)} fusion(bf16[1024,2048]{1,0:T(8,128)(2,1)} %fusion.85, bf16[128,2048]{1,0:T(8,128)(2,1)} %collective-permute-done.5, f32[2048]{0:T(1024)S(1)} %copy-done.2), kind=kLoop, calls=%fused_computation.85 | loop fusion | flops 786432 | bytes 1056768
  50.5 9.3 %all-gather.3.cloned.1.call-done = bf16[8192,256]{1,0:T(8,128)(2,1)} async-done(((bf16[2048,256]{1,0:T(8,128)(2,1)}), bf16[8192,256]{1,0:T(8,128)(2,1)}) %all-gather.3.cloned.1.call-update) | async-done | bytes 4194320 | tf_op jit(solution)/shard_map/all_gather | solution.py:177
  59.8 0.9 fusion.83
  60.7 3.4 %fusion.47 = bf16[512,256]{1,0:T(8,128)(2,1)} fusion(bf16[2048,256]{1,0:T(8,128)(2,1)} %pad_maximum_fusion.1, bf16[1024,2048]{1,0:T(8,128)(2,1)} %fusion.83, s32[]{:T(128)S(6)} %select_n.113), kind=kOutput, calls=%fused_computation.47 | convolution fusion | flops 537001984 | bytes 3407876 | tf_op jit(solution)/shard_map/dot_general | solution.py:227
  64.2 1.4 fusion.50
  66.4 1.2 fusion.66
  67.7 2.5 %fusion.44 = bf16[512,256]{1,0:T(8,128)(2,1)S(1)} fusion(bf16[2048,256]{1,0:T(8,128)(2,1)S(1)} %copy-done.1, bf16[1024,2048]{1,0:T(8,128)(2,1)} %fusion.83, s32[]{:T(128)S(6)} %select_n.110, bf16[512,256]{1,0:T(8,128)(2,1)} %collective-permute-done.7), kind=kOutput, calls=%fused_computation.46 | convolution fusion | flops 537264128 | bytes 3670020 | tf_op jit(solution)/shard_map/dot_general | solution.py:227
  70.3 1.7 collective-permute-start.14
  72.0 1.4 add_convert_fusion.3.home
  73.8 2.6 %convolution_convert_fusion.1 = bf16[1024,256]{1,0:T(8,128)(2,1)S(1)} fusion(bf16[1024,2048]{1,0:T(8,128)(2,1)S(1)} %copy-done.8, bf16[4,2048,256]{2,1,0:T(8,128)(2,1)} %bitcast.137, s32[]{:T(128)S(6)} %select_n.115), kind=kOutput, calls=%fused_computation.44 | convolution fusion | flops 1074003968 | bytes 5767172 | tf_op jit(solution)/shard_map/dot_general | solution.py:227
  76.5 2.6 %collective-permute-done.13 = f32[8,128]{1,0:T(8,128)S(1)} collective-permute-done((f32[8,128]{1,0:T(8,128)S(1)}, f32[8,128]{1,0:T(8,128)S(1)}, u32[]{:S(2)}, u32[]{:S(2)}) %collective-permute-start.13) | collective-permute-done | bytes 4128 | tf_op jit(solution)/shard_map/ppermute | solution.py:33
  79.1 1.1 copy.15.scale.scale0.scale1
  80.9 2.2 %shard_map.73.m0 = bf16[2,512,128]{2,1,0:T(8,128)(2,1)} custom-call(s32[1]{0:T(128)} %bitcast.9.core, bf16[512,256]{1,0:T(8,128)(2,1)} %add_convert_fusion.3.home, bf16[512,256]{1,0:T(8,128)(2,1)} %copy-done.4, f32[2,512,128]{2,1,0:T(8,128)} %get-tuple-element.83.cosine, f32[2,512,128]{2,1,0:T(8,128)} %get-tuple-element.84.sine, ...), custom_call_target="tpu_custom_call" | custom-call | flops 1048576 | bytes 2097152 | tf_op jit(solution)/shard_map/pallas_call | solution.py:49
  83.1 1.9 collective-permute-start.15
  84.9 2.1 %collective-permute-start.16 = (bf16[2,512,128]{2,1,0:T(8,128)(2,1)}, bf16[2,512,128]{2,1,0:T(8,128)(2,1)S(1)}, u32[]{:S(2)}, u32[]{:S(2)}) collective-permute-start(bf16[2,512,128]{2,1,0:T(8,128)(2,1)} %shard_map.73.m0), channel_id=1, source_target_pairs={{4,0},{6,2},{0,4},{2,6},{5,1},{7,3},{1,5},{3,7},{12,8},{14,10},{8,... | collective-permute-start | bytes 786440 | tf_op jit(solution)/shard_map/ppermute | solution.py:33
  87.0 1.4 collective-permute-start.17
  88.4 3.8 %convolution_convert_fusion = bf16[1024,256]{1,0:T(8,128)(2,1)S(1)} fusion(bf16[1024,2048]{1,0:T(8,128)(2,1)} %fusion.83, bf16[4,2048,256]{2,1,0:T(8,128)(2,1)} %bitcast.138, s32[]{:T(128)S(6)} %select_n.117), kind=kOutput, calls=%fused_computation.43 | convolution fusion | flops 1074003968 | bytes 5767172 | tf_op jit(solution)/shard_map/dot_general | solution.py:227
  92.3 2.5 %add_convert_fusion.1 = bf16[1024,256]{1,0:T(8,128)(2,1)S(1)} fusion(bf16[1024,256]{1,0:T(8,128)(2,1)S(1)} %collective-permute-done.9, bf16[1024,2048]{1,0:T(8,128)(2,1)S(1)} %copy-done.9, bf16[4,2048,256]{2,1,0:T(8,128)(2,1)} %bitcast.139, s32[]{:T(128)S(6)} %select_n.114), kind=kOutput, calls=%fused_computation.79 | convolution fusion | flops 1074528256 | bytes 6291460 | tf_op jit(solution)/shard_map/dot_general | solution.py:227
  94.8 1.5 collective-permute-start.11
  97.0 2.0 %collective-permute-done.15.m1 = bf16[2,512,128]{2,1,0:T(8,128)(2,1)S(1)} collective-permute-done((bf16[2,512,128]{2,1,0:T(8,128)(2,1)}, bf16[2,512,128]{2,1,0:T(8,128)(2,1)S(1)}, u32[]{:S(2)}, u32[]{:S(2)}) %collective-permute-start.15) | collective-permute-done | bytes 262176 | tf_op jit(solution)/shard_map/ppermute | solution.py:33
  99.0 11.8 %collective-permute-done.16.m2 = bf16[2,512,128]{2,1,0:T(8,128)(2,1)S(1)} collective-permute-done((bf16[2,512,128]{2,1,0:T(8,128)(2,1)}, bf16[2,512,128]{2,1,0:T(8,128)(2,1)S(1)}, u32[]{:S(2)}, u32[]{:S(2)}) %collective-permute-start.16) | collective-permute-done | bytes 262176 | tf_op jit(solution)/shard_map/ppermute | solution.py:33
  111.4 3.3 %add_convert_fusion.home0.home1 = bf16[1024,256]{1,0:T(8,128)(2,1)} fusion(bf16[1024,256]{1,0:T(8,128)(2,1)S(1)} %collective-permute-done.10, bf16[1024,2048]{1,0:T(8,128)(2,1)S(1)} %copy-done.9, bf16[4,2048,256]{2,1,0:T(8,128)(2,1)} %bitcast.140, s32[]{:T(128)S(6)} %select_n.116), kind=kOutput, calls=%fused_computation.76 | convolution fusion | flops 1074528256 | bytes 6291460 | tf_op jit(solution)/shard_map/dot_general | solution.py:227
  115.7 0.8 copy-done.11
  116.5 8.7 %shard_map.74 = bf16[2,2,128,256]{3,2,1,0:T(8,128)(2,1)} custom-call(s32[12]{0:T(128)} %concatenate.47.scalars, bf16[1024,256]{1,0:T(8,128)(2,1)} %add_convert_fusion.home0.home1, bf16[1024,256]{1,0:T(8,128)(2,1)} %add_convert_fusion.home0.home1, bf16[1024,256]{1,0:T(8,128)(2,1)} %copy-done.11, bf16[1024,256]{1,0:T(8,128)(2,1)} %copy-done.11, ...), custom_call_target="tpu_custom_call" | custom-call | flops 3000000000 | bytes 4194304 | tf_op jit(solution)/shard_map/pallas_call | solution.py:142
  125.2 1.8 collective-permute-start.22
  127.0 6.6 %shard_map.75 = bf16[2,2,128,256]{3,2,1,0:T(8,128)(2,1)} custom-call(s32[12]{0:T(128)} %concatenate.47.scalars, bf16[1024,256]{1,0:T(8,128)(2,1)} %add_convert_fusion.home0.home1, bf16[1024,256]{1,0:T(8,128)(2,1)} %add_convert_fusion.home0.home1, bf16[1024,256]{1,0:T(8,128)(2,1)} %copy-done.11, bf16[1024,256]{1,0:T(8,128)(2,1)} %copy-done.11, ...), custom_call_target="tpu_custom_call" | custom-call | flops 3000000000 | bytes 4194304 | tf_op jit(solution)/shard_map/pallas_call | solution.py:142
  134.5 1.5 collective-permute-start.23
  136.9 3.0 %fusion.12 = bf16[512,1024]{1,0:T(8,128)(2,1)S(1)} fusion(bf16[1024,2048]{1,0:T(8,128)(2,1)} %all-gather.5.cloned.1.call-done, bf16[512,256]{1,0:T(8,128)(2,1)S(1)} %get-tuple-element.72, bf16[512,256]{1,0:T(8,128)(2,1)S(1)} %get-tuple-element.70, bf16[512,256]{1,0:T(8,128)(2,1)S(1)} %get-tuple-element.71, bf16[512,256]{1,0:T(8,128)(2,1)S(1)} %get-tuple-element.69), kind=kOutput, calls=%fused_computation.12 | convolution fusion | flops 1078460416 | bytes 4194304 | tf_op jit(solution)/shard_map/dot_general | solution.py:283
  141.3 2.1 %collective-permute-done.23 = bf16[512,256]{1,0:T(8,128)(2,1)S(1)} collective-permute-done((bf16[512,256]{1,0:T(8,128)(2,1)}, bf16[512,256]{1,0:T(8,128)(2,1)S(1)}, u32[]{:S(2)}, u32[]{:S(2)}) %collective-permute-start.23) | collective-permute-done | bytes 262176 | tf_op jit(solution)/shard_map/ppermute | solution.py:33
  143.7 2.5 %collective-permute-start.26 = (bf16[256,1024]{1,0:T(8,128)(2,1)S(1)}, bf16[256,1024]{1,0:T(8,128)(2,1)S(1)}, u32[]{:S(2)}, u32[]{:S(2)}) collective-permute-start(bf16[256,1024]{1,0:T(8,128)(2,1)S(1)} %fusion.26), channel_id=1, source_target_pairs={{16,0},{24,8},{0,16},{8,24},{17,1},{25,9},{1,17},{9,25},{18,2},{26... | collective-permute-start | bytes 1572872 | tf_op jit(solution)/shard_map/ppermute | solution.py:33
  146.1 1.4 collective-permute-start.27
  147.6 3.1 %collective-permute-start.31 = (bf16[2,128,1024]{2,1,0:T(8,128)(2,1)S(1)}, bf16[2,128,1024]{2,1,0:T(8,128)(2,1)S(1)}, u32[]{:S(2)}, u32[]{:S(2)}) collective-permute-start(bf16[2,128,1024]{2,1,0:T(8,128)(2,1)S(1)} %slice_bitcast_fusion), channel_id=1, source_target_pairs={{1,0},{0,1},{3,2},{2,3},{5,4},{4,5},{7,6},{6,7},{9,8},{8,9},{11,10... | collective-permute-start | bytes 1572872 | tf_op jit(solution)/shard_map/ppermute | solution.py:33
  151.8 0.8 collective-permute-start.28
  152.7 1.2 fusion.15
  155.3 4.7 %collective-permute-done.26 = bf16[256,1024]{1,0:T(8,128)(2,1)S(1)} collective-permute-done((bf16[256,1024]{1,0:T(8,128)(2,1)S(1)}, bf16[256,1024]{1,0:T(8,128)(2,1)S(1)}, u32[]{:S(2)}, u32[]{:S(2)}) %collective-permute-start.26) | collective-permute-done | bytes 524320 | tf_op jit(solution)/shard_map/ppermute | solution.py:33
  160.0 11.8 %collective-permute-done.27 = bf16[256,1024]{1,0:T(8,128)(2,1)S(1)} collective-permute-done((bf16[256,1024]{1,0:T(8,128)(2,1)S(1)}, bf16[256,1024]{1,0:T(8,128)(2,1)S(1)}, u32[]{:S(2)}, u32[]{:S(2)}) %collective-permute-start.27) | collective-permute-done | bytes 524320 | tf_op jit(solution)/shard_map/ppermute | solution.py:33
  172.2 3.1 %collective-permute-start.29 = (bf16[128,1024]{1,0:T(8,128)(2,1)S(1)}, bf16[128,1024]{1,0:T(8,128)(2,1)S(1)}, u32[]{:S(2)}, u32[]{:S(2)}) collective-permute-start(bf16[128,1024]{1,0:T(8,128)(2,1)S(1)} %slice.193), channel_id=1, source_target_pairs={{1,0},{0,1},{3,2},{2,3},{5,4},{4,5},{7,6},{6,7},{9,8},{8,9},{11,10... | collective-permute-start | bytes 786440 | tf_op jit(solution)/shard_map/ppermute | solution.py:33
  175.9 3.6 %collective-permute-start.32 = (bf16[128,1024]{1,0:T(8,128)(2,1)S(1)}, bf16[128,1024]{1,0:T(8,128)(2,1)S(1)}, u32[]{:S(2)}, u32[]{:S(2)}) collective-permute-start(bf16[128,1024]{1,0:T(8,128)(2,1)S(1)} %get-tuple-element.49), channel_id=1, source_target_pairs={{16,0},{24,8},{0,16},{8,24},{17,1},{25,9},{1,17},{9,25},{18,2},{26... | collective-permute-start | bytes 786440 | tf_op jit(solution)/shard_map/ppermute | solution.py:33
  179.7 1.9 collective-permute-done.29
  181.7 3.6 %collective-permute-done.34 = bf16[128,1024]{1,0:T(8,128)(2,1)S(1)} collective-permute-done((bf16[128,1024]{1,0:T(8,128)(2,1)S(1)}, bf16[128,1024]{1,0:T(8,128)(2,1)S(1)}, u32[]{:S(2)}, u32[]{:S(2)}) %collective-permute-start.34) | collective-permute-done | bytes 262176 | tf_op jit(solution)/shard_map/ppermute | solution.py:33
  185.3 5.4 %collective-permute-done.32 = bf16[128,1024]{1,0:T(8,128)(2,1)S(1)} collective-permute-done((bf16[128,1024]{1,0:T(8,128)(2,1)S(1)}, bf16[128,1024]{1,0:T(8,128)(2,1)S(1)}, u32[]{:S(2)}, u32[]{:S(2)}) %collective-permute-start.32) | collective-permute-done | bytes 262176 | tf_op jit(solution)/shard_map/ppermute | solution.py:33
  191.0 0.8 pad_maximum_fusion.8
  (136 shorter events, 14.5 us)
Async XLA Ops:
  6.5 53.2 %all-gather.3.cloned.1.call-start = ((), (), s32[]{:S(2)}) async-start(), calls=%async_computation | async-start | bytes 5242880 | tf_op jit(solution)/shard_map/all_gather | solution.py:177
  6.5 15.4 %collective-permute-start = (bf16[128,2048]{1,0:T(8,128)(2,1)}, bf16[128,2048]{1,0:T(8,128)(2,1)S(1)}, u32[]{:S(2)}, u32[]{:S(2)}) collective-permute-start(bf16[128,2048]{1,0:T(8,128)(2,1)} %param.7), channel_id=1, source_target_pairs={{1,0},{0,1},{3,2},{2,3},{5,4},{4,5},{7,6},{6,7},{9,8},{8,9},{11,10... | collective-permute-start | bytes 1572872 | tf_op jit(solution)/shard_map/ppermute | solution.py:33
  9.6 20.4 %collective-permute-start.2 = (bf16[128,2048]{1,0:T(8,128)(2,1)}, bf16[128,2048]{1,0:T(8,128)(2,1)S(1)}, u32[]{:S(2)}, u32[]{:S(2)}) collective-permute-start(bf16[128,2048]{1,0:T(8,128)(2,1)} %param.7), channel_id=1, source_target_pairs={{16,0},{24,8},{0,16},{8,24},{17,1},{25,9},{1,17},{9,25},{18,2},{26... | collective-permute-start | bytes 1572872 | tf_op jit(solution)/shard_map/ppermute | solution.py:33
  12.8 25.0 %collective-permute-start.1 = (bf16[128,2048]{1,0:T(8,128)(2,1)}, bf16[128,2048]{1,0:T(8,128)(2,1)S(1)}, u32[]{:S(2)}, u32[]{:S(2)}) collective-permute-start(bf16[128,2048]{1,0:T(8,128)(2,1)} %param.7), channel_id=1, source_target_pairs={{8,0},{16,8},{24,16},{0,24},{9,1},{17,9},{25,17},{1,25},{10,2},{18... | collective-permute-start | bytes 1572872 | tf_op jit(solution)/shard_map/ppermute | solution.py:33
  13.8 24.1 %collective-permute-start.3 = (bf16[128,2048]{1,0:T(8,128)(2,1)}, bf16[128,2048]{1,0:T(8,128)(2,1)S(1)}, u32[]{:S(2)}, u32[]{:S(2)}) collective-permute-start(bf16[128,2048]{1,0:T(8,128)(2,1)} %param.7), channel_id=1, source_target_pairs={{24,0},{0,8},{8,16},{16,24},{25,1},{1,9},{9,17},{17,25},{26,2},{2,... | collective-permute-start | bytes 1572872 | tf_op jit(solution)/shard_map/ppermute | solution.py:33
  14.8 122.0 %all-gather.5.cloned.1.call-start = ((), (), s32[]{:S(2)}) async-start(), calls=%async_computation.1 | async-start | bytes 5242880 | tf_op jit(solution)/shard_map/all_gather | solution.py:180
  21.9 25.6 %collective-permute-start.4 = (bf16[128,2048]{1,0:T(8,128)(2,1)S(1)}, bf16[128,2048]{1,0:T(8,128)(2,1)S(1)}, u32[]{:S(2)}, u32[]{:S(2)}) collective-permute-start(bf16[128,2048]{1,0:T(8,128)(2,1)S(1)} %collective-permute-done), channel_id=1, source_target_pairs={{8,0},{16,8},{24,16},{0,24},{9,1},{17,9},{25,17},{1,25},{10,2},{18... | collective-permute-start | bytes 1572872 | tf_op jit(solution)/shard_map/ppermute | solution.py:33
  24.9 34.8 %collective-permute-start.6 = (bf16[128,2048]{1,0:T(8,128)(2,1)S(1)}, bf16[128,2048]{1,0:T(8,128)(2,1)S(1)}, u32[]{:S(2)}, u32[]{:S(2)}) collective-permute-start(bf16[128,2048]{1,0:T(8,128)(2,1)S(1)} %collective-permute-done), channel_id=1, source_target_pairs={{24,0},{0,8},{8,16},{16,24},{25,1},{1,9},{9,17},{17,25},{26,2},{2,... | collective-permute-start | bytes 1572872 | tf_op jit(solution)/shard_map/ppermute | solution.py:33
  30.0 18.4 %collective-permute-start.5 = (bf16[128,2048]{1,0:T(8,128)(2,1)S(1)}, bf16[128,2048]{1,0:T(8,128)(2,1)}, u32[]{:S(2)}, u32[]{:S(2)}) collective-permute-start(bf16[128,2048]{1,0:T(8,128)(2,1)S(1)} %collective-permute-done.2), channel_id=1, source_target_pairs={{1,0},{0,1},{3,2},{2,3},{5,4},{4,5},{7,6},{6,7},{9,8},{8,9},{11,10... | collective-permute-start | bytes 1572872 | tf_op jit(solution)/shard_map/ppermute | solution.py:33
  38.1 4.0 %copy-start.2 = (f32[2048]{0:T(1024)S(1)}, f32[2048]{0:T(1024)}, u32[]{:S(2)}) copy-start(f32[2048]{0:T(1024)} %param.8) | copy-start | bytes 24580
  48.4 15.7 %copy-start = (bf16[2048,256]{1,0:T(8,128)(2,1)S(1)}, bf16[2048,256]{1,0:T(8,128)(2,1)}, u32[]{:S(2)}) copy-start(bf16[2048,256]{1,0:T(8,128)(2,1)} %pad_maximum_fusion) | copy-start | bytes 3145732
  60.7 3.4 %copy-start.7 = (bf16[1024,2048]{1,0:T(8,128)(2,1)S(1)}, bf16[1024,2048]{1,0:T(8,128)(2,1)}, u32[]{:S(2)}) copy-start(bf16[1024,2048]{1,0:T(8,128)(2,1)} %fusion.83) | copy-start | bytes 12582916
  64.1 3.6 %copy-start.1 = (bf16[2048,256]{1,0:T(8,128)(2,1)S(1)}, bf16[2048,256]{1,0:T(8,128)(2,1)}, u32[]{:S(2)}) copy-start(bf16[2048,256]{1,0:T(8,128)(2,1)} %pad_maximum_fusion.1) | copy-start | bytes 3145732
  64.1 3.6 %collective-permute-start.7 = (bf16[512,256]{1,0:T(8,128)(2,1)}, bf16[512,256]{1,0:T(8,128)(2,1)}, u32[]{:S(2)}, u32[]{:S(2)}) collective-permute-start(bf16[512,256]{1,0:T(8,128)(2,1)} %fusion.47), channel_id=1, source_target_pairs={{32,0},{0,32},{33,1},{1,33},{34,2},{2,34},{35,3},{3,35},{36,4},{4,... | collective-permute-start | bytes 786440 | tf_op jit(solution)/shard_map/ppermute | solution.py:33
  65.6 6.4 %collective-permute-start.8 = (bf16[512,256]{1,0:T(8,128)(2,1)}, bf16[512,256]{1,0:T(8,128)(2,1)S(1)}, u32[]{:S(2)}, u32[]{:S(2)}) collective-permute-start(bf16[512,256]{1,0:T(8,128)(2,1)} %fusion.50), channel_id=1, source_target_pairs={{32,0},{0,32},{33,1},{1,33},{34,2},{2,34},{35,3},{3,35},{36,4},{4,... | collective-permute-start | bytes 786440 | tf_op jit(solution)/shard_map/ppermute | solution.py:33
  67.7 4.3 %copy-start.8 = (bf16[1024,2048]{1,0:T(8,128)(2,1)S(1)}, bf16[1024,2048]{1,0:T(8,128)(2,1)}, u32[]{:S(2)}) copy-start(bf16[1024,2048]{1,0:T(8,128)(2,1)} %fusion.83) | copy-start | bytes 12582916
  70.2 3.2 %collective-permute-start.12 = (f32[8,128]{1,0:T(8,128)S(1)}, f32[8,128]{1,0:T(8,128)S(1)}, u32[]{:S(2)}, u32[]{:S(2)}) collective-permute-start(f32[8,128]{1,0:T(8,128)S(1)} %stack.60), channel_id=1, source_target_pairs={{32,0},{0,32},{33,1},{1,33},{34,2},{2,34},{35,3},{3,35},{36,4},{4,... | collective-permute-start | bytes 12296 | tf_op jit(solution)/shard_map/ppermute | solution.py:33
  70.3 9.9 %collective-permute-start.14 = (bf16[512,256]{1,0:T(8,128)(2,1)S(1)}, bf16[512,256]{1,0:T(8,128)(2,1)S(1)}, u32[]{:S(2)}, u32[]{:S(2)}) collective-permute-start(bf16[512,256]{1,0:T(8,128)(2,1)S(1)} %fusion.44), channel_id=1, source_target_pairs={{64,0},{0,64},{65,1},{1,65},{66,2},{2,66},{67,3},{3,67},{68,4},{4,... | collective-permute-start | bytes 786440 | tf_op jit(solution)/shard_map/ppermute | solution.py:33
  73.4 5.7 %collective-permute-start.13 = (f32[8,128]{1,0:T(8,128)S(1)}, f32[8,128]{1,0:T(8,128)S(1)}, u32[]{:S(2)}, u32[]{:S(2)}) collective-permute-start(f32[8,128]{1,0:T(8,128)S(1)} %add.150), channel_id=1, source_target_pairs={{64,0},{0,64},{65,1},{1,65},{66,2},{2,66},{67,3},{3,67},{68,4},{4,... | collective-permute-start | bytes 12296 | tf_op jit(solution)/shard_map/ppermute | solution.py:33
  76.4 15.9 %collective-permute-start.9 = (bf16[1024,256]{1,0:T(8,128)(2,1)S(1)}, bf16[1024,256]{1,0:T(8,128)(2,1)S(1)}, u32[]{:S(2)}, u32[]{:S(2)}) collective-permute-start(bf16[1024,256]{1,0:T(8,128)(2,1)S(1)} %convolution_convert_fusion.1), channel_id=1, source_target_pairs={{32,0},{0,32},{33,1},{1,33},{34,2},{2,34},{35,3},{3,35},{36,4},{4,... | collective-permute-start | bytes 1572872 | tf_op jit(solution)/shard_map/ppermute | solution.py:33
  80.2 0.7 copy-start.4
  83.1 9.2 %copy-start.9 = (bf16[1024,2048]{1,0:T(8,128)(2,1)S(1)}, bf16[1024,2048]{1,0:T(8,128)(2,1)}, u32[]{:S(2)}) copy-start(bf16[1024,2048]{1,0:T(8,128)(2,1)} %fusion.83) | copy-start | bytes 12582916
  83.1 15.9 %collective-permute-start.15 = (bf16[2,512,128]{2,1,0:T(8,128)(2,1)}, bf16[2,512,128]{2,1,0:T(8,128)(2,1)S(1)}, u32[]{:S(2)}, u32[]{:S(2)}) collective-permute-start(bf16[2,512,128]{2,1,0:T(8,128)(2,1)} %shard_map.73.m0), channel_id=1, source_target_pairs={{2,0},{4,2},{6,4},{0,6},{3,1},{5,3},{7,5},{1,7},{10,8},{12,10},{14... | collective-permute-start | bytes 786440 | tf_op jit(solution)/shard_map/ppermute | solution.py:33
  84.9 25.8 %collective-permute-start.16 = (bf16[2,512,128]{2,1,0:T(8,128)(2,1)}, bf16[2,512,128]{2,1,0:T(8,128)(2,1)S(1)}, u32[]{:S(2)}, u32[]{:S(2)}) collective-permute-start(bf16[2,512,128]{2,1,0:T(8,128)(2,1)} %shard_map.73.m0), channel_id=1, source_target_pairs={{4,0},{6,2},{0,4},{2,6},{5,1},{7,3},{1,5},{3,7},{12,8},{14,10},{8,... | collective-permute-start | bytes 786440 | tf_op jit(solution)/shard_map/ppermute | solution.py:33
  87.0 23.8 %collective-permute-start.17 = (bf16[2,512,128]{2,1,0:T(8,128)(2,1)}, bf16[2,512,128]{2,1,0:T(8,128)(2,1)S(1)}, u32[]{:S(2)}, u32[]{:S(2)}) collective-permute-start(bf16[2,512,128]{2,1,0:T(8,128)(2,1)} %shard_map.73.m0), channel_id=1, source_target_pairs={{6,0},{0,2},{2,4},{4,6},{7,1},{1,3},{3,5},{5,7},{14,8},{8,10},{10,... | collective-permute-start | bytes 786440 | tf_op jit(solution)/shard_map/ppermute | solution.py:33
  92.2 6.8 %copy-start.3 = (bf16[2,512,128]{2,1,0:T(8,128)(2,1)S(1)}, bf16[2,512,128]{2,1,0:T(8,128)(2,1)}, u32[]{:S(2)}) copy-start(bf16[2,512,128]{2,1,0:T(8,128)(2,1)} %shard_map.73.m0) | copy-start | bytes 786436
  92.2 19.1 %collective-permute-start.10 = (bf16[1024,256]{1,0:T(8,128)(2,1)S(1)}, bf16[1024,256]{1,0:T(8,128)(2,1)S(1)}, u32[]{:S(2)}, u32[]{:S(2)}) collective-permute-start(bf16[1024,256]{1,0:T(8,128)(2,1)S(1)} %convolution_convert_fusion), channel_id=1, source_target_pairs={{32,0},{0,32},{33,1},{1,33},{34,2},{2,34},{35,3},{3,35},{36,4},{4,... | collective-permute-start | bytes 1572872 | tf_op jit(solution)/shard_map/ppermute | solution.py:33
  94.8 19.9 %collective-permute-start.11 = (bf16[1024,256]{1,0:T(8,128)(2,1)S(1)}, bf16[1024,256]{1,0:T(8,128)(2,1)S(1)}, u32[]{:S(2)}, u32[]{:S(2)}) collective-permute-start(bf16[1024,256]{1,0:T(8,128)(2,1)S(1)} %add_convert_fusion.1), channel_id=1, source_target_pairs={{64,0},{0,64},{65,1},{1,65},{66,2},{2,66},{67,3},{3,67},{68,4},{4,... | collective-permute-start | bytes 1572872 | tf_op jit(solution)/shard_map/ppermute | solution.py:33
  99.0 15.7 %copy-start.12 = (bf16[2,512,128]{2,1,0:T(8,128)(2,1)}, bf16[2,512,128]{2,1,0:T(8,128)(2,1)S(1)}, u32[]{:S(2)}) copy-start(bf16[2,512,128]{2,1,0:T(8,128)(2,1)S(1)} %collective-permute-done.15.m1) | copy-start | bytes 786436
  99.0 15.7 %collective-permute-start.18 = (bf16[2,512,128]{2,1,0:T(8,128)(2,1)S(1)}, bf16[2,512,128]{2,1,0:T(8,128)(2,1)S(1)}, u32[]{:S(2)}, u32[]{:S(2)}) collective-permute-start(bf16[2,512,128]{2,1,0:T(8,128)(2,1)S(1)} %copy-done.3), channel_id=1, source_target_pairs={{32,0},{0,32},{33,1},{1,33},{34,2},{2,34},{35,3},{3,35},{36,4},{4,... | collective-permute-start | bytes 786440 | tf_op jit(solution)/shard_map/ppermute | solution.py:33
  110.8 3.9 %copy-start.13 = (bf16[2,512,128]{2,1,0:T(8,128)(2,1)}, bf16[2,512,128]{2,1,0:T(8,128)(2,1)S(1)}, u32[]{:S(2)}) copy-start(bf16[2,512,128]{2,1,0:T(8,128)(2,1)S(1)} %collective-permute-done.16.m2) | copy-start | bytes 786436
  110.8 3.9 %collective-permute-start.19 = (bf16[2,512,128]{2,1,0:T(8,128)(2,1)S(1)}, bf16[2,512,128]{2,1,0:T(8,128)(2,1)S(1)}, u32[]{:S(2)}, u32[]{:S(2)}) collective-permute-start(bf16[2,512,128]{2,1,0:T(8,128)(2,1)S(1)} %collective-permute-done.15.m1), channel_id=1, source_target_pairs={{32,0},{0,32},{33,1},{1,33},{34,2},{2,34},{35,3},{3,35},{36,4},{4,... | collective-permute-start | bytes 786440 | tf_op jit(solution)/shard_map/ppermute | solution.py:33
  110.8 3.8 %copy-start.14 = (bf16[2,512,128]{2,1,0:T(8,128)(2,1)}, bf16[2,512,128]{2,1,0:T(8,128)(2,1)S(1)}, u32[]{:S(2)}) copy-start(bf16[2,512,128]{2,1,0:T(8,128)(2,1)S(1)} %collective-permute-done.17.m3) | copy-start | bytes 786436
  110.8 3.9 %collective-permute-start.20 = (bf16[2,512,128]{2,1,0:T(8,128)(2,1)S(1)}, bf16[2,512,128]{2,1,0:T(8,128)(2,1)S(1)}, u32[]{:S(2)}, u32[]{:S(2)}) collective-permute-start(bf16[2,512,128]{2,1,0:T(8,128)(2,1)S(1)} %collective-permute-done.16.m2), channel_id=1, source_target_pairs={{32,0},{0,32},{33,1},{1,33},{34,2},{2,34},{35,3},{3,35},{36,4},{4,... | collective-permute-start | bytes 786440 | tf_op jit(solution)/shard_map/ppermute | solution.py:33
  111.3 3.5 %collective-permute-start.21 = (bf16[2,512,128]{2,1,0:T(8,128)(2,1)S(1)}, bf16[2,512,128]{2,1,0:T(8,128)(2,1)S(1)}, u32[]{:S(2)}, u32[]{:S(2)}) collective-permute-start(bf16[2,512,128]{2,1,0:T(8,128)(2,1)S(1)} %collective-permute-done.17.m3), channel_id=1, source_target_pairs={{32,0},{0,32},{33,1},{1,33},{34,2},{2,34},{35,3},{3,35},{36,4},{4,... | collective-permute-start | bytes 786440 | tf_op jit(solution)/shard_map/ppermute | solution.py:33
  114.7 0.7 copy-start.15
  114.7 0.8 copy-start.16
  114.7 0.9 copy-start.17
  114.8 0.9 copy-start.18
  115.7 0.8 copy-start.11
  125.2 9.2 %copy-start.6 = (bf16[2,2,128,256]{3,2,1,0:T(8,128)(2,1)S(1)}, bf16[2,2,128,256]{3,2,1,0:T(8,128)(2,1)}, u32[]{:S(2)}) copy-start(bf16[2,2,128,256]{3,2,1,0:T(8,128)(2,1)} %shard_map.74) | copy-start | bytes 786436
  125.2 9.2 %collective-permute-start.22 = (bf16[512,256]{1,0:T(8,128)(2,1)}, bf16[512,256]{1,0:T(8,128)(2,1)S(1)}, u32[]{:S(2)}, u32[]{:S(2)}) collective-permute-start(bf16[512,256]{1,0:T(8,128)(2,1)} %bitcast.123), channel_id=1, source_target_pairs={{64,0},{0,64},{65,1},{1,65},{66,2},{2,66},{67,3},{3,67},{68,4},{4,... | collective-permute-start | bytes 786440 | tf_op jit(solution)/shard_map/ppermute | solution.py:33
  134.4 2.0 %collective-permute-start.24 = (bf16[512,512]{1,0:T(8,128)(2,1)S(1)}, bf16[512,512]{1,0:T(8,128)(2,1)S(1)}, u32[]{:S(2)}, u32[]{:S(2)}) collective-permute-start(bf16[512,512]{1,0:T(8,128)(2,1)S(1)} %pad_maximum_fusion.6), channel_id=1, source_target_pairs={{32,0},{0,32},{33,1},{1,33},{34,2},{2,34},{35,3},{3,35},{36,4},{4,... | collective-permute-start | bytes 1572872 | tf_op jit(solution)/shard_map/ppermute | solution.py:33
  134.5 8.9 %collective-permute-start.23 = (bf16[512,256]{1,0:T(8,128)(2,1)}, bf16[512,256]{1,0:T(8,128)(2,1)S(1)}, u32[]{:S(2)}, u32[]{:S(2)}) collective-permute-start(bf16[512,256]{1,0:T(8,128)(2,1)} %bitcast.122), channel_id=1, source_target_pairs={{64,0},{0,64},{65,1},{1,65},{66,2},{2,66},{67,3},{3,67},{68,4},{4,... | collective-permute-start | bytes 786440 | tf_op jit(solution)/shard_map/ppermute | solution.py:33
  136.9 3.0 %copy-start.10 = (bf16[1024,2048]{1,0:T(8,128)(2,1)S(1)}, bf16[1024,2048]{1,0:T(8,128)(2,1)}, u32[]{:S(2)}) copy-start(bf16[1024,2048]{1,0:T(8,128)(2,1)} %all-gather.5.cloned.1.call-done) | copy-start | bytes 12582916
  139.9 3.6 %copy-start.5 = (bf16[2,2,128,256]{3,2,1,0:T(8,128)(2,1)S(1)}, bf16[2,2,128,256]{3,2,1,0:T(8,128)(2,1)}, u32[]{:S(2)}) copy-start(bf16[2,2,128,256]{3,2,1,0:T(8,128)(2,1)} %shard_map.75) | copy-start | bytes 786436
  143.6 7.1 %collective-permute-start.25 = (bf16[512,512]{1,0:T(8,128)(2,1)S(1)}, bf16[512,512]{1,0:T(8,128)(2,1)S(1)}, u32[]{:S(2)}, u32[]{:S(2)}) collective-permute-start(bf16[512,512]{1,0:T(8,128)(2,1)S(1)} %pad_maximum_fusion.7), channel_id=1, source_target_pairs={{32,0},{0,32},{33,1},{1,33},{34,2},{2,34},{35,3},{3,35},{36,4},{4,... | collective-permute-start | bytes 1572872 | tf_op jit(solution)/shard_map/ppermute | solution.py:33
  143.7 16.4 %collective-permute-start.26 = (bf16[256,1024]{1,0:T(8,128)(2,1)S(1)}, bf16[256,1024]{1,0:T(8,128)(2,1)S(1)}, u32[]{:S(2)}, u32[]{:S(2)}) collective-permute-start(bf16[256,1024]{1,0:T(8,128)(2,1)S(1)} %fusion.26), channel_id=1, source_target_pairs={{16,0},{24,8},{0,16},{8,24},{17,1},{25,9},{1,17},{9,25},{18,2},{26... | collective-permute-start | bytes 1572872 | tf_op jit(solution)/shard_map/ppermute | solution.py:33
  146.1 25.7 %collective-permute-start.27 = (bf16[256,1024]{1,0:T(8,128)(2,1)S(1)}, bf16[256,1024]{1,0:T(8,128)(2,1)S(1)}, u32[]{:S(2)}, u32[]{:S(2)}) collective-permute-start(bf16[256,1024]{1,0:T(8,128)(2,1)S(1)} %fusion.29), channel_id=1, source_target_pairs={{8,0},{16,8},{24,16},{0,24},{9,1},{17,9},{25,17},{1,25},{10,2},{18... | collective-permute-start | bytes 1572872 | tf_op jit(solution)/shard_map/ppermute | solution.py:33
  147.6 27.7 %collective-permute-start.31 = (bf16[2,128,1024]{2,1,0:T(8,128)(2,1)S(1)}, bf16[2,128,1024]{2,1,0:T(8,128)(2,1)S(1)}, u32[]{:S(2)}, u32[]{:S(2)}) collective-permute-start(bf16[2,128,1024]{2,1,0:T(8,128)(2,1)S(1)} %slice_bitcast_fusion), channel_id=1, source_target_pairs={{1,0},{0,1},{3,2},{2,3},{5,4},{4,5},{7,6},{6,7},{9,8},{8,9},{11,10... | collective-permute-start | bytes 1572872 | tf_op jit(solution)/shard_map/ppermute | solution.py:33
  151.8 20.0 %collective-permute-start.28 = (bf16[256,1024]{1,0:T(8,128)(2,1)S(1)}, bf16[256,1024]{1,0:T(8,128)(2,1)S(1)}, u32[]{:S(2)}, u32[]{:S(2)}) collective-permute-start(bf16[256,1024]{1,0:T(8,128)(2,1)S(1)} %fusion.35), channel_id=1, source_target_pairs={{24,0},{0,8},{8,16},{16,24},{25,1},{1,9},{9,17},{17,25},{26,2},{2,... | collective-permute-start | bytes 1572872 | tf_op jit(solution)/shard_map/ppermute | solution.py:33
  154.0 21.5 %collective-permute-start.30 = (bf16[2,128,1024]{2,1,0:T(8,128)(2,1)S(1)}, bf16[2,128,1024]{2,1,0:T(8,128)(2,1)S(1)}, u32[]{:S(2)}, u32[]{:S(2)}) collective-permute-start(bf16[2,128,1024]{2,1,0:T(8,128)(2,1)S(1)} %slice_bitcast_fusion.1), channel_id=1, source_target_pairs={{1,0},{0,1},{3,2},{2,3},{5,4},{4,5},{7,6},{6,7},{9,8},{8,9},{11,10... | collective-permute-start | bytes 1572872 | tf_op jit(solution)/shard_map/ppermute | solution.py:33
  172.2 9.4 %collective-permute-start.29 = (bf16[128,1024]{1,0:T(8,128)(2,1)S(1)}, bf16[128,1024]{1,0:T(8,128)(2,1)S(1)}, u32[]{:S(2)}, u32[]{:S(2)}) collective-permute-start(bf16[128,1024]{1,0:T(8,128)(2,1)S(1)} %slice.193), channel_id=1, source_target_pairs={{1,0},{0,1},{3,2},{2,3},{5,4},{4,5},{7,6},{6,7},{9,8},{8,9},{11,10... | collective-permute-start | bytes 786440 | tf_op jit(solution)/shard_map/ppermute | solution.py:33
  175.6 9.7 %collective-permute-start.34 = (bf16[128,1024]{1,0:T(8,128)(2,1)S(1)}, bf16[128,1024]{1,0:T(8,128)(2,1)S(1)}, u32[]{:S(2)}, u32[]{:S(2)}) collective-permute-start(bf16[128,1024]{1,0:T(8,128)(2,1)S(1)} %fusion.96), channel_id=1, source_target_pairs={{24,0},{0,8},{8,16},{16,24},{25,1},{1,9},{9,17},{17,25},{26,2},{2,... | collective-permute-start | bytes 786440 | tf_op jit(solution)/shard_map/ppermute | solution.py:33
  175.9 14.8 %collective-permute-start.32 = (bf16[128,1024]{1,0:T(8,128)(2,1)S(1)}, bf16[128,1024]{1,0:T(8,128)(2,1)S(1)}, u32[]{:S(2)}, u32[]{:S(2)}) collective-permute-start(bf16[128,1024]{1,0:T(8,128)(2,1)S(1)} %get-tuple-element.49), channel_id=1, source_target_pairs={{16,0},{24,8},{0,16},{8,24},{17,1},{25,9},{1,17},{9,25},{18,2},{26... | collective-permute-start | bytes 786440 | tf_op jit(solution)/shard_map/ppermute | solution.py:33
  179.4 11.3 %collective-permute-start.33 = (bf16[128,1024]{1,0:T(8,128)(2,1)S(1)}, bf16[128,1024]{1,0:T(8,128)(2,1)S(1)}, u32[]{:S(2)}, u32[]{:S(2)}) collective-permute-start(bf16[128,1024]{1,0:T(8,128)(2,1)S(1)} %get-tuple-element.50), channel_id=1, source_target_pairs={{8,0},{16,8},{24,16},{0,24},{9,1},{17,9},{25,17},{1,25},{10,2},{18... | collective-permute-start | bytes 786440 | tf_op jit(solution)/shard_map/ppermute | solution.py:33
Sparse Core Ops, SparseCore 0:
  14.9 44.7 all-gather.2
  61.4 59.8 all-gather.4

commit v4 on v3

--- a/solution.py
+++ b/solution.py
@@ -23,6 +23,7 @@
 rope_base = 500000.0
 MASKED = -1e30
 VMEM = 60 * 2**20
+LIGHT = pl.CostEstimate(flops=1, bytes_accessed=1, transcendentals=0)
 
 f32 = jnp.float32
 bf16 = jnp.bfloat16
@@ -37,27 +38,11 @@
     return u * cosine + pltpu.roll(u, HEAD_SIZE // 2, 1) * sine
 
 
-def finish_kernel(core, home, far, cosine, sine, scale, out):
-    total = (home[...].astype(f32) + far[...].astype(f32)) * scale[...]
-    out[0] = turn(total[:, :HEAD_SIZE], cosine[0], sine[0]).astype(bf16)
-    out[1] = total[:, HEAD_SIZE:].astype(bf16)
-
-
-def finish_kv(core, home, far, cosine, sine, scale):
-    rows = pl.BlockSpec((PART, WIDE), lambda i, core: (0, 0))
-    angle = pl.BlockSpec((1, PART, HEAD_SIZE), lambda i, core: (core[0], 0, 0))
-    return pl.pallas_call(
-        finish_kernel,
-        grid_spec=pltpu.PrefetchScalarGridSpec(
-            num_scalar_prefetch=1,
-            grid=(1,),
-            in_specs=[rows, rows, angle, angle, pl.BlockSpec((PART, 1), lambda i, core: (core[0], 0))],
-            out_specs=pl.BlockSpec((2, PART, HEAD_SIZE), lambda i, core: (0, 0, 0)),
-        ),
-        out_shape=jax.ShapeDtypeStruct((2, PART, HEAD_SIZE), bf16),
-        compiler_params=pltpu.CompilerParams(vmem_limit_bytes=VMEM),
-        cost_estimate=pl.CostEstimate(flops=PART * 2048, bytes_accessed=2 * 2**20, transcendentals=0),
-    )(core, home, far, cosine, sine, scale)
+def pick(tiles, i):
+    chosen = jnp.int32(tiles[0])
+    for at, tile in enumerate(tiles[1:], 1):
+        chosen = jnp.where(i == at, jnp.int32(tile), chosen)
+    return chosen
 
 
 def attention_kernel(
@@ -65,7 +50,7 @@
     m0, m1, m2, m3, t0, t1, t2, t3, out_ref, keys, values,
 ):
     place = pl.program_id(0)
-    dy = jnp.where(place == 0, tiles[0], tiles[1])
+    dy = pick(tiles, place)
     y, z, xh, c = scalars[8], scalars[9], scalars[10], scalars[11]
 
     @pl.when(place == 0)
@@ -133,7 +118,7 @@
 
 def attention(tiles, scalars, home, far, cosine, sine, scale, bounds, mine, theirs):
     def tile(i):
-        return jnp.where(i == 0, tiles[0], tiles[1])
+        return pick(tiles, i)
 
     half = pl.BlockSpec((2, PART, HEAD_SIZE), lambda i: (0, 0, 0))
     rows = [pl.BlockSpec((128, WIDE), lambda i, dx=dx: (4 * dx + tile(i), 0)) for dx in (0, 1)]
@@ -141,7 +126,7 @@
     column = [pl.BlockSpec((128, 1), lambda i, dx=dx: (4 * dx + tile(i), 0)) for dx in (0, 1)]
     return pl.pallas_call(
         functools.partial(attention_kernel, tiles),
-        grid=(2,),
+        grid=(len(tiles),),
         in_specs=[pl.BlockSpec(memory_space=pltpu.SMEM)]
         + rows * 2
         + [angle] * 2
@@ -149,11 +134,11 @@
         + [pl.BlockSpec((1, 2, 2 * TILE), lambda i: (tile(i), 0, 0))]
         + [half] * 8,
         out_specs=pl.BlockSpec((1, 2, 128, WIDE), lambda i: (i, 0, 0, 0)),
-        out_shape=jax.ShapeDtypeStruct((2, 2, 128, WIDE), bf16),
+        out_shape=jax.ShapeDtypeStruct((len(tiles), 2, 128, WIDE), bf16),
         scratch_shapes=[pltpu.VMEM((TOKENS, HEAD_SIZE), bf16)] * 2,
         compiler_params=pltpu.CompilerParams(vmem_limit_bytes=VMEM),
         cost_estimate=pl.CostEstimate(
-            flops=3 * 10**9, bytes_accessed=4 * 2**20, transcendentals=4 * 10**6
+            flops=len(tiles) * 10**9, bytes_accessed=2**22, transcendentals=len(tiles) * 10**6
         ),
     )(scalars, home, home, far, far, cosine, sine, scale, scale, bounds, *mine, *theirs)
 
@@ -167,18 +152,16 @@
     x[3, 0] = receive(tokens, "y", -1)
     x[0, 1] = receive(tokens, "xh", 1)
     x[2, 0] = receive(tokens, "y", 2)
-    key_weight, value_weight, segment_ids, x[0, 1] = barrier(
-        (key_weight, value_weight, segment_ids, x[0, 1])
+    key_weight, value_weight, segment_ids, w_output, x[0, 1] = barrier(
+        (key_weight, value_weight, segment_ids, w_output, x[0, 1])
     )
     x[1, 1] = receive(x[0, 1], "y", 1)
     x[3, 1] = receive(x[0, 1], "y", -1)
     x[2, 1] = receive(x[2, 0], "xh", 1)
 
     weights = lax.all_gather(w_query, "z", axis=0, tiled=True)
-    w_output, weights = barrier((w_output, weights))
-    weights = weights.reshape(4, w_query.shape[0], w_query.shape[1])
     w_out = lax.all_gather(w_output, "z", axis=0, tiled=True)
-
+    columns = w_output.shape[1] // 2
     def relative(by_place):
         turned = lax.dynamic_slice_in_dim(jnp.concatenate([by_place, by_place], axis=0), y, 4, 0)
         swapped = jnp.where(xh == 0, turned, turned[:, ::-1])
@@ -219,6 +202,7 @@
     pieces = [x[dy, dx].astype(f32) for dx in (0, 1) for dy in range(4)]
     rows = jnp.concatenate([(piece * gain).astype(bf16) for piece in pieces], axis=0)
     squares = jnp.stack([jnp.sum(piece * piece, axis=1) for piece in pieces])
+    squares = squares + receive(squares, "c", 1)
 
     def half(rows, core):
         return lax.dynamic_slice_in_dim(rows, core * PART, PART, 0)
@@ -233,14 +217,18 @@
     rows, across, squares = barrier((rows, across, squares))
     kv_far = receive(across, "xl", 1)
     kv_home = (product(half(rows, c), kv_weights[0]) + got.astype(f32)).astype(bf16)
-    squares = squares + receive(squares, "c", 1)
     squares = squares + receive(squares, "xl", 1)
     scale = lax.rsqrt(squares.reshape(GROUP_ROWS, 1) / MODEL_WIDTH + norm_eps)
-    kv = finish_kv(c.astype(jnp.int32)[None], kv_home, kv_far, cosine, sine, scale)
+    total = (kv_home.astype(f32) + kv_far.astype(f32)) * half(scale, c)
+    key, value = total[:, :HEAD_SIZE], total[:, HEAD_SIZE:]
+    swapped_key = jnp.concatenate([key[:, HEAD_SIZE // 2 :], key[:, : HEAD_SIZE // 2]], axis=1)
+    cos_half, sin_half = (lax.dynamic_index_in_dim(t, c, 0, keepdims=False) for t in (cosine, sine))
+    key = key * cos_half + swapped_key * sin_half
+    kv = jnp.stack([key.astype(bf16), value.astype(bf16)])
+    rows, kv = barrier((rows, kv))
     mine = [kv] + [receive(kv, "z", step) for step in (1, 2, 3)]
-    theirs = [receive(part, "c", 1) for part in mine]
-
-    rows, kv_home = barrier((rows, kv_home))
+
+    weights = weights.reshape(4, w_query.shape[0], w_query.shape[1])
 
     def query_weight(core, across):
         return lax.dynamic_index_in_dim(weights, (xl ^ across) * 2 + core, 0, keepdims=False)
@@ -251,44 +239,45 @@
     rows, across = barrier((rows, across))
     q_far = receive(across, "xl", 1)
     q_home = (product(rows, query_weight(c, 0)) + got.astype(f32)).astype(bf16)
+    mine[1:], q_home, q_far = barrier((mine[1:], q_home, q_far))
+    theirs = [receive(part, "c", 1) for part in mine]
 
     def all_heads(mixed, before):
         across = receive(mixed, "xl", 1)
-        if before:
-            across, *before = barrier((across, *before))
-        low, high = jnp.where(xl == 0, mixed, across), jnp.where(xl == 0, across, mixed)
-        pair = jnp.concatenate([low, high], axis=1)
-        other = receive(pair, "c", 1)
-        even, odd = jnp.where(c == 0, pair, other), jnp.where(c == 0, other, pair)
-        heads = jnp.concatenate([even[:, :WIDE], odd[:, :WIDE], even[:, WIDE:], odd[:, WIDE:]], axis=1)
-        return heads, before
-
-    columns = w_out.shape[1] // 2
-    y_first, xh_first = {}, {}
-    mixed = [
-        attention(tiles, scalars, q_home, q_far, cosine, sine, scale, bounds, mine, theirs)
-        for tiles in ((2, 3), (1, 0))
-    ]
-    sent, seconds = [mixed[1]], []
-    for step, tiles in enumerate(((2, 3), (1, 0))):
-        heads, sent = all_heads(mixed[step].reshape(PART, WIDE), sent)
-        if step == 0:
-            mixed[1] = sent[0]
+        across, before = barrier((across, before))
+        beside, diagonal = receive(mixed, "c", 1), receive(across, "c", 1)
+        own = xl * 2 + c
+        blocks = []
+        for step in range(4):
+            far = own ^ step
+            near = jnp.where(far == 0, mixed, beside)
+            blocks.append(jnp.where(far < 2, near, jnp.where(far == 2, across, diagonal)))
+        return jnp.concatenate(blocks, axis=1), before
+
+    y_first, seconds = {}, {}
+    groups = ((2, 3), (1, 0))
+    everything = (scalars, q_home, q_far, cosine, sine, scale, bounds, mine, theirs)
+    mixed = [attention(tiles, *everything) for tiles in groups]
+    for step, tiles in enumerate(groups):
+        heads, before = all_heads(
+            mixed[step].reshape(len(tiles) * TILE, WIDE), [y_first, seconds] if step else mixed[1]
+        )
+        if step:
+            y_first, seconds = before
         else:
-            y_first[2], y_first[3], seconds[0] = sent
+            mixed[1] = before
+        second = jnp.dot(heads, w_out[:, columns:], preferred_element_type=f32).astype(bf16)
+        second = second.reshape(len(tiles), 2, 128, columns)
         for i, dy in enumerate(tiles):
+            seconds[dy] = second[i]
             y_first[dy] = jnp.dot(
                 heads[i * TILE : (i + 1) * TILE], w_out[:, :columns], preferred_element_type=f32
             ).astype(bf16)
-        seconds.append(jnp.dot(heads, w_out[:, columns:], preferred_element_type=f32).astype(bf16))
-        sent = [y_first[tiles[0]], y_first[tiles[1]], seconds[-1]]
-    for step, tiles in enumerate(((2, 3), (1, 0))):
-        second = seconds[step].reshape(2, 2, 128, columns)
-        got = receive(second[:, 1], "xh", 1)
-        if step == 1:
-            got, xh_first[2], xh_first[3] = barrier((got, xh_first[2], xh_first[3]))
+    xh_first = {}
+    for tiles in groups:
+        got = receive(jnp.stack([seconds[dy][1] for dy in tiles]), "xh", 1)
         for i, dy in enumerate(tiles):
-            xh_first[dy] = (second[i, 0].astype(f32) + got[i].astype(f32)).astype(bf16)
+            xh_first[dy] = (seconds[dy][0].astype(f32) + got[i].astype(f32)).astype(bf16)
 
     def sum_over_y(parts):
         total = parts[0].astype(f32)

time: 201 us -> 192 us (0.955)
  waiting for transfers between devices: 65.3 us -> 80.3 us
  other arithmetic: 23 us -> 14 us
  starting transfers between devices: 43.8 us -> 37.2 us
  matrix products: 28 us -> 22 us
    ppermute x35 -> x37, waiting for transfers between devices: 55.9 us -> 79.5 us  [receive(): return lax.ppermute(value, axis, [((i + step) % n, i) for i in range(n)])]
    all_gather x1, waiting for transfers between devices: 9.29 us -> 0.02 us  [shards(): weights = lax.all_gather(w_query, 'z', axis=0, tiled=True)]
    ppermute x35 -> x37, starting transfers between devices: 43.7 us -> 37.1 us  [receive(): return lax.ppermute(value, axis, [((i + step) % n, i) for i in range(n)])]
    dot_general x8, matrix products: 20.9 us -> 14.7 us  [product(): return jnp.dot(rows, weight, preferred_element_type=f32)]
    unnamed x8, other arithmetic: 8.59 us -> 2.66 us
    pallas_call x3 -> x2, Pallas kernels: 17.5 us -> 15.9 us  [attention(): pl.pallas_call(functools.partial(attention_kernel, tiles), grid=(len(tile...]
  transfers between devices with their start and end apart: 37 -> 39, of which waited for: 16 -> 16; matrix products, arithmetic and copies ran while one was open for 27% -> 21% of each run, Pallas kernels for 9% -> 8%
where the time goes in v4:
time: 192 us; the launch traced here: 190 us
  waiting for transfers between devices  80.3 us (42%)
  starting transfers between devices  37.2 us (19%)
  matrix products  22 us (11%)
  Pallas kernels  15.9 us (8%)
  between operations  14.1 us (7%)
  other arithmetic  14 us (7%)
  local copies, waits for them, and re-layouts  7.02 us (4%)
    ppermute x37, waiting for transfers between devices, receive(): return lax.ppermute(value, axis, [((i + step) % n, i) for i in range(n)])  79.5 us
    ppermute x37, starting transfers between devices, receive(): return lax.ppermute(value, axis, [((i + step) % n, i) for i in range(n)])  37.1 us
    pallas_call x2, Pallas kernels, attention(): pl.pallas_call(functools.partial(attention_kernel, tiles), grid=(len(tile...  15.9 us
    dot_general x8, matrix products, product(): return jnp.dot(rows, weight, preferred_element_type=f32)  14.7 us
    dot_general x2, matrix products, shards(): jnp.dot(heads, w_out[:, columns:], preferred_element_type=f32).astype(bf16)  4.24 us
  transfers between devices with their start and end apart: 39, of which 16 were waited for; matrix products, arithmetic and copies ran while one was open for 21% of the time, Pallas kernels for 8%

profile of v4, /device:TPU:96, one launch (start us, length us, event | category | flops | bytes accessed | tf_op | source)
XLA Modules:
  0.0 190.5 jit_solution(15474242229836376394)
XLA Ops:
  6.5 0.7 all-gather.3.cloned.1.call-update
  7.3 3.1 %collective-permute-start = (bf16[128,2048]{1,0:T(8,128)(2,1)}, bf16[128,2048]{1,0:T(8,128)(2,1)S(1)}, u32[]{:S(2)}, u32[]{:S(2)}) collective-permute-start(bf16[128,2048]{1,0:T(8,128)(2,1)} %param.7), channel_id=1, source_target_pairs={{1,0},{0,1},{3,2},{2,3},{5,4},{4,5},{7,6},{6,7},{9,8},{8,9},{11,10... | collective-permute-start | bytes 1572872 | tf_op jit(solution)/shard_map/ppermute | solution.py:34
  10.4 3.2 %collective-permute-start.2 = (bf16[128,2048]{1,0:T(8,128)(2,1)}, bf16[128,2048]{1,0:T(8,128)(2,1)S(1)}, u32[]{:S(2)}, u32[]{:S(2)}) collective-permute-start(bf16[128,2048]{1,0:T(8,128)(2,1)} %param.7), channel_id=1, source_target_pairs={{16,0},{24,8},{0,16},{8,24},{17,1},{25,9},{1,17},{9,25},{18,2},{26... | collective-permute-start | bytes 1572872 | tf_op jit(solution)/shard_map/ppermute | solution.py:34
  13.6 1.1 collective-permute-start.1
  14.7 1.0 collective-permute-start.3
  15.7 1.2 fusion.78
  17.0 2.0 %fusion.114 = bf16[1024,2048]{1,0:T(8,128)(2,1)} fusion(bf16[128,2048]{1,0:T(8,128)(2,1)} %param.7, f32[2048]{0:T(1024)} %param.8), kind=kLoop, calls=%fused_computation.98 | loop fusion | flops 786431 | bytes 1056768
  19.0 3.7 %collective-permute-done = bf16[128,2048]{1,0:T(8,128)(2,1)S(1)} collective-permute-done((bf16[128,2048]{1,0:T(8,128)(2,1)}, bf16[128,2048]{1,0:T(8,128)(2,1)S(1)}, u32[]{:S(2)}, u32[]{:S(2)}) %collective-permute-start) | collective-permute-done | bytes 524320 | tf_op jit(solution)/shard_map/ppermute | solution.py:34
  22.8 3.0 %collective-permute-start.4 = (bf16[128,2048]{1,0:T(8,128)(2,1)S(1)}, bf16[128,2048]{1,0:T(8,128)(2,1)S(1)}, u32[]{:S(2)}, u32[]{:S(2)}) collective-permute-start(bf16[128,2048]{1,0:T(8,128)(2,1)S(1)} %collective-permute-done), channel_id=1, source_target_pairs={{8,0},{16,8},{24,16},{0,24},{9,1},{17,9},{25,17},{1,25},{10,2},{18... | collective-permute-start | bytes 1572872 | tf_op jit(solution)/shard_map/ppermute | solution.py:34
  25.8 0.7 fusion.143
  26.5 0.9 convert_reduce_fusion
  27.8 1.9 constant_dynamic-slice_fusion.1
  29.7 3.1 %collective-permute-start.5 = (bf16[128,2048]{1,0:T(8,128)(2,1)S(1)}, bf16[128,2048]{1,0:T(8,128)(2,1)S(1)}, u32[]{:S(2)}, u32[]{:S(2)}) collective-permute-start(bf16[128,2048]{1,0:T(8,128)(2,1)S(1)} %collective-permute-done.2), channel_id=1, source_target_pairs={{1,0},{0,1},{3,2},{2,3},{5,4},{4,5},{7,6},{6,7},{9,8},{8,9},{11,10... | collective-permute-start | bytes 1572872 | tf_op jit(solution)/shard_map/ppermute | solution.py:34
  32.9 1.1 pad_maximum_fusion
  34.2 4.4 %collective-permute-done.1 = bf16[128,2048]{1,0:T(8,128)(2,1)S(1)} collective-permute-done((bf16[128,2048]{1,0:T(8,128)(2,1)}, bf16[128,2048]{1,0:T(8,128)(2,1)S(1)}, u32[]{:S(2)}, u32[]{:S(2)}) %collective-permute-start.1) | collective-permute-done | bytes 524320 | tf_op jit(solution)/shard_map/ppermute | solution.py:34
  39.4 8.9 %collective-permute-done.4 = bf16[128,2048]{1,0:T(8,128)(2,1)S(1)} collective-permute-done((bf16[128,2048]{1,0:T(8,128)(2,1)S(1)}, bf16[128,2048]{1,0:T(8,128)(2,1)S(1)}, u32[]{:S(2)}, u32[]{:S(2)}) %collective-permute-start.4) | collective-permute-done | bytes 524320 | tf_op jit(solution)/shard_map/ppermute | solution.py:34
  48.7 1.9 fusion.71
  51.8 1.9 multiply_cosine_fusion
  53.8 2.6 %fusion.68 = bf16[512,256]{1,0:T(8,128)(2,1)S(1)} fusion(bf16[2048,256]{1,0:T(8,128)(2,1)} %copy-done.1, bf16[1024,2048]{1,0:T(8,128)(2,1)} %copy-done.7, s32[]{:T(128)S(6)} %select_n.198, bf16[512,256]{1,0:T(8,128)(2,1)S(1)} %collective-permute-done.7), kind=kOutput, calls=%fused_computation.54 | convolution fusion | flops 537264128 | bytes 3670020 | tf_op jit(solution)/shard_map/dot_general | solution.py:211
  56.3 0.7 collective-permute-start.11
  57.0 0.7 fusion.74
  57.8 1.7 collective-permute-start.10
  60.0 6.5 %collective-permute-done.10 = bf16[512,256]{1,0:T(8,128)(2,1)S(1)} collective-permute-done((bf16[512,256]{1,0:T(8,128)(2,1)S(1)}, bf16[512,256]{1,0:T(8,128)(2,1)S(1)}, u32[]{:S(2)}, u32[]{:S(2)}) %collective-permute-start.10) | collective-permute-done | bytes 262176 | tf_op jit(solution)/shard_map/ppermute | solution.py:34
  66.5 0.7 fusion.65
  67.8 4.2 %convolution_convert_fusion.1 = bf16[1024,256]{1,0:T(8,128)(2,1)S(1)} fusion(bf16[1024,2048]{1,0:T(8,128)(2,1)} %copy-done.7, bf16[4,2048,256]{2,1,0:T(8,128)(2,1)} %bitcast.145, s32[]{:T(128)S(6)} %select_n.205), kind=kOutput, calls=%fused_computation.47 | convolution fusion | flops 1074003968 | bytes 5767172 | tf_op jit(solution)/shard_map/dot_general | solution.py:211
  72.4 1.5 copy-done.11
  73.9 1.3 convolution_convert_fusion
  75.3 1.3 add_convert_fusion.1
  76.5 1.5 collective-permute-start.17
  78.6 2.8 %collective-permute-start.14 = (bf16[2,512,128]{2,1,0:T(8,128)(2,1)S(1)}, bf16[2,512,128]{2,1,0:T(8,128)(2,1)}, u32[]{:S(2)}, u32[]{:S(2)}) collective-permute-start(bf16[2,512,128]{2,1,0:T(8,128)(2,1)S(1)} %pad_maximum_fusion.9.m0), channel_id=1, source_target_pairs={{6,0},{0,2},{2,4},{4,6},{7,1},{1,3},{3,5},{5,7},{14,8},{8,10},{10,... | collective-permute-start | bytes 786440 | tf_op jit(solution)/shard_map/ppermute | solution.py:34
  81.4 2.1 %add_convert_fusion.home0.home1 = bf16[1024,256]{1,0:T(8,128)(2,1)} fusion(bf16[1024,256]{1,0:T(8,128)(2,1)S(1)} %collective-permute-done.16, bf16[1024,2048]{1,0:T(8,128)(2,1)S(1)} %copy-done.9, bf16[4,2048,256]{2,1,0:T(8,128)(2,1)S(1)} %bitcast.148, s32[]{:T(128)S(6)} %select_n.206), kind=kOutput, calls=%fused_computation.83 | convolution fusion | flops 1074528256 | bytes 6291460 | tf_op jit(solution)/shard_map/dot_general | solution.py:211
  83.5 13.3 %collective-permute-done.12.m1 = bf16[2,512,128]{2,1,0:T(8,128)(2,1)S(1)} collective-permute-done((bf16[2,512,128]{2,1,0:T(8,128)(2,1)S(1)}, bf16[2,512,128]{2,1,0:T(8,128)(2,1)S(1)}, u32[]{:S(2)}, u32[]{:S(2)}) %collective-permute-start.12) | collective-permute-done | bytes 262176 | tf_op jit(solution)/shard_map/ppermute | solution.py:34
  96.8 5.6 %collective-permute-done.13.m2 = bf16[2,512,128]{2,1,0:T(8,128)(2,1)} collective-permute-done((bf16[2,512,128]{2,1,0:T(8,128)(2,1)S(1)}, bf16[2,512,128]{2,1,0:T(8,128)(2,1)}, u32[]{:S(2)}, u32[]{:S(2)}) %collective-permute-start.13) | collective-permute-done | bytes 262176 | tf_op jit(solution)/shard_map/ppermute | solution.py:34
  102.4 3.5 %collective-permute-done.14.m3 = bf16[2,512,128]{2,1,0:T(8,128)(2,1)} collective-permute-done((bf16[2,512,128]{2,1,0:T(8,128)(2,1)S(1)}, bf16[2,512,128]{2,1,0:T(8,128)(2,1)}, u32[]{:S(2)}, u32[]{:S(2)}) %collective-permute-start.14) | collective-permute-done | bytes 262176 | tf_op jit(solution)/shard_map/ppermute | solution.py:34
  107.8 1.4 pad_maximum_fusion.7
  109.2 1.0 copy.16.scale0.scale1
  110.3 0.7 copy-done.14
  111.1 9.2 %shard_map.73 = bf16[2,2,128,256]{3,2,1,0:T(8,128)(2,1)} custom-call(s32[12]{0:T(128)} %concatenate.44.scalars, bf16[1024,256]{1,0:T(8,128)(2,1)} %add_convert_fusion.home0.home1, bf16[1024,256]{1,0:T(8,128)(2,1)} %add_convert_fusion.home0.home1, bf16[1024,256]{1,0:T(8,128)(2,1)} %copy-done.12, bf16[1024,256]{1,0:T(8,128)(2,1)} %copy-done.12, ...), custom_call_target="tpu_custom_call" | custom-call | flops 2000000000 | bytes 4194304 | tf_op jit(solution)/shard_map/pallas_call | solution.py:127
  120.3 0.7 collective-permute-start.22
  121.1 6.7 %shard_map.74 = bf16[2,2,128,256]{3,2,1,0:T(8,128)(2,1)} custom-call(s32[12]{0:T(128)} %concatenate.44.scalars, bf16[1024,256]{1,0:T(8,128)(2,1)} %add_convert_fusion.home0.home1, bf16[1024,256]{1,0:T(8,128)(2,1)} %add_convert_fusion.home0.home1, bf16[1024,256]{1,0:T(8,128)(2,1)} %copy-done.12, bf16[1024,256]{1,0:T(8,128)(2,1)} %copy-done.12, ...), custom_call_target="tpu_custom_call" | custom-call | flops 2000000000 | bytes 4194304 | tf_op jit(solution)/shard_map/pallas_call | solution.py:127
  127.8 1.4 collective-permute-done.22
  130.1 0.7 collective-permute-done.26
  131.1 3.0 %fusion.12 = bf16[512,1024]{1,0:T(8,128)(2,1)S(1)} fusion(bf16[1024,2048]{1,0:T(8,128)(2,1)} %all-gather.5.cloned.1.call-done, bf16[512,256]{1,0:T(8,128)(2,1)S(1)} %get-tuple-element.72, bf16[512,256]{1,0:T(8,128)(2,1)S(1)} %get-tuple-element.73, bf16[512,256]{1,0:T(8,128)(2,1)S(1)} %get-tuple-element.74, bf16[512,256]{1,0:T(8,128)(2,1)S(1)} %get-tuple-element.71), kind=kOutput, calls=%fused_computation.12 | convolution fusion | flops 1078460416 | bytes 4194304 | tf_op jit(solution)/shard_map/dot_general | solution.py:269
  134.1 0.7 fusion.29
  134.9 0.7 fusion.26
  135.7 2.5 %collective-permute-done.24 = bf16[512,256]{1,0:T(8,128)(2,1)S(1)} collective-permute-done((bf16[512,256]{1,0:T(8,128)(2,1)}, bf16[512,256]{1,0:T(8,128)(2,1)S(1)}, u32[]{:S(2)}, u32[]{:S(2)}) %collective-permute-start.24) | collective-permute-done | bytes 262176 | tf_op jit(solution)/shard_map/ppermute | solution.py:34
  138.2 1.1 collective-permute-start.28
  139.3 2.0 %collective-permute-start.29 = (bf16[256,1024]{1,0:T(8,128)(2,1)S(1)}, bf16[256,1024]{1,0:T(8,128)(2,1)S(1)}, u32[]{:S(2)}, u32[]{:S(2)}) collective-permute-start(bf16[256,1024]{1,0:T(8,128)(2,1)S(1)} %fusion.29), channel_id=1, source_target_pairs={{8,0},{16,8},{24,16},{0,24},{9,1},{17,9},{25,17},{1,25},{10,2},{18... | collective-permute-start | bytes 1572872 | tf_op jit(solution)/shard_map/ppermute | solution.py:34
  141.4 1.2 collective-permute-start.33
  142.9 0.7 fusion.35
  143.6 0.8 collective-permute-start.30
  144.4 1.2 fusion.15
  145.8 2.6 %collective-permute-start.32 = (bf16[2,128,1024]{2,1,0:T(8,128)(2,1)S(1)}, bf16[2,128,1024]{2,1,0:T(8,128)(2,1)S(1)}, u32[]{:S(2)}, u32[]{:S(2)}) collective-permute-start(bf16[2,128,1024]{2,1,0:T(8,128)(2,1)S(1)} %pad_maximum_fusion.4), channel_id=1, source_target_pairs={{1,0},{0,1},{3,2},{2,3},{5,4},{4,5},{7,6},{6,7},{9,8},{8,9},{11,10... | collective-permute-start | bytes 1572872 | tf_op jit(solution)/shard_map/ppermute | solution.py:34
  148.4 6.0 %collective-permute-done.28 = bf16[256,1024]{1,0:T(8,128)(2,1)S(1)} collective-permute-done((bf16[256,1024]{1,0:T(8,128)(2,1)S(1)}, bf16[256,1024]{1,0:T(8,128)(2,1)S(1)}, u32[]{:S(2)}, u32[]{:S(2)}) %collective-permute-start.28) | collective-permute-done | bytes 524320 | tf_op jit(solution)/shard_map/ppermute | solution.py:34
  154.5 11.3 %collective-permute-done.29 = bf16[256,1024]{1,0:T(8,128)(2,1)S(1)} collective-permute-done((bf16[256,1024]{1,0:T(8,128)(2,1)S(1)}, bf16[256,1024]{1,0:T(8,128)(2,1)S(1)}, u32[]{:S(2)}, u32[]{:S(2)}) %collective-permute-start.29) | collective-permute-done | bytes 524320 | tf_op jit(solution)/shard_map/ppermute | solution.py:34
  165.7 0.9 fusion.47
  166.7 0.7 collective-permute-start.31
  167.5 1.9 collective-permute-start.34
  169.4 1.3 collective-permute-start.35
  170.9 0.8 collective-permute-start.36
  171.6 4.6 %collective-permute-done.31 = bf16[128,1024]{1,0:T(8,128)(2,1)S(1)} collective-permute-done((bf16[128,1024]{1,0:T(8,128)(2,1)S(1)}, bf16[128,1024]{1,0:T(8,128)(2,1)S(1)}, u32[]{:S(2)}, u32[]{:S(2)}) %collective-permute-start.31) | collective-permute-done | bytes 262176 | tf_op jit(solution)/shard_map/ppermute | solution.py:34
  176.2 2.1 %collective-permute-done.34 = bf16[128,1024]{1,0:T(8,128)(2,1)S(1)} collective-permute-done((bf16[128,1024]{1,0:T(8,128)(2,1)S(1)}, bf16[128,1024]{1,0:T(8,128)(2,1)S(1)}, u32[]{:S(2)}, u32[]{:S(2)}) %collective-permute-start.34) | collective-permute-done | bytes 262176 | tf_op jit(solution)/shard_map/ppermute | solution.py:34
  178.4 4.2 %collective-permute-done.35 = bf16[128,1024]{1,0:T(8,128)(2,1)S(1)} collective-permute-done((bf16[128,1024]{1,0:T(8,128)(2,1)S(1)}, bf16[128,1024]{1,0:T(8,128)(2,1)S(1)}, u32[]{:S(2)}, u32[]{:S(2)}) %collective-permute-start.35) | collective-permute-done | bytes 262176 | tf_op jit(solution)/shard_map/ppermute | solution.py:34
  182.8 0.8 pad_maximum_fusion.6
  (133 shorter events, 9.5 us)
Async XLA Ops:
  6.5 61.3 %all-gather.3.cloned.1.call-start = ((), (), s32[]{:S(2)}) async-start(), calls=%async_computation | async-start | bytes 5242880 | tf_op jit(solution)/shard_map/all_gather | solution.py:162
  7.3 123.8 %all-gather.5.cloned.1.call-start = ((), (), s32[]{:S(2)}) async-start(), calls=%async_computation.1 | async-start | bytes 5242880 | tf_op jit(solution)/shard_map/all_gather | solution.py:163
  7.3 15.5 %collective-permute-start = (bf16[128,2048]{1,0:T(8,128)(2,1)}, bf16[128,2048]{1,0:T(8,128)(2,1)S(1)}, u32[]{:S(2)}, u32[]{:S(2)}) collective-permute-start(bf16[128,2048]{1,0:T(8,128)(2,1)} %param.7), channel_id=1, source_target_pairs={{1,0},{0,1},{3,2},{2,3},{5,4},{4,5},{7,6},{6,7},{9,8},{8,9},{11,10... | collective-permute-start | bytes 1572872 | tf_op jit(solution)/shard_map/ppermute | solution.py:34
  10.4 19.2 %collective-permute-start.2 = (bf16[128,2048]{1,0:T(8,128)(2,1)}, bf16[128,2048]{1,0:T(8,128)(2,1)S(1)}, u32[]{:S(2)}, u32[]{:S(2)}) collective-permute-start(bf16[128,2048]{1,0:T(8,128)(2,1)} %param.7), channel_id=1, source_target_pairs={{16,0},{24,8},{0,16},{8,24},{17,1},{25,9},{1,17},{9,25},{18,2},{26... | collective-permute-start | bytes 1572872 | tf_op jit(solution)/shard_map/ppermute | solution.py:34
  13.6 25.0 %collective-permute-start.1 = (bf16[128,2048]{1,0:T(8,128)(2,1)}, bf16[128,2048]{1,0:T(8,128)(2,1)S(1)}, u32[]{:S(2)}, u32[]{:S(2)}) collective-permute-start(bf16[128,2048]{1,0:T(8,128)(2,1)} %param.7), channel_id=1, source_target_pairs={{8,0},{16,8},{24,16},{0,24},{9,1},{17,9},{25,17},{1,25},{10,2},{18... | collective-permute-start | bytes 1572872 | tf_op jit(solution)/shard_map/ppermute | solution.py:34
  14.7 24.4 %collective-permute-start.3 = (bf16[128,2048]{1,0:T(8,128)(2,1)}, bf16[128,2048]{1,0:T(8,128)(2,1)S(1)}, u32[]{:S(2)}, u32[]{:S(2)}) collective-permute-start(bf16[128,2048]{1,0:T(8,128)(2,1)} %param.7), channel_id=1, source_target_pairs={{24,0},{0,8},{8,16},{16,24},{25,1},{1,9},{9,17},{17,25},{26,2},{2,... | collective-permute-start | bytes 1572872 | tf_op jit(solution)/shard_map/ppermute | solution.py:34
  22.8 25.6 %collective-permute-start.4 = (bf16[128,2048]{1,0:T(8,128)(2,1)S(1)}, bf16[128,2048]{1,0:T(8,128)(2,1)S(1)}, u32[]{:S(2)}, u32[]{:S(2)}) collective-permute-start(bf16[128,2048]{1,0:T(8,128)(2,1)S(1)} %collective-permute-done), channel_id=1, source_target_pairs={{8,0},{16,8},{24,16},{0,24},{9,1},{17,9},{25,17},{1,25},{10,2},{18... | collective-permute-start | bytes 1572872 | tf_op jit(solution)/shard_map/ppermute | solution.py:34
  25.8 22.8 %collective-permute-start.6 = (bf16[128,2048]{1,0:T(8,128)(2,1)S(1)}, bf16[128,2048]{1,0:T(8,128)(2,1)S(1)}, u32[]{:S(2)}, u32[]{:S(2)}) collective-permute-start(bf16[128,2048]{1,0:T(8,128)(2,1)S(1)} %collective-permute-done), channel_id=1, source_target_pairs={{24,0},{0,8},{8,16},{16,24},{25,1},{1,9},{9,17},{17,25},{26,2},{2,... | collective-permute-start | bytes 1572872 | tf_op jit(solution)/shard_map/ppermute | solution.py:34
  27.7 10.8 %copy-start.2 = (f32[2048]{0:T(1024)S(1)}, f32[2048]{0:T(1024)}, u32[]{:S(2)}) copy-start(f32[2048]{0:T(1024)} %param.8) | copy-start | bytes 24580
  27.8 10.8 %copy-start.6 = (bf16[1024,2048]{1,0:T(8,128)(2,1)S(1)}, bf16[1024,2048]{1,0:T(8,128)(2,1)}, u32[]{:S(2)}) copy-start(bf16[1024,2048]{1,0:T(8,128)(2,1)} %fusion.114) | copy-start | bytes 12582916
  29.7 18.8 %collective-permute-start.5 = (bf16[128,2048]{1,0:T(8,128)(2,1)S(1)}, bf16[128,2048]{1,0:T(8,128)(2,1)S(1)}, u32[]{:S(2)}, u32[]{:S(2)}) collective-permute-start(bf16[128,2048]{1,0:T(8,128)(2,1)S(1)} %collective-permute-done.2), channel_id=1, source_target_pairs={{1,0},{0,1},{3,2},{2,3},{5,4},{4,5},{7,6},{6,7},{9,8},{8,9},{11,10... | collective-permute-start | bytes 1572872 | tf_op jit(solution)/shard_map/ppermute | solution.py:34
  34.2 14.5 %copy-start.1 = (bf16[2048,256]{1,0:T(8,128)(2,1)}, bf16[2048,256]{1,0:T(8,128)(2,1)S(1)}, u32[]{:S(2)}) copy-start(bf16[2048,256]{1,0:T(8,128)(2,1)S(1)} %pad_maximum_fusion.1) | copy-start | bytes 3145732
  48.7 2.5 %copy-start.7 = (bf16[1024,2048]{1,0:T(8,128)(2,1)}, bf16[1024,2048]{1,0:T(8,128)(2,1)S(1)}, u32[]{:S(2)}) copy-start(bf16[1024,2048]{1,0:T(8,128)(2,1)S(1)} %fusion.107) | copy-start | bytes 12582916
  50.6 3.1 %collective-permute-start.7 = (bf16[512,256]{1,0:T(8,128)(2,1)}, bf16[512,256]{1,0:T(8,128)(2,1)S(1)}, u32[]{:S(2)}, u32[]{:S(2)}) collective-permute-start(bf16[512,256]{1,0:T(8,128)(2,1)} %fusion.71), channel_id=1, source_target_pairs={{32,0},{0,32},{33,1},{1,33},{34,2},{2,34},{35,3},{3,35},{36,4},{4,... | collective-permute-start | bytes 786440 | tf_op jit(solution)/shard_map/ppermute | solution.py:34
  51.0 6.0 %copy-start = (bf16[2048,256]{1,0:T(8,128)(2,1)S(1)}, bf16[2048,256]{1,0:T(8,128)(2,1)}, u32[]{:S(2)}) copy-start(bf16[2048,256]{1,0:T(8,128)(2,1)} %pad_maximum_fusion) | copy-start | bytes 3145732
  51.2 5.8 %copy-start.8 = (bf16[1024,2048]{1,0:T(8,128)(2,1)S(1)}, bf16[1024,2048]{1,0:T(8,128)(2,1)}, u32[]{:S(2)}) copy-start(bf16[1024,2048]{1,0:T(8,128)(2,1)} %copy-done.7) | copy-start | bytes 12582916
  51.2 2.5 %collective-permute-start.8 = (f32[8,128]{1,0:T(8,128)S(1)}, f32[8,128]{1,0:T(8,128)S(1)}, u32[]{:S(2)}, u32[]{:S(2)}) collective-permute-start(f32[8,128]{1,0:T(8,128)S(1)} %stack.75), channel_id=1, source_target_pairs={{32,0},{0,32},{33,1},{1,33},{34,2},{2,34},{35,3},{3,35},{36,4},{4,... | collective-permute-start | bytes 12296 | tf_op jit(solution)/shard_map/ppermute | solution.py:34
  56.3 3.7 %collective-permute-start.11 = (f32[8,128]{1,0:T(8,128)S(1)}, f32[8,128]{1,0:T(8,128)S(1)}, u32[]{:S(2)}, u32[]{:S(2)}) collective-permute-start(f32[8,128]{1,0:T(8,128)S(1)} %add.156), channel_id=1, source_target_pairs={{64,0},{0,64},{65,1},{1,65},{66,2},{2,66},{67,3},{3,67},{68,4},{4,... | collective-permute-start | bytes 12296 | tf_op jit(solution)/shard_map/ppermute | solution.py:34
  57.7 2.3 %collective-permute-start.9 = (bf16[512,256]{1,0:T(8,128)(2,1)S(1)}, bf16[512,256]{1,0:T(8,128)(2,1)S(1)}, u32[]{:S(2)}, u32[]{:S(2)}) collective-permute-start(bf16[512,256]{1,0:T(8,128)(2,1)S(1)} %fusion.74), channel_id=1, source_target_pairs={{32,0},{0,32},{33,1},{1,33},{34,2},{2,34},{35,3},{3,35},{36,4},{4,... | collective-permute-start | bytes 786440 | tf_op jit(solution)/shard_map/ppermute | solution.py:34
  57.8 8.7 %collective-permute-start.10 = (bf16[512,256]{1,0:T(8,128)(2,1)S(1)}, bf16[512,256]{1,0:T(8,128)(2,1)S(1)}, u32[]{:S(2)}, u32[]{:S(2)}) collective-permute-start(bf16[512,256]{1,0:T(8,128)(2,1)S(1)} %fusion.68), channel_id=1, source_target_pairs={{64,0},{0,64},{65,1},{1,65},{66,2},{2,66},{67,3},{3,67},{68,4},{4,... | collective-permute-start | bytes 786440 | tf_op jit(solution)/shard_map/ppermute | solution.py:34
  67.8 13.6 %copy-start.5 = (bf16[2,512,128]{2,1,0:T(8,128)(2,1)}, bf16[2,512,128]{2,1,0:T(8,128)(2,1)S(1)}, u32[]{:S(2)}) copy-start(bf16[2,512,128]{2,1,0:T(8,128)(2,1)S(1)} %pad_maximum_fusion.9.m0) | copy-start | bytes 786436
  67.8 4.6 %copy-start.9 = (bf16[1024,2048]{1,0:T(8,128)(2,1)S(1)}, bf16[1024,2048]{1,0:T(8,128)(2,1)}, u32[]{:S(2)}) copy-start(bf16[1024,2048]{1,0:T(8,128)(2,1)} %copy-done.7) | copy-start | bytes 12582916
  67.8 6.1 %copy-start.11 = (bf16[8192,256]{1,0:T(8,128)(2,1)S(1)}, bf16[8192,256]{1,0:T(8,128)(2,1)}, u32[]{:S(2)}) copy-start(bf16[8192,256]{1,0:T(8,128)(2,1)} %all-gather.3.cloned.1.call-done) | copy-start | bytes 12582916
  72.1 3.2 %collective-permute-start.15 = (bf16[1024,256]{1,0:T(8,128)(2,1)S(1)}, bf16[1024,256]{1,0:T(8,128)(2,1)S(1)}, u32[]{:S(2)}, u32[]{:S(2)}) collective-permute-start(bf16[1024,256]{1,0:T(8,128)(2,1)S(1)} %convolution_convert_fusion.1), channel_id=1, source_target_pairs={{32,0},{0,32},{33,1},{1,33},{34,2},{2,34},{35,3},{3,35},{36,4},{4,... | collective-permute-start | bytes 1572872 | tf_op jit(solution)/shard_map/ppermute | solution.py:34
  75.2 6.2 %collective-permute-start.16 = (bf16[1024,256]{1,0:T(8,128)(2,1)S(1)}, bf16[1024,256]{1,0:T(8,128)(2,1)S(1)}, u32[]{:S(2)}, u32[]{:S(2)}) collective-permute-start(bf16[1024,256]{1,0:T(8,128)(2,1)S(1)} %convolution_convert_fusion), channel_id=1, source_target_pairs={{32,0},{0,32},{33,1},{1,33},{34,2},{2,34},{35,3},{3,35},{36,4},{4,... | collective-permute-start | bytes 1572872 | tf_op jit(solution)/shard_map/ppermute | solution.py:34
  76.5 29.4 %collective-permute-start.17 = (bf16[1024,256]{1,0:T(8,128)(2,1)S(1)}, bf16[1024,256]{1,0:T(8,128)(2,1)S(1)}, u32[]{:S(2)}, u32[]{:S(2)}) collective-permute-start(bf16[1024,256]{1,0:T(8,128)(2,1)S(1)} %add_convert_fusion.1), channel_id=1, source_target_pairs={{64,0},{0,64},{65,1},{1,65},{66,2},{2,66},{67,3},{3,67},{68,4},{4,... | collective-permute-start | bytes 1572872 | tf_op jit(solution)/shard_map/ppermute | solution.py:34
  78.1 18.7 %collective-permute-start.12 = (bf16[2,512,128]{2,1,0:T(8,128)(2,1)S(1)}, bf16[2,512,128]{2,1,0:T(8,128)(2,1)S(1)}, u32[]{:S(2)}, u32[]{:S(2)}) collective-permute-start(bf16[2,512,128]{2,1,0:T(8,128)(2,1)S(1)} %pad_maximum_fusion.9.m0), channel_id=1, source_target_pairs={{2,0},{4,2},{6,4},{0,6},{3,1},{5,3},{7,5},{1,7},{10,8},{12,10},{14... | collective-permute-start | bytes 786440 | tf_op jit(solution)/shard_map/ppermute | solution.py:34
  78.4 24.0 %collective-permute-start.13 = (bf16[2,512,128]{2,1,0:T(8,128)(2,1)S(1)}, bf16[2,512,128]{2,1,0:T(8,128)(2,1)}, u32[]{:S(2)}, u32[]{:S(2)}) collective-permute-start(bf16[2,512,128]{2,1,0:T(8,128)(2,1)S(1)} %pad_maximum_fusion.9.m0), channel_id=1, source_target_pairs={{4,0},{6,2},{0,4},{2,6},{5,1},{7,3},{1,5},{3,7},{12,8},{14,10},{8,... | collective-permute-start | bytes 786440 | tf_op jit(solution)/shard_map/ppermute | solution.py:34
  78.6 27.4 %collective-permute-start.14 = (bf16[2,512,128]{2,1,0:T(8,128)(2,1)S(1)}, bf16[2,512,128]{2,1,0:T(8,128)(2,1)}, u32[]{:S(2)}, u32[]{:S(2)}) collective-permute-start(bf16[2,512,128]{2,1,0:T(8,128)(2,1)S(1)} %pad_maximum_fusion.9.m0), channel_id=1, source_target_pairs={{6,0},{0,2},{2,4},{4,6},{7,1},{1,3},{3,5},{5,7},{14,8},{8,10},{10,... | collective-permute-start | bytes 786440 | tf_op jit(solution)/shard_map/ppermute | solution.py:34
  81.4 28.8 %collective-permute-start.18 = (bf16[2,512,128]{2,1,0:T(8,128)(2,1)S(1)}, bf16[2,512,128]{2,1,0:T(8,128)(2,1)}, u32[]{:S(2)}, u32[]{:S(2)}) collective-permute-start(bf16[2,512,128]{2,1,0:T(8,128)(2,1)S(1)} %pad_maximum_fusion.9.m0), channel_id=1, source_target_pairs={{32,0},{0,32},{33,1},{1,33},{34,2},{2,34},{35,3},{3,35},{36,4},{4,... | collective-permute-start | bytes 786440 | tf_op jit(solution)/shard_map/ppermute | solution.py:34
  96.8 13.4 %copy-start.13 = (bf16[2,512,128]{2,1,0:T(8,128)(2,1)}, bf16[2,512,128]{2,1,0:T(8,128)(2,1)S(1)}, u32[]{:S(2)}) copy-start(bf16[2,512,128]{2,1,0:T(8,128)(2,1)S(1)} %collective-permute-done.12.m1) | copy-start | bytes 786436
  106.0 4.3 %copy-start.12 = (bf16[1024,256]{1,0:T(8,128)(2,1)}, bf16[1024,256]{1,0:T(8,128)(2,1)S(1)}, u32[]{:S(2)}) copy-start(bf16[1024,256]{1,0:T(8,128)(2,1)S(1)} %collective-permute-done.17.far0.far1) | copy-start | bytes 1572868
  106.0 4.2 %collective-permute-start.19 = (bf16[2,512,128]{2,1,0:T(8,128)(2,1)S(1)}, bf16[2,512,128]{2,1,0:T(8,128)(2,1)S(1)}, u32[]{:S(2)}, u32[]{:S(2)}) collective-permute-start(bf16[2,512,128]{2,1,0:T(8,128)(2,1)S(1)} %collective-permute-done.12.m1), channel_id=1, source_target_pairs={{32,0},{0,32},{33,1},{1,33},{34,2},{2,34},{35,3},{3,35},{36,4},{4,... | collective-permute-start | bytes 786440 | tf_op jit(solution)/shard_map/ppermute | solution.py:34
  106.0 4.2 %collective-permute-start.20 = (bf16[2,512,128]{2,1,0:T(8,128)(2,1)}, bf16[2,512,128]{2,1,0:T(8,128)(2,1)S(1)}, u32[]{:S(2)}, u32[]{:S(2)}) collective-permute-start(bf16[2,512,128]{2,1,0:T(8,128)(2,1)} %collective-permute-done.13.m2), channel_id=1, source_target_pairs={{32,0},{0,32},{33,1},{1,33},{34,2},{2,34},{35,3},{3,35},{36,4},{4,... | collective-permute-start | bytes 786440 | tf_op jit(solution)/shard_map/ppermute | solution.py:34
  106.5 3.8 %collective-permute-start.21 = (bf16[2,512,128]{2,1,0:T(8,128)(2,1)}, bf16[2,512,128]{2,1,0:T(8,128)(2,1)}, u32[]{:S(2)}, u32[]{:S(2)}) collective-permute-start(bf16[2,512,128]{2,1,0:T(8,128)(2,1)} %collective-permute-done.14.m3), channel_id=1, source_target_pairs={{32,0},{0,32},{33,1},{1,33},{34,2},{2,34},{35,3},{3,35},{36,4},{4,... | collective-permute-start | bytes 786440 | tf_op jit(solution)/shard_map/ppermute | solution.py:34
  110.2 0.7 copy-start.14
  110.2 0.8 copy-start.15
  120.3 10.5 %copy-start.4 = (bf16[2,2,128,256]{3,2,1,0:T(8,128)(2,1)S(1)}, bf16[2,2,128,256]{3,2,1,0:T(8,128)(2,1)}, u32[]{:S(2)}) copy-start(bf16[2,2,128,256]{3,2,1,0:T(8,128)(2,1)} %shard_map.73) | copy-start | bytes 786436
  120.3 8.9 %collective-permute-start.22 = (bf16[512,256]{1,0:T(8,128)(2,1)}, bf16[512,256]{1,0:T(8,128)(2,1)S(1)}, u32[]{:S(2)}, u32[]{:S(2)}) collective-permute-start(bf16[512,256]{1,0:T(8,128)(2,1)} %bitcast.128), channel_id=1, source_target_pairs={{64,0},{0,64},{65,1},{1,65},{66,2},{2,66},{67,3},{3,67},{68,4},{4,... | collective-permute-start | bytes 786440 | tf_op jit(solution)/shard_map/ppermute | solution.py:34
  121.0 9.1 %collective-permute-start.25 = (bf16[512,256]{1,0:T(8,128)(2,1)}, bf16[512,256]{1,0:T(8,128)(2,1)S(1)}, u32[]{:S(2)}, u32[]{:S(2)}) collective-permute-start(bf16[512,256]{1,0:T(8,128)(2,1)} %bitcast.129), channel_id=1, source_target_pairs={{32,0},{0,32},{33,1},{1,33},{34,2},{2,34},{35,3},{3,35},{36,4},{4,... | collective-permute-start | bytes 786440 | tf_op jit(solution)/shard_map/ppermute | solution.py:34
  129.2 1.5 collective-permute-start.26
  129.2 8.9 %collective-permute-start.24 = (bf16[512,256]{1,0:T(8,128)(2,1)}, bf16[512,256]{1,0:T(8,128)(2,1)S(1)}, u32[]{:S(2)}, u32[]{:S(2)}) collective-permute-start(bf16[512,256]{1,0:T(8,128)(2,1)} %bitcast.126), channel_id=1, source_target_pairs={{64,0},{0,64},{65,1},{1,65},{66,2},{2,66},{67,3},{3,67},{68,4},{4,... | collective-permute-start | bytes 786440 | tf_op jit(solution)/shard_map/ppermute | solution.py:34
  129.8 12.8 %collective-permute-start.23 = (bf16[512,256]{1,0:T(8,128)(2,1)}, bf16[512,256]{1,0:T(8,128)(2,1)S(1)}, u32[]{:S(2)}, u32[]{:S(2)}) collective-permute-start(bf16[512,256]{1,0:T(8,128)(2,1)} %bitcast.127), channel_id=1, source_target_pairs={{32,0},{0,32},{33,1},{1,33},{34,2},{2,34},{35,3},{3,35},{36,4},{4,... | collective-permute-start | bytes 786440 | tf_op jit(solution)/shard_map/ppermute | solution.py:34
  131.1 3.0 %copy-start.10 = (bf16[1024,2048]{1,0:T(8,128)(2,1)S(1)}, bf16[1024,2048]{1,0:T(8,128)(2,1)}, u32[]{:S(2)}) copy-start(bf16[1024,2048]{1,0:T(8,128)(2,1)} %all-gather.5.cloned.1.call-done) | copy-start | bytes 12582916
  134.8 7.8 %copy-start.3 = (bf16[2,2,128,256]{3,2,1,0:T(8,128)(2,1)S(1)}, bf16[2,2,128,256]{3,2,1,0:T(8,128)(2,1)}, u32[]{:S(2)}) copy-start(bf16[2,2,128,256]{3,2,1,0:T(8,128)(2,1)} %shard_map.74) | copy-start | bytes 786436
  138.2 4.4 %collective-permute-start.27 = (bf16[512,256]{1,0:T(8,128)(2,1)S(1)}, bf16[512,256]{1,0:T(8,128)(2,1)S(1)}, u32[]{:S(2)}, u32[]{:S(2)}) collective-permute-start(bf16[512,256]{1,0:T(8,128)(2,1)S(1)} %collective-permute-done.24), channel_id=1, source_target_pairs={{32,0},{0,32},{33,1},{1,33},{34,2},{2,34},{35,3},{3,35},{36,4},{4,... | collective-permute-start | bytes 786440 | tf_op jit(solution)/shard_map/ppermute | solution.py:34
  138.2 16.3 %collective-permute-start.28 = (bf16[256,1024]{1,0:T(8,128)(2,1)S(1)}, bf16[256,1024]{1,0:T(8,128)(2,1)S(1)}, u32[]{:S(2)}, u32[]{:S(2)}) collective-permute-start(bf16[256,1024]{1,0:T(8,128)(2,1)S(1)} %fusion.26), channel_id=1, source_target_pairs={{16,0},{24,8},{0,16},{8,24},{17,1},{25,9},{1,17},{9,25},{18,2},{26... | collective-permute-start | bytes 1572872 | tf_op jit(solution)/shard_map/ppermute | solution.py:34
  139.3 26.4 %collective-permute-start.29 = (bf16[256,1024]{1,0:T(8,128)(2,1)S(1)}, bf16[256,1024]{1,0:T(8,128)(2,1)S(1)}, u32[]{:S(2)}, u32[]{:S(2)}) collective-permute-start(bf16[256,1024]{1,0:T(8,128)(2,1)S(1)} %fusion.29), channel_id=1, source_target_pairs={{8,0},{16,8},{24,16},{0,24},{9,1},{17,9},{25,17},{1,25},{10,2},{18... | collective-permute-start | bytes 1572872 | tf_op jit(solution)/shard_map/ppermute | solution.py:34
  141.4 26.0 %collective-permute-start.33 = (bf16[2,128,1024]{2,1,0:T(8,128)(2,1)S(1)}, bf16[2,128,1024]{2,1,0:T(8,128)(2,1)S(1)}, u32[]{:S(2)}, u32[]{:S(2)}) collective-permute-start(bf16[2,128,1024]{2,1,0:T(8,128)(2,1)S(1)} %pad_maximum_fusion.5), channel_id=1, source_target_pairs={{1,0},{0,1},{3,2},{2,3},{5,4},{4,5},{7,6},{6,7},{9,8},{8,9},{11,10... | collective-permute-start | bytes 1572872 | tf_op jit(solution)/shard_map/ppermute | solution.py:34
  143.6 22.1 %collective-permute-start.30 = (bf16[256,1024]{1,0:T(8,128)(2,1)S(1)}, bf16[256,1024]{1,0:T(8,128)(2,1)S(1)}, u32[]{:S(2)}, u32[]{:S(2)}) collective-permute-start(bf16[256,1024]{1,0:T(8,128)(2,1)S(1)} %fusion.35), channel_id=1, source_target_pairs={{24,0},{0,8},{8,16},{16,24},{25,1},{1,9},{9,17},{17,25},{26,2},{2,... | collective-permute-start | bytes 1572872 | tf_op jit(solution)/shard_map/ppermute | solution.py:34
  145.8 25.0 %collective-permute-start.32 = (bf16[2,128,1024]{2,1,0:T(8,128)(2,1)S(1)}, bf16[2,128,1024]{2,1,0:T(8,128)(2,1)S(1)}, u32[]{:S(2)}, u32[]{:S(2)}) collective-permute-start(bf16[2,128,1024]{2,1,0:T(8,128)(2,1)S(1)} %pad_maximum_fusion.4), channel_id=1, source_target_pairs={{1,0},{0,1},{3,2},{2,3},{5,4},{4,5},{7,6},{6,7},{9,8},{8,9},{11,10... | collective-permute-start | bytes 1572872 | tf_op jit(solution)/shard_map/ppermute | solution.py:34
  166.7 9.5 %collective-permute-start.31 = (bf16[128,1024]{1,0:T(8,128)(2,1)S(1)}, bf16[128,1024]{1,0:T(8,128)(2,1)S(1)}, u32[]{:S(2)}, u32[]{:S(2)}) collective-permute-start(bf16[128,1024]{1,0:T(8,128)(2,1)S(1)} %slice.218), channel_id=1, source_target_pairs={{1,0},{0,1},{3,2},{2,3},{5,4},{4,5},{7,6},{6,7},{9,8},{8,9},{11,10... | collective-permute-start | bytes 786440 | tf_op jit(solution)/shard_map/ppermute | solution.py:34
  167.5 10.8 %collective-permute-start.34 = (bf16[128,1024]{1,0:T(8,128)(2,1)S(1)}, bf16[128,1024]{1,0:T(8,128)(2,1)S(1)}, u32[]{:S(2)}, u32[]{:S(2)}) collective-permute-start(bf16[128,1024]{1,0:T(8,128)(2,1)S(1)} %get-tuple-element.75), channel_id=1, source_target_pairs={{16,0},{24,8},{0,16},{8,24},{17,1},{25,9},{1,17},{9,25},{18,2},{26... | collective-permute-start | bytes 786440 | tf_op jit(solution)/shard_map/ppermute | solution.py:34
  169.4 13.2 %collective-permute-start.35 = (bf16[128,1024]{1,0:T(8,128)(2,1)S(1)}, bf16[128,1024]{1,0:T(8,128)(2,1)S(1)}, u32[]{:S(2)}, u32[]{:S(2)}) collective-permute-start(bf16[128,1024]{1,0:T(8,128)(2,1)S(1)} %get-tuple-element.76), channel_id=1, source_target_pairs={{8,0},{16,8},{24,16},{0,24},{9,1},{17,9},{25,17},{1,25},{10,2},{18... | collective-permute-start | bytes 786440 | tf_op jit(solution)/shard_map/ppermute | solution.py:34
  170.9 11.7 %collective-permute-start.36 = (bf16[128,1024]{1,0:T(8,128)(2,1)S(1)}, bf16[128,1024]{1,0:T(8,128)(2,1)S(1)}, u32[]{:S(2)}, u32[]{:S(2)}) collective-permute-start(bf16[128,1024]{1,0:T(8,128)(2,1)S(1)} %fusion.120), channel_id=1, source_target_pairs={{24,0},{0,8},{8,16},{16,24},{25,1},{1,9},{9,17},{17,25},{26,2},{2,... | collective-permute-start | bytes 786440 | tf_op jit(solution)/shard_map/ppermute | solution.py:34
Sparse Core Ops, SparseCore 0:
  9.0 47.6 all-gather.2
  58.3 59.8 all-gather.4

commit v5 on v4

--- a/solution.py
+++ b/solution.py
@@ -199,9 +199,13 @@
 
     kv_weights = barrier([kv_weight(0), kv_weight(1)])
     gain = norm_gain[None, :]
+    early = [x[dy, dx].astype(f32) for dx, dy in ((0, 0), (0, 1), (0, 2), (0, 3), (1, 0))]
+    early = [jnp.sum(piece * piece, axis=1) for piece in early]
+    x[1, 1], x[2, 1], x[3, 1], early = barrier((x[1, 1], x[2, 1], x[3, 1], early))
     pieces = [x[dy, dx].astype(f32) for dx in (0, 1) for dy in range(4)]
     rows = jnp.concatenate([(piece * gain).astype(bf16) for piece in pieces], axis=0)
-    squares = jnp.stack([jnp.sum(piece * piece, axis=1) for piece in pieces])
+    squares = early + [jnp.sum(piece * piece, axis=1) for piece in pieces[5:]]
+    squares = jnp.stack(squares)
     squares = squares + receive(squares, "c", 1)
 
     def half(rows, core):
@@ -218,6 +222,12 @@
     kv_far = receive(across, "xl", 1)
     kv_home = (product(half(rows, c), kv_weights[0]) + got.astype(f32)).astype(bf16)
     squares = squares + receive(squares, "xl", 1)
+    def query_weight(core, across):
+        return lax.dynamic_index_in_dim(weights, (xl ^ across) * 2 + core, 0, keepdims=False)
+
+    weights = weights.reshape(4, w_query.shape[0], w_query.shape[1])
+    away = [product(rows, query_weight(1 - c, across)).astype(bf16) for across in (1, 0)]
+    kv_far, away = barrier((kv_far, away))
     scale = lax.rsqrt(squares.reshape(GROUP_ROWS, 1) / MODEL_WIDTH + norm_eps)
     total = (kv_home.astype(f32) + kv_far.astype(f32)) * half(scale, c)
     key, value = total[:, :HEAD_SIZE], total[:, HEAD_SIZE:]
@@ -225,21 +235,16 @@
     cos_half, sin_half = (lax.dynamic_index_in_dim(t, c, 0, keepdims=False) for t in (cosine, sine))
     key = key * cos_half + swapped_key * sin_half
     kv = jnp.stack([key.astype(bf16), value.astype(bf16)])
-    rows, kv = barrier((rows, kv))
     mine = [kv] + [receive(kv, "z", step) for step in (1, 2, 3)]
 
-    weights = weights.reshape(4, w_query.shape[0], w_query.shape[1])
-
-    def query_weight(core, across):
-        return lax.dynamic_index_in_dim(weights, (xl ^ across) * 2 + core, 0, keepdims=False)
-
-    got_across = receive(product(rows, query_weight(1 - c, 1)).astype(bf16), "c", 1)
-    got = receive(product(rows, query_weight(1 - c, 0)).astype(bf16), "c", 1)
+    got_across, got = (receive(part, "c", 1) for part in away)
     across = (product(rows, query_weight(c, 1)) + got_across.astype(f32)).astype(bf16)
     rows, across = barrier((rows, across))
     q_far = receive(across, "xl", 1)
     q_home = (product(rows, query_weight(c, 0)) + got.astype(f32)).astype(bf16)
-    mine[1:], q_home, q_far = barrier((mine[1:], q_home, q_far))
+    mine[1:], q_home, q_far, scalars, bounds, scale, cosine, sine = barrier(
+        (mine[1:], q_home, q_far, scalars, bounds, scale, cosine, sine)
+    )
     theirs = [receive(part, "c", 1) for part in mine]
 
     def all_heads(mixed, before):
@@ -273,20 +278,20 @@
             y_first[dy] = jnp.dot(
                 heads[i * TILE : (i + 1) * TILE], w_out[:, :columns], preferred_element_type=f32
             ).astype(bf16)
-    xh_first = {}
-    for tiles in groups:
+    def over_y(parts, dy):
+        return receive(parts[dy], "y", -dy).astype(f32)
+
+    xh_first, arrived = {}, {}
+    for step, tiles in enumerate(groups):
         got = receive(jnp.stack([seconds[dy][1] for dy in tiles]), "xh", 1)
+        if step == 1:
+            got, arrived = barrier((got, arrived))
         for i, dy in enumerate(tiles):
             xh_first[dy] = (seconds[dy][0].astype(f32) + got[i].astype(f32)).astype(bf16)
-
-    def sum_over_y(parts):
-        total = parts[0].astype(f32)
-        for dy in (2, 3, 1):
-            total = total + receive(parts[dy], "y", -dy).astype(f32)
-        return total
-
-    first = sum_over_y(y_first)
-    second = sum_over_y(xh_first)
+            arrived[dy] = over_y(xh_first, dy) if dy else xh_first[0].astype(f32)
+
+    first = y_first[0].astype(f32) + over_y(y_first, 2) + over_y(y_first, 3) + over_y(y_first, 1)
+    second = arrived[0] + arrived[1] + arrived[2] + arrived[3]
     first = first[:128] + receive(first[128:].astype(bf16), "xh", 1).astype(f32)
     return jnp.concatenate([first, second], axis=1).astype(bf16)
 

time: 192 us -> 185 us (0.964)
  waiting for transfers between devices: 80.3 us -> 64.4 us
  other arithmetic: 14 us -> 21.3 us
  starting transfers between devices: 37.2 us -> 40.6 us
    ppermute x37, waiting for transfers between devices: 79.5 us -> 63.6 us  [receive(): return lax.ppermute(value, axis, [((i + step) % n, i) for i in range(n)])]
    ppermute x37, starting transfers between devices: 37.1 us -> 40.5 us  [receive(): return lax.ppermute(value, axis, [((i + step) % n, i) for i in range(n)])]
    reduce_sum x8 -> x7, other arithmetic: 2.54 us -> 5.62 us  [the longest x5 4.07 us: shards(): early = [jnp.sum(piece * piece, axis=1) for piece in early]]
    unnamed x8, other arithmetic: 2.66 us -> 4.7 us
  transfers between devices with their start and end apart: 39 -> 39, of which waited for: 16 -> 17; matrix products, arithmetic and copies ran while one was open for 21% -> 26% of each run, Pallas kernels for 8% -> 8%
where the time goes in v5:
time: 185 us; the launch traced here: 184 us
  waiting for transfers between devices  64.4 us (35%)
  starting transfers between devices  40.6 us (22%)
  matrix products  23 us (12%)
  other arithmetic  21.3 us (12%)
  Pallas kernels  15.4 us (8%)
  between operations  14.1 us (8%)
  local copies, waits for them, and re-layouts  5.71 us (3%)
    ppermute x37, waiting for transfers between devices, receive(): return lax.ppermute(value, axis, [((i + step) % n, i) for i in range(n)])  63.6 us
    ppermute x37, starting transfers between devices, receive(): return lax.ppermute(value, axis, [((i + step) % n, i) for i in range(n)])  40.5 us
    dot_general x8, matrix products, product(): return jnp.dot(rows, weight, preferred_element_type=f32)  15.7 us
    pallas_call x2, Pallas kernels, attention(): pl.pallas_call(functools.partial(attention_kernel, tiles), grid=(len(tile...  15.4 us
    unnamed x8, other arithmetic  4.7 us
    dot_general x2, matrix products, shards(): jnp.dot(heads, w_out[:, columns:], preferred_element_type=f32).astype(bf16)  4.24 us
    reduce_sum x5, other arithmetic, shards(): early = [jnp.sum(piece * piece, axis=1) for piece in early]  4.07 us
  transfers between devices with their start and end apart: 39, of which 17 were waited for; matrix products, arithmetic and copies ran while one was open for 26% of the time, Pallas kernels for 8%

profile of v5, /device:TPU:96, one launch (start us, length us, event | category | flops | bytes accessed | tf_op | source)
XLA Modules:
  0.0 184.4 jit_solution(12230252782234388674)
XLA Ops:
  6.5 0.7 all-gather.3.cloned.1.call-update
  7.3 3.1 %collective-permute-start.3 = (bf16[128,2048]{1,0:T(8,128)(2,1)}, bf16[128,2048]{1,0:T(8,128)(2,1)S(1)}, u32[]{:S(2)}, u32[]{:S(2)}) collective-permute-start(bf16[128,2048]{1,0:T(8,128)(2,1)} %param.7), channel_id=1, source_target_pairs={{1,0},{0,1},{3,2},{2,3},{5,4},{4,5},{7,6},{6,7},{9,8},{8,9},{11,10... | collective-permute-start | bytes 1572872 | tf_op jit(solution)/shard_map/ppermute | solution.py:34
  10.4 3.2 %collective-permute-start.1 = (bf16[128,2048]{1,0:T(8,128)(2,1)}, bf16[128,2048]{1,0:T(8,128)(2,1)S(1)}, u32[]{:S(2)}, u32[]{:S(2)}) collective-permute-start(bf16[128,2048]{1,0:T(8,128)(2,1)} %param.7), channel_id=1, source_target_pairs={{16,0},{24,8},{0,16},{8,24},{17,1},{25,9},{1,17},{9,25},{18,2},{26... | collective-permute-start | bytes 1572872 | tf_op jit(solution)/shard_map/ppermute | solution.py:34
  13.6 1.1 collective-permute-start
  14.7 1.0 collective-permute-start.2
  15.7 1.2 fusion.73
  17.0 2.0 %fusion.104 = bf16[1024,2048]{1,0:T(8,128)(2,1)} fusion(bf16[128,2048]{1,0:T(8,128)(2,1)} %param.7, f32[2048]{0:T(1024)} %param.8), kind=kLoop, calls=%fused_computation.96 | loop fusion | flops 786431 | bytes 1056768
  19.0 3.7 %collective-permute-done.3 = bf16[128,2048]{1,0:T(8,128)(2,1)S(1)} collective-permute-done((bf16[128,2048]{1,0:T(8,128)(2,1)}, bf16[128,2048]{1,0:T(8,128)(2,1)S(1)}, u32[]{:S(2)}, u32[]{:S(2)}) %collective-permute-start.3) | collective-permute-done | bytes 524320 | tf_op jit(solution)/shard_map/ppermute | solution.py:34
  22.8 3.0 %collective-permute-start.4 = (bf16[128,2048]{1,0:T(8,128)(2,1)S(1)}, bf16[128,2048]{1,0:T(8,128)(2,1)S(1)}, u32[]{:S(2)}, u32[]{:S(2)}) collective-permute-start(bf16[128,2048]{1,0:T(8,128)(2,1)S(1)} %collective-permute-done.3), channel_id=1, source_target_pairs={{8,0},{16,8},{24,16},{0,24},{9,1},{17,9},{25,17},{1,25},{10,2},{18... | collective-permute-start | bytes 1572872 | tf_op jit(solution)/shard_map/ppermute | solution.py:34
  26.5 0.9 convert_reduce_fusion
  27.7 1.9 %multiply_cosine_fusion = (f32[2,512,64]{2,1,0:T(8,128)S(1)}, f32[2,512,64]{2,1,0:T(8,128)S(1)}, f32[2,512,64]{2,1,0:T(8,128)S(1)}) fusion(f32[64]{0:T(128)S(1)} %multiply_exponential_fusion, f32[2,512]{1,0:T(2,128)S(1)} %get-tuple-element.116), kind=kLoop, calls=%fused_computation.88 | loop fusion | flops 131072 | bytes 790784 | tf_op jit(solution)/shard_map/cos | solution.py:181
  29.6 1.3 pad_maximum_fusion.7
  31.1 3.1 %collective-permute-start.5 = (bf16[128,2048]{1,0:T(8,128)(2,1)S(1)}, bf16[128,2048]{1,0:T(8,128)(2,1)S(1)}, u32[]{:S(2)}, u32[]{:S(2)}) collective-permute-start(bf16[128,2048]{1,0:T(8,128)(2,1)S(1)} %collective-permute-done.1), channel_id=1, source_target_pairs={{1,0},{0,1},{3,2},{2,3},{5,4},{4,5},{7,6},{6,7},{9,8},{8,9},{11,10... | collective-permute-start | bytes 1572872 | tf_op jit(solution)/shard_map/ppermute | solution.py:34
  34.6 1.9 %constant_dynamic-slice_fusion.2 = (bf16[2048,128]{1,0:T(8,128)(2,1)S(1)}, bf16[2048,128]{1,0:T(8,128)(2,1)S(1)}, bf16[2048,128]{1,0:T(8,128)(2,1)S(1)}, bf16[2048,128]{1,0:T(8,128)(2,1)S(1)}) fusion(bf16[2048,1024]{1,0:T(8,128)(2,1)} %param.12, s32[]{:T(128)S(6)} %select_n.193, s32[]{:T(128)S(6)} %select_n.192, bf16[2048,1024]{1,0:T(8,128)(2,1)} %param.11), kind=kLoop, calls=%fused_computation.166 | loop fusion | bytes 4194312 | tf_op jit(solution)/shard_map/dynamic_slice | solution.py:197
  36.5 2.2 %collective-permute-done = bf16[128,2048]{1,0:T(8,128)(2,1)} collective-permute-done((bf16[128,2048]{1,0:T(8,128)(2,1)}, bf16[128,2048]{1,0:T(8,128)(2,1)}, u32[]{:S(2)}, u32[]{:S(2)}) %collective-permute-start) | collective-permute-done | bytes 524320 | tf_op jit(solution)/shard_map/ppermute | solution.py:34
  38.7 1.2 fusion.75
  40.1 1.2 pad_maximum_fusion
  41.3 1.2 fusion.79
  42.5 1.1 fusion.103
  43.8 1.1 fusion.101
  45.1 3.3 %collective-permute-done.4 = bf16[128,2048]{1,0:T(8,128)(2,1)S(1)} collective-permute-done((bf16[128,2048]{1,0:T(8,128)(2,1)S(1)}, bf16[128,2048]{1,0:T(8,128)(2,1)S(1)}, u32[]{:S(2)}, u32[]{:S(2)}) %collective-permute-start.4) | collective-permute-done | bytes 524320 | tf_op jit(solution)/shard_map/ppermute | solution.py:34
  48.6 1.1 fusion.97
  49.7 1.9 %fusion.66 = bf16[512,256]{1,0:T(8,128)(2,1)} fusion(bf16[2048,256]{1,0:T(8,128)(2,1)S(1)} %pad_maximum_fusion.1, bf16[1024,2048]{1,0:T(8,128)(2,1)S(1)} %fusion.97, s32[]{:T(128)S(6)} %select_n.194), kind=kOutput, calls=%fused_computation.55 | convolution fusion | flops 537001984 | bytes 3407876 | tf_op jit(solution)/shard_map/dot_general | solution.py:215
  52.0 1.3 fusion.87
  55.0 3.4 %add_convert_fusion.4 = bf16[512,256]{1,0:T(8,128)(2,1)} fusion(bf16[512,256]{1,0:T(8,128)(2,1)S(1)} %collective-permute-done.7, bf16[2048,256]{1,0:T(8,128)(2,1)} %copy-done.1, bf16[1024,2048]{1,0:T(8,128)(2,1)} %copy-done.7, s32[]{:T(128)S(6)} %select_n.191), kind=kOutput, calls=%fused_computation.114 | convolution fusion | flops 537264128 | bytes 3670020 | tf_op jit(solution)/shard_map/dot_general | solution.py:215
  59.0 0.7 fusion.69
  59.9 1.7 collective-permute-start.10
  62.1 3.9 %convolution_convert_fusion.1 = bf16[1024,256]{1,0:T(8,128)(2,1)S(1)} fusion(bf16[1024,2048]{1,0:T(8,128)(2,1)} %copy-done.7, bf16[4,2048,256]{2,1,0:T(8,128)(2,1)} %bitcast.137, s32[]{:T(128)S(6)} %select_n.195), kind=kOutput, calls=%fused_computation.49 | convolution fusion | flops 1074003968 | bytes 5767172 | tf_op jit(solution)/shard_map/dot_general | solution.py:215
  66.0 2.5 %convolution_convert_fusion = bf16[1024,256]{1,0:T(8,128)(2,1)S(1)} fusion(bf16[1024,2048]{1,0:T(8,128)(2,1)S(1)} %copy-done.9, bf16[4,2048,256]{2,1,0:T(8,128)(2,1)} %bitcast.138, s32[]{:T(128)S(6)} %select_n.196), kind=kOutput, calls=%fused_computation.48 | convolution fusion | flops 1074003968 | bytes 5767172 | tf_op jit(solution)/shard_map/dot_general | solution.py:215
  68.8 0.7 fusion.63
  70.8 2.5 %collective-permute-start.14 = (bf16[2,512,128]{2,1,0:T(8,128)(2,1)S(1)}, bf16[2,512,128]{2,1,0:T(8,128)(2,1)S(1)}, u32[]{:S(2)}, u32[]{:S(2)}) collective-permute-start(bf16[2,512,128]{2,1,0:T(8,128)(2,1)S(1)} %pad_maximum_fusion.9.m0), channel_id=1, source_target_pairs={{6,0},{0,2},{2,4},{4,6},{7,1},{1,3},{3,5},{5,7},{14,8},{8,10},{10,... | collective-permute-start | bytes 786440 | tf_op jit(solution)/shard_map/ppermute | solution.py:34
  73.3 1.3 fusion.26
  74.6 1.5 collective-permute-start.17
  76.2 1.2 fusion.88
  77.7 1.0 add_convert_fusion.home0.home1
  78.7 11.8 %collective-permute-done.12.m1 = bf16[2,512,128]{2,1,0:T(8,128)(2,1)S(1)} collective-permute-done((bf16[2,512,128]{2,1,0:T(8,128)(2,1)S(1)}, bf16[2,512,128]{2,1,0:T(8,128)(2,1)S(1)}, u32[]{:S(2)}, u32[]{:S(2)}) %collective-permute-start.12) | collective-permute-done | bytes 262176 | tf_op jit(solution)/shard_map/ppermute | solution.py:34
  90.5 2.4 %collective-permute-done.13.m2 = bf16[2,512,128]{2,1,0:T(8,128)(2,1)S(1)} collective-permute-done((bf16[2,512,128]{2,1,0:T(8,128)(2,1)S(1)}, bf16[2,512,128]{2,1,0:T(8,128)(2,1)S(1)}, u32[]{:S(2)}, u32[]{:S(2)}) %collective-permute-start.13) | collective-permute-done | bytes 262176 | tf_op jit(solution)/shard_map/ppermute | solution.py:34
  92.9 5.0 %collective-permute-done.14.m3 = bf16[2,512,128]{2,1,0:T(8,128)(2,1)S(1)} collective-permute-done((bf16[2,512,128]{2,1,0:T(8,128)(2,1)S(1)}, bf16[2,512,128]{2,1,0:T(8,128)(2,1)S(1)}, u32[]{:S(2)}, u32[]{:S(2)}) %collective-permute-start.14) | collective-permute-done | bytes 262176 | tf_op jit(solution)/shard_map/ppermute | solution.py:34
  98.6 1.0 copy.16.scale0.scale1
  100.6 0.7 copy-done.19
  101.3 8.7 %shard_map.73 = bf16[2,2,128,256]{3,2,1,0:T(8,128)(2,1)} custom-call(s32[12]{0:T(128)} %concatenate.51.scalars, bf16[1024,256]{1,0:T(8,128)(2,1)} %add_convert_fusion.home0.home1, bf16[1024,256]{1,0:T(8,128)(2,1)} %add_convert_fusion.home0.home1, bf16[1024,256]{1,0:T(8,128)(2,1)} %copy-done.12, bf16[1024,256]{1,0:T(8,128)(2,1)} %copy-done.12, ...), custom_call_target="tpu_custom_call" | custom-call | flops 2000000000 | bytes 4194304 | tf_op jit(solution)/shard_map/pallas_call | solution.py:127
  110.0 1.6 collective-permute-start.22
  111.7 6.7 %shard_map.74 = bf16[2,2,128,256]{3,2,1,0:T(8,128)(2,1)} custom-call(s32[12]{0:T(128)} %concatenate.51.scalars, bf16[1024,256]{1,0:T(8,128)(2,1)} %add_convert_fusion.home0.home1, bf16[1024,256]{1,0:T(8,128)(2,1)} %add_convert_fusion.home0.home1, bf16[1024,256]{1,0:T(8,128)(2,1)} %copy-done.12, bf16[1024,256]{1,0:T(8,128)(2,1)} %copy-done.12, ...), custom_call_target="tpu_custom_call" | custom-call | flops 2000000000 | bytes 4194304 | tf_op jit(solution)/shard_map/pallas_call | solution.py:127
  118.9 1.5 collective-permute-start.24
  120.9 3.0 %fusion.12 = bf16[512,1024]{1,0:T(8,128)(2,1)S(1)} fusion(bf16[1024,2048]{1,0:T(8,128)(2,1)} %all-gather.5.cloned.1.call-done, bf16[512,256]{1,0:T(8,128)(2,1)S(1)} %get-tuple-element.106, bf16[512,256]{1,0:T(8,128)(2,1)S(1)} %get-tuple-element.107, bf16[512,256]{1,0:T(8,128)(2,1)S(1)} %get-tuple-element.108, bf16[512,256]{1,0:T(8,128)(2,1)S(1)} %get-tuple-element.105), kind=kOutput, calls=%fused_computation.12 | convolution fusion | flops 1078460416 | bytes 4194304 | tf_op jit(solution)/shard_map/dot_general | solution.py:274
  123.9 0.7 fusion.30
  124.7 0.7 fusion.27
  125.5 2.3 %collective-permute-done.24 = bf16[512,256]{1,0:T(8,128)(2,1)S(1)} collective-permute-done((bf16[512,256]{1,0:T(8,128)(2,1)}, bf16[512,256]{1,0:T(8,128)(2,1)S(1)}, u32[]{:S(2)}, u32[]{:S(2)}) %collective-permute-start.24) | collective-permute-done | bytes 262176 | tf_op jit(solution)/shard_map/ppermute | solution.py:34
  127.8 2.5 %collective-permute-start.28 = (bf16[256,1024]{1,0:T(8,128)(2,1)S(1)}, bf16[256,1024]{1,0:T(8,128)(2,1)S(1)}, u32[]{:S(2)}, u32[]{:S(2)}) collective-permute-start(bf16[256,1024]{1,0:T(8,128)(2,1)S(1)} %fusion.27), channel_id=1, source_target_pairs={{16,0},{24,8},{0,16},{8,24},{17,1},{25,9},{1,17},{9,25},{18,2},{26... | collective-permute-start | bytes 1572872 | tf_op jit(solution)/shard_map/ppermute | solution.py:34
  130.3 1.2 collective-permute-start.29
  131.6 1.9 %collective-permute-start.33 = (bf16[2,128,1024]{2,1,0:T(8,128)(2,1)S(1)}, bf16[2,128,1024]{2,1,0:T(8,128)(2,1)S(1)}, u32[]{:S(2)}, u32[]{:S(2)}) collective-permute-start(bf16[2,128,1024]{2,1,0:T(8,128)(2,1)S(1)} %pad_maximum_fusion.5), channel_id=1, source_target_pairs={{1,0},{0,1},{3,2},{2,3},{5,4},{4,5},{7,6},{6,7},{9,8},{8,9},{11,10... | collective-permute-start | bytes 1572872 | tf_op jit(solution)/shard_map/ppermute | solution.py:34
  133.8 0.7 fusion.36
  134.5 0.9 collective-permute-start.30
  135.5 1.2 fusion.15
  136.8 1.8 collective-permute-start.32
  138.6 9.4 %collective-permute-done.33 = bf16[2,128,1024]{2,1,0:T(8,128)(2,1)S(1)} collective-permute-done((bf16[2,128,1024]{2,1,0:T(8,128)(2,1)S(1)}, bf16[2,128,1024]{2,1,0:T(8,128)(2,1)S(1)}, u32[]{:S(2)}, u32[]{:S(2)}) %collective-permute-start.33) | collective-permute-done | bytes 524320 | tf_op jit(solution)/shard_map/ppermute | solution.py:34
  148.2 3.0 %collective-permute-start.34 = (bf16[128,1024]{1,0:T(8,128)(2,1)S(1)}, bf16[128,1024]{1,0:T(8,128)(2,1)S(1)}, u32[]{:S(2)}, u32[]{:S(2)}) collective-permute-start(bf16[128,1024]{1,0:T(8,128)(2,1)S(1)} %get-tuple-element.110), channel_id=1, source_target_pairs={{16,0},{24,8},{0,16},{8,24},{17,1},{25,9},{1,17},{9,25},{18,2},{26... | collective-permute-start | bytes 786440 | tf_op jit(solution)/shard_map/ppermute | solution.py:34
  151.8 4.6 %collective-permute-done.29 = bf16[256,1024]{1,0:T(8,128)(2,1)S(1)} collective-permute-done((bf16[256,1024]{1,0:T(8,128)(2,1)S(1)}, bf16[256,1024]{1,0:T(8,128)(2,1)S(1)}, u32[]{:S(2)}, u32[]{:S(2)}) %collective-permute-start.29) | collective-permute-done | bytes 524320 | tf_op jit(solution)/shard_map/ppermute | solution.py:34
  156.3 0.9 fusion.48
  157.2 1.9 %collective-permute-start.31 = (bf16[128,1024]{1,0:T(8,128)(2,1)S(1)}, bf16[128,1024]{1,0:T(8,128)(2,1)S(1)}, u32[]{:S(2)}, u32[]{:S(2)}) collective-permute-start(bf16[128,1024]{1,0:T(8,128)(2,1)S(1)} %slice.212), channel_id=1, source_target_pairs={{1,0},{0,1},{3,2},{2,3},{5,4},{4,5},{7,6},{6,7},{9,8},{8,9},{11,10... | collective-permute-start | bytes 786440 | tf_op jit(solution)/shard_map/ppermute | solution.py:34
  159.1 1.4 collective-permute-done.34
  160.6 6.6 %collective-permute-done.35 = bf16[128,1024]{1,0:T(8,128)(2,1)S(1)} collective-permute-done((bf16[128,1024]{1,0:T(8,128)(2,1)S(1)}, bf16[128,1024]{1,0:T(8,128)(2,1)S(1)}, u32[]{:S(2)}, u32[]{:S(2)}) %collective-permute-start.35) | collective-permute-done | bytes 262176 | tf_op jit(solution)/shard_map/ppermute | solution.py:34
  167.7 8.9 %collective-permute-done.36 = bf16[128,1024]{1,0:T(8,128)(2,1)S(1)} collective-permute-done((bf16[128,1024]{1,0:T(8,128)(2,1)S(1)}, bf16[128,1024]{1,0:T(8,128)(2,1)S(1)}, u32[]{:S(2)}, u32[]{:S(2)}) %collective-permute-start.36) | collective-permute-done | bytes 262176 | tf_op jit(solution)/shard_map/ppermute | solution.py:34
  176.8 0.8 pad_maximum_fusion.6
  (143 shorter events, 12.1 us)
Async XLA Ops:
  6.5 55.6 %all-gather.3.cloned.1.call-start = ((), (), s32[]{:S(2)}) async-start(), calls=%async_computation | async-start | bytes 5242880 | tf_op jit(solution)/shard_map/all_gather | solution.py:162
  7.3 113.7 %all-gather.5.cloned.1.call-start = ((), (), s32[]{:S(2)}) async-start(), calls=%async_computation.1 | async-start | bytes 5242880 | tf_op jit(solution)/shard_map/all_gather | solution.py:163
  7.3 15.5 %collective-permute-start.3 = (bf16[128,2048]{1,0:T(8,128)(2,1)}, bf16[128,2048]{1,0:T(8,128)(2,1)S(1)}, u32[]{:S(2)}, u32[]{:S(2)}) collective-permute-start(bf16[128,2048]{1,0:T(8,128)(2,1)} %param.7), channel_id=1, source_target_pairs={{1,0},{0,1},{3,2},{2,3},{5,4},{4,5},{7,6},{6,7},{9,8},{8,9},{11,10... | collective-permute-start | bytes 1572872 | tf_op jit(solution)/shard_map/ppermute | solution.py:34
  10.4 20.7 %collective-permute-start.1 = (bf16[128,2048]{1,0:T(8,128)(2,1)}, bf16[128,2048]{1,0:T(8,128)(2,1)S(1)}, u32[]{:S(2)}, u32[]{:S(2)}) collective-permute-start(bf16[128,2048]{1,0:T(8,128)(2,1)} %param.7), channel_id=1, source_target_pairs={{16,0},{24,8},{0,16},{8,24},{17,1},{25,9},{1,17},{9,25},{18,2},{26... | collective-permute-start | bytes 1572872 | tf_op jit(solution)/shard_map/ppermute | solution.py:34
  13.6 25.1 %collective-permute-start = (bf16[128,2048]{1,0:T(8,128)(2,1)}, bf16[128,2048]{1,0:T(8,128)(2,1)}, u32[]{:S(2)}, u32[]{:S(2)}) collective-permute-start(bf16[128,2048]{1,0:T(8,128)(2,1)} %param.7), channel_id=1, source_target_pairs={{8,0},{16,8},{24,16},{0,24},{9,1},{17,9},{25,17},{1,25},{10,2},{18... | collective-permute-start | bytes 1572872 | tf_op jit(solution)/shard_map/ppermute | solution.py:34
  14.7 26.6 %collective-permute-start.2 = (bf16[128,2048]{1,0:T(8,128)(2,1)}, bf16[128,2048]{1,0:T(8,128)(2,1)}, u32[]{:S(2)}, u32[]{:S(2)}) collective-permute-start(bf16[128,2048]{1,0:T(8,128)(2,1)} %param.7), channel_id=1, source_target_pairs={{24,0},{0,8},{8,16},{16,24},{25,1},{1,9},{9,17},{17,25},{26,2},{2,... | collective-permute-start | bytes 1572872 | tf_op jit(solution)/shard_map/ppermute | solution.py:34
  22.8 25.6 %collective-permute-start.4 = (bf16[128,2048]{1,0:T(8,128)(2,1)S(1)}, bf16[128,2048]{1,0:T(8,128)(2,1)S(1)}, u32[]{:S(2)}, u32[]{:S(2)}) collective-permute-start(bf16[128,2048]{1,0:T(8,128)(2,1)S(1)} %collective-permute-done.3), channel_id=1, source_target_pairs={{8,0},{16,8},{24,16},{0,24},{9,1},{17,9},{25,17},{1,25},{10,2},{18... | collective-permute-start | bytes 1572872 | tf_op jit(solution)/shard_map/ppermute | solution.py:34
  25.8 22.6 %collective-permute-start.6 = (bf16[128,2048]{1,0:T(8,128)(2,1)S(1)}, bf16[128,2048]{1,0:T(8,128)(2,1)}, u32[]{:S(2)}, u32[]{:S(2)}) collective-permute-start(bf16[128,2048]{1,0:T(8,128)(2,1)S(1)} %collective-permute-done.3), channel_id=1, source_target_pairs={{24,0},{0,8},{8,16},{16,24},{25,1},{1,9},{9,17},{17,25},{26,2},{2,... | collective-permute-start | bytes 1572872 | tf_op jit(solution)/shard_map/ppermute | solution.py:34
  31.1 17.2 %collective-permute-start.5 = (bf16[128,2048]{1,0:T(8,128)(2,1)S(1)}, bf16[128,2048]{1,0:T(8,128)(2,1)S(1)}, u32[]{:S(2)}, u32[]{:S(2)}) collective-permute-start(bf16[128,2048]{1,0:T(8,128)(2,1)S(1)} %collective-permute-done.1), channel_id=1, source_target_pairs={{1,0},{0,1},{3,2},{2,3},{5,4},{4,5},{7,6},{6,7},{9,8},{8,9},{11,10... | collective-permute-start | bytes 1572872 | tf_op jit(solution)/shard_map/ppermute | solution.py:34
  34.6 8.0 %copy-start.2 = (f32[2048]{0:T(1024)S(1)}, f32[2048]{0:T(1024)}, u32[]{:S(2)}) copy-start(f32[2048]{0:T(1024)} %param.8) | copy-start | bytes 24580
  34.6 7.9 %copy-start.6 = (bf16[1024,2048]{1,0:T(8,128)(2,1)S(1)}, bf16[1024,2048]{1,0:T(8,128)(2,1)}, u32[]{:S(2)}) copy-start(bf16[1024,2048]{1,0:T(8,128)(2,1)} %fusion.104) | copy-start | bytes 12582916
  40.0 9.7 %copy-start.1 = (bf16[2048,256]{1,0:T(8,128)(2,1)}, bf16[2048,256]{1,0:T(8,128)(2,1)S(1)}, u32[]{:S(2)}) copy-start(bf16[2048,256]{1,0:T(8,128)(2,1)S(1)} %pad_maximum_fusion.1) | copy-start | bytes 3145732
  49.7 2.2 %copy-start.7 = (bf16[1024,2048]{1,0:T(8,128)(2,1)}, bf16[1024,2048]{1,0:T(8,128)(2,1)S(1)}, u32[]{:S(2)}) copy-start(bf16[1024,2048]{1,0:T(8,128)(2,1)S(1)} %fusion.97) | copy-start | bytes 12582916
  51.7 7.4 %copy-start = (bf16[2048,256]{1,0:T(8,128)(2,1)S(1)}, bf16[2048,256]{1,0:T(8,128)(2,1)}, u32[]{:S(2)}) copy-start(bf16[2048,256]{1,0:T(8,128)(2,1)} %pad_maximum_fusion) | copy-start | bytes 3145732
  51.7 3.3 %collective-permute-start.7 = (bf16[512,256]{1,0:T(8,128)(2,1)}, bf16[512,256]{1,0:T(8,128)(2,1)S(1)}, u32[]{:S(2)}, u32[]{:S(2)}) collective-permute-start(bf16[512,256]{1,0:T(8,128)(2,1)} %fusion.66), channel_id=1, source_target_pairs={{32,0},{0,32},{33,1},{1,33},{34,2},{2,34},{35,3},{3,35},{36,4},{4,... | collective-permute-start | bytes 786440 | tf_op jit(solution)/shard_map/ppermute | solution.py:34
  53.3 1.7 collective-permute-start.8
  55.0 4.0 %copy-start.8 = (bf16[1024,2048]{1,0:T(8,128)(2,1)S(1)}, bf16[1024,2048]{1,0:T(8,128)(2,1)}, u32[]{:S(2)}) copy-start(bf16[1024,2048]{1,0:T(8,128)(2,1)} %copy-done.7) | copy-start | bytes 12582916
  58.5 3.6 %collective-permute-start.11 = (f32[8,128]{1,0:T(8,128)S(1)}, f32[8,128]{1,0:T(8,128)S(1)}, u32[]{:S(2)}, u32[]{:S(2)}) collective-permute-start(f32[8,128]{1,0:T(8,128)S(1)} %add.154), channel_id=1, source_target_pairs={{64,0},{0,64},{65,1},{1,65},{66,2},{2,66},{67,3},{3,67},{68,4},{4,... | collective-permute-start | bytes 12296 | tf_op jit(solution)/shard_map/ppermute | solution.py:34
  59.8 9.0 %collective-permute-start.9 = (bf16[512,256]{1,0:T(8,128)(2,1)S(1)}, bf16[512,256]{1,0:T(8,128)(2,1)S(1)}, u32[]{:S(2)}, u32[]{:S(2)}) collective-permute-start(bf16[512,256]{1,0:T(8,128)(2,1)S(1)} %fusion.69), channel_id=1, source_target_pairs={{32,0},{0,32},{33,1},{1,33},{34,2},{2,34},{35,3},{3,35},{36,4},{4,... | collective-permute-start | bytes 786440 | tf_op jit(solution)/shard_map/ppermute | solution.py:34
  59.9 8.9 %collective-permute-start.10 = (bf16[512,256]{1,0:T(8,128)(2,1)}, bf16[512,256]{1,0:T(8,128)(2,1)S(1)}, u32[]{:S(2)}, u32[]{:S(2)}) collective-permute-start(bf16[512,256]{1,0:T(8,128)(2,1)} %add_convert_fusion.4), channel_id=1, source_target_pairs={{64,0},{0,64},{65,1},{1,65},{66,2},{2,66},{67,3},{3,67},{68,4},{4,... | collective-permute-start | bytes 786440 | tf_op jit(solution)/shard_map/ppermute | solution.py:34
  62.1 3.9 %copy-start.9 = (bf16[1024,2048]{1,0:T(8,128)(2,1)S(1)}, bf16[1024,2048]{1,0:T(8,128)(2,1)}, u32[]{:S(2)}) copy-start(bf16[1024,2048]{1,0:T(8,128)(2,1)} %copy-done.7) | copy-start | bytes 12582916
  68.8 4.6 %collective-permute-start.15 = (bf16[1024,256]{1,0:T(8,128)(2,1)S(1)}, bf16[1024,256]{1,0:T(8,128)(2,1)S(1)}, u32[]{:S(2)}, u32[]{:S(2)}) collective-permute-start(bf16[1024,256]{1,0:T(8,128)(2,1)S(1)} %convolution_convert_fusion.1), channel_id=1, source_target_pairs={{32,0},{0,32},{33,1},{1,33},{34,2},{2,34},{35,3},{3,35},{36,4},{4,... | collective-permute-start | bytes 1572872 | tf_op jit(solution)/shard_map/ppermute | solution.py:34
  68.8 4.6 %copy-start.11 = (bf16[8192,256]{1,0:T(8,128)(2,1)S(1)}, bf16[8192,256]{1,0:T(8,128)(2,1)}, u32[]{:S(2)}) copy-start(bf16[8192,256]{1,0:T(8,128)(2,1)} %all-gather.3.cloned.1.call-done) | copy-start | bytes 12582916
  70.0 7.4 %copy-start.5 = (bf16[2,512,128]{2,1,0:T(8,128)(2,1)}, bf16[2,512,128]{2,1,0:T(8,128)(2,1)S(1)}, u32[]{:S(2)}) copy-start(bf16[2,512,128]{2,1,0:T(8,128)(2,1)S(1)} %pad_maximum_fusion.9.m0) | copy-start | bytes 786436
  70.0 20.5 %collective-permute-start.12 = (bf16[2,512,128]{2,1,0:T(8,128)(2,1)S(1)}, bf16[2,512,128]{2,1,0:T(8,128)(2,1)S(1)}, u32[]{:S(2)}, u32[]{:S(2)}) collective-permute-start(bf16[2,512,128]{2,1,0:T(8,128)(2,1)S(1)} %pad_maximum_fusion.9.m0), channel_id=1, source_target_pairs={{2,0},{4,2},{6,4},{0,6},{3,1},{5,3},{7,5},{1,7},{10,8},{12,10},{14... | collective-permute-start | bytes 786440 | tf_op jit(solution)/shard_map/ppermute | solution.py:34
  70.5 22.4 %collective-permute-start.13 = (bf16[2,512,128]{2,1,0:T(8,128)(2,1)S(1)}, bf16[2,512,128]{2,1,0:T(8,128)(2,1)S(1)}, u32[]{:S(2)}, u32[]{:S(2)}) collective-permute-start(bf16[2,512,128]{2,1,0:T(8,128)(2,1)S(1)} %pad_maximum_fusion.9.m0), channel_id=1, source_target_pairs={{4,0},{6,2},{0,4},{2,6},{5,1},{7,3},{1,5},{3,7},{12,8},{14,10},{8,... | collective-permute-start | bytes 786440 | tf_op jit(solution)/shard_map/ppermute | solution.py:34
  70.8 27.1 %collective-permute-start.14 = (bf16[2,512,128]{2,1,0:T(8,128)(2,1)S(1)}, bf16[2,512,128]{2,1,0:T(8,128)(2,1)S(1)}, u32[]{:S(2)}, u32[]{:S(2)}) collective-permute-start(bf16[2,512,128]{2,1,0:T(8,128)(2,1)S(1)} %pad_maximum_fusion.9.m0), channel_id=1, source_target_pairs={{6,0},{0,2},{2,4},{4,6},{7,1},{1,3},{3,5},{5,7},{14,8},{8,10},{10,... | collective-permute-start | bytes 786440 | tf_op jit(solution)/shard_map/ppermute | solution.py:34
  73.3 4.1 %collective-permute-start.16 = (bf16[1024,256]{1,0:T(8,128)(2,1)S(1)}, bf16[1024,256]{1,0:T(8,128)(2,1)S(1)}, u32[]{:S(2)}, u32[]{:S(2)}) collective-permute-start(bf16[1024,256]{1,0:T(8,128)(2,1)S(1)} %convolution_convert_fusion), channel_id=1, source_target_pairs={{32,0},{0,32},{33,1},{1,33},{34,2},{2,34},{35,3},{3,35},{36,4},{4,... | collective-permute-start | bytes 1572872 | tf_op jit(solution)/shard_map/ppermute | solution.py:34
  74.6 23.3 %collective-permute-start.17 = (bf16[1024,256]{1,0:T(8,128)(2,1)S(1)}, bf16[1024,256]{1,0:T(8,128)(2,1)S(1)}, u32[]{:S(2)}, u32[]{:S(2)}) collective-permute-start(bf16[1024,256]{1,0:T(8,128)(2,1)S(1)} %fusion.26), channel_id=1, source_target_pairs={{64,0},{0,64},{65,1},{1,65},{66,2},{2,66},{67,3},{3,67},{68,4},{4,... | collective-permute-start | bytes 1572872 | tf_op jit(solution)/shard_map/ppermute | solution.py:34
  77.4 22.2 %collective-permute-start.18 = (bf16[2,512,128]{2,1,0:T(8,128)(2,1)S(1)}, bf16[2,512,128]{2,1,0:T(8,128)(2,1)S(1)}, u32[]{:S(2)}, u32[]{:S(2)}) collective-permute-start(bf16[2,512,128]{2,1,0:T(8,128)(2,1)S(1)} %pad_maximum_fusion.9.m0), channel_id=1, source_target_pairs={{32,0},{0,32},{33,1},{1,33},{34,2},{2,34},{35,3},{3,35},{36,4},{4,... | collective-permute-start | bytes 786440 | tf_op jit(solution)/shard_map/ppermute | solution.py:34
  90.5 9.7 %copy-start.13 = (bf16[2,512,128]{2,1,0:T(8,128)(2,1)}, bf16[2,512,128]{2,1,0:T(8,128)(2,1)S(1)}, u32[]{:S(2)}) copy-start(bf16[2,512,128]{2,1,0:T(8,128)(2,1)S(1)} %collective-permute-done.12.m1) | copy-start | bytes 786436
  92.9 7.4 %copy-start.14 = (bf16[2,512,128]{2,1,0:T(8,128)(2,1)}, bf16[2,512,128]{2,1,0:T(8,128)(2,1)S(1)}, u32[]{:S(2)}) copy-start(bf16[2,512,128]{2,1,0:T(8,128)(2,1)S(1)} %collective-permute-done.13.m2) | copy-start | bytes 786436
  97.9 2.4 %copy-start.15 = (bf16[2,512,128]{2,1,0:T(8,128)(2,1)}, bf16[2,512,128]{2,1,0:T(8,128)(2,1)S(1)}, u32[]{:S(2)}) copy-start(bf16[2,512,128]{2,1,0:T(8,128)(2,1)S(1)} %collective-permute-done.14.m3) | copy-start | bytes 786436
  97.9 2.4 %copy-start.12 = (bf16[1024,256]{1,0:T(8,128)(2,1)}, bf16[1024,256]{1,0:T(8,128)(2,1)S(1)}, u32[]{:S(2)}) copy-start(bf16[1024,256]{1,0:T(8,128)(2,1)S(1)} %collective-permute-done.17.far0.far1) | copy-start | bytes 1572868
  97.9 1.7 collective-permute-start.19
  98.0 1.9 %collective-permute-start.20 = (bf16[2,512,128]{2,1,0:T(8,128)(2,1)S(1)}, bf16[2,512,128]{2,1,0:T(8,128)(2,1)S(1)}, u32[]{:S(2)}, u32[]{:S(2)}) collective-permute-start(bf16[2,512,128]{2,1,0:T(8,128)(2,1)S(1)} %collective-permute-done.13.m2), channel_id=1, source_target_pairs={{32,0},{0,32},{33,1},{1,33},{34,2},{2,34},{35,3},{3,35},{36,4},{4,... | collective-permute-start | bytes 786440 | tf_op jit(solution)/shard_map/ppermute | solution.py:34
  98.5 1.8 collective-permute-start.21
  99.6 0.7 copy-start.16
  99.6 0.8 copy-start.17
  99.9 0.7 copy-start.18
  100.6 0.7 copy-start.19
  110.0 10.6 %copy-start.4 = (bf16[2,2,128,256]{3,2,1,0:T(8,128)(2,1)S(1)}, bf16[2,2,128,256]{3,2,1,0:T(8,128)(2,1)}, u32[]{:S(2)}) copy-start(bf16[2,2,128,256]{3,2,1,0:T(8,128)(2,1)} %shard_map.73) | copy-start | bytes 786436
  110.0 8.9 %collective-permute-start.22 = (bf16[512,256]{1,0:T(8,128)(2,1)}, bf16[512,256]{1,0:T(8,128)(2,1)S(1)}, u32[]{:S(2)}, u32[]{:S(2)}) collective-permute-start(bf16[512,256]{1,0:T(8,128)(2,1)} %bitcast.120), channel_id=1, source_target_pairs={{64,0},{0,64},{65,1},{1,65},{66,2},{2,66},{67,3},{3,67},{68,4},{4,... | collective-permute-start | bytes 786440 | tf_op jit(solution)/shard_map/ppermute | solution.py:34
  111.6 9.0 %collective-permute-start.25 = (bf16[512,256]{1,0:T(8,128)(2,1)}, bf16[512,256]{1,0:T(8,128)(2,1)S(1)}, u32[]{:S(2)}, u32[]{:S(2)}) collective-permute-start(bf16[512,256]{1,0:T(8,128)(2,1)} %bitcast.121), channel_id=1, source_target_pairs={{32,0},{0,32},{33,1},{1,33},{34,2},{2,34},{35,3},{3,35},{36,4},{4,... | collective-permute-start | bytes 786440 | tf_op jit(solution)/shard_map/ppermute | solution.py:34
  118.9 1.7 collective-permute-start.26
  118.9 8.9 %collective-permute-start.24 = (bf16[512,256]{1,0:T(8,128)(2,1)}, bf16[512,256]{1,0:T(8,128)(2,1)S(1)}, u32[]{:S(2)}, u32[]{:S(2)}) collective-permute-start(bf16[512,256]{1,0:T(8,128)(2,1)} %bitcast.118), channel_id=1, source_target_pairs={{64,0},{0,64},{65,1},{1,65},{66,2},{2,66},{67,3},{3,67},{68,4},{4,... | collective-permute-start | bytes 786440 | tf_op jit(solution)/shard_map/ppermute | solution.py:34
  120.4 13.1 %collective-permute-start.23 = (bf16[512,256]{1,0:T(8,128)(2,1)}, bf16[512,256]{1,0:T(8,128)(2,1)S(1)}, u32[]{:S(2)}, u32[]{:S(2)}) collective-permute-start(bf16[512,256]{1,0:T(8,128)(2,1)} %bitcast.119), channel_id=1, source_target_pairs={{32,0},{0,32},{33,1},{1,33},{34,2},{2,34},{35,3},{3,35},{36,4},{4,... | collective-permute-start | bytes 786440 | tf_op jit(solution)/shard_map/ppermute | solution.py:34
  120.9 3.0 %copy-start.10 = (bf16[1024,2048]{1,0:T(8,128)(2,1)S(1)}, bf16[1024,2048]{1,0:T(8,128)(2,1)}, u32[]{:S(2)}) copy-start(bf16[1024,2048]{1,0:T(8,128)(2,1)} %all-gather.5.cloned.1.call-done) | copy-start | bytes 12582916
  124.7 8.8 %copy-start.3 = (bf16[2,2,128,256]{3,2,1,0:T(8,128)(2,1)S(1)}, bf16[2,2,128,256]{3,2,1,0:T(8,128)(2,1)}, u32[]{:S(2)}) copy-start(bf16[2,2,128,256]{3,2,1,0:T(8,128)(2,1)} %shard_map.74) | copy-start | bytes 786436
  127.8 5.7 %collective-permute-start.27 = (bf16[512,256]{1,0:T(8,128)(2,1)S(1)}, bf16[512,256]{1,0:T(8,128)(2,1)S(1)}, u32[]{:S(2)}, u32[]{:S(2)}) collective-permute-start(bf16[512,256]{1,0:T(8,128)(2,1)S(1)} %collective-permute-done.24), channel_id=1, source_target_pairs={{32,0},{0,32},{33,1},{1,33},{34,2},{2,34},{35,3},{3,35},{36,4},{4,... | collective-permute-start | bytes 786440 | tf_op jit(solution)/shard_map/ppermute | solution.py:34
  127.8 23.4 %collective-permute-start.28 = (bf16[256,1024]{1,0:T(8,128)(2,1)S(1)}, bf16[256,1024]{1,0:T(8,128)(2,1)S(1)}, u32[]{:S(2)}, u32[]{:S(2)}) collective-permute-start(bf16[256,1024]{1,0:T(8,128)(2,1)S(1)} %fusion.27), channel_id=1, source_target_pairs={{16,0},{24,8},{0,16},{8,24},{17,1},{25,9},{1,17},{9,25},{18,2},{26... | collective-permute-start | bytes 1572872 | tf_op jit(solution)/shard_map/ppermute | solution.py:34
  130.3 26.0 %collective-permute-start.29 = (bf16[256,1024]{1,0:T(8,128)(2,1)S(1)}, bf16[256,1024]{1,0:T(8,128)(2,1)S(1)}, u32[]{:S(2)}, u32[]{:S(2)}) collective-permute-start(bf16[256,1024]{1,0:T(8,128)(2,1)S(1)} %fusion.30), channel_id=1, source_target_pairs={{8,0},{16,8},{24,16},{0,24},{9,1},{17,9},{25,17},{1,25},{10,2},{18... | collective-permute-start | bytes 1572872 | tf_op jit(solution)/shard_map/ppermute | solution.py:34
  131.6 16.3 %collective-permute-start.33 = (bf16[2,128,1024]{2,1,0:T(8,128)(2,1)S(1)}, bf16[2,128,1024]{2,1,0:T(8,128)(2,1)S(1)}, u32[]{:S(2)}, u32[]{:S(2)}) collective-permute-start(bf16[2,128,1024]{2,1,0:T(8,128)(2,1)S(1)} %pad_maximum_fusion.5), channel_id=1, source_target_pairs={{1,0},{0,1},{3,2},{2,3},{5,4},{4,5},{7,6},{6,7},{9,8},{8,9},{11,10... | collective-permute-start | bytes 1572872 | tf_op jit(solution)/shard_map/ppermute | solution.py:34
  134.5 21.8 %collective-permute-start.30 = (bf16[256,1024]{1,0:T(8,128)(2,1)S(1)}, bf16[256,1024]{1,0:T(8,128)(2,1)S(1)}, u32[]{:S(2)}, u32[]{:S(2)}) collective-permute-start(bf16[256,1024]{1,0:T(8,128)(2,1)S(1)} %fusion.36), channel_id=1, source_target_pairs={{24,0},{0,8},{8,16},{16,24},{25,1},{1,9},{9,17},{17,25},{26,2},{2,... | collective-permute-start | bytes 1572872 | tf_op jit(solution)/shard_map/ppermute | solution.py:34
  136.8 30.5 %collective-permute-start.32 = (bf16[2,128,1024]{2,1,0:T(8,128)(2,1)S(1)}, bf16[2,128,1024]{2,1,0:T(8,128)(2,1)S(1)}, u32[]{:S(2)}, u32[]{:S(2)}) collective-permute-start(bf16[2,128,1024]{2,1,0:T(8,128)(2,1)S(1)} %pad_maximum_fusion.4), channel_id=1, source_target_pairs={{1,0},{0,1},{3,2},{2,3},{5,4},{4,5},{7,6},{6,7},{9,8},{8,9},{11,10... | collective-permute-start | bytes 1572872 | tf_op jit(solution)/shard_map/ppermute | solution.py:34
  148.2 12.4 %collective-permute-start.34 = (bf16[128,1024]{1,0:T(8,128)(2,1)S(1)}, bf16[128,1024]{1,0:T(8,128)(2,1)S(1)}, u32[]{:S(2)}, u32[]{:S(2)}) collective-permute-start(bf16[128,1024]{1,0:T(8,128)(2,1)S(1)} %get-tuple-element.110), channel_id=1, source_target_pairs={{16,0},{24,8},{0,16},{8,24},{17,1},{25,9},{1,17},{9,25},{18,2},{26... | collective-permute-start | bytes 786440 | tf_op jit(solution)/shard_map/ppermute | solution.py:34
  151.2 16.0 %collective-permute-start.35 = (bf16[128,1024]{1,0:T(8,128)(2,1)S(1)}, bf16[128,1024]{1,0:T(8,128)(2,1)S(1)}, u32[]{:S(2)}, u32[]{:S(2)}) collective-permute-start(bf16[128,1024]{1,0:T(8,128)(2,1)S(1)} %get-tuple-element.109), channel_id=1, source_target_pairs={{8,0},{16,8},{24,16},{0,24},{9,1},{17,9},{25,17},{1,25},{10,2},{18... | collective-permute-start | bytes 786440 | tf_op jit(solution)/shard_map/ppermute | solution.py:34
  157.2 10.4 %collective-permute-start.31 = (bf16[128,1024]{1,0:T(8,128)(2,1)S(1)}, bf16[128,1024]{1,0:T(8,128)(2,1)S(1)}, u32[]{:S(2)}, u32[]{:S(2)}) collective-permute-start(bf16[128,1024]{1,0:T(8,128)(2,1)S(1)} %slice.212), channel_id=1, source_target_pairs={{1,0},{0,1},{3,2},{2,3},{5,4},{4,5},{7,6},{6,7},{9,8},{8,9},{11,10... | collective-permute-start | bytes 786440 | tf_op jit(solution)/shard_map/ppermute | solution.py:34
  167.3 9.2 %collective-permute-start.36 = (bf16[128,1024]{1,0:T(8,128)(2,1)S(1)}, bf16[128,1024]{1,0:T(8,128)(2,1)S(1)}, u32[]{:S(2)}, u32[]{:S(2)}) collective-permute-start(bf16[128,1024]{1,0:T(8,128)(2,1)S(1)} %fusion.110), channel_id=1, source_target_pairs={{24,0},{0,8},{8,16},{16,24},{25,1},{1,9},{9,17},{17,25},{26,2},{2,... | collective-permute-start | bytes 786440 | tf_op jit(solution)/shard_map/ppermute | solution.py:34
Sparse Core Ops, SparseCore 0:
  9.0 47.5 all-gather.2
  58.3 59.8 all-gather.4

commit v6 on v5

--- a/solution.py
+++ b/solution.py
@@ -76,7 +76,7 @@
 
     def step(masked, width, tile, carry):
         top, total, acc = carry
-        first_key = tile * width
+        first_key = tile * TILE
         at = pl.ds(pl.multiple_of(first_key, TILE), width)
         s = lax.dot_general(keys[at, :], q, (((1,), (1,)), ((), ())), preferred_element_type=f32)
         if masked:
@@ -99,15 +99,18 @@
     last = lax.rem(y + dy, 4) * 4 + z
     first = scalars[dy]
     clear = jnp.minimum(scalars[4 + dy], last)
-    big = 4
-    big_first = (clear + big - 1) // big
-    big_last = jnp.maximum(last // big, big_first)
-    middle = jnp.minimum(big_first * big, last)
-    one = functools.partial(step, False, TILE)
+    count = last - clear
     carry = lax.fori_loop(first, clear, functools.partial(step, True, TILE), carry)
-    carry = lax.fori_loop(clear, middle, one, carry)
-    carry = lax.fori_loop(big_first, big_last, functools.partial(step, False, big * TILE), carry)
-    carry = lax.fori_loop(jnp.maximum(big_last * big, middle), last, one, carry)
+    carry = lax.fori_loop(
+        0, count // 4, lambda i, carry: step(False, 4 * TILE, clear + 4 * i, carry), carry
+    )
+    rest = clear + count // 4 * 4
+    carry = lax.fori_loop(
+        0, lax.rem(count // 2, 2), lambda i, carry: step(False, 2 * TILE, rest, carry), carry
+    )
+    carry = lax.fori_loop(
+        0, lax.rem(count, 2), lambda i, carry: step(False, TILE, last - 1, carry), carry
+    )
     top, total, acc = step(True, TILE, last, carry)
     result = (acc / total).T.astype(bf16)
     for head in (0, 1):
@@ -272,6 +275,7 @@
         else:
             mixed[1] = before
         second = jnp.dot(heads, w_out[:, columns:], preferred_element_type=f32).astype(bf16)
+        heads, second = barrier((heads, second))
         second = second.reshape(len(tiles), 2, 128, columns)
         for i, dy in enumerate(tiles):
             seconds[dy] = second[i]
@@ -281,14 +285,12 @@
     def over_y(parts, dy):
         return receive(parts[dy], "y", -dy).astype(f32)
 
-    xh_first, arrived = {}, {}
-    for step, tiles in enumerate(groups):
+    arrived = {}
+    for tiles in ((2, 3), (1,), (0,)):
         got = receive(jnp.stack([seconds[dy][1] for dy in tiles]), "xh", 1)
-        if step == 1:
-            got, arrived = barrier((got, arrived))
         for i, dy in enumerate(tiles):
-            xh_first[dy] = (seconds[dy][0].astype(f32) + got[i].astype(f32)).astype(bf16)
-            arrived[dy] = over_y(xh_first, dy) if dy else xh_first[0].astype(f32)
+            both = seconds[dy][0].astype(f32) + got[i].astype(f32)
+            arrived[dy] = over_y({dy: both.astype(bf16)}, dy) if dy else both
 
     first = y_first[0].astype(f32) + over_y(y_first, 2) + over_y(y_first, 3) + over_y(y_first, 1)
     second = arrived[0] + arrived[1] + arrived[2] + arrived[3]

time: 185 us -> 185 us (level)
  waiting for transfers between devices: 64.4 us -> 58.2 us
  starting transfers between devices: 40.6 us -> 46.5 us
    ppermute x37 -> x38, waiting for transfers between devices: 63.6 us -> 57.4 us  [receive(): return lax.ppermute(value, axis, [((i + step) % n, i) for i in range(n)])]
    ppermute x37 -> x38, starting transfers between devices: 40.5 us -> 46.4 us  [receive(): return lax.ppermute(value, axis, [((i + step) % n, i) for i in range(n)])]
  transfers between devices with their start and end apart: 39 -> 40, of which waited for: 17 -> 19; matrix products, arithmetic and copies ran while one was open for 26% -> 26% of each run, Pallas kernels for 8% -> 9%
where the time goes in v6:
time: 185 us
  waiting for transfers between devices  58.2 us (31%)
  starting transfers between devices  46.5 us (25%)
  matrix products  23.1 us (12%)
  other arithmetic  21.1 us (11%)
  Pallas kernels  16.2 us (9%)
  between operations  14.1 us (8%)
  local copies, waits for them, and re-layouts  5.56 us (3%)
    ppermute x38, waiting for transfers between devices, receive(): return lax.ppermute(value, axis, [((i + step) % n, i) for i in range(n)])  57.4 us
    ppermute x38, starting transfers between devices, receive(): return lax.ppermute(value, axis, [((i + step) % n, i) for i in range(n)])  46.4 us
    pallas_call x2, Pallas kernels, attention(): pl.pallas_call(functools.partial(attention_kernel, tiles), grid=(len(tile...  16.2 us
    dot_general x8, matrix products, product(): return jnp.dot(rows, weight, preferred_element_type=f32)  15.8 us
    unnamed x8, other arithmetic  4.7 us
    dot_general x2, matrix products, shards(): jnp.dot(heads, w_out[:, columns:], preferred_element_type=f32).astype(bf16)  4.25 us
    reduce_sum x5, other arithmetic, shards(): early = [jnp.sum(piece * piece, axis=1) for piece in early]  4.07 us
  transfers between devices with their start and end apart: 40, of which 19 were waited for; matrix products, arithmetic and copies ran while one was open for 26% of the time, Pallas kernels for 9%

profile of v6, /device:TPU:96, one launch (start us, length us, event | category | flops | bytes accessed | tf_op | source)
XLA Modules:
  0.0 184.6 jit_solution(17682668163938153385)
XLA Ops:
  6.5 0.7 all-gather.3.cloned.1.call-update
  7.3 3.1 %collective-permute-start.3 = (bf16[128,2048]{1,0:T(8,128)(2,1)}, bf16[128,2048]{1,0:T(8,128)(2,1)S(1)}, u32[]{:S(2)}, u32[]{:S(2)}) collective-permute-start(bf16[128,2048]{1,0:T(8,128)(2,1)} %param.7), channel_id=1, source_target_pairs={{1,0},{0,1},{3,2},{2,3},{5,4},{4,5},{7,6},{6,7},{9,8},{8,9},{11,10... | collective-permute-start | bytes 1572872 | tf_op jit(solution)/shard_map/ppermute | solution.py:34
  10.4 3.0 %collective-permute-start = (bf16[128,2048]{1,0:T(8,128)(2,1)}, bf16[128,2048]{1,0:T(8,128)(2,1)}, u32[]{:S(2)}, u32[]{:S(2)}) collective-permute-start(bf16[128,2048]{1,0:T(8,128)(2,1)} %param.7), channel_id=1, source_target_pairs={{8,0},{16,8},{24,16},{0,24},{9,1},{17,9},{25,17},{1,25},{10,2},{18... | collective-permute-start | bytes 1572872 | tf_op jit(solution)/shard_map/ppermute | solution.py:34
  14.1 1.0 collective-permute-start.2
  15.1 1.2 fusion.73
  16.4 2.0 %fusion.104 = bf16[1024,2048]{1,0:T(8,128)(2,1)} fusion(bf16[128,2048]{1,0:T(8,128)(2,1)} %param.7, f32[2048]{0:T(1024)} %param.8), kind=kLoop, calls=%fused_computation.96 | loop fusion | flops 786431 | bytes 1056768
  18.4 4.3 %collective-permute-done.3 = bf16[128,2048]{1,0:T(8,128)(2,1)S(1)} collective-permute-done((bf16[128,2048]{1,0:T(8,128)(2,1)}, bf16[128,2048]{1,0:T(8,128)(2,1)S(1)}, u32[]{:S(2)}, u32[]{:S(2)}) %collective-permute-start.3) | collective-permute-done | bytes 524320 | tf_op jit(solution)/shard_map/ppermute | solution.py:34
  22.8 3.0 %collective-permute-start.4 = (bf16[128,2048]{1,0:T(8,128)(2,1)S(1)}, bf16[128,2048]{1,0:T(8,128)(2,1)S(1)}, u32[]{:S(2)}, u32[]{:S(2)}) collective-permute-start(bf16[128,2048]{1,0:T(8,128)(2,1)S(1)} %collective-permute-done.3), channel_id=1, source_target_pairs={{8,0},{16,8},{24,16},{0,24},{9,1},{17,9},{25,17},{1,25},{10,2},{18... | collective-permute-start | bytes 1572872 | tf_op jit(solution)/shard_map/ppermute | solution.py:34
  26.5 0.9 convert_reduce_fusion
  27.8 1.7 constant_dynamic-slice_fusion.2
  29.5 1.1 pad_maximum_fusion
  31.0 1.9 %multiply_cosine_fusion = (f32[2,512,64]{2,1,0:T(8,128)S(1)}, f32[2,512,64]{2,1,0:T(8,128)S(1)}, f32[2,512,64]{2,1,0:T(8,128)S(1)}) fusion(f32[64]{0:T(128)S(1)} %multiply_exponential_fusion, f32[2,512]{1,0:T(2,128)S(1)} %get-tuple-element.118), kind=kLoop, calls=%fused_computation.88 | loop fusion | flops 131072 | bytes 790784 | tf_op jit(solution)/shard_map/cos | solution.py:184
  32.9 4.3 %collective-permute-done = bf16[128,2048]{1,0:T(8,128)(2,1)} collective-permute-done((bf16[128,2048]{1,0:T(8,128)(2,1)}, bf16[128,2048]{1,0:T(8,128)(2,1)}, u32[]{:S(2)}, u32[]{:S(2)}) %collective-permute-start) | collective-permute-done | bytes 524320 | tf_op jit(solution)/shard_map/ppermute | solution.py:34
  37.3 1.2 fusion.75
  38.5 1.3 pad_maximum_fusion.6
  39.8 1.1 fusion.103
  41.9 1.2 fusion.79
  43.1 1.1 fusion.101
  44.4 2.6 %collective-permute-done.4 = bf16[128,2048]{1,0:T(8,128)(2,1)S(1)} collective-permute-done((bf16[128,2048]{1,0:T(8,128)(2,1)S(1)}, bf16[128,2048]{1,0:T(8,128)(2,1)S(1)}, u32[]{:S(2)}, u32[]{:S(2)}) %collective-permute-start.4) | collective-permute-done | bytes 524320 | tf_op jit(solution)/shard_map/ppermute | solution.py:34
  47.0 4.7 %collective-permute-done.5 = bf16[128,2048]{1,0:T(8,128)(2,1)S(1)} collective-permute-done((bf16[128,2048]{1,0:T(8,128)(2,1)S(1)}, bf16[128,2048]{1,0:T(8,128)(2,1)S(1)}, u32[]{:S(2)}, u32[]{:S(2)}) %collective-permute-start.5) | collective-permute-done | bytes 524320 | tf_op jit(solution)/shard_map/ppermute | solution.py:34
  52.0 1.1 fusion.97
  53.1 1.9 %fusion.66 = bf16[512,256]{1,0:T(8,128)(2,1)} fusion(bf16[2048,256]{1,0:T(8,128)(2,1)S(1)} %pad_maximum_fusion.1, bf16[1024,2048]{1,0:T(8,128)(2,1)S(1)} %fusion.97, s32[]{:T(128)S(6)} %select_n.194), kind=kOutput, calls=%fused_computation.55 | convolution fusion | flops 537001984 | bytes 3407876 | tf_op jit(solution)/shard_map/dot_general | solution.py:218
  55.3 1.3 fusion.87
  58.4 3.4 %add_convert_fusion.3 = bf16[512,256]{1,0:T(8,128)(2,1)} fusion(bf16[512,256]{1,0:T(8,128)(2,1)S(1)} %collective-permute-done.7, bf16[2048,256]{1,0:T(8,128)(2,1)} %copy-done.1, bf16[1024,2048]{1,0:T(8,128)(2,1)} %copy-done.7, s32[]{:T(128)S(6)} %select_n.191), kind=kOutput, calls=%fused_computation.115 | convolution fusion | flops 537264128 | bytes 3670020 | tf_op jit(solution)/shard_map/dot_general | solution.py:218
  62.5 0.7 fusion.69
  63.3 1.7 collective-permute-start.10
  65.5 3.9 %convolution_convert_fusion.1 = bf16[1024,256]{1,0:T(8,128)(2,1)S(1)} fusion(bf16[1024,2048]{1,0:T(8,128)(2,1)} %copy-done.7, bf16[4,2048,256]{2,1,0:T(8,128)(2,1)} %bitcast.137, s32[]{:T(128)S(6)} %select_n.195), kind=kOutput, calls=%fused_computation.49 | convolution fusion | flops 1074003968 | bytes 5767172 | tf_op jit(solution)/shard_map/dot_general | solution.py:218
  69.4 2.6 %convolution_convert_fusion = bf16[1024,256]{1,0:T(8,128)(2,1)S(1)} fusion(bf16[1024,2048]{1,0:T(8,128)(2,1)S(1)} %copy-done.9, bf16[4,2048,256]{2,1,0:T(8,128)(2,1)} %bitcast.138, s32[]{:T(128)S(6)} %select_n.196), kind=kOutput, calls=%fused_computation.48 | convolution fusion | flops 1074003968 | bytes 5767172 | tf_op jit(solution)/shard_map/dot_general | solution.py:218
  72.2 0.7 fusion.63
  74.2 2.6 %collective-permute-start.14 = (bf16[2,512,128]{2,1,0:T(8,128)(2,1)S(1)}, bf16[2,512,128]{2,1,0:T(8,128)(2,1)S(1)}, u32[]{:S(2)}, u32[]{:S(2)}) collective-permute-start(bf16[2,512,128]{2,1,0:T(8,128)(2,1)S(1)} %pad_maximum_fusion.8.m0), channel_id=1, source_target_pairs={{6,0},{0,2},{2,4},{4,6},{7,1},{1,3},{3,5},{5,7},{14,8},{8,10},{10,... | collective-permute-start | bytes 786440 | tf_op jit(solution)/shard_map/ppermute | solution.py:34
  76.8 1.3 fusion.26
  78.1 1.5 collective-permute-start.17
  79.5 1.3 fusion.88
  81.1 0.9 add_convert_fusion.home0.home1
  82.1 10.1 %collective-permute-done.12.m1 = bf16[2,512,128]{2,1,0:T(8,128)(2,1)S(1)} collective-permute-done((bf16[2,512,128]{2,1,0:T(8,128)(2,1)S(1)}, bf16[2,512,128]{2,1,0:T(8,128)(2,1)S(1)}, u32[]{:S(2)}, u32[]{:S(2)}) %collective-permute-start.12) | collective-permute-done | bytes 262176 | tf_op jit(solution)/shard_map/ppermute | solution.py:34
  92.1 5.8 %collective-permute-done.13.m2 = bf16[2,512,128]{2,1,0:T(8,128)(2,1)S(1)} collective-permute-done((bf16[2,512,128]{2,1,0:T(8,128)(2,1)S(1)}, bf16[2,512,128]{2,1,0:T(8,128)(2,1)S(1)}, u32[]{:S(2)}, u32[]{:S(2)}) %collective-permute-start.13) | collective-permute-done | bytes 262176 | tf_op jit(solution)/shard_map/ppermute | solution.py:34
  97.9 3.5 %collective-permute-done.14.m3 = bf16[2,512,128]{2,1,0:T(8,128)(2,1)S(1)} collective-permute-done((bf16[2,512,128]{2,1,0:T(8,128)(2,1)S(1)}, bf16[2,512,128]{2,1,0:T(8,128)(2,1)S(1)}, u32[]{:S(2)}, u32[]{:S(2)}) %collective-permute-start.14) | collective-permute-done | bytes 262176 | tf_op jit(solution)/shard_map/ppermute | solution.py:34
  102.1 1.1 copy.16.scale0.scale1
  104.1 0.7 copy-done.19
  104.8 9.3 %shard_map.73 = bf16[2,2,128,256]{3,2,1,0:T(8,128)(2,1)} custom-call(s32[12]{0:T(128)} %concatenate.51.scalars, bf16[1024,256]{1,0:T(8,128)(2,1)} %add_convert_fusion.home0.home1, bf16[1024,256]{1,0:T(8,128)(2,1)} %add_convert_fusion.home0.home1, bf16[1024,256]{1,0:T(8,128)(2,1)} %copy-done.12, bf16[1024,256]{1,0:T(8,128)(2,1)} %copy-done.12, ...), custom_call_target="tpu_custom_call" | custom-call | flops 2000000000 | bytes 4194304 | tf_op jit(solution)/shard_map/pallas_call | solution.py:130
  114.1 1.5 collective-permute-start.22
  115.6 6.9 %shard_map.74 = bf16[2,2,128,256]{3,2,1,0:T(8,128)(2,1)} custom-call(s32[12]{0:T(128)} %concatenate.51.scalars, bf16[1024,256]{1,0:T(8,128)(2,1)} %add_convert_fusion.home0.home1, bf16[1024,256]{1,0:T(8,128)(2,1)} %add_convert_fusion.home0.home1, bf16[1024,256]{1,0:T(8,128)(2,1)} %copy-done.12, bf16[1024,256]{1,0:T(8,128)(2,1)} %copy-done.12, ...), custom_call_target="tpu_custom_call" | custom-call | flops 2000000000 | bytes 4194304 | tf_op jit(solution)/shard_map/pallas_call | solution.py:130
  123.0 1.3 collective-permute-start.24
  124.9 3.0 %fusion.12 = bf16[512,1024]{1,0:T(8,128)(2,1)S(1)} fusion(bf16[1024,2048]{1,0:T(8,128)(2,1)} %all-gather.5.cloned.1.call-done, bf16[512,256]{1,0:T(8,128)(2,1)S(1)} %get-tuple-element.108, bf16[512,256]{1,0:T(8,128)(2,1)S(1)} %get-tuple-element.109, bf16[512,256]{1,0:T(8,128)(2,1)S(1)} %get-tuple-element.110, bf16[512,256]{1,0:T(8,128)(2,1)S(1)} %get-tuple-element.107), kind=kOutput, calls=%fused_computation.12 | convolution fusion | flops 1078460416 | bytes 4194304 | tf_op jit(solution)/shard_map/dot_general | solution.py:277
  127.9 0.7 fusion.27
  128.6 0.7 fusion.30
  129.4 2.4 %collective-permute-done.24 = bf16[512,256]{1,0:T(8,128)(2,1)S(1)} collective-permute-done((bf16[512,256]{1,0:T(8,128)(2,1)}, bf16[512,256]{1,0:T(8,128)(2,1)S(1)}, u32[]{:S(2)}, u32[]{:S(2)}) %collective-permute-start.24) | collective-permute-done | bytes 262176 | tf_op jit(solution)/shard_map/ppermute | solution.py:34
  131.9 2.7 %collective-permute-start.35 = (bf16[2,128,1024]{2,1,0:T(8,128)(2,1)S(1)}, bf16[2,128,1024]{2,1,0:T(8,128)(2,1)S(1)}, u32[]{:S(2)}, u32[]{:S(2)}) collective-permute-start(bf16[2,128,1024]{2,1,0:T(8,128)(2,1)S(1)} %pad_maximum_fusion.4), channel_id=1, source_target_pairs={{1,0},{0,1},{3,2},{2,3},{5,4},{4,5},{7,6},{6,7},{9,8},{8,9},{11,10... | collective-permute-start | bytes 1572872 | tf_op jit(solution)/shard_map/ppermute | solution.py:34
  134.7 4.2 %collective-permute-start.29 = (bf16[256,1024]{1,0:T(8,128)(2,1)S(1)}, bf16[256,1024]{1,0:T(8,128)(2,1)S(1)}, u32[]{:S(2)}, u32[]{:S(2)}) collective-permute-start(bf16[256,1024]{1,0:T(8,128)(2,1)S(1)} %fusion.30), channel_id=1, source_target_pairs={{8,0},{16,8},{24,16},{0,24},{9,1},{17,9},{25,17},{1,25},{10,2},{18... | collective-permute-start | bytes 1572872 | tf_op jit(solution)/shard_map/ppermute | solution.py:34
  139.2 1.3 fusion.15
  140.5 0.7 fusion.36
  141.2 0.9 collective-permute-start.30
  142.1 1.6 collective-permute-start.33
  143.8 4.4 %collective-permute-done.35 = bf16[2,128,1024]{2,1,0:T(8,128)(2,1)S(1)} collective-permute-done((bf16[2,128,1024]{2,1,0:T(8,128)(2,1)S(1)}, bf16[2,128,1024]{2,1,0:T(8,128)(2,1)S(1)}, u32[]{:S(2)}, u32[]{:S(2)}) %collective-permute-start.35) | collective-permute-done | bytes 524320 | tf_op jit(solution)/shard_map/ppermute | solution.py:34
  148.2 2.7 %collective-permute-start.32 = (bf16[1,128,1024]{2,1,0:T(8,128)(2,1)S(1)}, bf16[1,128,1024]{2,1,0:T(8,128)(2,1)S(1)}, u32[]{:S(2)}, u32[]{:S(2)}) collective-permute-start(bf16[1,128,1024]{2,1,0:T(8,128)(2,1)S(1)} %get-tuple-element.99), channel_id=1, source_target_pairs={{1,0},{0,1},{3,2},{2,3},{5,4},{4,5},{7,6},{6,7},{9,8},{8,9},{11,10... | collective-permute-start | bytes 786440 | tf_op jit(solution)/shard_map/ppermute | solution.py:34
  151.1 2.8 %collective-permute-done.33 = bf16[1,128,1024]{2,1,0:T(8,128)(2,1)S(1)} collective-permute-done((bf16[1,128,1024]{2,1,0:T(8,128)(2,1)S(1)}, bf16[1,128,1024]{2,1,0:T(8,128)(2,1)S(1)}, u32[]{:S(2)}, u32[]{:S(2)}) %collective-permute-start.33) | collective-permute-done | bytes 262176 | tf_op jit(solution)/shard_map/ppermute | solution.py:34
  153.9 4.9 %collective-permute-start.37 = (bf16[128,1024]{1,0:T(8,128)(2,1)S(1)}, bf16[128,1024]{1,0:T(8,128)(2,1)S(1)}, u32[]{:S(2)}, u32[]{:S(2)}) collective-permute-start(bf16[128,1024]{1,0:T(8,128)(2,1)S(1)} %get-tuple-element.112), channel_id=1, source_target_pairs={{8,0},{16,8},{24,16},{0,24},{9,1},{17,9},{25,17},{1,25},{10,2},{18... | collective-permute-start | bytes 786440 | tf_op jit(solution)/shard_map/ppermute | solution.py:34
  158.8 3.6 %collective-permute-done.29 = bf16[256,1024]{1,0:T(8,128)(2,1)S(1)} collective-permute-done((bf16[256,1024]{1,0:T(8,128)(2,1)S(1)}, bf16[256,1024]{1,0:T(8,128)(2,1)S(1)}, u32[]{:S(2)}, u32[]{:S(2)}) %collective-permute-start.29) | collective-permute-done | bytes 524320 | tf_op jit(solution)/shard_map/ppermute | solution.py:34
  162.4 4.5 %collective-permute-start.34 = (bf16[128,1024]{1,0:T(8,128)(2,1)S(1)}, bf16[128,1024]{1,0:T(8,128)(2,1)S(1)}, u32[]{:S(2)}, u32[]{:S(2)}) collective-permute-start(bf16[128,1024]{1,0:T(8,128)(2,1)S(1)} %fusion.106), channel_id=1, source_target_pairs={{24,0},{0,8},{8,16},{16,24},{25,1},{1,9},{9,17},{17,25},{26,2},{2,... | collective-permute-start | bytes 786440 | tf_op jit(solution)/shard_map/ppermute | solution.py:34
  167.0 0.9 fusion.48
  167.9 1.6 collective-permute-start.31
  169.5 3.4 %collective-permute-done.37 = bf16[128,1024]{1,0:T(8,128)(2,1)S(1)} collective-permute-done((bf16[128,1024]{1,0:T(8,128)(2,1)S(1)}, bf16[128,1024]{1,0:T(8,128)(2,1)S(1)}, u32[]{:S(2)}, u32[]{:S(2)}) %collective-permute-start.37) | collective-permute-done | bytes 262176 | tf_op jit(solution)/shard_map/ppermute | solution.py:34
  173.1 3.5 %collective-permute-done.34 = bf16[128,1024]{1,0:T(8,128)(2,1)S(1)} collective-permute-done((bf16[128,1024]{1,0:T(8,128)(2,1)S(1)}, bf16[128,1024]{1,0:T(8,128)(2,1)S(1)}, u32[]{:S(2)}, u32[]{:S(2)}) %collective-permute-start.34) | collective-permute-done | bytes 262176 | tf_op jit(solution)/shard_map/ppermute | solution.py:34
  176.9 0.8 pad_maximum_fusion.5
  (142 shorter events, 12.5 us)
Async XLA Ops:
  6.5 59.0 %all-gather.3.cloned.1.call-start = ((), (), s32[]{:S(2)}) async-start(), calls=%async_computation | async-start | bytes 5242880 | tf_op jit(solution)/shard_map/all_gather | solution.py:165
  7.3 117.6 %all-gather.5.cloned.1.call-start = ((), (), s32[]{:S(2)}) async-start(), calls=%async_computation.1 | async-start | bytes 5242880 | tf_op jit(solution)/shard_map/all_gather | solution.py:166
  7.3 15.5 %collective-permute-start.3 = (bf16[128,2048]{1,0:T(8,128)(2,1)}, bf16[128,2048]{1,0:T(8,128)(2,1)S(1)}, u32[]{:S(2)}, u32[]{:S(2)}) collective-permute-start(bf16[128,2048]{1,0:T(8,128)(2,1)} %param.7), channel_id=1, source_target_pairs={{1,0},{0,1},{3,2},{2,3},{5,4},{4,5},{7,6},{6,7},{9,8},{8,9},{11,10... | collective-permute-start | bytes 1572872 | tf_op jit(solution)/shard_map/ppermute | solution.py:34
  10.4 26.9 %collective-permute-start = (bf16[128,2048]{1,0:T(8,128)(2,1)}, bf16[128,2048]{1,0:T(8,128)(2,1)}, u32[]{:S(2)}, u32[]{:S(2)}) collective-permute-start(bf16[128,2048]{1,0:T(8,128)(2,1)} %param.7), channel_id=1, source_target_pairs={{8,0},{16,8},{24,16},{0,24},{9,1},{17,9},{25,17},{1,25},{10,2},{18... | collective-permute-start | bytes 1572872 | tf_op jit(solution)/shard_map/ppermute | solution.py:34
  13.4 27.6 %collective-permute-start.1 = (bf16[128,2048]{1,0:T(8,128)(2,1)}, bf16[128,2048]{1,0:T(8,128)(2,1)S(1)}, u32[]{:S(2)}, u32[]{:S(2)}) collective-permute-start(bf16[128,2048]{1,0:T(8,128)(2,1)} %param.7), channel_id=1, source_target_pairs={{16,0},{24,8},{0,16},{8,24},{17,1},{25,9},{1,17},{9,25},{18,2},{26... | collective-permute-start | bytes 1572872 | tf_op jit(solution)/shard_map/ppermute | solution.py:34
  14.1 27.8 %collective-permute-start.2 = (bf16[128,2048]{1,0:T(8,128)(2,1)}, bf16[128,2048]{1,0:T(8,128)(2,1)}, u32[]{:S(2)}, u32[]{:S(2)}) collective-permute-start(bf16[128,2048]{1,0:T(8,128)(2,1)} %param.7), channel_id=1, source_target_pairs={{24,0},{0,8},{8,16},{16,24},{25,1},{1,9},{9,17},{17,25},{26,2},{2,... | collective-permute-start | bytes 1572872 | tf_op jit(solution)/shard_map/ppermute | solution.py:34
  22.8 24.2 %collective-permute-start.4 = (bf16[128,2048]{1,0:T(8,128)(2,1)S(1)}, bf16[128,2048]{1,0:T(8,128)(2,1)S(1)}, u32[]{:S(2)}, u32[]{:S(2)}) collective-permute-start(bf16[128,2048]{1,0:T(8,128)(2,1)S(1)} %collective-permute-done.3), channel_id=1, source_target_pairs={{8,0},{16,8},{24,16},{0,24},{9,1},{17,9},{25,17},{1,25},{10,2},{18... | collective-permute-start | bytes 1572872 | tf_op jit(solution)/shard_map/ppermute | solution.py:34
  25.8 26.0 %collective-permute-start.6 = (bf16[128,2048]{1,0:T(8,128)(2,1)S(1)}, bf16[128,2048]{1,0:T(8,128)(2,1)}, u32[]{:S(2)}, u32[]{:S(2)}) collective-permute-start(bf16[128,2048]{1,0:T(8,128)(2,1)S(1)} %collective-permute-done.3), channel_id=1, source_target_pairs={{24,0},{0,8},{8,16},{16,24},{25,1},{1,9},{9,17},{17,25},{26,2},{2,... | collective-permute-start | bytes 1572872 | tf_op jit(solution)/shard_map/ppermute | solution.py:34
  30.6 9.2 %copy-start.2 = (f32[2048]{0:T(1024)S(1)}, f32[2048]{0:T(1024)}, u32[]{:S(2)}) copy-start(f32[2048]{0:T(1024)} %param.8) | copy-start | bytes 24580
  30.9 9.0 %copy-start.6 = (bf16[1024,2048]{1,0:T(8,128)(2,1)S(1)}, bf16[1024,2048]{1,0:T(8,128)(2,1)}, u32[]{:S(2)}) copy-start(bf16[1024,2048]{1,0:T(8,128)(2,1)} %fusion.104) | copy-start | bytes 12582916
  31.0 22.1 %copy-start.1 = (bf16[2048,256]{1,0:T(8,128)(2,1)}, bf16[2048,256]{1,0:T(8,128)(2,1)S(1)}, u32[]{:S(2)}) copy-start(bf16[2048,256]{1,0:T(8,128)(2,1)S(1)} %pad_maximum_fusion.1) | copy-start | bytes 3145732
  41.0 10.8 %collective-permute-start.5 = (bf16[128,2048]{1,0:T(8,128)(2,1)S(1)}, bf16[128,2048]{1,0:T(8,128)(2,1)S(1)}, u32[]{:S(2)}, u32[]{:S(2)}) collective-permute-start(bf16[128,2048]{1,0:T(8,128)(2,1)S(1)} %collective-permute-done.1), channel_id=1, source_target_pairs={{1,0},{0,1},{3,2},{2,3},{5,4},{4,5},{7,6},{6,7},{9,8},{8,9},{11,10... | collective-permute-start | bytes 1572872 | tf_op jit(solution)/shard_map/ppermute | solution.py:34
  53.1 2.2 %copy-start.7 = (bf16[1024,2048]{1,0:T(8,128)(2,1)}, bf16[1024,2048]{1,0:T(8,128)(2,1)S(1)}, u32[]{:S(2)}) copy-start(bf16[1024,2048]{1,0:T(8,128)(2,1)S(1)} %fusion.97) | copy-start | bytes 12582916
  55.0 7.4 %copy-start = (bf16[2048,256]{1,0:T(8,128)(2,1)S(1)}, bf16[2048,256]{1,0:T(8,128)(2,1)}, u32[]{:S(2)}) copy-start(bf16[2048,256]{1,0:T(8,128)(2,1)} %pad_maximum_fusion) | copy-start | bytes 3145732
  55.0 3.4 %collective-permute-start.7 = (bf16[512,256]{1,0:T(8,128)(2,1)}, bf16[512,256]{1,0:T(8,128)(2,1)S(1)}, u32[]{:S(2)}, u32[]{:S(2)}) collective-permute-start(bf16[512,256]{1,0:T(8,128)(2,1)} %fusion.66), channel_id=1, source_target_pairs={{32,0},{0,32},{33,1},{1,33},{34,2},{2,34},{35,3},{3,35},{36,4},{4,... | collective-permute-start | bytes 786440 | tf_op jit(solution)/shard_map/ppermute | solution.py:34
  56.6 1.8 collective-permute-start.8
  58.4 4.1 %copy-start.8 = (bf16[1024,2048]{1,0:T(8,128)(2,1)S(1)}, bf16[1024,2048]{1,0:T(8,128)(2,1)}, u32[]{:S(2)}) copy-start(bf16[1024,2048]{1,0:T(8,128)(2,1)} %copy-done.7) | copy-start | bytes 12582916
  61.9 3.6 %collective-permute-start.11 = (f32[8,128]{1,0:T(8,128)S(1)}, f32[8,128]{1,0:T(8,128)S(1)}, u32[]{:S(2)}, u32[]{:S(2)}) collective-permute-start(f32[8,128]{1,0:T(8,128)S(1)} %add.154), channel_id=1, source_target_pairs={{64,0},{0,64},{65,1},{1,65},{66,2},{2,66},{67,3},{3,67},{68,4},{4,... | collective-permute-start | bytes 12296 | tf_op jit(solution)/shard_map/ppermute | solution.py:34
  63.2 9.0 %collective-permute-start.9 = (bf16[512,256]{1,0:T(8,128)(2,1)S(1)}, bf16[512,256]{1,0:T(8,128)(2,1)S(1)}, u32[]{:S(2)}, u32[]{:S(2)}) collective-permute-start(bf16[512,256]{1,0:T(8,128)(2,1)S(1)} %fusion.69), channel_id=1, source_target_pairs={{32,0},{0,32},{33,1},{1,33},{34,2},{2,34},{35,3},{3,35},{36,4},{4,... | collective-permute-start | bytes 786440 | tf_op jit(solution)/shard_map/ppermute | solution.py:34
  63.3 8.9 %collective-permute-start.10 = (bf16[512,256]{1,0:T(8,128)(2,1)}, bf16[512,256]{1,0:T(8,128)(2,1)S(1)}, u32[]{:S(2)}, u32[]{:S(2)}) collective-permute-start(bf16[512,256]{1,0:T(8,128)(2,1)} %add_convert_fusion.3), channel_id=1, source_target_pairs={{64,0},{0,64},{65,1},{1,65},{66,2},{2,66},{67,3},{3,67},{68,4},{4,... | collective-permute-start | bytes 786440 | tf_op jit(solution)/shard_map/ppermute | solution.py:34
  65.5 3.9 %copy-start.9 = (bf16[1024,2048]{1,0:T(8,128)(2,1)S(1)}, bf16[1024,2048]{1,0:T(8,128)(2,1)}, u32[]{:S(2)}) copy-start(bf16[1024,2048]{1,0:T(8,128)(2,1)} %copy-done.7) | copy-start | bytes 12582916
  72.2 4.6 %collective-permute-start.15 = (bf16[1024,256]{1,0:T(8,128)(2,1)S(1)}, bf16[1024,256]{1,0:T(8,128)(2,1)S(1)}, u32[]{:S(2)}, u32[]{:S(2)}) collective-permute-start(bf16[1024,256]{1,0:T(8,128)(2,1)S(1)} %convolution_convert_fusion.1), channel_id=1, source_target_pairs={{32,0},{0,32},{33,1},{1,33},{34,2},{2,34},{35,3},{3,35},{36,4},{4,... | collective-permute-start | bytes 1572872 | tf_op jit(solution)/shard_map/ppermute | solution.py:34
  72.2 4.6 %copy-start.11 = (bf16[8192,256]{1,0:T(8,128)(2,1)S(1)}, bf16[8192,256]{1,0:T(8,128)(2,1)}, u32[]{:S(2)}) copy-start(bf16[8192,256]{1,0:T(8,128)(2,1)} %all-gather.3.cloned.1.call-done) | copy-start | bytes 12582916
  73.5 7.3 %copy-start.5 = (bf16[2,512,128]{2,1,0:T(8,128)(2,1)}, bf16[2,512,128]{2,1,0:T(8,128)(2,1)S(1)}, u32[]{:S(2)}) copy-start(bf16[2,512,128]{2,1,0:T(8,128)(2,1)S(1)} %pad_maximum_fusion.8.m0) | copy-start | bytes 786436
  73.5 18.7 %collective-permute-start.12 = (bf16[2,512,128]{2,1,0:T(8,128)(2,1)S(1)}, bf16[2,512,128]{2,1,0:T(8,128)(2,1)S(1)}, u32[]{:S(2)}, u32[]{:S(2)}) collective-permute-start(bf16[2,512,128]{2,1,0:T(8,128)(2,1)S(1)} %pad_maximum_fusion.8.m0), channel_id=1, source_target_pairs={{2,0},{4,2},{6,4},{0,6},{3,1},{5,3},{7,5},{1,7},{10,8},{12,10},{14... | collective-permute-start | bytes 786440 | tf_op jit(solution)/shard_map/ppermute | solution.py:34
  73.9 24.0 %collective-permute-start.13 = (bf16[2,512,128]{2,1,0:T(8,128)(2,1)S(1)}, bf16[2,512,128]{2,1,0:T(8,128)(2,1)S(1)}, u32[]{:S(2)}, u32[]{:S(2)}) collective-permute-start(bf16[2,512,128]{2,1,0:T(8,128)(2,1)S(1)} %pad_maximum_fusion.8.m0), channel_id=1, source_target_pairs={{4,0},{6,2},{0,4},{2,6},{5,1},{7,3},{1,5},{3,7},{12,8},{14,10},{8,... | collective-permute-start | bytes 786440 | tf_op jit(solution)/shard_map/ppermute | solution.py:34
  74.2 27.2 %collective-permute-start.14 = (bf16[2,512,128]{2,1,0:T(8,128)(2,1)S(1)}, bf16[2,512,128]{2,1,0:T(8,128)(2,1)S(1)}, u32[]{:S(2)}, u32[]{:S(2)}) collective-permute-start(bf16[2,512,128]{2,1,0:T(8,128)(2,1)S(1)} %pad_maximum_fusion.8.m0), channel_id=1, source_target_pairs={{6,0},{0,2},{2,4},{4,6},{7,1},{1,3},{3,5},{5,7},{14,8},{8,10},{10,... | collective-permute-start | bytes 786440 | tf_op jit(solution)/shard_map/ppermute | solution.py:34
  76.8 4.0 %collective-permute-start.16 = (bf16[1024,256]{1,0:T(8,128)(2,1)S(1)}, bf16[1024,256]{1,0:T(8,128)(2,1)S(1)}, u32[]{:S(2)}, u32[]{:S(2)}) collective-permute-start(bf16[1024,256]{1,0:T(8,128)(2,1)S(1)} %convolution_convert_fusion), channel_id=1, source_target_pairs={{32,0},{0,32},{33,1},{1,33},{34,2},{2,34},{35,3},{3,35},{36,4},{4,... | collective-permute-start | bytes 1572872 | tf_op jit(solution)/shard_map/ppermute | solution.py:34
  78.1 23.3 %collective-permute-start.17 = (bf16[1024,256]{1,0:T(8,128)(2,1)S(1)}, bf16[1024,256]{1,0:T(8,128)(2,1)S(1)}, u32[]{:S(2)}, u32[]{:S(2)}) collective-permute-start(bf16[1024,256]{1,0:T(8,128)(2,1)S(1)} %fusion.26), channel_id=1, source_target_pairs={{64,0},{0,64},{65,1},{1,65},{66,2},{2,66},{67,3},{3,67},{68,4},{4,... | collective-permute-start | bytes 1572872 | tf_op jit(solution)/shard_map/ppermute | solution.py:34
  80.8 22.3 %collective-permute-start.18 = (bf16[2,512,128]{2,1,0:T(8,128)(2,1)S(1)}, bf16[2,512,128]{2,1,0:T(8,128)(2,1)S(1)}, u32[]{:S(2)}, u32[]{:S(2)}) collective-permute-start(bf16[2,512,128]{2,1,0:T(8,128)(2,1)S(1)} %pad_maximum_fusion.8.m0), channel_id=1, source_target_pairs={{32,0},{0,32},{33,1},{1,33},{34,2},{2,34},{35,3},{3,35},{36,4},{4,... | collective-permute-start | bytes 786440 | tf_op jit(solution)/shard_map/ppermute | solution.py:34
  92.1 11.6 %copy-start.13 = (bf16[2,512,128]{2,1,0:T(8,128)(2,1)}, bf16[2,512,128]{2,1,0:T(8,128)(2,1)S(1)}, u32[]{:S(2)}) copy-start(bf16[2,512,128]{2,1,0:T(8,128)(2,1)S(1)} %collective-permute-done.12.m1) | copy-start | bytes 786436
  97.9 5.8 %copy-start.14 = (bf16[2,512,128]{2,1,0:T(8,128)(2,1)}, bf16[2,512,128]{2,1,0:T(8,128)(2,1)S(1)}, u32[]{:S(2)}) copy-start(bf16[2,512,128]{2,1,0:T(8,128)(2,1)S(1)} %collective-permute-done.13.m2) | copy-start | bytes 786436
  101.4 2.4 %copy-start.15 = (bf16[2,512,128]{2,1,0:T(8,128)(2,1)}, bf16[2,512,128]{2,1,0:T(8,128)(2,1)S(1)}, u32[]{:S(2)}) copy-start(bf16[2,512,128]{2,1,0:T(8,128)(2,1)S(1)} %collective-permute-done.14.m3) | copy-start | bytes 786436
  101.4 2.4 %copy-start.12 = (bf16[1024,256]{1,0:T(8,128)(2,1)}, bf16[1024,256]{1,0:T(8,128)(2,1)S(1)}, u32[]{:S(2)}) copy-start(bf16[1024,256]{1,0:T(8,128)(2,1)S(1)} %collective-permute-done.17.far0.far1) | copy-start | bytes 1572868
  101.4 1.7 collective-permute-start.19
  101.5 1.9 %collective-permute-start.20 = (bf16[2,512,128]{2,1,0:T(8,128)(2,1)S(1)}, bf16[2,512,128]{2,1,0:T(8,128)(2,1)S(1)}, u32[]{:S(2)}, u32[]{:S(2)}) collective-permute-start(bf16[2,512,128]{2,1,0:T(8,128)(2,1)S(1)} %collective-permute-done.13.m2), channel_id=1, source_target_pairs={{32,0},{0,32},{33,1},{1,33},{34,2},{2,34},{35,3},{3,35},{36,4},{4,... | collective-permute-start | bytes 786440 | tf_op jit(solution)/shard_map/ppermute | solution.py:34
  102.0 1.8 collective-permute-start.21
  103.1 0.7 copy-start.16
  103.1 0.8 copy-start.17
  103.4 0.7 copy-start.18
  104.1 0.7 copy-start.19
  114.1 10.5 %copy-start.4 = (bf16[2,2,128,256]{3,2,1,0:T(8,128)(2,1)S(1)}, bf16[2,2,128,256]{3,2,1,0:T(8,128)(2,1)}, u32[]{:S(2)}) copy-start(bf16[2,2,128,256]{3,2,1,0:T(8,128)(2,1)} %shard_map.73) | copy-start | bytes 786436
  114.1 8.8 %collective-permute-start.22 = (bf16[512,256]{1,0:T(8,128)(2,1)}, bf16[512,256]{1,0:T(8,128)(2,1)S(1)}, u32[]{:S(2)}, u32[]{:S(2)}) collective-permute-start(bf16[512,256]{1,0:T(8,128)(2,1)} %bitcast.120), channel_id=1, source_target_pairs={{64,0},{0,64},{65,1},{1,65},{66,2},{2,66},{67,3},{3,67},{68,4},{4,... | collective-permute-start | bytes 786440 | tf_op jit(solution)/shard_map/ppermute | solution.py:34
  115.5 9.0 %collective-permute-start.25 = (bf16[512,256]{1,0:T(8,128)(2,1)}, bf16[512,256]{1,0:T(8,128)(2,1)S(1)}, u32[]{:S(2)}, u32[]{:S(2)}) collective-permute-start(bf16[512,256]{1,0:T(8,128)(2,1)} %bitcast.121), channel_id=1, source_target_pairs={{32,0},{0,32},{33,1},{1,33},{34,2},{2,34},{35,3},{3,35},{36,4},{4,... | collective-permute-start | bytes 786440 | tf_op jit(solution)/shard_map/ppermute | solution.py:34
  122.9 1.6 collective-permute-start.26
  123.0 8.8 %collective-permute-start.24 = (bf16[512,256]{1,0:T(8,128)(2,1)}, bf16[512,256]{1,0:T(8,128)(2,1)S(1)}, u32[]{:S(2)}, u32[]{:S(2)}) collective-permute-start(bf16[512,256]{1,0:T(8,128)(2,1)} %bitcast.118), channel_id=1, source_target_pairs={{64,0},{0,64},{65,1},{1,65},{66,2},{2,66},{67,3},{3,67},{68,4},{4,... | collective-permute-start | bytes 786440 | tf_op jit(solution)/shard_map/ppermute | solution.py:34
  124.3 14.6 %collective-permute-start.23 = (bf16[512,256]{1,0:T(8,128)(2,1)}, bf16[512,256]{1,0:T(8,128)(2,1)S(1)}, u32[]{:S(2)}, u32[]{:S(2)}) collective-permute-start(bf16[512,256]{1,0:T(8,128)(2,1)} %bitcast.119), channel_id=1, source_target_pairs={{32,0},{0,32},{33,1},{1,33},{34,2},{2,34},{35,3},{3,35},{36,4},{4,... | collective-permute-start | bytes 786440 | tf_op jit(solution)/shard_map/ppermute | solution.py:34
  124.9 3.0 %copy-start.10 = (bf16[1024,2048]{1,0:T(8,128)(2,1)S(1)}, bf16[1024,2048]{1,0:T(8,128)(2,1)}, u32[]{:S(2)}) copy-start(bf16[1024,2048]{1,0:T(8,128)(2,1)} %all-gather.5.cloned.1.call-done) | copy-start | bytes 12582916
  128.6 10.3 %copy-start.3 = (bf16[2,2,128,256]{3,2,1,0:T(8,128)(2,1)S(1)}, bf16[2,2,128,256]{3,2,1,0:T(8,128)(2,1)}, u32[]{:S(2)}) copy-start(bf16[2,2,128,256]{3,2,1,0:T(8,128)(2,1)} %shard_map.74) | copy-start | bytes 786436
  131.8 7.1 %collective-permute-start.27 = (bf16[512,256]{1,0:T(8,128)(2,1)S(1)}, bf16[512,256]{1,0:T(8,128)(2,1)S(1)}, u32[]{:S(2)}, u32[]{:S(2)}) collective-permute-start(bf16[512,256]{1,0:T(8,128)(2,1)S(1)} %collective-permute-done.24), channel_id=1, source_target_pairs={{32,0},{0,32},{33,1},{1,33},{34,2},{2,34},{35,3},{3,35},{36,4},{4,... | collective-permute-start | bytes 786440 | tf_op jit(solution)/shard_map/ppermute | solution.py:34
  131.9 16.3 %collective-permute-start.35 = (bf16[2,128,1024]{2,1,0:T(8,128)(2,1)S(1)}, bf16[2,128,1024]{2,1,0:T(8,128)(2,1)S(1)}, u32[]{:S(2)}, u32[]{:S(2)}) collective-permute-start(bf16[2,128,1024]{2,1,0:T(8,128)(2,1)S(1)} %pad_maximum_fusion.4), channel_id=1, source_target_pairs={{1,0},{0,1},{3,2},{2,3},{5,4},{4,5},{7,6},{6,7},{9,8},{8,9},{11,10... | collective-permute-start | bytes 1572872 | tf_op jit(solution)/shard_map/ppermute | solution.py:34
  134.7 27.7 %collective-permute-start.29 = (bf16[256,1024]{1,0:T(8,128)(2,1)S(1)}, bf16[256,1024]{1,0:T(8,128)(2,1)S(1)}, u32[]{:S(2)}, u32[]{:S(2)}) collective-permute-start(bf16[256,1024]{1,0:T(8,128)(2,1)S(1)} %fusion.30), channel_id=1, source_target_pairs={{8,0},{16,8},{24,16},{0,24},{9,1},{17,9},{25,17},{1,25},{10,2},{18... | collective-permute-start | bytes 1572872 | tf_op jit(solution)/shard_map/ppermute | solution.py:34
  138.9 23.5 %collective-permute-start.28 = (bf16[256,1024]{1,0:T(8,128)(2,1)S(1)}, bf16[256,1024]{1,0:T(8,128)(2,1)S(1)}, u32[]{:S(2)}, u32[]{:S(2)}) collective-permute-start(bf16[256,1024]{1,0:T(8,128)(2,1)S(1)} %fusion.27), channel_id=1, source_target_pairs={{16,0},{24,8},{0,16},{8,24},{17,1},{25,9},{1,17},{9,25},{18,2},{26... | collective-permute-start | bytes 1572872 | tf_op jit(solution)/shard_map/ppermute | solution.py:34
  141.2 25.8 %collective-permute-start.30 = (bf16[256,1024]{1,0:T(8,128)(2,1)S(1)}, bf16[256,1024]{1,0:T(8,128)(2,1)S(1)}, u32[]{:S(2)}, u32[]{:S(2)}) collective-permute-start(bf16[256,1024]{1,0:T(8,128)(2,1)S(1)} %fusion.36), channel_id=1, source_target_pairs={{24,0},{0,8},{8,16},{16,24},{25,1},{1,9},{9,17},{17,25},{26,2},{2,... | collective-permute-start | bytes 1572872 | tf_op jit(solution)/shard_map/ppermute | solution.py:34
  142.1 11.7 %collective-permute-start.33 = (bf16[1,128,1024]{2,1,0:T(8,128)(2,1)S(1)}, bf16[1,128,1024]{2,1,0:T(8,128)(2,1)S(1)}, u32[]{:S(2)}, u32[]{:S(2)}) collective-permute-start(bf16[1,128,1024]{2,1,0:T(8,128)(2,1)S(1)} %get-tuple-element.100), channel_id=1, source_target_pairs={{1,0},{0,1},{3,2},{2,3},{5,4},{4,5},{7,6},{6,7},{9,8},{8,9},{11,10... | collective-permute-start | bytes 786440 | tf_op jit(solution)/shard_map/ppermute | solution.py:34
  148.2 21.3 %collective-permute-start.32 = (bf16[1,128,1024]{2,1,0:T(8,128)(2,1)S(1)}, bf16[1,128,1024]{2,1,0:T(8,128)(2,1)S(1)}, u32[]{:S(2)}, u32[]{:S(2)}) collective-permute-start(bf16[1,128,1024]{2,1,0:T(8,128)(2,1)S(1)} %get-tuple-element.99), channel_id=1, source_target_pairs={{1,0},{0,1},{3,2},{2,3},{5,4},{4,5},{7,6},{6,7},{9,8},{8,9},{11,10... | collective-permute-start | bytes 786440 | tf_op jit(solution)/shard_map/ppermute | solution.py:34
  153.9 19.1 %collective-permute-start.37 = (bf16[128,1024]{1,0:T(8,128)(2,1)S(1)}, bf16[128,1024]{1,0:T(8,128)(2,1)S(1)}, u32[]{:S(2)}, u32[]{:S(2)}) collective-permute-start(bf16[128,1024]{1,0:T(8,128)(2,1)S(1)} %get-tuple-element.112), channel_id=1, source_target_pairs={{8,0},{16,8},{24,16},{0,24},{9,1},{17,9},{25,17},{1,25},{10,2},{18... | collective-permute-start | bytes 786440 | tf_op jit(solution)/shard_map/ppermute | solution.py:34
  162.4 10.7 %collective-permute-start.36 = (bf16[128,1024]{1,0:T(8,128)(2,1)S(1)}, bf16[128,1024]{1,0:T(8,128)(2,1)S(1)}, u32[]{:S(2)}, u32[]{:S(2)}) collective-permute-start(bf16[128,1024]{1,0:T(8,128)(2,1)S(1)} %get-tuple-element.111), channel_id=1, source_target_pairs={{16,0},{24,8},{0,16},{8,24},{17,1},{25,9},{1,17},{9,25},{18,2},{26... | collective-permute-start | bytes 786440 | tf_op jit(solution)/shard_map/ppermute | solution.py:34
  162.4 14.2 %collective-permute-start.34 = (bf16[128,1024]{1,0:T(8,128)(2,1)S(1)}, bf16[128,1024]{1,0:T(8,128)(2,1)S(1)}, u32[]{:S(2)}, u32[]{:S(2)}) collective-permute-start(bf16[128,1024]{1,0:T(8,128)(2,1)S(1)} %fusion.106), channel_id=1, source_target_pairs={{24,0},{0,8},{8,16},{16,24},{25,1},{1,9},{9,17},{17,25},{26,2},{2,... | collective-permute-start | bytes 786440 | tf_op jit(solution)/shard_map/ppermute | solution.py:34
  167.9 9.0 %collective-permute-start.31 = (bf16[128,1024]{1,0:T(8,128)(2,1)S(1)}, bf16[128,1024]{1,0:T(8,128)(2,1)S(1)}, u32[]{:S(2)}, u32[]{:S(2)}) collective-permute-start(bf16[128,1024]{1,0:T(8,128)(2,1)S(1)} %slice.192), channel_id=1, source_target_pairs={{1,0},{0,1},{3,2},{2,3},{5,4},{4,5},{7,6},{6,7},{9,8},{8,9},{11,10... | collective-permute-start | bytes 786440 | tf_op jit(solution)/shard_map/ppermute | solution.py:34
Sparse Core Ops, SparseCore 0:
  9.0 47.5 all-gather.2
  58.3 59.9 all-gather.4

commit v7 on v6

--- a/solution.py
+++ b/solution.py
@@ -292,9 +292,12 @@
             both = seconds[dy][0].astype(f32) + got[i].astype(f32)
             arrived[dy] = over_y({dy: both.astype(bf16)}, dy) if dy else both
 
-    first = y_first[0].astype(f32) + over_y(y_first, 2) + over_y(y_first, 3) + over_y(y_first, 1)
+    leaving = receive(y_first[2][128:], "y", -2).astype(f32)
+    staying = receive(y_first[2][:128], "y", -2).astype(f32)
+    near = y_first[0].astype(f32) + over_y(y_first, 3) + over_y(y_first, 1)
     second = arrived[0] + arrived[1] + arrived[2] + arrived[3]
-    first = first[:128] + receive(first[128:].astype(bf16), "xh", 1).astype(f32)
+    last = receive((near[128:] + leaving).astype(bf16), "xh", 1).astype(f32)
+    first = near[:128] + staying + last
     return jnp.concatenate([first, second], axis=1).astype(bf16)
 
 

time: 185 us -> 188 us (1.016); the launches traced: 185 us -> 185 us
  waiting for transfers between devices: 58.2 us -> 69 us
  starting transfers between devices: 46.5 us -> 37.9 us
    ppermute x38 -> x39, waiting for transfers between devices: 57.4 us -> 68.2 us  [receive(): return lax.ppermute(value, axis, [((i + step) % n, i) for i in range(n)])]
    ppermute x38 -> x39, starting transfers between devices: 46.4 us -> 37.9 us  [receive(): return lax.ppermute(value, axis, [((i + step) % n, i) for i in range(n)])]
  transfers between devices with their start and end apart: 40 -> 41, of which waited for: 19 -> 17; matrix products, arithmetic and copies ran while one was open for 26% -> 26% of each run, Pallas kernels for 9% -> 8%
where the time goes in v7:
time: 188 us; the launch traced here: 185 us
  waiting for transfers between devices  69 us (37%)
  starting transfers between devices  37.9 us (20%)
  matrix products  22.9 us (12%)
  other arithmetic  21.2 us (11%)
  Pallas kernels  14.8 us (8%)
  between operations  14.1 us (8%)
  local copies, waits for them, and re-layouts  5.58 us (3%)
    ppermute x39, waiting for transfers between devices, receive(): return lax.ppermute(value, axis, [((i + step) % n, i) for i in range(n)])  68.2 us
    ppermute x39, starting transfers between devices, receive(): return lax.ppermute(value, axis, [((i + step) % n, i) for i in range(n)])  37.9 us
    dot_general x8, matrix products, product(): return jnp.dot(rows, weight, preferred_element_type=f32)  15.8 us
    pallas_call x2, Pallas kernels, attention(): pl.pallas_call(functools.partial(attention_kernel, tiles), grid=(len(tile...  14.8 us
    unnamed x8, other arithmetic  4.69 us
    dot_general x2, matrix products, shards(): jnp.dot(heads, w_out[:, columns:], preferred_element_type=f32).astype(bf16)  4.25 us
    reduce_sum x5, other arithmetic, shards(): early = [jnp.sum(piece * piece, axis=1) for piece in early]  4.07 us
  transfers between devices with their start and end apart: 41, of which 17 were waited for; matrix products, arithmetic and copies ran while one was open for 26% of the time, Pallas kernels for 8%

profile of v7, /device:TPU:96, one launch (start us, length us, event | category | flops | bytes accessed | tf_op | source)
XLA Modules:
  0.0 185.5 jit_solution(307942838306443915)
XLA Ops:
  6.5 0.7 all-gather.3.cloned.1.call-update
  7.3 3.1 %collective-permute-start.3 = (bf16[128,2048]{1,0:T(8,128)(2,1)}, bf16[128,2048]{1,0:T(8,128)(2,1)S(1)}, u32[]{:S(2)}, u32[]{:S(2)}) collective-permute-start(bf16[128,2048]{1,0:T(8,128)(2,1)} %param.7), channel_id=1, source_target_pairs={{1,0},{0,1},{3,2},{2,3},{5,4},{4,5},{7,6},{6,7},{9,8},{8,9},{11,10... | collective-permute-start | bytes 1572872 | tf_op jit(solution)/shard_map/ppermute | solution.py:34
  10.4 3.0 %collective-permute-start = (bf16[128,2048]{1,0:T(8,128)(2,1)}, bf16[128,2048]{1,0:T(8,128)(2,1)}, u32[]{:S(2)}, u32[]{:S(2)}) collective-permute-start(bf16[128,2048]{1,0:T(8,128)(2,1)} %param.7), channel_id=1, source_target_pairs={{8,0},{16,8},{24,16},{0,24},{9,1},{17,9},{25,17},{1,25},{10,2},{18... | collective-permute-start | bytes 1572872 | tf_op jit(solution)/shard_map/ppermute | solution.py:34
  14.1 1.0 collective-permute-start.2
  15.1 1.2 fusion.70
  16.4 2.0 %fusion.101 = bf16[1024,2048]{1,0:T(8,128)(2,1)} fusion(bf16[128,2048]{1,0:T(8,128)(2,1)} %param.7, f32[2048]{0:T(1024)} %param.8), kind=kLoop, calls=%fused_computation.95 | loop fusion | flops 786431 | bytes 1056768
  18.4 4.4 %collective-permute-done.3 = bf16[128,2048]{1,0:T(8,128)(2,1)S(1)} collective-permute-done((bf16[128,2048]{1,0:T(8,128)(2,1)}, bf16[128,2048]{1,0:T(8,128)(2,1)S(1)}, u32[]{:S(2)}, u32[]{:S(2)}) %collective-permute-start.3) | collective-permute-done | bytes 524320 | tf_op jit(solution)/shard_map/ppermute | solution.py:34
  22.8 3.0 %collective-permute-start.4 = (bf16[128,2048]{1,0:T(8,128)(2,1)S(1)}, bf16[128,2048]{1,0:T(8,128)(2,1)S(1)}, u32[]{:S(2)}, u32[]{:S(2)}) collective-permute-start(bf16[128,2048]{1,0:T(8,128)(2,1)S(1)} %collective-permute-done.3), channel_id=1, source_target_pairs={{8,0},{16,8},{24,16},{0,24},{9,1},{17,9},{25,17},{1,25},{10,2},{18... | collective-permute-start | bytes 1572872 | tf_op jit(solution)/shard_map/ppermute | solution.py:34
  26.5 0.9 convert_reduce_fusion
  27.8 1.7 constant_dynamic-slice_fusion.2
  29.5 1.1 pad_maximum_fusion
  31.0 1.9 %multiply_cosine_fusion = (f32[2,512,64]{2,1,0:T(8,128)S(1)}, f32[2,512,64]{2,1,0:T(8,128)S(1)}, f32[2,512,64]{2,1,0:T(8,128)S(1)}) fusion(f32[64]{0:T(128)S(1)} %multiply_exponential_fusion, f32[2,512]{1,0:T(2,128)S(1)} %get-tuple-element.120), kind=kLoop, calls=%fused_computation.87 | loop fusion | flops 131072 | bytes 790784 | tf_op jit(solution)/shard_map/cos | solution.py:184
  32.9 4.4 %collective-permute-done = bf16[128,2048]{1,0:T(8,128)(2,1)} collective-permute-done((bf16[128,2048]{1,0:T(8,128)(2,1)}, bf16[128,2048]{1,0:T(8,128)(2,1)}, u32[]{:S(2)}, u32[]{:S(2)}) %collective-permute-start) | collective-permute-done | bytes 524320 | tf_op jit(solution)/shard_map/ppermute | solution.py:34
  37.3 1.2 fusion.72
  38.5 1.3 pad_maximum_fusion.6
  39.8 1.1 fusion.100
  41.9 1.2 fusion.76
  43.1 1.1 fusion.98
  44.4 2.6 %collective-permute-done.4 = bf16[128,2048]{1,0:T(8,128)(2,1)S(1)} collective-permute-done((bf16[128,2048]{1,0:T(8,128)(2,1)S(1)}, bf16[128,2048]{1,0:T(8,128)(2,1)S(1)}, u32[]{:S(2)}, u32[]{:S(2)}) %collective-permute-start.4) | collective-permute-done | bytes 524320 | tf_op jit(solution)/shard_map/ppermute | solution.py:34
  47.0 4.8 %collective-permute-done.5 = bf16[128,2048]{1,0:T(8,128)(2,1)S(1)} collective-permute-done((bf16[128,2048]{1,0:T(8,128)(2,1)S(1)}, bf16[128,2048]{1,0:T(8,128)(2,1)S(1)}, u32[]{:S(2)}, u32[]{:S(2)}) %collective-permute-start.5) | collective-permute-done | bytes 524320 | tf_op jit(solution)/shard_map/ppermute | solution.py:34
  52.0 1.1 fusion.94
  53.1 1.9 %fusion.63 = bf16[512,256]{1,0:T(8,128)(2,1)} fusion(bf16[2048,256]{1,0:T(8,128)(2,1)S(1)} %pad_maximum_fusion.1, bf16[1024,2048]{1,0:T(8,128)(2,1)S(1)} %fusion.94, s32[]{:T(128)S(6)} %select_n.194), kind=kOutput, calls=%fused_computation.54 | convolution fusion | flops 537001984 | bytes 3407876 | tf_op jit(solution)/shard_map/dot_general | solution.py:218
  55.4 1.3 fusion.84
  58.5 3.4 %add_convert_fusion.3 = bf16[512,256]{1,0:T(8,128)(2,1)} fusion(bf16[512,256]{1,0:T(8,128)(2,1)S(1)} %collective-permute-done.7, bf16[2048,256]{1,0:T(8,128)(2,1)} %copy-done.1, bf16[1024,2048]{1,0:T(8,128)(2,1)} %copy-done.7, s32[]{:T(128)S(6)} %select_n.191), kind=kOutput, calls=%fused_computation.116 | convolution fusion | flops 537264128 | bytes 3670020 | tf_op jit(solution)/shard_map/dot_general | solution.py:218
  62.5 0.7 fusion.66
  63.3 1.7 collective-permute-start.10
  65.5 3.9 %convolution_convert_fusion.1 = bf16[1024,256]{1,0:T(8,128)(2,1)S(1)} fusion(bf16[1024,2048]{1,0:T(8,128)(2,1)} %copy-done.7, bf16[4,2048,256]{2,1,0:T(8,128)(2,1)} %bitcast.137, s32[]{:T(128)S(6)} %select_n.195), kind=kOutput, calls=%fused_computation.48 | convolution fusion | flops 1074003968 | bytes 5767172 | tf_op jit(solution)/shard_map/dot_general | solution.py:218
  69.4 2.6 %convolution_convert_fusion = bf16[1024,256]{1,0:T(8,128)(2,1)S(1)} fusion(bf16[1024,2048]{1,0:T(8,128)(2,1)S(1)} %copy-done.9, bf16[4,2048,256]{2,1,0:T(8,128)(2,1)} %bitcast.138, s32[]{:T(128)S(6)} %select_n.196), kind=kOutput, calls=%fused_computation.47 | convolution fusion | flops 1074003968 | bytes 5767172 | tf_op jit(solution)/shard_map/dot_general | solution.py:218
  72.3 0.7 fusion.60
  74.2 2.6 %collective-permute-start.14 = (bf16[2,512,128]{2,1,0:T(8,128)(2,1)S(1)}, bf16[2,512,128]{2,1,0:T(8,128)(2,1)S(1)}, u32[]{:S(2)}, u32[]{:S(2)}) collective-permute-start(bf16[2,512,128]{2,1,0:T(8,128)(2,1)S(1)} %pad_maximum_fusion.8.m0), channel_id=1, source_target_pairs={{6,0},{0,2},{2,4},{4,6},{7,1},{1,3},{3,5},{5,7},{14,8},{8,10},{10,... | collective-permute-start | bytes 786440 | tf_op jit(solution)/shard_map/ppermute | solution.py:34
  76.8 1.3 fusion.26
  78.1 1.5 collective-permute-start.17
  79.6 1.3 fusion.85
  81.2 0.9 add_convert_fusion.home0.home1
  82.1 10.1 %collective-permute-done.12.m1 = bf16[2,512,128]{2,1,0:T(8,128)(2,1)S(1)} collective-permute-done((bf16[2,512,128]{2,1,0:T(8,128)(2,1)S(1)}, bf16[2,512,128]{2,1,0:T(8,128)(2,1)S(1)}, u32[]{:S(2)}, u32[]{:S(2)}) %collective-permute-start.12) | collective-permute-done | bytes 262176 | tf_op jit(solution)/shard_map/ppermute | solution.py:34
  92.2 5.8 %collective-permute-done.13.m2 = bf16[2,512,128]{2,1,0:T(8,128)(2,1)S(1)} collective-permute-done((bf16[2,512,128]{2,1,0:T(8,128)(2,1)S(1)}, bf16[2,512,128]{2,1,0:T(8,128)(2,1)S(1)}, u32[]{:S(2)}, u32[]{:S(2)}) %collective-permute-start.13) | collective-permute-done | bytes 262176 | tf_op jit(solution)/shard_map/ppermute | solution.py:34
  97.9 3.5 %collective-permute-done.14.m3 = bf16[2,512,128]{2,1,0:T(8,128)(2,1)S(1)} collective-permute-done((bf16[2,512,128]{2,1,0:T(8,128)(2,1)S(1)}, bf16[2,512,128]{2,1,0:T(8,128)(2,1)S(1)}, u32[]{:S(2)}, u32[]{:S(2)}) %collective-permute-start.14) | collective-permute-done | bytes 262176 | tf_op jit(solution)/shard_map/ppermute | solution.py:34
  102.1 1.0 copy.16.scale0.scale1
  104.1 0.7 copy-done.19
  104.8 9.2 %shard_map.73 = bf16[2,2,128,256]{3,2,1,0:T(8,128)(2,1)} custom-call(s32[12]{0:T(128)} %concatenate.51.scalars, bf16[1024,256]{1,0:T(8,128)(2,1)} %add_convert_fusion.home0.home1, bf16[1024,256]{1,0:T(8,128)(2,1)} %add_convert_fusion.home0.home1, bf16[1024,256]{1,0:T(8,128)(2,1)} %copy-done.12, bf16[1024,256]{1,0:T(8,128)(2,1)} %copy-done.12, ...), custom_call_target="tpu_custom_call" | custom-call | flops 2000000000 | bytes 4194304 | tf_op jit(solution)/shard_map/pallas_call | solution.py:130
  114.0 1.5 collective-permute-start.22
  115.4 5.6 %shard_map.74 = bf16[2,2,128,256]{3,2,1,0:T(8,128)(2,1)} custom-call(s32[12]{0:T(128)} %concatenate.51.scalars, bf16[1024,256]{1,0:T(8,128)(2,1)} %add_convert_fusion.home0.home1, bf16[1024,256]{1,0:T(8,128)(2,1)} %add_convert_fusion.home0.home1, bf16[1024,256]{1,0:T(8,128)(2,1)} %copy-done.12, bf16[1024,256]{1,0:T(8,128)(2,1)} %copy-done.12, ...), custom_call_target="tpu_custom_call" | custom-call | flops 2000000000 | bytes 4194304 | tf_op jit(solution)/shard_map/pallas_call | solution.py:130
  121.1 1.7 collective-permute-done.22
  122.8 1.4 collective-permute-start.24
  124.7 3.0 %fusion.12 = bf16[512,1024]{1,0:T(8,128)(2,1)S(1)} fusion(bf16[1024,2048]{1,0:T(8,128)(2,1)} %all-gather.5.cloned.1.call-done, bf16[512,256]{1,0:T(8,128)(2,1)S(1)} %get-tuple-element.108, bf16[512,256]{1,0:T(8,128)(2,1)S(1)} %get-tuple-element.109, bf16[512,256]{1,0:T(8,128)(2,1)S(1)} %get-tuple-element.110, bf16[512,256]{1,0:T(8,128)(2,1)S(1)} %get-tuple-element.107), kind=kOutput, calls=%fused_computation.12 | convolution fusion | flops 1078460416 | bytes 4194304 | tf_op jit(solution)/shard_map/dot_general | solution.py:277
  127.7 0.7 fusion.27
  128.5 0.7 fusion.30
  129.3 2.4 %collective-permute-done.24 = bf16[512,256]{1,0:T(8,128)(2,1)S(1)} collective-permute-done((bf16[512,256]{1,0:T(8,128)(2,1)}, bf16[512,256]{1,0:T(8,128)(2,1)S(1)}, u32[]{:S(2)}, u32[]{:S(2)}) %collective-permute-start.24) | collective-permute-done | bytes 262176 | tf_op jit(solution)/shard_map/ppermute | solution.py:34
  131.8 2.7 %collective-permute-start.36 = (bf16[2,128,1024]{2,1,0:T(8,128)(2,1)S(1)}, bf16[2,128,1024]{2,1,0:T(8,128)(2,1)S(1)}, u32[]{:S(2)}, u32[]{:S(2)}) collective-permute-start(bf16[2,128,1024]{2,1,0:T(8,128)(2,1)S(1)} %pad_maximum_fusion.4), channel_id=1, source_target_pairs={{1,0},{0,1},{3,2},{2,3},{5,4},{4,5},{7,6},{6,7},{9,8},{8,9},{11,10... | collective-permute-start | bytes 1572872 | tf_op jit(solution)/shard_map/ppermute | solution.py:34
  134.5 1.0 collective-permute-start.28
  135.8 1.3 fusion.15
  137.1 2.2 %collective-permute-start.34 = (bf16[1,128,1024]{2,1,0:T(8,128)(2,1)S(1)}, bf16[1,128,1024]{2,1,0:T(8,128)(2,1)S(1)}, u32[]{:S(2)}, u32[]{:S(2)}) collective-permute-start(bf16[1,128,1024]{2,1,0:T(8,128)(2,1)S(1)} %get-tuple-element.100), channel_id=1, source_target_pairs={{1,0},{0,1},{3,2},{2,3},{5,4},{4,5},{7,6},{6,7},{9,8},{8,9},{11,10... | collective-permute-start | bytes 786440 | tf_op jit(solution)/shard_map/ppermute | solution.py:34
  139.3 0.7 fusion.36
  140.2 1.5 collective-permute-start.31
  141.7 6.4 %collective-permute-done.36 = bf16[2,128,1024]{2,1,0:T(8,128)(2,1)S(1)} collective-permute-done((bf16[2,128,1024]{2,1,0:T(8,128)(2,1)S(1)}, bf16[2,128,1024]{2,1,0:T(8,128)(2,1)S(1)}, u32[]{:S(2)}, u32[]{:S(2)}) %collective-permute-start.36) | collective-permute-done | bytes 524320 | tf_op jit(solution)/shard_map/ppermute | solution.py:34
  148.1 2.6 %collective-permute-start.33 = (bf16[1,128,1024]{2,1,0:T(8,128)(2,1)S(1)}, bf16[1,128,1024]{2,1,0:T(8,128)(2,1)S(1)}, u32[]{:S(2)}, u32[]{:S(2)}) collective-permute-start(bf16[1,128,1024]{2,1,0:T(8,128)(2,1)S(1)} %get-tuple-element.99), channel_id=1, source_target_pairs={{1,0},{0,1},{3,2},{2,3},{5,4},{4,5},{7,6},{6,7},{9,8},{8,9},{11,10... | collective-permute-start | bytes 786440 | tf_op jit(solution)/shard_map/ppermute | solution.py:34
  150.9 2.8 %collective-permute-done.34 = bf16[1,128,1024]{2,1,0:T(8,128)(2,1)S(1)} collective-permute-done((bf16[1,128,1024]{2,1,0:T(8,128)(2,1)S(1)}, bf16[1,128,1024]{2,1,0:T(8,128)(2,1)S(1)}, u32[]{:S(2)}, u32[]{:S(2)}) %collective-permute-start.34) | collective-permute-done | bytes 262176 | tf_op jit(solution)/shard_map/ppermute | solution.py:34
  153.7 2.2 %collective-permute-start.38 = (bf16[128,1024]{1,0:T(8,128)(2,1)S(1)}, bf16[128,1024]{1,0:T(8,128)(2,1)S(1)}, u32[]{:S(2)}, u32[]{:S(2)}) collective-permute-start(bf16[128,1024]{1,0:T(8,128)(2,1)S(1)} %get-tuple-element.114), channel_id=1, source_target_pairs={{8,0},{16,8},{24,16},{0,24},{9,1},{17,9},{25,17},{1,25},{10,2},{18... | collective-permute-start | bytes 786440 | tf_op jit(solution)/shard_map/ppermute | solution.py:34
  156.1 11.0 %collective-permute-done.29 = bf16[256,1024]{1,0:T(8,128)(2,1)S(1)} collective-permute-done((bf16[256,1024]{1,0:T(8,128)(2,1)S(1)}, bf16[256,1024]{1,0:T(8,128)(2,1)S(1)}, u32[]{:S(2)}, u32[]{:S(2)}) %collective-permute-start.29) | collective-permute-done | bytes 524320 | tf_op jit(solution)/shard_map/ppermute | solution.py:34
  167.1 0.8 fusion.45
  167.9 0.8 collective-permute-start.30
  168.8 1.5 collective-permute-start.32
  170.3 7.2 %collective-permute-done.35 = bf16[128,1024]{1,0:T(8,128)(2,1)S(1)} collective-permute-done((bf16[128,1024]{1,0:T(8,128)(2,1)S(1)}, bf16[128,1024]{1,0:T(8,128)(2,1)S(1)}, u32[]{:S(2)}, u32[]{:S(2)}) %collective-permute-start.35) | collective-permute-done | bytes 262176 | tf_op jit(solution)/shard_map/ppermute | solution.py:34
  177.8 0.8 pad_maximum_fusion.5
  (145 shorter events, 12.0 us)
Async XLA Ops:
  6.5 59.0 %all-gather.3.cloned.1.call-start = ((), (), s32[]{:S(2)}) async-start(), calls=%async_computation | async-start | bytes 5242880 | tf_op jit(solution)/shard_map/all_gather | solution.py:165
  7.3 117.4 %all-gather.5.cloned.1.call-start = ((), (), s32[]{:S(2)}) async-start(), calls=%async_computation.1 | async-start | bytes 5242880 | tf_op jit(solution)/shard_map/all_gather | solution.py:166
  7.3 15.5 %collective-permute-start.3 = (bf16[128,2048]{1,0:T(8,128)(2,1)}, bf16[128,2048]{1,0:T(8,128)(2,1)S(1)}, u32[]{:S(2)}, u32[]{:S(2)}) collective-permute-start(bf16[128,2048]{1,0:T(8,128)(2,1)} %param.7), channel_id=1, source_target_pairs={{1,0},{0,1},{3,2},{2,3},{5,4},{4,5},{7,6},{6,7},{9,8},{8,9},{11,10... | collective-permute-start | bytes 1572872 | tf_op jit(solution)/shard_map/ppermute | solution.py:34
  10.4 26.9 %collective-permute-start = (bf16[128,2048]{1,0:T(8,128)(2,1)}, bf16[128,2048]{1,0:T(8,128)(2,1)}, u32[]{:S(2)}, u32[]{:S(2)}) collective-permute-start(bf16[128,2048]{1,0:T(8,128)(2,1)} %param.7), channel_id=1, source_target_pairs={{8,0},{16,8},{24,16},{0,24},{9,1},{17,9},{25,17},{1,25},{10,2},{18... | collective-permute-start | bytes 1572872 | tf_op jit(solution)/shard_map/ppermute | solution.py:34
  13.4 27.6 %collective-permute-start.1 = (bf16[128,2048]{1,0:T(8,128)(2,1)}, bf16[128,2048]{1,0:T(8,128)(2,1)S(1)}, u32[]{:S(2)}, u32[]{:S(2)}) collective-permute-start(bf16[128,2048]{1,0:T(8,128)(2,1)} %param.7), channel_id=1, source_target_pairs={{16,0},{24,8},{0,16},{8,24},{17,1},{25,9},{1,17},{9,25},{18,2},{26... | collective-permute-start | bytes 1572872 | tf_op jit(solution)/shard_map/ppermute | solution.py:34
  14.1 27.8 %collective-permute-start.2 = (bf16[128,2048]{1,0:T(8,128)(2,1)}, bf16[128,2048]{1,0:T(8,128)(2,1)}, u32[]{:S(2)}, u32[]{:S(2)}) collective-permute-start(bf16[128,2048]{1,0:T(8,128)(2,1)} %param.7), channel_id=1, source_target_pairs={{24,0},{0,8},{8,16},{16,24},{25,1},{1,9},{9,17},{17,25},{26,2},{2,... | collective-permute-start | bytes 1572872 | tf_op jit(solution)/shard_map/ppermute | solution.py:34
  22.8 24.2 %collective-permute-start.4 = (bf16[128,2048]{1,0:T(8,128)(2,1)S(1)}, bf16[128,2048]{1,0:T(8,128)(2,1)S(1)}, u32[]{:S(2)}, u32[]{:S(2)}) collective-permute-start(bf16[128,2048]{1,0:T(8,128)(2,1)S(1)} %collective-permute-done.3), channel_id=1, source_target_pairs={{8,0},{16,8},{24,16},{0,24},{9,1},{17,9},{25,17},{1,25},{10,2},{18... | collective-permute-start | bytes 1572872 | tf_op jit(solution)/shard_map/ppermute | solution.py:34
  25.8 26.0 %collective-permute-start.6 = (bf16[128,2048]{1,0:T(8,128)(2,1)S(1)}, bf16[128,2048]{1,0:T(8,128)(2,1)}, u32[]{:S(2)}, u32[]{:S(2)}) collective-permute-start(bf16[128,2048]{1,0:T(8,128)(2,1)S(1)} %collective-permute-done.3), channel_id=1, source_target_pairs={{24,0},{0,8},{8,16},{16,24},{25,1},{1,9},{9,17},{17,25},{26,2},{2,... | collective-permute-start | bytes 1572872 | tf_op jit(solution)/shard_map/ppermute | solution.py:34
  30.6 9.2 %copy-start.2 = (f32[2048]{0:T(1024)S(1)}, f32[2048]{0:T(1024)}, u32[]{:S(2)}) copy-start(f32[2048]{0:T(1024)} %param.8) | copy-start | bytes 24580
  30.9 9.0 %copy-start.6 = (bf16[1024,2048]{1,0:T(8,128)(2,1)S(1)}, bf16[1024,2048]{1,0:T(8,128)(2,1)}, u32[]{:S(2)}) copy-start(bf16[1024,2048]{1,0:T(8,128)(2,1)} %fusion.101) | copy-start | bytes 12582916
  31.0 22.1 %copy-start.1 = (bf16[2048,256]{1,0:T(8,128)(2,1)}, bf16[2048,256]{1,0:T(8,128)(2,1)S(1)}, u32[]{:S(2)}) copy-start(bf16[2048,256]{1,0:T(8,128)(2,1)S(1)} %pad_maximum_fusion.1) | copy-start | bytes 3145732
  41.0 10.8 %collective-permute-start.5 = (bf16[128,2048]{1,0:T(8,128)(2,1)S(1)}, bf16[128,2048]{1,0:T(8,128)(2,1)S(1)}, u32[]{:S(2)}, u32[]{:S(2)}) collective-permute-start(bf16[128,2048]{1,0:T(8,128)(2,1)S(1)} %collective-permute-done.1), channel_id=1, source_target_pairs={{1,0},{0,1},{3,2},{2,3},{5,4},{4,5},{7,6},{6,7},{9,8},{8,9},{11,10... | collective-permute-start | bytes 1572872 | tf_op jit(solution)/shard_map/ppermute | solution.py:34
  53.1 2.2 %copy-start.7 = (bf16[1024,2048]{1,0:T(8,128)(2,1)}, bf16[1024,2048]{1,0:T(8,128)(2,1)S(1)}, u32[]{:S(2)}) copy-start(bf16[1024,2048]{1,0:T(8,128)(2,1)S(1)} %fusion.94) | copy-start | bytes 12582916
  55.1 7.5 %copy-start = (bf16[2048,256]{1,0:T(8,128)(2,1)S(1)}, bf16[2048,256]{1,0:T(8,128)(2,1)}, u32[]{:S(2)}) copy-start(bf16[2048,256]{1,0:T(8,128)(2,1)} %pad_maximum_fusion) | copy-start | bytes 3145732
  55.1 3.4 %collective-permute-start.7 = (bf16[512,256]{1,0:T(8,128)(2,1)}, bf16[512,256]{1,0:T(8,128)(2,1)S(1)}, u32[]{:S(2)}, u32[]{:S(2)}) collective-permute-start(bf16[512,256]{1,0:T(8,128)(2,1)} %fusion.63), channel_id=1, source_target_pairs={{32,0},{0,32},{33,1},{1,33},{34,2},{2,34},{35,3},{3,35},{36,4},{4,... | collective-permute-start | bytes 786440 | tf_op jit(solution)/shard_map/ppermute | solution.py:34
  56.6 1.8 collective-permute-start.8
  58.4 4.1 %copy-start.8 = (bf16[1024,2048]{1,0:T(8,128)(2,1)S(1)}, bf16[1024,2048]{1,0:T(8,128)(2,1)}, u32[]{:S(2)}) copy-start(bf16[1024,2048]{1,0:T(8,128)(2,1)} %copy-done.7) | copy-start | bytes 12582916
  61.9 3.6 %collective-permute-start.11 = (f32[8,128]{1,0:T(8,128)S(1)}, f32[8,128]{1,0:T(8,128)S(1)}, u32[]{:S(2)}, u32[]{:S(2)}) collective-permute-start(f32[8,128]{1,0:T(8,128)S(1)} %add.157), channel_id=1, source_target_pairs={{64,0},{0,64},{65,1},{1,65},{66,2},{2,66},{67,3},{3,67},{68,4},{4,... | collective-permute-start | bytes 12296 | tf_op jit(solution)/shard_map/ppermute | solution.py:34
  63.2 9.0 %collective-permute-start.9 = (bf16[512,256]{1,0:T(8,128)(2,1)S(1)}, bf16[512,256]{1,0:T(8,128)(2,1)S(1)}, u32[]{:S(2)}, u32[]{:S(2)}) collective-permute-start(bf16[512,256]{1,0:T(8,128)(2,1)S(1)} %fusion.66), channel_id=1, source_target_pairs={{32,0},{0,32},{33,1},{1,33},{34,2},{2,34},{35,3},{3,35},{36,4},{4,... | collective-permute-start | bytes 786440 | tf_op jit(solution)/shard_map/ppermute | solution.py:34
  63.3 8.9 %collective-permute-start.10 = (bf16[512,256]{1,0:T(8,128)(2,1)}, bf16[512,256]{1,0:T(8,128)(2,1)S(1)}, u32[]{:S(2)}, u32[]{:S(2)}) collective-permute-start(bf16[512,256]{1,0:T(8,128)(2,1)} %add_convert_fusion.3), channel_id=1, source_target_pairs={{64,0},{0,64},{65,1},{1,65},{66,2},{2,66},{67,3},{3,67},{68,4},{4,... | collective-permute-start | bytes 786440 | tf_op jit(solution)/shard_map/ppermute | solution.py:34
  65.5 3.9 %copy-start.9 = (bf16[1024,2048]{1,0:T(8,128)(2,1)S(1)}, bf16[1024,2048]{1,0:T(8,128)(2,1)}, u32[]{:S(2)}) copy-start(bf16[1024,2048]{1,0:T(8,128)(2,1)} %copy-done.7) | copy-start | bytes 12582916
  72.3 4.6 %collective-permute-start.15 = (bf16[1024,256]{1,0:T(8,128)(2,1)S(1)}, bf16[1024,256]{1,0:T(8,128)(2,1)S(1)}, u32[]{:S(2)}, u32[]{:S(2)}) collective-permute-start(bf16[1024,256]{1,0:T(8,128)(2,1)S(1)} %convolution_convert_fusion.1), channel_id=1, source_target_pairs={{32,0},{0,32},{33,1},{1,33},{34,2},{2,34},{35,3},{3,35},{36,4},{4,... | collective-permute-start | bytes 1572872 | tf_op jit(solution)/shard_map/ppermute | solution.py:34
  72.3 4.6 %copy-start.11 = (bf16[8192,256]{1,0:T(8,128)(2,1)S(1)}, bf16[8192,256]{1,0:T(8,128)(2,1)}, u32[]{:S(2)}) copy-start(bf16[8192,256]{1,0:T(8,128)(2,1)} %all-gather.3.cloned.1.call-done) | copy-start | bytes 12582916
  73.5 7.3 %copy-start.5 = (bf16[2,512,128]{2,1,0:T(8,128)(2,1)}, bf16[2,512,128]{2,1,0:T(8,128)(2,1)S(1)}, u32[]{:S(2)}) copy-start(bf16[2,512,128]{2,1,0:T(8,128)(2,1)S(1)} %pad_maximum_fusion.8.m0) | copy-start | bytes 786436
  73.5 18.7 %collective-permute-start.12 = (bf16[2,512,128]{2,1,0:T(8,128)(2,1)S(1)}, bf16[2,512,128]{2,1,0:T(8,128)(2,1)S(1)}, u32[]{:S(2)}, u32[]{:S(2)}) collective-permute-start(bf16[2,512,128]{2,1,0:T(8,128)(2,1)S(1)} %pad_maximum_fusion.8.m0), channel_id=1, source_target_pairs={{2,0},{4,2},{6,4},{0,6},{3,1},{5,3},{7,5},{1,7},{10,8},{12,10},{14... | collective-permute-start | bytes 786440 | tf_op jit(solution)/shard_map/ppermute | solution.py:34
  74.0 24.0 %collective-permute-start.13 = (bf16[2,512,128]{2,1,0:T(8,128)(2,1)S(1)}, bf16[2,512,128]{2,1,0:T(8,128)(2,1)S(1)}, u32[]{:S(2)}, u32[]{:S(2)}) collective-permute-start(bf16[2,512,128]{2,1,0:T(8,128)(2,1)S(1)} %pad_maximum_fusion.8.m0), channel_id=1, source_target_pairs={{4,0},{6,2},{0,4},{2,6},{5,1},{7,3},{1,5},{3,7},{12,8},{14,10},{8,... | collective-permute-start | bytes 786440 | tf_op jit(solution)/shard_map/ppermute | solution.py:34
  74.2 27.2 %collective-permute-start.14 = (bf16[2,512,128]{2,1,0:T(8,128)(2,1)S(1)}, bf16[2,512,128]{2,1,0:T(8,128)(2,1)S(1)}, u32[]{:S(2)}, u32[]{:S(2)}) collective-permute-start(bf16[2,512,128]{2,1,0:T(8,128)(2,1)S(1)} %pad_maximum_fusion.8.m0), channel_id=1, source_target_pairs={{6,0},{0,2},{2,4},{4,6},{7,1},{1,3},{3,5},{5,7},{14,8},{8,10},{10,... | collective-permute-start | bytes 786440 | tf_op jit(solution)/shard_map/ppermute | solution.py:34
  76.8 4.0 %collective-permute-start.16 = (bf16[1024,256]{1,0:T(8,128)(2,1)S(1)}, bf16[1024,256]{1,0:T(8,128)(2,1)S(1)}, u32[]{:S(2)}, u32[]{:S(2)}) collective-permute-start(bf16[1024,256]{1,0:T(8,128)(2,1)S(1)} %convolution_convert_fusion), channel_id=1, source_target_pairs={{32,0},{0,32},{33,1},{1,33},{34,2},{2,34},{35,3},{3,35},{36,4},{4,... | collective-permute-start | bytes 1572872 | tf_op jit(solution)/shard_map/ppermute | solution.py:34
  78.1 23.3 %collective-permute-start.17 = (bf16[1024,256]{1,0:T(8,128)(2,1)S(1)}, bf16[1024,256]{1,0:T(8,128)(2,1)S(1)}, u32[]{:S(2)}, u32[]{:S(2)}) collective-permute-start(bf16[1024,256]{1,0:T(8,128)(2,1)S(1)} %fusion.26), channel_id=1, source_target_pairs={{64,0},{0,64},{65,1},{1,65},{66,2},{2,66},{67,3},{3,67},{68,4},{4,... | collective-permute-start | bytes 1572872 | tf_op jit(solution)/shard_map/ppermute | solution.py:34
  80.9 22.3 %collective-permute-start.18 = (bf16[2,512,128]{2,1,0:T(8,128)(2,1)S(1)}, bf16[2,512,128]{2,1,0:T(8,128)(2,1)S(1)}, u32[]{:S(2)}, u32[]{:S(2)}) collective-permute-start(bf16[2,512,128]{2,1,0:T(8,128)(2,1)S(1)} %pad_maximum_fusion.8.m0), channel_id=1, source_target_pairs={{32,0},{0,32},{33,1},{1,33},{34,2},{2,34},{35,3},{3,35},{36,4},{4,... | collective-permute-start | bytes 786440 | tf_op jit(solution)/shard_map/ppermute | solution.py:34
  92.2 11.6 %copy-start.13 = (bf16[2,512,128]{2,1,0:T(8,128)(2,1)}, bf16[2,512,128]{2,1,0:T(8,128)(2,1)S(1)}, u32[]{:S(2)}) copy-start(bf16[2,512,128]{2,1,0:T(8,128)(2,1)S(1)} %collective-permute-done.12.m1) | copy-start | bytes 786436
  97.9 5.8 %copy-start.14 = (bf16[2,512,128]{2,1,0:T(8,128)(2,1)}, bf16[2,512,128]{2,1,0:T(8,128)(2,1)S(1)}, u32[]{:S(2)}) copy-start(bf16[2,512,128]{2,1,0:T(8,128)(2,1)S(1)} %collective-permute-done.13.m2) | copy-start | bytes 786436
  101.4 2.4 %copy-start.15 = (bf16[2,512,128]{2,1,0:T(8,128)(2,1)}, bf16[2,512,128]{2,1,0:T(8,128)(2,1)S(1)}, u32[]{:S(2)}) copy-start(bf16[2,512,128]{2,1,0:T(8,128)(2,1)S(1)} %collective-permute-done.14.m3) | copy-start | bytes 786436
  101.4 2.4 %copy-start.12 = (bf16[1024,256]{1,0:T(8,128)(2,1)}, bf16[1024,256]{1,0:T(8,128)(2,1)S(1)}, u32[]{:S(2)}) copy-start(bf16[1024,256]{1,0:T(8,128)(2,1)S(1)} %collective-permute-done.17.far0.far1) | copy-start | bytes 1572868
  101.4 1.7 collective-permute-start.19
  101.5 1.9 %collective-permute-start.20 = (bf16[2,512,128]{2,1,0:T(8,128)(2,1)S(1)}, bf16[2,512,128]{2,1,0:T(8,128)(2,1)S(1)}, u32[]{:S(2)}, u32[]{:S(2)}) collective-permute-start(bf16[2,512,128]{2,1,0:T(8,128)(2,1)S(1)} %collective-permute-done.13.m2), channel_id=1, source_target_pairs={{32,0},{0,32},{33,1},{1,33},{34,2},{2,34},{35,3},{3,35},{36,4},{4,... | collective-permute-start | bytes 786440 | tf_op jit(solution)/shard_map/ppermute | solution.py:34
  102.0 1.8 collective-permute-start.21
  103.1 0.7 copy-start.16
  103.1 0.8 copy-start.17
  103.4 0.7 copy-start.18
  104.1 0.7 copy-start.19
  113.9 10.4 %copy-start.4 = (bf16[2,2,128,256]{3,2,1,0:T(8,128)(2,1)S(1)}, bf16[2,2,128,256]{3,2,1,0:T(8,128)(2,1)}, u32[]{:S(2)}) copy-start(bf16[2,2,128,256]{3,2,1,0:T(8,128)(2,1)} %shard_map.73) | copy-start | bytes 786436
  114.0 8.8 %collective-permute-start.22 = (bf16[512,256]{1,0:T(8,128)(2,1)}, bf16[512,256]{1,0:T(8,128)(2,1)S(1)}, u32[]{:S(2)}, u32[]{:S(2)}) collective-permute-start(bf16[512,256]{1,0:T(8,128)(2,1)} %bitcast.120), channel_id=1, source_target_pairs={{64,0},{0,64},{65,1},{1,65},{66,2},{2,66},{67,3},{3,67},{68,4},{4,... | collective-permute-start | bytes 786440 | tf_op jit(solution)/shard_map/ppermute | solution.py:34
  115.4 9.0 %collective-permute-start.25 = (bf16[512,256]{1,0:T(8,128)(2,1)}, bf16[512,256]{1,0:T(8,128)(2,1)S(1)}, u32[]{:S(2)}, u32[]{:S(2)}) collective-permute-start(bf16[512,256]{1,0:T(8,128)(2,1)} %bitcast.121), channel_id=1, source_target_pairs={{32,0},{0,32},{33,1},{1,33},{34,2},{2,34},{35,3},{3,35},{36,4},{4,... | collective-permute-start | bytes 786440 | tf_op jit(solution)/shard_map/ppermute | solution.py:34
  122.8 1.6 collective-permute-start.26
  122.8 8.9 %collective-permute-start.24 = (bf16[512,256]{1,0:T(8,128)(2,1)}, bf16[512,256]{1,0:T(8,128)(2,1)S(1)}, u32[]{:S(2)}, u32[]{:S(2)}) collective-permute-start(bf16[512,256]{1,0:T(8,128)(2,1)} %bitcast.118), channel_id=1, source_target_pairs={{64,0},{0,64},{65,1},{1,65},{66,2},{2,66},{67,3},{3,67},{68,4},{4,... | collective-permute-start | bytes 786440 | tf_op jit(solution)/shard_map/ppermute | solution.py:34
  124.2 11.4 %collective-permute-start.23 = (bf16[512,256]{1,0:T(8,128)(2,1)}, bf16[512,256]{1,0:T(8,128)(2,1)S(1)}, u32[]{:S(2)}, u32[]{:S(2)}) collective-permute-start(bf16[512,256]{1,0:T(8,128)(2,1)} %bitcast.119), channel_id=1, source_target_pairs={{32,0},{0,32},{33,1},{1,33},{34,2},{2,34},{35,3},{3,35},{36,4},{4,... | collective-permute-start | bytes 786440 | tf_op jit(solution)/shard_map/ppermute | solution.py:34
  124.7 3.0 %copy-start.10 = (bf16[1024,2048]{1,0:T(8,128)(2,1)S(1)}, bf16[1024,2048]{1,0:T(8,128)(2,1)}, u32[]{:S(2)}) copy-start(bf16[1024,2048]{1,0:T(8,128)(2,1)} %all-gather.5.cloned.1.call-done) | copy-start | bytes 12582916
  128.5 7.1 %copy-start.3 = (bf16[2,2,128,256]{3,2,1,0:T(8,128)(2,1)S(1)}, bf16[2,2,128,256]{3,2,1,0:T(8,128)(2,1)}, u32[]{:S(2)}) copy-start(bf16[2,2,128,256]{3,2,1,0:T(8,128)(2,1)} %shard_map.74) | copy-start | bytes 786436
  131.7 3.8 %collective-permute-start.27 = (bf16[512,256]{1,0:T(8,128)(2,1)S(1)}, bf16[512,256]{1,0:T(8,128)(2,1)S(1)}, u32[]{:S(2)}, u32[]{:S(2)}) collective-permute-start(bf16[512,256]{1,0:T(8,128)(2,1)S(1)} %collective-permute-done.24), channel_id=1, source_target_pairs={{32,0},{0,32},{33,1},{1,33},{34,2},{2,34},{35,3},{3,35},{36,4},{4,... | collective-permute-start | bytes 786440 | tf_op jit(solution)/shard_map/ppermute | solution.py:34
  131.8 16.3 %collective-permute-start.36 = (bf16[2,128,1024]{2,1,0:T(8,128)(2,1)S(1)}, bf16[2,128,1024]{2,1,0:T(8,128)(2,1)S(1)}, u32[]{:S(2)}, u32[]{:S(2)}) collective-permute-start(bf16[2,128,1024]{2,1,0:T(8,128)(2,1)S(1)} %pad_maximum_fusion.4), channel_id=1, source_target_pairs={{1,0},{0,1},{3,2},{2,3},{5,4},{4,5},{7,6},{6,7},{9,8},{8,9},{11,10... | collective-permute-start | bytes 1572872 | tf_op jit(solution)/shard_map/ppermute | solution.py:34
  134.5 21.5 %collective-permute-start.28 = (bf16[256,1024]{1,0:T(8,128)(2,1)S(1)}, bf16[256,1024]{1,0:T(8,128)(2,1)S(1)}, u32[]{:S(2)}, u32[]{:S(2)}) collective-permute-start(bf16[256,1024]{1,0:T(8,128)(2,1)S(1)} %fusion.30), channel_id=1, source_target_pairs={{8,0},{16,8},{24,16},{0,24},{9,1},{17,9},{25,17},{1,25},{10,2},{18... | collective-permute-start | bytes 1572872 | tf_op jit(solution)/shard_map/ppermute | solution.py:34
  137.1 16.6 %collective-permute-start.34 = (bf16[1,128,1024]{2,1,0:T(8,128)(2,1)S(1)}, bf16[1,128,1024]{2,1,0:T(8,128)(2,1)S(1)}, u32[]{:S(2)}, u32[]{:S(2)}) collective-permute-start(bf16[1,128,1024]{2,1,0:T(8,128)(2,1)S(1)} %get-tuple-element.100), channel_id=1, source_target_pairs={{1,0},{0,1},{3,2},{2,3},{5,4},{4,5},{7,6},{6,7},{9,8},{8,9},{11,10... | collective-permute-start | bytes 786440 | tf_op jit(solution)/shard_map/ppermute | solution.py:34
  140.0 27.1 %collective-permute-start.29 = (bf16[256,1024]{1,0:T(8,128)(2,1)S(1)}, bf16[256,1024]{1,0:T(8,128)(2,1)S(1)}, u32[]{:S(2)}, u32[]{:S(2)}) collective-permute-start(bf16[256,1024]{1,0:T(8,128)(2,1)S(1)} %fusion.36), channel_id=1, source_target_pairs={{24,0},{0,8},{8,16},{16,24},{25,1},{1,9},{9,17},{17,25},{26,2},{2,... | collective-permute-start | bytes 1572872 | tf_op jit(solution)/shard_map/ppermute | solution.py:34
  140.2 27.7 %collective-permute-start.31 = (bf16[128,1024]{1,0:T(8,128)(2,1)S(1)}, bf16[128,1024]{1,0:T(8,128)(2,1)S(1)}, u32[]{:S(2)}, u32[]{:S(2)}) collective-permute-start(bf16[128,1024]{1,0:T(8,128)(2,1)S(1)} %get-tuple-element.112), channel_id=1, source_target_pairs={{16,0},{24,8},{0,16},{8,24},{17,1},{25,9},{1,17},{9,25},{18,2},{26... | collective-permute-start | bytes 786440 | tf_op jit(solution)/shard_map/ppermute | solution.py:34
  148.1 20.7 %collective-permute-start.33 = (bf16[1,128,1024]{2,1,0:T(8,128)(2,1)S(1)}, bf16[1,128,1024]{2,1,0:T(8,128)(2,1)S(1)}, u32[]{:S(2)}, u32[]{:S(2)}) collective-permute-start(bf16[1,128,1024]{2,1,0:T(8,128)(2,1)S(1)} %get-tuple-element.99), channel_id=1, source_target_pairs={{1,0},{0,1},{3,2},{2,3},{5,4},{4,5},{7,6},{6,7},{9,8},{8,9},{11,10... | collective-permute-start | bytes 786440 | tf_op jit(solution)/shard_map/ppermute | solution.py:34
  153.7 16.6 %collective-permute-start.38 = (bf16[128,1024]{1,0:T(8,128)(2,1)S(1)}, bf16[128,1024]{1,0:T(8,128)(2,1)S(1)}, u32[]{:S(2)}, u32[]{:S(2)}) collective-permute-start(bf16[128,1024]{1,0:T(8,128)(2,1)S(1)} %get-tuple-element.114), channel_id=1, source_target_pairs={{8,0},{16,8},{24,16},{0,24},{9,1},{17,9},{25,17},{1,25},{10,2},{18... | collective-permute-start | bytes 786440 | tf_op jit(solution)/shard_map/ppermute | solution.py:34
  156.0 14.3 %collective-permute-start.37 = (bf16[128,1024]{1,0:T(8,128)(2,1)S(1)}, bf16[128,1024]{1,0:T(8,128)(2,1)S(1)}, u32[]{:S(2)}, u32[]{:S(2)}) collective-permute-start(bf16[128,1024]{1,0:T(8,128)(2,1)S(1)} %get-tuple-element.113), channel_id=1, source_target_pairs={{16,0},{24,8},{0,16},{8,24},{17,1},{25,9},{1,17},{9,25},{18,2},{26... | collective-permute-start | bytes 786440 | tf_op jit(solution)/shard_map/ppermute | solution.py:34
  167.1 10.4 %collective-permute-start.35 = (bf16[128,1024]{1,0:T(8,128)(2,1)S(1)}, bf16[128,1024]{1,0:T(8,128)(2,1)S(1)}, u32[]{:S(2)}, u32[]{:S(2)}) collective-permute-start(bf16[128,1024]{1,0:T(8,128)(2,1)S(1)} %fusion.105), channel_id=1, source_target_pairs={{24,0},{0,8},{8,16},{16,24},{25,1},{1,9},{9,17},{17,25},{26,2},{2,... | collective-permute-start | bytes 786440 | tf_op jit(solution)/shard_map/ppermute | solution.py:34
  167.9 9.8 %collective-permute-start.30 = (bf16[128,1024]{1,0:T(8,128)(2,1)S(1)}, bf16[128,1024]{1,0:T(8,128)(2,1)S(1)}, u32[]{:S(2)}, u32[]{:S(2)}) collective-permute-start(bf16[128,1024]{1,0:T(8,128)(2,1)S(1)} %get-tuple-element.111), channel_id=1, source_target_pairs={{16,0},{24,8},{0,16},{8,24},{17,1},{25,9},{1,17},{9,25},{18,2},{26... | collective-permute-start | bytes 786440 | tf_op jit(solution)/shard_map/ppermute | solution.py:34
  168.8 8.9 %collective-permute-start.32 = (bf16[128,1024]{1,0:T(8,128)(2,1)S(1)}, bf16[128,1024]{1,0:T(8,128)(2,1)S(1)}, u32[]{:S(2)}, u32[]{:S(2)}) collective-permute-start(bf16[128,1024]{1,0:T(8,128)(2,1)S(1)} %fusion.102), channel_id=1, source_target_pairs={{1,0},{0,1},{3,2},{2,3},{5,4},{4,5},{7,6},{6,7},{9,8},{8,9},{11,10... | collective-permute-start | bytes 786440 | tf_op jit(solution)/shard_map/ppermute | solution.py:34
Sparse Core Ops, SparseCore 0:
  9.0 47.5 all-gather.2
  58.3 59.8 all-gather.4
